TPU v7x, 32 devices: a whole 2x2x4 slice. The times are simulated.
32 devices in a mesh: dp: 8 (over z, y), kv: 4 (over x, core).
Axes of the slice: x: 2, y: 2, z: 4, core: 2. Of those that a mesh axis runs over, the one named last changes fastest.
Arguments:
- residual_in: bfloat16 [2048, 1536], P(('dp', 'kv')), may hold values from -30 to 30
- queries: bfloat16 [2048, 1536], P('dp'), may hold values from -13 to 13
- key_cache: bfloat16 [24, 4096, 512], P('dp', 'kv'), may hold values from -16 to 16
- value_cache: bfloat16 [24, 4096, 512], P('dp', 'kv'), may hold values from -4 to 4
- cache_lengths: int32 [24], P('dp'), may hold values from 2 to 4096, as said below
- out_weight: bfloat16 [1536, 1536], P('kv'), may hold values from -0.15625 to 0.15625
- norm_gain: float32 [1536], replicated, may hold values from 0.1 to 1.9
- gate_weight: bfloat16 [1536, 6912], P('dp', 'kv'), may hold values from -0.15625 to 0.15625
- up_weight: bfloat16 [1536, 6912], P('dp', 'kv'), may hold values from -0.15625 to 0.15625
- down_weight: bfloat16 [6912, 1536], P('kv', 'dp'), may hold values from -0.078125 to 0.078125
Outputs:
- layer_out: bfloat16 [2048, 1536], P(('dp', 'kv'))
Inputs may be any that keep to these rules, and one draw needn't show every extreme that they name: `cache_lengths`: for the first request of each block of 3 (the prefill span) the length lies between 255 and 4096; for the others between 2 and 4096. In every block of 3 requests some decode request has length exactly 4096.
All inputs are finite; a program needn't handle non-finite values.
Results may differ from a plain program's by a relative error of at most 0.013.
Values may be sent and summed in bfloat16 or wider, within the bound.
No kernel may reach another device: no remote copies, remote signals or barrier semaphores. Data moves between devices by JAX's collectives and lax.ppermute only.
A program may use at most 128 MiB of HBM per device.

v0:
```python
import jax
import jax.numpy as jnp
from jax import lax
from jax.sharding import PartitionSpec as P

H = 24
HD = 64
KVH = 8


def joined(array, axis, join):
    gathered = jax.tree.map(
        lambda a, kind: lax.all_gather(a.astype(kind), axis),
        array,
        (jnp.bfloat16, jnp.bfloat16, jnp.bfloat16),
    )

    def take(source):
        return jax.tree.map(
            lambda a, own: lax.dynamic_index_in_dim(a, source, 0, False).astype(own.dtype),
            gathered,
            array,
        )

    return lax.fori_loop(
        1, lax.axis_size(axis), lambda source, state: join(state, take(source)), take(0)
    )


def partials(query_rows, keys, values, lengths, first_key):
    row_count = query_rows.shape[0]
    request_count = keys.shape[0]
    slab_width = keys.shape[1]
    head_groups = keys.shape[2] // HD
    group_size = H // KVH
    span_rows = row_count - (request_count - 1)
    query_heads = query_rows.reshape(row_count, head_groups, group_size, HD).transpose(1, 0, 2, 3)
    key_heads = keys.reshape(request_count, slab_width, head_groups, HD).transpose(2, 0, 1, 3)
    value_heads = values.reshape(request_count, slab_width, head_groups, HD).transpose(2, 0, 1, 3)
    score_scale = HD ** (-0.5)
    key_place = first_key + jnp.arange(slab_width, dtype=jnp.int32)
    limits = jnp.concatenate(
        [lengths[0] - span_rows + jnp.arange(span_rows, dtype=jnp.int32), lengths[1:] - 1]
    )
    usable = (key_place[None, :] <= limits[:, None])[:, None, :]

    def one_group(operands):
        query_group, key_group, value_group = operands
        score_first = jnp.einsum(
            "tcd,pd->tcp", query_group[:span_rows], key_group[0], preferred_element_type=jnp.float32
        )
        score_rest = jnp.einsum(
            "rcd,rpd->rcp",
            query_group[span_rows:],
            key_group[1:],
            preferred_element_type=jnp.float32,
        )
        scores = jnp.concatenate([score_first, score_rest], 0) * score_scale
        top_score = jnp.max(jnp.where(usable, scores, -1e30), axis=-1)
        weights = jnp.where(usable, jnp.exp(scores - top_score[..., None]), 0.0)
        weight_sum = jnp.sum(weights, axis=-1)
        weight_low = weights.astype(jnp.bfloat16)
        acc_first = jnp.einsum(
            "tcp,pd->tcd",
            weight_low[:span_rows],
            value_group[0],
            preferred_element_type=jnp.float32,
        )
        acc_rest = jnp.einsum(
            "rcp,rpd->rcd",
            weight_low[span_rows:],
            value_group[1:],
            preferred_element_type=jnp.float32,
        )
        return (top_score, weight_sum, jnp.concatenate([acc_first, acc_rest], 0))

    tops, sums, accs = lax.map(one_group, (query_heads, key_heads, value_heads))
    head_count = head_groups * group_size
    return (
        tops.transpose(1, 0, 2).reshape(row_count, head_count),
        sums.transpose(1, 0, 2).reshape(row_count, head_count),
        accs.transpose(1, 0, 2, 3).reshape(row_count, head_count * HD),
    )


def combine(earlier, later):
    joined_top = jnp.maximum(earlier[0], later[0])
    scale_first = jnp.exp(earlier[0] - joined_top)
    scale_second = jnp.exp(later[0] - joined_top)
    weight_sum = earlier[1] * scale_first + later[1] * scale_second
    weighted = earlier[2] * jnp.repeat(scale_first, HD, axis=-1) + later[2] * jnp.repeat(
        scale_second, HD, axis=-1
    )
    return (joined_top, weight_sum, weighted)


def per_device(
    residual_in,
    queries,
    key_cache,
    value_cache,
    cache_lengths,
    out_weight,
    norm_gain,
    gate_weight,
    up_weight,
    down_weight,
):
    kv_index = lax.axis_index("kv")
    slab_width = key_cache.shape[1]
    head_width = out_weight.shape[0]
    rows_dev = residual_in.shape[0]
    top_here, sum_here, acc_here = partials(
        queries, key_cache, value_cache, cache_lengths, kv_index * slab_width
    )
    top_all, sum_all, acc_all = joined((top_here, sum_here, acc_here), "kv", combine)
    attended_all = (acc_all / jnp.repeat(sum_all, HD, axis=-1)).astype(jnp.bfloat16)
    attended = lax.dynamic_slice_in_dim(attended_all, kv_index * head_width, head_width, 1)
    mixed = lax.psum_scatter(
        jnp.dot(attended, out_weight, preferred_element_type=jnp.float32).astype(jnp.bfloat16),
        "kv",
        scatter_dimension=0,
        tiled=True,
    ).astype(jnp.float32)
    residual = (residual_in.astype(jnp.float32) + mixed).astype(jnp.bfloat16)
    wide = residual.astype(jnp.float32)
    normed = (
        wide * lax.rsqrt(jnp.mean(wide * wide, axis=-1, keepdims=True) + 1e-05) * norm_gain
    ).astype(jnp.bfloat16)
    features = lax.all_gather(normed, "kv", axis=0, tiled=True)
    gate_sum = jnp.dot(
        features,
        lax.all_gather(gate_weight, "dp", axis=0, tiled=True),
        preferred_element_type=jnp.float32,
    )
    up_sum = jnp.dot(
        features,
        lax.all_gather(up_weight, "dp", axis=0, tiled=True),
        preferred_element_type=jnp.float32,
    )
    hidden = (jax.nn.silu(gate_sum) * up_sum).astype(jnp.bfloat16)
    unit_terms = jnp.dot(
        hidden,
        lax.all_gather(down_weight, "dp", axis=1, tiled=True),
        preferred_element_type=jnp.float32,
    )
    summed_all = lax.psum(unit_terms.astype(jnp.bfloat16), "kv").astype(jnp.float32)
    mlp_rows = lax.dynamic_slice_in_dim(summed_all, kv_index * rows_dev, rows_dev, 0)
    return (wide + mlp_rows).astype(jnp.bfloat16)


def solution(mesh):
    placed = (
        P(("dp", "kv"), None),
        P("dp", None),
        P("dp", "kv", None),
        P("dp", "kv", None),
        P("dp"),
        P("kv", None),
        P(),
        P("dp", "kv"),
        P("dp", "kv"),
        P("kv", "dp"),
    )
    return jax.shard_map(
        per_device, mesh=mesh, in_specs=placed, out_specs=P(("dp", "kv"), None), check_vma=False
    )
```

profile of v0, /device:TPU:0, one launch (start us, length us, event | category | flops | bytes accessed | tf_op | source)
XLA Modules:
  0.0 471.3 jit_solution(14770817926608432638)
XLA Ops:
  7.4 4.8 %copy.48 = bf16[3,1024,512]{1,2,0:T(8,128)(2,1)} copy(bf16[3,1024,512]{2,1,0:T(8,128)(2,1)} %param.17) | data formatting | bytes 6291456 | tf_op args[3]
  12.2 4.7 %copy.47 = bf16[3,1024,512]{1,2,0:T(8,128)(2,1)} copy(bf16[3,1024,512]{2,1,0:T(8,128)(2,1)} %param.16) | data formatting | bytes 6291456 | tf_op args[2]
  17.4 77.1 %while.35 = (s32[]{:T(128)}, bf16[8,256,3]{1,2,0:T(4,128)(2,1)S(1)}, bf16[8,256,3]{1,2,0:T(4,128)(2,1)S(1)}, bf16[8,256,3,64]{1,3,2,0:T(8,128)(2,1)}, bf16[8,256...) while((s32[]{:T(128)}, ...), condition=%wide.region_3.4_spmd.clone, body=%wide.region_0.3_spmd.clone.sunk | while | flops 209648128 | bytes 28724916 | solution.py:77
  17.4 1.2 dynamic-slice_bitcast_fusion.10
  18.6 2.3 fusion.53
  21.5 2.7 select_reduce_fusion.2
  24.2 1.1 fusion.54
  26.3 0.7 fusion.57
  27.0 1.2 dynamic-slice_bitcast_fusion.10
  28.2 2.3 fusion.53
  31.1 2.7 select_reduce_fusion.2
  33.8 1.1 fusion.54
  36.7 1.2 dynamic-slice_bitcast_fusion.10
  37.8 2.3 fusion.53
  40.8 2.7 select_reduce_fusion.2
  43.5 1.1 fusion.54
  46.3 1.2 dynamic-slice_bitcast_fusion.10
  47.5 2.3 fusion.53
  50.4 2.7 select_reduce_fusion.2
  53.1 1.1 fusion.54
  56.0 1.2 dynamic-slice_bitcast_fusion.10
  57.1 2.3 fusion.53
  60.0 2.7 select_reduce_fusion.2
  62.8 1.1 fusion.54
  65.6 1.2 dynamic-slice_bitcast_fusion.10
  66.8 2.3 fusion.53
  69.7 2.7 select_reduce_fusion.2
  72.4 1.1 fusion.54
  74.5 0.7 fusion.57
  75.2 1.2 dynamic-slice_bitcast_fusion.10
  76.4 2.3 fusion.53
  79.3 2.7 select_reduce_fusion.2
  82.0 1.1 fusion.54
  84.1 0.7 fusion.57
  84.9 1.2 dynamic-slice_bitcast_fusion.10
  86.1 2.3 fusion.53
  89.0 2.7 select_reduce_fusion.2
  91.7 1.1 fusion.54
  93.8 0.7 fusion.57
  94.5 2.3 copy.51
  97.0 6.2 %all_gather.25 = bf16[4,256,24]{1,2,0:T(8,128)(2,1)S(1)} all-gather(bf16[1,256,24]{1,2,0:T(8,128)(2,1)S(1)} %convert_element_type.149), channel_id=1, replica_groups=mesh['dp'=8,'kv'=4] {'kv'}, dimensions={0}, use_global_device_ids=true | all-gather | bytes 61440 | tf_op jit(solution)/shard_map/all_gather | solution.py:13
  103.1 5.5 %all_gather.24 = bf16[4,256,24]{1,2,0:T(8,128)(2,1)S(1)} all-gather(bf16[1,256,24]{1,2,0:T(8,128)(2,1)S(1)} %convert_element_type.144), channel_id=1, replica_groups=mesh['dp'=8,'kv'=4] {'kv'}, dimensions={0}, use_global_device_ids=true | all-gather | bytes 61440 | tf_op jit(solution)/shard_map/all_gather | solution.py:13
  108.6 19.6 %all-gather.5.cloned.1.call-done = bf16[4,256,1536]{2,1,0:T(8,128)(2,1)} async-done(((bf16[1,256,1536]{2,1,0:T(8,128)(2,1)}), bf16[4,256,1536]{2,1,0:T(8,128)(2,1)}) %all-gather.5.cloned.1.call-update) | async-done | bytes 3145744 | tf_op jit(solution)/shard_map/all_gather | solution.py:13
  128.2 1.3 fusion.16
  129.5 1.6 copy.52
  131.2 12.8 %while.34 = (s32[]{:T(128)}, f32[256,24]{0,1:T(8,128)S(1)}, f32[256,24]{0,1:T(8,128)S(1)}, f32[256,1536]{0,1:T(8,128)}, bf16[4,256,24]{1,2,0:T(8,128)(2,1)S(1)},...) while((s32[]{:T(128)}, f32[256,24]{0,1:T(8,128)S(1)}, ...), condition=%wide.region_5.6_spmd, body=%wide.region_4.5_spmd.sunk | while | flops 1622021 | bytes 7299223 | solution.py:25
  131.2 1.2 constant_dynamic-slice_fusion.2
  132.7 2.8 fusion.48
  135.5 1.2 constant_dynamic-slice_fusion.2
  136.9 2.8 fusion.48
  139.8 1.2 constant_dynamic-slice_fusion.2
  141.2 2.8 fusion.48
  144.2 2.6 convolution_convert_fusion
  148.5 21.6 %reduce-scatter.2.cloned.1.call-done = bf16[64,1536]{1,0:T(8,128)(2,1)} async-done(((bf16[256,1536]{1,0:T(8,128)(2,1)}), bf16[64,1536]{1,0:T(8,128)(2,1)}) %reduce-scatter.2.cloned.1.call-update) | async-done | bytes 196624 | tf_op jit(solution)/shard_map/reduce_scatter | solution.py:119
  170.2 1.1 fusion.17
  171.3 1.0 fusion.19
  172.3 8.4 %all_gather.27 = bf16[256,1536]{1,0:T(8,128)(2,1)S(1)} all-gather(bf16[64,1536]{1,0:T(8,128)(2,1)S(1)} %fusion.19), channel_id=1, replica_groups=mesh['dp'=8,'kv'=4] {'kv'}, dimensions={0}, use_global_device_ids=true | all-gather | bytes 983040 | tf_op jit(solution)/shard_map/all_gather | solution.py:130
  180.7 58.1 %all-gather.7.cloned.1.call-done = bf16[1536,1728]{1,0:T(8,128)(2,1)} async-done(((bf16[192,1728]{1,0:T(8,128)(2,1)}), bf16[1536,1728]{1,0:T(8,128)(2,1)}) %all-gather.7.cloned.1.call-update) | async-done | bytes 5308432 | tf_op jit(solution)/shard_map/all_gather | solution.py:133
  238.8 6.0 %fusion.28 = f32[256,1728]{0,1:T(8,128)} fusion(bf16[256,1536]{1,0:T(8,128)(2,1)S(1)} %all_gather.27, bf16[1536,1728]{1,0:T(8,128)(2,1)} %all-gather.7.cloned.1.call-done), kind=kOutput, calls=%fused_computation.65 | convolution fusion | flops 1358954496 | bytes 7864320 | tf_op jit(solution)/shard_map/dot_general | solution.py:131
  244.9 83.6 %all-gather.11.cloned.1.call-done = bf16[1728,1536]{0,1:T(8,128)(2,1)} async-done(((bf16[1728,192]{0,1:T(8,128)(2,1)}), bf16[1728,1536]{0,1:T(8,128)(2,1)}) %all-gather.11.cloned.1.call-update) | async-done | bytes 5308432 | tf_op jit(solution)/shard_map/all_gather | solution.py:144
  328.5 89.7 %all-gather.9.cloned.1.call-done = bf16[1536,1728]{1,0:T(8,128)(2,1)} async-done(((bf16[192,1728]{1,0:T(8,128)(2,1)}), bf16[1536,1728]{1,0:T(8,128)(2,1)}) %all-gather.9.cloned.1.call-update) | async-done | bytes 5308432 | tf_op jit(solution)/shard_map/all_gather | solution.py:138
  418.1 11.2 %convolution_convert_fusion.1 = bf16[256,1536]{1,0:T(8,128)(2,1)} fusion(bf16[1728,1536]{0,1:T(8,128)(2,1)} %all-gather.11.cloned.1.call-done, bf16[256,1536]{1,0:T(8,128)(2,1)S(1)} %all_gather.27, bf16[1536,1728]{1,0:T(8,128)(2,1)} %all-gather.9.cloned.1.call-done, f32[256,1728]{0,1:T(8,128)} %fusion.28), kind=kOutput, calls=%fused_computation.39 | convolution fusion | flops 2720956416 | bytes 13959168 | tf_op jit(solution)/shard_map/dot_general | solution.py:142
  429.3 33.0 %all-reduce.2.cloned.1.call-done = bf16[256,1536]{1,0:T(8,128)(2,1)} async-done(((bf16[256,1536]{1,0:T(8,128)(2,1)}), bf16[256,1536]{1,0:T(8,128)(2,1)}) %all-reduce.2.cloned.1.call-update) | async-done | bytes 786448 | tf_op jit(solution)/shard_map/psum | solution.py:147
  462.3 1.7 fusion.20
  (152 shorter events, 18.7 us)
Async XLA Ops:
  7.4 136.8 %copy-start = (bf16[384,1536]{1,0:T(8,128)(2,1)S(1)}, bf16[384,1536]{1,0:T(8,128)(2,1)}, u32[]{:S(2)}) copy-start(bf16[384,1536]{1,0:T(8,128)(2,1)} %param.19) | copy-start | bytes 3538948
  7.4 120.9 %all-gather.5.cloned.1.call-start = ((), (), s32[]{:S(2)}) async-start(), calls=%async_computation.1 | async-start | bytes 3932160 | tf_op jit(solution)/shard_map/all_gather | solution.py:13
  12.2 4.7 %copy-start.4 = (bf16[256,1536]{1,0:T(8,128)(2,1)S(1)}, bf16[256,1536]{1,0:T(8,128)(2,1)}, u32[]{:S(2)}) copy-start(bf16[256,1536]{1,0:T(8,128)(2,1)} %param.15) | copy-start | bytes 2359300
  12.2 5.0 %copy-start.6 = (s32[3]{0:T(128)S(1)}, s32[3]{0:T(128)}, u32[]{:S(2)}) copy-start(s32[3]{0:T(128)} %param.18) | copy-start | bytes 40
  21.1 3.1 copy-start.1
  30.7 3.1 copy-start.1
  40.4 3.1 copy-start.1
  50.0 3.1 copy-start.1
  59.6 3.1 copy-start.1
  69.3 3.1 copy-start.1
  78.9 3.1 copy-start.1
  88.6 3.1 copy-start.1
  96.9 73.3 %reduce-scatter.2.cloned.1.call-start = ((), (), s32[]{:S(2)}) async-start(), calls=%async_computation.2 | async-start | bytes 983040 | tf_op jit(solution)/shard_map/reduce_scatter | solution.py:119
  144.1 26.0 %copy-start.2 = (bf16[64,1536]{1,0:T(8,128)(2,1)S(1)}, bf16[64,1536]{1,0:T(8,128)(2,1)}, u32[]{:S(2)}) copy-start(bf16[64,1536]{1,0:T(8,128)(2,1)} %param.14) | copy-start | bytes 589828
  144.1 27.1 %copy-start.5 = (f32[1536]{0:T(1024)S(1)}, f32[1536]{0:T(1024)}, u32[]{:S(2)}) copy-start(f32[1536]{0:T(1024)} %param.20) | copy-start | bytes 18436
  146.7 92.1 %all-gather.7.cloned.1.call-start = ((), (), s32[]{:S(2)}) async-start(), calls=%async_computation.3 | async-start | bytes 6193152 | tf_op jit(solution)/shard_map/all_gather | solution.py:133
  147.3 181.2 %all-gather.11.cloned.1.call-start = ((), (), s32[]{:S(2)}) async-start(), calls=%async_computation.5 | async-start | bytes 6193152 | tf_op jit(solution)/shard_map/all_gather | solution.py:144
  147.9 270.2 %all-gather.9.cloned.1.call-start = ((), (), s32[]{:S(2)}) async-start(), calls=%async_computation.4 | async-start | bytes 6193152 | tf_op jit(solution)/shard_map/all_gather | solution.py:138
  148.5 313.8 %all-reduce.2.cloned.1.call-start = ((), (), s32[]{:S(2)}) async-start(), calls=%async_computation.6 | async-start | bytes 1572864 | tf_op jit(solution)/shard_map/psum | solution.py:147
  244.9 217.4 %copy-start.3 = (bf16[64,1536]{1,0:T(8,128)(2,1)S(1)}, bf16[64,1536]{1,0:T(8,128)(2,1)}, u32[]{:S(2)}) copy-start(bf16[64,1536]{1,0:T(8,128)(2,1)} %reduce-scatter.2.cloned.1.call-done) | copy-start | bytes 589828
Sparse Core Ops, SparseCore 0:
  97.0 31.2 all-gather.4
  146.9 23.2 reduce-scatter.1
  429.5 32.7 all-reduce.1
Sparse Core Ops, SparseCore 1:
  149.6 89.1 all-gather.6
  241.1 87.3 all-gather.10
  330.8 87.3 all-gather.8
where the time goes:
time: 472 us; the launch traced here: 471 us
  waiting for transfers between devices  307 us (65%)
  other arithmetic  52 us (11%)
  matrix products  45.7 us (10%)
  local copies, waits for them, and re-layouts  30.9 us (7%)
  blocking collectives  20.1 us (4%)
  between operations  14.9 us (3%)
    all_gather x1, waiting for transfers between devices, per_device(): lax.all_gather(up_weight, 'dp', axis=0, tiled=True)  89.7 us
    all_gather x1, waiting for transfers between devices, per_device(): lax.all_gather(down_weight, 'dp', axis=1, tiled=True)  83.6 us
    all_gather x1, waiting for transfers between devices, per_device(): lax.all_gather(gate_weight, 'dp', axis=0, tiled=True)  58.1 us
    psum x1, waiting for transfers between devices, per_device(): lax.psum(unit_terms.astype(jnp.bfloat16), 'kv').astype(jnp.float32)  33 us
    reduce_max x8, other arithmetic, one_group(): top_score = jnp.max(jnp.where(usable, scores, -1e+30), axis=-1)  21.8 us
    reduce_scatter x1, waiting for transfers between devices, per_device(): lax.psum_scatter(jnp.dot(attended, out_weight, preferred_element_type=jnp...  21.6 us
    all_gather x1, waiting for transfers between devices, joined(): lax.all_gather(a.astype(kind), axis)  19.6 us
    dot_general x8, matrix products, one_group(): jnp.einsum('tcd,pd->tcp', query_group[:span_rows], key_group[0], preferre...  18.5 us
  transfers between devices with their start and end apart: 6, of which 6 were waited for; matrix products, arithmetic and copies ran while one was open for 2% of the time, Pallas kernels for 0%

commit v1 on v0

v1 whole, which is shorter than its diff:
```python
import functools

import jax
import jax.numpy as jnp
from jax import lax
from jax.experimental import pallas as pl
from jax.experimental.pallas import tpu as pltpu
from jax.sharding import PartitionSpec as P

H = 24
HD = 64
KVH = 8
LANES = 128
SUM_HIGH = 32
SUM_LOW = 64
OUTER = 4

VMEM = pl.BlockSpec(memory_space=pltpu.VMEM)
SMEM = pl.BlockSpec(memory_space=pltpu.SMEM)
NT = (((1,), (1,)), ((), ()))
BF16 = jnp.bfloat16
F32 = jnp.float32


def params(mib=48):
    return pltpu.CompilerParams(vmem_limit_bytes=mib * 1024 * 1024)


def iota(shape, dim):
    return lax.broadcasted_iota(jnp.int32, shape, dim)


def dot(a, b):
    return jnp.dot(a, b, preferred_element_type=F32)


def one_hot(condition):
    return jnp.where(condition, 1.0, 0.0).astype(BF16)


def pack_kernel(main, tail, z_ref, gate_ref, up_ref, down_ref, *outs):
    rows = gate_ref.shape[0]
    width = down_ref.shape[1]
    tail_at = OUTER * main
    gate_tail = gate_ref[:, tail_at:]
    up_tail = up_ref[:, tail_at:]
    for shift in range(OUTER):
        target = lax.rem(z_ref[0] + shift, OUTER)
        out, down_out = outs[shift], outs[OUTER + shift]
        column = pl.multiple_of(target * main, LANES)
        out[:, :main] = gate_ref[:, pl.ds(column, main)]
        out[:, main : 2 * main] = up_ref[:, pl.ds(column, main)]
        shape = (OUTER * tail, LANES)
        k, lane = iota(shape, 0), iota(shape, 1)
        pick_gate = one_hot((lane < tail) & (k == lane + target * tail))
        pick_up = one_hot((lane >= tail) & (lane < 2 * tail) & (k == lane - tail + target * tail))
        out[:, 2 * main :] = (dot(gate_tail, pick_gate) + dot(up_tail, pick_up)).astype(BF16)
        down_main = down_ref[pl.ds(pl.multiple_of(target * main, 16), main), :]
        down_tail = down_ref[pl.ds(pl.multiple_of(tail_at + target * tail, 16), tail), :]
        shape = (width, 2 * width)
        k, lane = iota(shape, 0), iota(shape, 1)
        low, high = one_hot(k == lane), one_hot(k == lane - width)
        half = main // 2
        down_out[:half, :] = (dot(down_main[:half], low) + dot(down_main[half:], high)).astype(BF16)
        down_out[half:, :] = dot(down_tail, low).astype(BF16)


def unpack_kernel(main, tail, at_ref, *refs):
    parts = 2 * OUTER
    gate_up, down, out, down_out = refs[:parts], refs[parts : 2 * parts], refs[-2], refs[-1]
    rows = gate_up[0].shape[0]
    width = down[0].shape[1] // 2
    half = main // 2
    out_rows = down_out.shape[0]
    shape = (2 * width, 2 * width)
    k, lane = iota(shape, 0), iota(shape, 1)
    high = at_ref[1]
    for shift in range(OUTER):
        source = lax.rem(at_ref[0] + OUTER - shift, OUTER)
        column = pl.multiple_of(source * 2 * width, LANES)
        top = bottom = end = None
        for part in range(2):
            index = 2 * shift + part
            place = high if part == 0 else 1 - high
            row = pl.multiple_of((source * 2 + place) * rows, 16)
            out[pl.ds(row, rows), :] = gate_up[index][...]
            move = place * width
            inside = (lane >= move) & (lane < move + width)
            pick_top = one_hot(inside & (k == lane - move))
            pick_bottom = one_hot(inside & (k == lane - move + width))
            block = down[index][...]
            a, b, c = dot(block[:half], pick_top), dot(block[:half], pick_bottom), dot(block[half:], pick_top)
            top, bottom, end = (a, b, c) if top is None else (top + a, bottom + b, end + c)
        down_out[:half, pl.ds(column, 2 * width)] = top.astype(BF16)
        down_out[half:main, pl.ds(column, 2 * width)] = bottom.astype(BF16)
        down_out[main : main + tail, pl.ds(column, 2 * width)] = end.astype(BF16)
    down_out[main + tail :, :] = jnp.zeros((out_rows - main - tail, down_out.shape[1]), BF16)


def attention_kernel(at_ref, q_ref, k_ref, v_ref, keep_ref, send_ref, bias, result, stats):
    step = pl.program_id(0)
    rows, block = q_ref.shape
    requests, slab, _ = k_ref.shape
    span = rows - (requests - 1)
    heads = block // HD
    group = H // KVH
    first_key, half_row = at_ref[0], at_ref[1]

    @pl.when(step == 0)
    def _():
        place = first_key + iota((rows, slab), 1)
        limit = at_ref[2] - span + iota((rows, slab), 0)
        bias[...] = jnp.where(place <= limit, 0.0, -1e30)
        stats[...] = jnp.zeros_like(stats)

    lane = iota((1, LANES), 1)
    low_lanes = lane < HD

    def in_half(a):
        return low_lanes if a == 0 else ~low_lanes

    def aligned(h):
        tile = q_ref[:, (h // 2) * LANES : (h // 2 + 1) * LANES].astype(F32) * HD**-0.5
        a = h // group
        if h % 2 != a:
            tile = pltpu.roll(tile, HD, 1)
        return jnp.where(in_half(a), tile, 0.0)

    def placed(value, h):
        return pltpu.roll(value, HD, 1) if h % 2 != h // group else value

    def record(old, h, top, total):
        column = step * heads + h
        high = total.astype(BF16).astype(F32)
        old = jnp.where(lane == column, top, old)
        old = jnp.where(lane == column + SUM_HIGH, high, old)
        return jnp.where(lane == column + SUM_LOW, total - high, old)

    keys = k_ref[0]
    values = [jnp.where(in_half(a), v_ref[0], jnp.ones((), BF16)) for a in range(2)]
    stat = stats[...]
    decode = []
    outs = []
    for h in range(heads):
        a = h // group
        query = aligned(h)
        decode.append(query[rows - 8 :])
        scores = lax.dot_general(query.astype(BF16), keys, NT, preferred_element_type=F32) + bias[...]
        top = jnp.maximum(jnp.max(scores, axis=1, keepdims=True), -1e29).astype(BF16).astype(F32)
        weights = jnp.exp(scores - top).astype(BF16)
        out = dot(weights, values[a])
        total = jnp.where(in_half(a), pltpu.roll(out, HD, 1), out)
        stat = record(stat, h, top, total)
        outs.append(placed(out, h))
        if h % 2 == 1:
            result[:, (h // 2) * LANES : (h // 2 + 1) * LANES] = jnp.where(low_lanes, outs[h - 1], outs[h])
    stats[...] = stat

    sub = iota((16, 1), 0)
    for r in range(1, requests):
        row = rows - requests + r
        query = jnp.zeros((16, LANES), F32)
        for h in range(heads):
            line = decode[h][8 - requests + r : 9 - requests + r]
            query = jnp.where(sub == h, jnp.broadcast_to(line, (16, LANES)), query)
        scores = lax.dot_general(query.astype(BF16), k_ref[r], NT, preferred_element_type=F32)
        usable = first_key + iota((16, slab), 1) < at_ref[2 + r]
        scores = jnp.where(usable, scores, -1e30)
        top = jnp.maximum(jnp.max(scores, axis=1, keepdims=True), -1e29).astype(BF16).astype(F32)
        weights = jnp.exp(scores - top)
        total = jnp.sum(weights, axis=1, keepdims=True)
        out = dot(weights.astype(BF16), v_ref[r])
        line = stats[row : row + 1, :]
        for h in range(heads):
            line = record(line, h, top[h : h + 1], total[h : h + 1])
        stats[row : row + 1, :] = line
        for h in range(1, heads, 2):
            pair = jnp.where(low_lanes, placed(out[h - 1 : h], h - 1), placed(out[h : h + 1], h))
            result[row : row + 1, (h // 2) * LANES : (h // 2 + 1) * LANES] = pair

    quarter = rows // 4
    column = pl.multiple_of(step * block, LANES)
    for ref, which in ((keep_ref, half_row), (send_ref, 1 - half_row)):
        for part in range(2):
            row = pl.multiple_of((2 * part + which) * quarter, 16)
            ref[part * quarter : (part + 1) * quarter, pl.ds(column, block)] = result[
                pl.ds(row, quarter), :
            ].astype(BF16)

    @pl.when(step == pl.num_programs(0) - 1)
    def _():
        for ref, which in ((keep_ref, half_row), (send_ref, 1 - half_row)):
            for part in range(2):
                row = pl.multiple_of((2 * part + which) * quarter, 16)
                ref[part * quarter : (part + 1) * quarter, H * HD :] = stats[pl.ds(row, quarter), :].astype(BF16)


def attention(queries, keys, values, at):
    rows, width = queries.shape
    requests, slab, _ = keys.shape
    block = 2 * (H // KVH) * HD
    half = jax.ShapeDtypeStruct((rows // 2, width + LANES), BF16)
    whole = pl.BlockSpec((rows // 2, width + LANES), lambda g: (0, 0))
    return pl.pallas_call(
        attention_kernel,
        grid=(width // block,),
        in_specs=[
            SMEM,
            pl.BlockSpec((rows, block), lambda g: (0, g)),
            pl.BlockSpec((requests, slab, LANES), lambda g: (0, 0, g)),
            pl.BlockSpec((requests, slab, LANES), lambda g: (0, 0, g)),
        ],
        out_specs=[whole, whole],
        out_shape=[half, half],
        scratch_shapes=[
            pltpu.VMEM((rows, slab), F32),
            pltpu.VMEM((rows, block), F32),
            pltpu.VMEM((rows, LANES), F32),
        ],
        compiler_params=params(),
        cost_estimate=pl.CostEstimate(
            flops=4 * rows * width * slab * 4, bytes_accessed=8 * 1024 * 1024, transcendentals=rows * H * slab
        ),
        name="attention",
    )(at, queries, keys, values)


def expanded(scale, width):
    high = scale.astype(BF16).astype(F32)
    both = (high + pltpu.roll(scale - high, SUM_HIGH, 1)).astype(BF16)
    shape = (LANES, width)
    k, column = iota(shape, 0), iota(shape, 1)
    spread = one_hot(((k & (SUM_HIGH - 1)) == column // HD) & (k < 2 * SUM_HIGH))
    return dot(both, spread)


def merged(first, second, width):
    a, b = first[:, width:].astype(F32), second[:, width:].astype(F32)
    valid = iota((1, LANES), 1) < H
    top = jnp.maximum(a, b)
    scale_a = jnp.where(valid, jnp.exp(a - top), 0.0)
    scale_b = jnp.where(valid, jnp.exp(b - top), 0.0)

    def total(s):
        return pltpu.roll(s, LANES - SUM_HIGH, 1) + pltpu.roll(s, LANES - SUM_LOW, 1)

    return top, total(a) * scale_a + total(b) * scale_b, scale_a, scale_b, valid


def join_kernel(at_ref, own_ref, other_ref, keep_ref, send_ref):
    half, total_width = own_ref.shape
    width = total_width - LANES
    rows = half // 2
    for ref, which in ((send_ref, 1 - at_ref[0]), (keep_ref, at_ref[0])):
        pick = pl.ds(pl.multiple_of(which * rows, 16), rows)
        first, second = own_ref[pick, :], other_ref[pick, :]
        top, total, scale_a, scale_b, valid = merged(first, second, width)
        ref[:, :width] = (
            first[:, :width].astype(F32) * expanded(scale_a, width)
            + second[:, :width].astype(F32) * expanded(scale_b, width)
        ).astype(BF16)
        high = total.astype(BF16).astype(F32)
        stat = jnp.where(valid, top, 0.0)
        stat = stat + pltpu.roll(jnp.where(valid, high, 0.0), SUM_HIGH, 1)
        stat = stat + pltpu.roll(jnp.where(valid, total - high, 0.0), SUM_LOW, 1)
        ref[:, width:] = stat.astype(BF16)


def project_kernel(at_ref, own_ref, other_ref, w0, w1, w2, w3, residual_ref, gain_ref, normed_ref, out_ref, attended):
    rows, total_width = own_ref.shape
    width = total_width - LANES
    first, second = own_ref[...], other_ref[...]
    _, total, scale_a, scale_b, valid = merged(first, second, width)
    inverse = 1.0 / jnp.where(valid, total, 1.0)
    attended[...] = (
        first[:, :width].astype(F32) * expanded(scale_a * inverse, width)
        + second[:, :width].astype(F32) * expanded(scale_b * inverse, width)
    ).astype(BF16)
    mixed = None
    depth = w0.shape[0]
    for flip, weight in enumerate((w0, w1, w2, w3)):
        column = pl.multiple_of((at_ref[0] ^ flip) * depth, LANES)
        term = dot(attended[:, pl.ds(column, depth)], weight[...])
        mixed = term if mixed is None else mixed + term
    residual = (residual_ref[...].astype(F32) + mixed).astype(BF16)
    out_ref[...] = residual
    wide = residual.astype(F32)
    scale = lax.rsqrt(jnp.mean(wide * wide, axis=-1, keepdims=True) + 1e-05)
    normed_ref[...] = (wide * scale * gain_ref[...]).astype(BF16)


def feed_kernel(main, tail, x0, x1, x2, x3, weight_ref, down_ref, keep_ref, send_ref):
    x = jnp.concatenate([x0[...], x1[...], x2[...], x3[...]], 0)
    sums = dot(x, weight_ref[...])

    def silu(v):
        return v / (1.0 + jnp.exp(-v))

    lane = iota((1, LANES), 1)
    end = sums[:, 2 * main :]
    last = silu(end) * pltpu.roll(end, LANES - tail, 1)
    hidden = jnp.concatenate(
        [
            (silu(sums[:, :main]) * sums[:, main : 2 * main]).astype(BF16),
            jnp.where(lane < tail, last, 0.0).astype(BF16),
        ],
        1,
    )
    out = dot(hidden, down_ref[...]).astype(BF16)
    half = out.shape[0] // 2
    keep_ref[...] = out[:half]
    send_ref[...] = out[half:]


def feed(main, tail, parts, weight, down):
    rows, width = parts[0].shape
    half = jax.ShapeDtypeStruct((2 * rows, width), BF16)
    return pl.pallas_call(
        functools.partial(feed_kernel, main, tail),
        in_specs=[VMEM] * 6,
        out_specs=[VMEM] * 2,
        out_shape=[half, half],
        compiler_params=params(),
        cost_estimate=pl.CostEstimate(
            flops=2 * 4 * rows * width * 1408, bytes_accessed=6 * 1024 * 1024, transcendentals=4 * rows * main
        ),
        name="feed",
    )(*parts, weight, down)


def per_device(
    residual_in,
    queries,
    key_cache,
    value_cache,
    cache_lengths,
    out_weight,
    norm_gain,
    gate_weight,
    up_weight,
    down_weight,
):
    dp_size, kv_size = lax.axis_size("dp"), lax.axis_size("kv")
    inner = dp_size // OUTER
    dp_index, kv_index = lax.axis_index("dp"), lax.axis_index("kv")
    z, y = dp_index // inner, dp_index % inner
    units = gate_weight.shape[1]
    main = units // OUTER // LANES * LANES
    tail = units // OUTER - main
    width = residual_in.shape[1]

    def kv_flip(a, bit):
        return lax.ppermute(a, "kv", [(i, i ^ bit) for i in range(kv_size)])

    def z_shift(a, by):
        return lax.ppermute(a, "dp", [(i, (i + by * inner) % dp_size) for i in range(dp_size)])

    def y_flip(a, bit):
        return lax.ppermute(a, "dp", [(i, i ^ bit) for i in range(dp_size)])

    rows = gate_weight.shape[0]
    columns = down_weight.shape[1]
    packed = pl.pallas_call(
        functools.partial(pack_kernel, main, tail),
        in_specs=[SMEM] + [VMEM] * 3,
        out_specs=[VMEM] * (2 * OUTER),
        out_shape=[jax.ShapeDtypeStruct((rows, 2 * main + LANES), BF16)] * OUTER
        + [jax.ShapeDtypeStruct((main // 2 + tail, 2 * columns), BF16)] * OUTER,
        compiler_params=params(),
        name="pack",
    )(z.reshape(1), gate_weight, up_weight, down_weight)

    gate_up = [packed[0]] + [z_shift(packed[s], s) for s in range(1, OUTER)]
    downs = [packed[OUTER]] + [z_shift(packed[OUTER + s], s) for s in range(1, OUTER)]

    def shared(block, axis, folded):
        bit = 1
        while 2 * bit < inner:
            other = y_flip(block, bit)
            upper = (y & bit) > 0
            low, high = jnp.where(upper, other, block), jnp.where(upper, block, other)
            if folded:
                size = low.shape[1] // 2
                block = jnp.concatenate([low[:, :size], high[:, :size], low[:, size:], high[:, size:]], 1)
            else:
                block = jnp.concatenate([low, high], 0)
            bit *= 2
        return [block, y_flip(block, bit)]

    gate_up = [part for block in gate_up for part in shared(block, 0, False)]
    downs = [part for block in downs for part in shared(block, 1, True)]
    unit_rows = (main + tail + LANES - 1) // LANES * LANES
    weight, down = pl.pallas_call(
        functools.partial(unpack_kernel, main, tail),
        in_specs=[SMEM] + [VMEM] * (4 * OUTER),
        out_specs=[VMEM] * 2,
        out_shape=[
            jax.ShapeDtypeStruct((width, 2 * main + LANES), BF16),
            jax.ShapeDtypeStruct((unit_rows, width), BF16),
        ],
        compiler_params=params(),
        name="unpack",
    )(jnp.stack([z, (y >= inner // 2).astype(jnp.int32)]), *gate_up, *downs)

    core, chip = kv_index % 2, kv_index // 2
    at = jnp.concatenate([jnp.stack([kv_index * key_cache.shape[1], core]), cache_lengths])
    keep, send = attention(queries, key_cache, value_cache, at)
    other = kv_flip(send, 1)
    half = jax.ShapeDtypeStruct((keep.shape[0] // 2, keep.shape[1]), BF16)
    keep, send = pl.pallas_call(
        join_kernel,
        in_specs=[SMEM, VMEM, VMEM],
        out_specs=[VMEM, VMEM],
        out_shape=[half, half],
        compiler_params=params(),
        name="join",
    )(chip.reshape(1), keep, other)
    other = kv_flip(send, 2)
    w1, w2 = kv_flip(out_weight, 1), kv_flip(out_weight, 2)
    w3 = kv_flip(w2, 1)
    tokens = jax.ShapeDtypeStruct(residual_in.shape, BF16)
    normed, residual = pl.pallas_call(
        project_kernel,
        in_specs=[SMEM] + [VMEM] * 8,
        out_specs=[VMEM, VMEM],
        out_shape=[tokens, tokens],
        scratch_shapes=[pltpu.VMEM(residual_in.shape, BF16)],
        compiler_params=params(),
        name="project",
    )(kv_index.reshape(1), keep, other, out_weight, w1, w2, w3, residual_in, norm_gain.reshape(1, width))

    def added(a, b):
        return (a.astype(F32) + b.astype(F32)).astype(BF16)

    mlp = None
    for shift in (0, 1, 3, 2):
        here = normed if shift == 0 else z_shift(normed, shift)
        there = kv_flip(here, 2)
        parts = [here, there, kv_flip(here, 1), kv_flip(there, 1)]
        keep, send = feed(main, tail, parts, weight, down)
        both = added(keep, kv_flip(send, 1))
        count = residual_in.shape[0]
        term = added(both[:count], kv_flip(both[count:], 2))
        if shift:
            term = z_shift(term, -shift)
        term = term.astype(F32)
        mlp = term if mlp is None else mlp + term
    return (residual.astype(F32) + mlp).astype(BF16)


def solution(mesh):
    placed = (
        P(("dp", "kv"), None),
        P("dp", None),
        P("dp", "kv", None),
        P("dp", "kv", None),
        P("dp"),
        P("kv", None),
        P(),
        P("dp", "kv"),
        P("dp", "kv"),
        P("kv", "dp"),
    )
    return jax.shard_map(
        per_device, mesh=mesh, in_specs=placed, out_specs=P(("dp", "kv"), None), check_vma=False
    )
```

time: 472 us -> 185 us (0.39)
  waiting for transfers between devices: 307 us -> 74.8 us
  starting transfers between devices: 0.21 us -> 51.5 us
  other arithmetic: 52 us -> 1.49 us
  matrix products: 45.7 us -> 0 us
  Pallas kernels: 0 us -> 34.4 us
  blocking collectives: 20.1 us -> 0 us
  between operations: 14.9 us -> 0.29 us
  local copies, waits for them, and re-layouts: 30.9 us -> 21.7 us
    all_gather x4 -> x0, waiting for transfers between devices: 251 us -> none  [the longest x1 89.7 us: per_device(): lax.all_gather(up_weight, 'dp', axis=0, tiled=True)]
    ppermute x0 -> x45, waiting for transfers between devices: none -> 74.8 us  [the longest x12 44 us: z_shift(): lax.ppermute(a, 'dp', [(i, (i + by * inner) % dp_size) for i in range(dp_...]
    ppermute x0 -> x45, starting transfers between devices: none -> 51.5 us  [the longest x12 27.1 us: z_shift(): lax.ppermute(a, 'dp', [(i, (i + by * inner) % dp_size) for i in range(dp_...]
    dot_general x35 -> x0, matrix products: 45.7 us -> none  [the longest x8 18.5 us: one_group(): jnp.einsum('tcd,pd->tcp', query_group[:span_rows], key_group[0], preferre...]
    pallas_call x0 -> x9, Pallas kernels: none -> 34.4 us  [the longest x1 16.1 us: attention(): pl.pallas_call(attention_kernel, grid=(width // block,), in_specs=[SMEM,...]
    psum x1 -> x0, waiting for transfers between devices: 33 us -> none  [per_device(): lax.psum(unit_terms.astype(jnp.bfloat16), 'kv').astype(jnp.float32)]
    reduce_max x8 -> x0, other arithmetic: 21.8 us -> none  [one_group(): top_score = jnp.max(jnp.where(usable, scores, -1e+30), axis=-1)]
    reduce_scatter x1 -> x0, waiting for transfers between devices: 21.6 us -> none  [per_device(): lax.psum_scatter(jnp.dot(attended, out_weight, preferred_element_type=jnp...]
  transfers between devices with their start and end apart: 6 -> 45, of which waited for: 6 -> 12; matrix products, arithmetic and copies ran while one was open for 2% -> 2% of each run, Pallas kernels for 0% -> 19%
where the time goes in v1:
time: 185 us; the launch traced here: 184 us
  waiting for transfers between devices  74.8 us (40%)
  starting transfers between devices  51.5 us (28%)
  Pallas kernels  34.4 us (19%)
  local copies, waits for them, and re-layouts  21.7 us (12%)
    ppermute x12, waiting for transfers between devices, z_shift(): lax.ppermute(a, 'dp', [(i, (i + by * inner) % dp_size) for i in range(dp_...  44 us
    ppermute x12, starting transfers between devices, z_shift(): lax.ppermute(a, 'dp', [(i, (i + by * inner) % dp_size) for i in range(dp_...  27.1 us
    unnamed x55, local copies, waits for them, and re-layouts  20.9 us
    ppermute x25, waiting for transfers between devices, kv_flip(): return lax.ppermute(a, 'kv', [(i, i ^ bit) for i in range(kv_size)])  16.8 us
    ppermute x25, starting transfers between devices, kv_flip(): return lax.ppermute(a, 'kv', [(i, i ^ bit) for i in range(kv_size)])  16.4 us
    pallas_call x1, Pallas kernels, attention(): pl.pallas_call(attention_kernel, grid=(width // block,), in_specs=[SMEM,...  16.1 us
    ppermute x8, waiting for transfers between devices, y_flip(): return lax.ppermute(a, 'dp', [(i, i ^ bit) for i in range(dp_size)])  13.9 us
    ppermute x8, starting transfers between devices, y_flip(): return lax.ppermute(a, 'dp', [(i, i ^ bit) for i in range(dp_size)])  7.88 us
  transfers between devices with their start and end apart: 45, of which 12 were waited for; matrix products, arithmetic and copies ran while one was open for 2% of the time, Pallas kernels for 19%

profile of v1, /device:TPU:0, one launch (start us, length us, event | category | flops | bytes accessed | tf_op | source)
XLA Modules:
  0.0 184.1 jit_solution(9612279128442323766)
XLA Ops:
  0.0 2.9 %collective-permute-start.3 = (bf16[384,1536]{1,0:T(8,128)(2,1)}, bf16[384,1536]{1,0:T(8,128)(2,1)S(1)}, u32[]{:S(2)}, u32[]{:S(2)}) collective-permute-start(bf16[384,1536]{1,0:T(8,128)(2,1)} %w0.1), channel_id=1, source_target_pairs={{0,2},{1,3},{2,0},{3,1},{4,6},{5,7},{6,4},{7,5},{8,10},{9,11},{10,... | collective-permute-start | bytes 3538952 | tf_op jit(solution)/shard_map/ppermute | solution.py:353
  2.9 1.5 copy.11.down_ref
  4.5 1.1 copy-done.3
  5.6 1.1 copy-done.4
  6.7 1.8 pack.1
  8.4 0.8 copy-done.24
  9.2 0.7 copy-done.25
  9.9 1.6 collective-permute-start.16
  11.5 2.6 %collective-permute-start.18 = (bf16[240,384]{1,0:T(8,128)(2,1)}, bf16[240,384]{1,0:T(8,128)(2,1)}, u32[]{:S(2)}, u32[]{:S(2)}) collective-permute-start(bf16[240,384]{1,0:T(8,128)(2,1)} %get-tuple-element.41), channel_id=1, source_target_pairs={{0,16},{4,20},{8,24},{12,28},{16,0},{20,4},{24,8},{28,12},{1,17},{... | collective-permute-start | bytes 552968 | tf_op jit(solution)/shard_map/ppermute | solution.py:356
  14.1 1.3 collective-permute-start.20
  15.5 4.2 %collective-permute-done.16.refs_10_ = bf16[240,384]{1,0:T(8,128)(2,1)} collective-permute-done((bf16[240,384]{1,0:T(8,128)(2,1)}, bf16[240,384]{1,0:T(8,128)(2,1)}, u32[]{:S(2)}, u32[]{:S(2)}) %collective-permute-start.16) | collective-permute-done | bytes 184352 | tf_op jit(solution)/shard_map/ppermute | solution.py:356
  19.7 6.3 %collective-permute-start.9 = (bf16[192,896]{1,0:T(8,128)(2,1)}, bf16[192,896]{1,0:T(8,128)(2,1)S(1)}, u32[]{:S(2)}, u32[]{:S(2)}) collective-permute-start(bf16[192,896]{1,0:T(8,128)(2,1)} %copy-done.25), channel_id=1, source_target_pairs={{0,8},{4,12},{8,16},{12,20},{16,24},{20,28},{24,0},{28,4},{1,9},{5... | collective-permute-start | bytes 1032200 | tf_op jit(solution)/shard_map/ppermute | solution.py:356
  26.0 1.6 collective-permute-done.18.refs_12_
  27.6 0.7 collective-permute-start.11
  28.3 1.5 collective-permute-start.15
  29.9 1.9 %copy-done.22 = bf16[3,1024,512]{2,1,0:T(8,128)(2,1)S(1)} copy-done((bf16[3,1024,512]{2,1,0:T(8,128)(2,1)S(1)}, bf16[3,1024,512]{2,1,0:T(8,128)(2,1)}, u32[]{:S(2)}) %copy-start.22) | copy-done | bytes 3145752
  31.8 1.1 copy-done.23
  32.9 16.1 %attention.1 = (bf16[128,1664]{1,0:T(8,128)(2,1)S(1)}, bf16[128,1664]{1,0:T(8,128)(2,1)S(1)}) custom-call(s32[5]{0:T(128)S(1)} %pad_add_fusion.at_ref, bf16[256,1536]{1,0:T(8,128)(2,1)S(1)} %copy-done.23, bf16[3,1024,512]{2,1,0:T(8,128)(2,1)S(1)} %copy-done.22, bf16[3,1024,512]{2,1,0:T(8,128)(2,1)} %v_ref.1), custom_call_target="tpu_custom_call" | custom-call | flops 6442450944 | bytes 8388608 | tf_op jit(solution)/shard_map/attention/pallas_call | solution.py:204
  49.0 0.7 copy-done.16
  50.2 5.7 %collective-permute-start.13 = (bf16[192,896]{1,0:T(8,128)(2,1)}, bf16[192,896]{1,0:T(8,128)(2,1)}, u32[]{:S(2)}, u32[]{:S(2)}) collective-permute-start(bf16[192,896]{1,0:T(8,128)(2,1)} %get-tuple-element.38), channel_id=1, source_target_pairs={{0,24},{4,28},{8,0},{12,4},{16,8},{20,12},{24,16},{28,20},{1,25},{... | collective-permute-start | bytes 1032200 | tf_op jit(solution)/shard_map/ppermute | solution.py:356
  56.6 1.3 collective-permute-start.17
  58.4 17.4 %collective-permute-done.13.refs_6_ = bf16[192,896]{1,0:T(8,128)(2,1)} collective-permute-done((bf16[192,896]{1,0:T(8,128)(2,1)}, bf16[192,896]{1,0:T(8,128)(2,1)}, u32[]{:S(2)}, u32[]{:S(2)}) %collective-permute-start.13) | collective-permute-done | bytes 344096 | tf_op jit(solution)/shard_map/ppermute | solution.py:356
  76.9 1.5 collective-permute-start.19
  78.4 4.1 %collective-permute-done.1.other_ref = bf16[64,1664]{1,0:T(8,128)(2,1)S(1)} collective-permute-done((bf16[64,1664]{1,0:T(8,128)(2,1)S(1)}, bf16[64,1664]{1,0:T(8,128)(2,1)S(1)}, u32[]{:S(2)}, u32[]{:S(2)}) %collective-permute-start.1) | collective-permute-done | bytes 213024 | tf_op jit(solution)/shard_map/ppermute | solution.py:353
  83.0 1.5 collective-permute-start.14
  85.0 0.7 reshape.12.gain_ref
  85.7 0.9 copy-done.11
  86.7 3.8 %project.1 = (bf16[64,1536]{1,0:T(8,128)(2,1)}, bf16[64,1536]{1,0:T(8,128)(2,1)S(1)}) custom-call(s32[1]{0:T(128)} %bitcast.at_ref, bf16[64,1664]{1,0:T(8,128)(2,1)S(1)} %get-tuple-element.31.own_ref, bf16[64,1664]{1,0:T(8,128)(2,1)S(1)} %collective-permute-done.1.other_ref, bf16[384,1536]{1,0:T(8,128)(2,1)S(1)} %copy-done.2, ...), custom_call_target="tpu_custom_call" | custom-call | tf_op jit(solution)/shard_map/project/pallas_call | solution.py:422
  90.5 0.7 copy-done.12
  91.3 0.7 copy-done.18
  92.0 2.5 %collective-permute-start.24 = (bf16[64,1536]{1,0:T(8,128)(2,1)}, bf16[64,1536]{1,0:T(8,128)(2,1)S(1)}, u32[]{:S(2)}, u32[]{:S(2)}) collective-permute-start(bf16[64,1536]{1,0:T(8,128)(2,1)} %get-tuple-element.34.x0), channel_id=1, source_target_pairs={{0,8},{4,12},{8,16},{12,20},{16,24},{20,28},{24,0},{28,4},{1,9},{5... | collective-permute-start | bytes 589832 | tf_op jit(solution)/shard_map/ppermute | solution.py:356
  94.5 13.7 %collective-permute-done.21.refs_15_ = bf16[240,384]{1,0:T(8,128)(2,1)S(1)} collective-permute-done((bf16[240,384]{1,0:T(8,128)(2,1)}, bf16[240,384]{1,0:T(8,128)(2,1)S(1)}, u32[]{:S(2)}, u32[]{:S(2)}) %collective-permute-start.21) | collective-permute-done | bytes 184352 | tf_op jit(solution)/shard_map/ppermute | solution.py:359
  108.2 0.7 copy-done.20
  108.9 1.5 collective-permute-start.5
  110.4 2.5 %collective-permute-start.31 = (bf16[64,1536]{1,0:T(8,128)(2,1)}, bf16[64,1536]{1,0:T(8,128)(2,1)S(1)}, u32[]{:S(2)}, u32[]{:S(2)}) collective-permute-start(bf16[64,1536]{1,0:T(8,128)(2,1)} %get-tuple-element.34.x0), channel_id=1, source_target_pairs={{0,24},{4,28},{8,0},{12,4},{16,8},{20,12},{24,16},{28,20},{1,25},{... | collective-permute-start | bytes 589832 | tf_op jit(solution)/shard_map/ppermute | solution.py:356
  112.8 0.7 copy-done.7
  113.6 0.7 copy-done.9
  114.3 1.4 collective-permute-start.38
  115.7 1.5 collective-permute-start.25
  117.2 1.2 collective-permute-start.32
  118.4 8.4 %collective-permute-done.38.x0 = bf16[64,1536]{1,0:T(8,128)(2,1)S(1)} collective-permute-done((bf16[64,1536]{1,0:T(8,128)(2,1)}, bf16[64,1536]{1,0:T(8,128)(2,1)S(1)}, u32[]{:S(2)}, u32[]{:S(2)}) %collective-permute-start.38) | collective-permute-done | bytes 196640 | tf_op jit(solution)/shard_map/ppermute | solution.py:356
  126.9 1.5 collective-permute-start.39
  128.5 1.0 copy-done.8
  129.4 1.0 copy-done.10
  130.4 0.9 copy-done.15
  131.3 0.9 copy-done.17
  132.3 0.9 copy-done.19
  133.2 0.9 copy-done.21
  134.1 5.3 %unpack.1 = (bf16[1536,896]{1,0:T(8,128)(2,1)}, bf16[512,1536]{1,0:T(8,128)(2,1)S(1)}) custom-call(s32[2]{0:T(128)S(1)} %pad_add_fusion.1.at_ref, bf16[192,896]{1,0:T(8,128)(2,1)} %get-tuple-element.35.refs_0_, bf16[192,896]{1,0:T(8,128)(2,1)} %collective-permute-done.8.refs_1_, bf16[192,896]{1,0:T(8,128)(2,1)S(1)} %collective-permute-done.9.refs_2_, ...), custom_call_target="tpu_custom_call" | custom-call | tf_op jit(solution)/shard_map/unpack/pallas_call | solution.py:393
  140.0 1.8 copy-done
  141.8 2.5 %feed.4 = (bf16[128,1536]{1,0:T(8,128)(2,1)S(1)}, bf16[128,1536]{1,0:T(8,128)(2,1)S(1)}) custom-call(bf16[64,1536]{1,0:T(8,128)(2,1)} %get-tuple-element.34.x0, bf16[64,1536]{1,0:T(8,128)(2,1)S(1)} %collective-permute-done.5.x1, bf16[64,1536]{1,0:T(8,128)(2,1)S(1)} %collective-permute-done.6.x2, bf16[64,1536]{1,0:T(8,128)(2,1)S(1)} %collective-permute-done.7.x3, ...), custom_call_target="tpu_custom_call" | custom-call | flops 1107296256 | bytes 6291456 | tf_op jit(solution)/shard_map/feed/pallas_call | solution.py:318
  145.3 1.5 feed.5
  147.0 1.5 feed.6
  149.0 1.5 feed.7
  150.7 0.6 collective-permute-start.23
  151.4 1.6 collective-permute-start.29
  153.8 1.6 collective-permute-start.43
  155.4 7.3 %collective-permute-done.29 = bf16[64,1536]{1,0:T(8,128)(2,1)S(1)} collective-permute-done((bf16[64,1536]{1,0:T(8,128)(2,1)S(1)}, bf16[64,1536]{1,0:T(8,128)(2,1)S(1)}, u32[]{:S(2)}, u32[]{:S(2)}) %collective-permute-start.29) | collective-permute-done | bytes 196640 | tf_op jit(solution)/shard_map/ppermute | solution.py:353
  162.7 2.4 %collective-permute-start.30 = (bf16[64,1536]{1,0:T(8,128)(2,1)S(1)}, bf16[64,1536]{1,0:T(8,128)(2,1)S(1)}, u32[]{:S(2)}, u32[]{:S(2)}) collective-permute-start(bf16[64,1536]{1,0:T(8,128)(2,1)S(1)} %add_convert_fusion.7), channel_id=1, source_target_pairs={{0,24},{4,28},{8,0},{12,4},{16,8},{20,12},{24,16},{28,20},{1,25},{... | collective-permute-start | bytes 589832 | tf_op jit(solution)/shard_map/ppermute | solution.py:356
  165.1 1.8 collective-permute-done.36
  167.0 3.6 %collective-permute-done.43 = bf16[64,1536]{1,0:T(8,128)(2,1)S(1)} collective-permute-done((bf16[64,1536]{1,0:T(8,128)(2,1)S(1)}, bf16[64,1536]{1,0:T(8,128)(2,1)S(1)}, u32[]{:S(2)}, u32[]{:S(2)}) %collective-permute-start.43) | collective-permute-done | bytes 196640 | tf_op jit(solution)/shard_map/ppermute | solution.py:353
  170.8 5.2 %collective-permute-done.37 = bf16[64,1536]{1,0:T(8,128)(2,1)S(1)} collective-permute-done((bf16[64,1536]{1,0:T(8,128)(2,1)S(1)}, bf16[64,1536]{1,0:T(8,128)(2,1)S(1)}, u32[]{:S(2)}, u32[]{:S(2)}) %collective-permute-start.37) | collective-permute-done | bytes 196640 | tf_op jit(solution)/shard_map/ppermute | solution.py:356
  176.0 7.2 %collective-permute-done.44 = bf16[64,1536]{1,0:T(8,128)(2,1)S(1)} collective-permute-done((bf16[64,1536]{1,0:T(8,128)(2,1)S(1)}, bf16[64,1536]{1,0:T(8,128)(2,1)S(1)}, u32[]{:S(2)}, u32[]{:S(2)}) %collective-permute-start.44) | collective-permute-done | bytes 196640 | tf_op jit(solution)/shard_map/ppermute | solution.py:356
  183.2 0.8 add_convert_fusion.4
  (105 shorter events, 7.9 us)
Async XLA Ops:
  0.0 29.9 %collective-permute-start.3 = (bf16[384,1536]{1,0:T(8,128)(2,1)}, bf16[384,1536]{1,0:T(8,128)(2,1)S(1)}, u32[]{:S(2)}, u32[]{:S(2)}) collective-permute-start(bf16[384,1536]{1,0:T(8,128)(2,1)} %w0.1), channel_id=1, source_target_pairs={{0,2},{1,3},{2,0},{3,1},{4,6},{5,7},{6,4},{7,5},{8,10},{9,11},{10,... | collective-permute-start | bytes 3538952 | tf_op jit(solution)/shard_map/ppermute | solution.py:353
  2.9 12.5 %copy-start.2 = (bf16[384,1536]{1,0:T(8,128)(2,1)S(1)}, bf16[384,1536]{1,0:T(8,128)(2,1)}, u32[]{:S(2)}) copy-start(bf16[384,1536]{1,0:T(8,128)(2,1)} %w0.1) | copy-start | bytes 3538948
  2.9 12.5 %copy-start.26 = (s32[3]{0:T(128)S(1)}, s32[3]{0:T(128)}, u32[]{:S(2)}) copy-start(s32[3]{0:T(128)} %param.14) | copy-start | bytes 40
  4.5 1.1 copy-start.3
  5.6 1.1 copy-start.4
  8.4 0.8 copy-start.24
  9.9 39.1 %copy-start.14 = (bf16[240,384]{1,0:T(8,128)(2,1)}, bf16[240,384]{1,0:T(8,128)(2,1)S(1)}, u32[]{:S(2)}) copy-start(bf16[240,384]{1,0:T(8,128)(2,1)S(1)} %get-tuple-element.39.refs_8_) | copy-start | bytes 552964
  9.9 9.8 %collective-permute-start.16 = (bf16[240,384]{1,0:T(8,128)(2,1)}, bf16[240,384]{1,0:T(8,128)(2,1)}, u32[]{:S(2)}, u32[]{:S(2)}) collective-permute-start(bf16[240,384]{1,0:T(8,128)(2,1)} %get-tuple-element.40), channel_id=1, source_target_pairs={{0,8},{4,12},{8,16},{12,20},{16,24},{20,28},{24,0},{28,4},{1,9},{5... | collective-permute-start | bytes 552968 | tf_op jit(solution)/shard_map/ppermute | solution.py:356
  11.5 16.1 %collective-permute-start.18 = (bf16[240,384]{1,0:T(8,128)(2,1)}, bf16[240,384]{1,0:T(8,128)(2,1)}, u32[]{:S(2)}, u32[]{:S(2)}) collective-permute-start(bf16[240,384]{1,0:T(8,128)(2,1)} %get-tuple-element.41), channel_id=1, source_target_pairs={{0,16},{4,20},{8,24},{12,28},{16,0},{20,4},{24,8},{28,12},{1,17},{... | collective-permute-start | bytes 552968 | tf_op jit(solution)/shard_map/ppermute | solution.py:356
  14.1 14.2 %collective-permute-start.20 = (bf16[240,384]{1,0:T(8,128)(2,1)}, bf16[240,384]{1,0:T(8,128)(2,1)}, u32[]{:S(2)}, u32[]{:S(2)}) collective-permute-start(bf16[240,384]{1,0:T(8,128)(2,1)} %get-tuple-element.42), channel_id=1, source_target_pairs={{0,24},{4,28},{8,0},{12,4},{16,8},{20,12},{24,16},{28,20},{1,25},{... | collective-permute-start | bytes 552968 | tf_op jit(solution)/shard_map/ppermute | solution.py:356
  15.4 67.6 %collective-permute-start.2 = (bf16[384,1536]{1,0:T(8,128)(2,1)S(1)}, bf16[384,1536]{1,0:T(8,128)(2,1)}, u32[]{:S(2)}, u32[]{:S(2)}) collective-permute-start(bf16[384,1536]{1,0:T(8,128)(2,1)S(1)} %copy-done.2), channel_id=1, source_target_pairs={{0,1},{1,0},{2,3},{3,2},{4,5},{5,4},{6,7},{7,6},{8,9},{9,8},{10,11... | collective-permute-start | bytes 3538952 | tf_op jit(solution)/shard_map/ppermute | solution.py:353
  19.7 30.5 %collective-permute-start.9 = (bf16[192,896]{1,0:T(8,128)(2,1)}, bf16[192,896]{1,0:T(8,128)(2,1)S(1)}, u32[]{:S(2)}, u32[]{:S(2)}) collective-permute-start(bf16[192,896]{1,0:T(8,128)(2,1)} %copy-done.25), channel_id=1, source_target_pairs={{0,8},{4,12},{8,16},{12,20},{16,24},{20,28},{24,0},{28,4},{1,9},{5... | collective-permute-start | bytes 1032200 | tf_op jit(solution)/shard_map/ppermute | solution.py:356
  27.6 28.3 %collective-permute-start.11 = (bf16[192,896]{1,0:T(8,128)(2,1)}, bf16[192,896]{1,0:T(8,128)(2,1)S(1)}, u32[]{:S(2)}, u32[]{:S(2)}) collective-permute-start(bf16[192,896]{1,0:T(8,128)(2,1)} %copy-done.24), channel_id=1, source_target_pairs={{0,16},{4,20},{8,24},{12,28},{16,0},{20,4},{24,8},{28,12},{1,17},{... | collective-permute-start | bytes 1032200 | tf_op jit(solution)/shard_map/ppermute | solution.py:356
  28.3 20.7 %collective-permute-start.15 = (bf16[240,384]{1,0:T(8,128)(2,1)S(1)}, bf16[240,384]{1,0:T(8,128)(2,1)S(1)}, u32[]{:S(2)}, u32[]{:S(2)}) collective-permute-start(bf16[240,384]{1,0:T(8,128)(2,1)S(1)} %get-tuple-element.39.refs_8_), channel_id=1, source_target_pairs={{0,4},{4,0},{8,12},{12,8},{16,20},{20,16},{24,28},{28,24},{1,5},{5... | collective-permute-start | bytes 552968 | tf_op jit(solution)/shard_map/ppermute | solution.py:359
  29.9 54.7 %collective-permute-start.4 = (bf16[384,1536]{1,0:T(8,128)(2,1)S(1)}, bf16[384,1536]{1,0:T(8,128)(2,1)}, u32[]{:S(2)}, u32[]{:S(2)}) collective-permute-start(bf16[384,1536]{1,0:T(8,128)(2,1)S(1)} %collective-permute-done.3.w2), channel_id=1, source_target_pairs={{0,1},{1,0},{2,3},{3,2},{4,5},{5,4},{6,7},{7,6},{8,9},{9,8},{10,11... | collective-permute-start | bytes 3538952 | tf_op jit(solution)/shard_map/ppermute | solution.py:353
  29.9 1.9 %copy-start.22 = (bf16[3,1024,512]{2,1,0:T(8,128)(2,1)S(1)}, bf16[3,1024,512]{2,1,0:T(8,128)(2,1)}, u32[]{:S(2)}) copy-start(bf16[3,1024,512]{2,1,0:T(8,128)(2,1)} %k_ref.1) | copy-start | bytes 9437188
  31.8 1.1 copy-start.23
  49.7 6.8 %collective-permute-start = (bf16[128,1664]{1,0:T(8,128)(2,1)S(1)}, bf16[128,1664]{1,0:T(8,128)(2,1)S(1)}, u32[]{:S(2)}, u32[]{:S(2)}) collective-permute-start(bf16[128,1664]{1,0:T(8,128)(2,1)S(1)} %get-tuple-element.30), channel_id=1, source_target_pairs={{0,1},{1,0},{2,3},{3,2},{4,5},{5,4},{6,7},{7,6},{8,9},{9,8},{10,11... | collective-permute-start | bytes 1277960 | tf_op jit(solution)/shard_map/ppermute | solution.py:353
  50.2 25.7 %collective-permute-start.13 = (bf16[192,896]{1,0:T(8,128)(2,1)}, bf16[192,896]{1,0:T(8,128)(2,1)}, u32[]{:S(2)}, u32[]{:S(2)}) collective-permute-start(bf16[192,896]{1,0:T(8,128)(2,1)} %get-tuple-element.38), channel_id=1, source_target_pairs={{0,24},{4,28},{8,0},{12,4},{16,8},{20,12},{24,16},{28,20},{1,25},{... | collective-permute-start | bytes 1032200 | tf_op jit(solution)/shard_map/ppermute | solution.py:356
  55.9 20.5 %collective-permute-start.8 = (bf16[192,896]{1,0:T(8,128)(2,1)}, bf16[192,896]{1,0:T(8,128)(2,1)}, u32[]{:S(2)}, u32[]{:S(2)}) collective-permute-start(bf16[192,896]{1,0:T(8,128)(2,1)} %get-tuple-element.35.refs_0_), channel_id=1, source_target_pairs={{0,4},{4,0},{8,12},{12,8},{16,20},{20,16},{24,28},{28,24},{1,5},{5... | collective-permute-start | bytes 1032200 | tf_op jit(solution)/shard_map/ppermute | solution.py:359
  56.6 20.3 %collective-permute-start.17 = (bf16[240,384]{1,0:T(8,128)(2,1)}, bf16[240,384]{1,0:T(8,128)(2,1)}, u32[]{:S(2)}, u32[]{:S(2)}) collective-permute-start(bf16[240,384]{1,0:T(8,128)(2,1)} %collective-permute-done.16.refs_10_), channel_id=1, source_target_pairs={{0,4},{4,0},{8,12},{12,8},{16,20},{20,16},{24,28},{28,24},{1,5},{5... | collective-permute-start | bytes 552968 | tf_op jit(solution)/shard_map/ppermute | solution.py:359
  75.9 6.6 %collective-permute-start.1 = (bf16[64,1664]{1,0:T(8,128)(2,1)S(1)}, bf16[64,1664]{1,0:T(8,128)(2,1)S(1)}, u32[]{:S(2)}, u32[]{:S(2)}) collective-permute-start(bf16[64,1664]{1,0:T(8,128)(2,1)S(1)} %get-tuple-element.32), channel_id=1, source_target_pairs={{0,2},{1,3},{2,0},{3,1},{4,6},{5,7},{6,4},{7,5},{8,10},{9,11},{10,... | collective-permute-start | bytes 638984 | tf_op jit(solution)/shard_map/ppermute | solution.py:353
  76.4 34.0 %collective-permute-start.10 = (bf16[192,896]{1,0:T(8,128)(2,1)S(1)}, bf16[192,896]{1,0:T(8,128)(2,1)S(1)}, u32[]{:S(2)}, u32[]{:S(2)}) collective-permute-start(bf16[192,896]{1,0:T(8,128)(2,1)S(1)} %collective-permute-done.9.refs_2_), channel_id=1, source_target_pairs={{0,4},{4,0},{8,12},{12,8},{16,20},{20,16},{24,28},{28,24},{1,5},{5... | collective-permute-start | bytes 1032200 | tf_op jit(solution)/shard_map/ppermute | solution.py:359
  76.9 14.4 %collective-permute-start.19 = (bf16[240,384]{1,0:T(8,128)(2,1)}, bf16[240,384]{1,0:T(8,128)(2,1)S(1)}, u32[]{:S(2)}, u32[]{:S(2)}) collective-permute-start(bf16[240,384]{1,0:T(8,128)(2,1)} %collective-permute-done.18.refs_12_), channel_id=1, source_target_pairs={{0,4},{4,0},{8,12},{12,8},{16,20},{20,16},{24,28},{28,24},{1,5},{5... | collective-permute-start | bytes 552968 | tf_op jit(solution)/shard_map/ppermute | solution.py:359
  82.5 30.3 %collective-permute-start.12 = (bf16[192,896]{1,0:T(8,128)(2,1)}, bf16[192,896]{1,0:T(8,128)(2,1)S(1)}, u32[]{:S(2)}, u32[]{:S(2)}) collective-permute-start(bf16[192,896]{1,0:T(8,128)(2,1)} %copy-done.5), channel_id=1, source_target_pairs={{0,4},{4,0},{8,12},{12,8},{16,20},{20,16},{24,28},{28,24},{1,5},{5... | collective-permute-start | bytes 1032200 | tf_op jit(solution)/shard_map/ppermute | solution.py:359
  83.0 30.6 %collective-permute-start.14 = (bf16[192,896]{1,0:T(8,128)(2,1)}, bf16[192,896]{1,0:T(8,128)(2,1)S(1)}, u32[]{:S(2)}, u32[]{:S(2)}) collective-permute-start(bf16[192,896]{1,0:T(8,128)(2,1)} %collective-permute-done.13.refs_6_), channel_id=1, source_target_pairs={{0,4},{4,0},{8,12},{12,8},{16,20},{20,16},{24,28},{28,24},{1,5},{5... | collective-permute-start | bytes 1032200 | tf_op jit(solution)/shard_map/ppermute | solution.py:359
  84.5 23.7 %collective-permute-start.21 = (bf16[240,384]{1,0:T(8,128)(2,1)}, bf16[240,384]{1,0:T(8,128)(2,1)S(1)}, u32[]{:S(2)}, u32[]{:S(2)}) collective-permute-start(bf16[240,384]{1,0:T(8,128)(2,1)} %collective-permute-done.20.refs_14_), channel_id=1, source_target_pairs={{0,4},{4,0},{8,12},{12,8},{16,20},{20,16},{24,28},{28,24},{1,5},{5... | collective-permute-start | bytes 552968 | tf_op jit(solution)/shard_map/ppermute | solution.py:359
  85.7 0.9 copy-start.11
  86.7 41.8 %copy-start.6 = (bf16[192,896]{1,0:T(8,128)(2,1)S(1)}, bf16[192,896]{1,0:T(8,128)(2,1)}, u32[]{:S(2)}) copy-start(bf16[192,896]{1,0:T(8,128)(2,1)} %copy-done.5) | copy-start | bytes 1032196
  92.0 23.7 %collective-permute-start.24 = (bf16[64,1536]{1,0:T(8,128)(2,1)}, bf16[64,1536]{1,0:T(8,128)(2,1)S(1)}, u32[]{:S(2)}, u32[]{:S(2)}) collective-permute-start(bf16[64,1536]{1,0:T(8,128)(2,1)} %get-tuple-element.34.x0), channel_id=1, source_target_pairs={{0,8},{4,12},{8,16},{12,20},{16,24},{20,28},{24,0},{28,4},{1,9},{5... | collective-permute-start | bytes 589832 | tf_op jit(solution)/shard_map/ppermute | solution.py:356
  108.9 8.3 %collective-permute-start.5 = (bf16[64,1536]{1,0:T(8,128)(2,1)}, bf16[64,1536]{1,0:T(8,128)(2,1)S(1)}, u32[]{:S(2)}, u32[]{:S(2)}) collective-permute-start(bf16[64,1536]{1,0:T(8,128)(2,1)} %get-tuple-element.34.x0), channel_id=1, source_target_pairs={{0,2},{1,3},{2,0},{3,1},{4,6},{5,7},{6,4},{7,5},{8,10},{9,11},{10,... | collective-permute-start | bytes 589832 | tf_op jit(solution)/shard_map/ppermute | solution.py:353
  110.4 6.8 %collective-permute-start.31 = (bf16[64,1536]{1,0:T(8,128)(2,1)}, bf16[64,1536]{1,0:T(8,128)(2,1)S(1)}, u32[]{:S(2)}, u32[]{:S(2)}) collective-permute-start(bf16[64,1536]{1,0:T(8,128)(2,1)} %get-tuple-element.34.x0), channel_id=1, source_target_pairs={{0,24},{4,28},{8,0},{12,4},{16,8},{20,12},{24,16},{28,20},{1,25},{... | collective-permute-start | bytes 589832 | tf_op jit(solution)/shard_map/ppermute | solution.py:356
  113.6 4.9 %collective-permute-start.6 = (bf16[64,1536]{1,0:T(8,128)(2,1)}, bf16[64,1536]{1,0:T(8,128)(2,1)S(1)}, u32[]{:S(2)}, u32[]{:S(2)}) collective-permute-start(bf16[64,1536]{1,0:T(8,128)(2,1)} %get-tuple-element.34.x0), channel_id=1, source_target_pairs={{0,1},{1,0},{2,3},{3,2},{4,5},{5,4},{6,7},{7,6},{8,9},{9,8},{10,11... | collective-permute-start | bytes 589832 | tf_op jit(solution)/shard_map/ppermute | solution.py:353
  114.3 12.6 %collective-permute-start.38 = (bf16[64,1536]{1,0:T(8,128)(2,1)}, bf16[64,1536]{1,0:T(8,128)(2,1)S(1)}, u32[]{:S(2)}, u32[]{:S(2)}) collective-permute-start(bf16[64,1536]{1,0:T(8,128)(2,1)} %get-tuple-element.34.x0), channel_id=1, source_target_pairs={{0,16},{4,20},{8,24},{12,28},{16,0},{20,4},{24,8},{28,12},{1,17},{... | collective-permute-start | bytes 589832 | tf_op jit(solution)/shard_map/ppermute | solution.py:356
  115.7 12.7 %collective-permute-start.25 = (bf16[64,1536]{1,0:T(8,128)(2,1)S(1)}, bf16[64,1536]{1,0:T(8,128)(2,1)S(1)}, u32[]{:S(2)}, u32[]{:S(2)}) collective-permute-start(bf16[64,1536]{1,0:T(8,128)(2,1)S(1)} %collective-permute-done.24.x0), channel_id=1, source_target_pairs={{0,2},{1,3},{2,0},{3,1},{4,6},{5,7},{6,4},{7,5},{8,10},{9,11},{10,... | collective-permute-start | bytes 589832 | tf_op jit(solution)/shard_map/ppermute | solution.py:353
  117.2 22.2 %collective-permute-start.7 = (bf16[64,1536]{1,0:T(8,128)(2,1)S(1)}, bf16[64,1536]{1,0:T(8,128)(2,1)S(1)}, u32[]{:S(2)}, u32[]{:S(2)}) collective-permute-start(bf16[64,1536]{1,0:T(8,128)(2,1)S(1)} %collective-permute-done.5.x1), channel_id=1, source_target_pairs={{0,1},{1,0},{2,3},{3,2},{4,5},{5,4},{6,7},{7,6},{8,9},{9,8},{10,11... | collective-permute-start | bytes 589832 | tf_op jit(solution)/shard_map/ppermute | solution.py:353
  117.2 22.7 %collective-permute-start.32 = (bf16[64,1536]{1,0:T(8,128)(2,1)S(1)}, bf16[64,1536]{1,0:T(8,128)(2,1)S(1)}, u32[]{:S(2)}, u32[]{:S(2)}) collective-permute-start(bf16[64,1536]{1,0:T(8,128)(2,1)S(1)} %collective-permute-done.31.x0), channel_id=1, source_target_pairs={{0,2},{1,3},{2,0},{3,1},{4,6},{5,7},{6,4},{7,5},{8,10},{9,11},{10,... | collective-permute-start | bytes 589832 | tf_op jit(solution)/shard_map/ppermute | solution.py:353
  118.4 25.9 %collective-permute-start.26 = (bf16[64,1536]{1,0:T(8,128)(2,1)S(1)}, bf16[64,1536]{1,0:T(8,128)(2,1)S(1)}, u32[]{:S(2)}, u32[]{:S(2)}) collective-permute-start(bf16[64,1536]{1,0:T(8,128)(2,1)S(1)} %collective-permute-done.24.x0), channel_id=1, source_target_pairs={{0,1},{1,0},{2,3},{3,2},{4,5},{5,4},{6,7},{7,6},{8,9},{9,8},{10,11... | collective-permute-start | bytes 589832 | tf_op jit(solution)/shard_map/ppermute | solution.py:353
  126.9 18.0 %collective-permute-start.39 = (bf16[64,1536]{1,0:T(8,128)(2,1)S(1)}, bf16[64,1536]{1,0:T(8,128)(2,1)S(1)}, u32[]{:S(2)}, u32[]{:S(2)}) collective-permute-start(bf16[64,1536]{1,0:T(8,128)(2,1)S(1)} %collective-permute-done.38.x0), channel_id=1, source_target_pairs={{0,2},{1,3},{2,0},{3,1},{4,6},{5,7},{6,4},{7,5},{8,10},{9,11},{10,... | collective-permute-start | bytes 589832 | tf_op jit(solution)/shard_map/ppermute | solution.py:353
  128.4 16.5 %collective-permute-start.27 = (bf16[64,1536]{1,0:T(8,128)(2,1)S(1)}, bf16[64,1536]{1,0:T(8,128)(2,1)S(1)}, u32[]{:S(2)}, u32[]{:S(2)}) collective-permute-start(bf16[64,1536]{1,0:T(8,128)(2,1)S(1)} %collective-permute-done.25.x1), channel_id=1, source_target_pairs={{0,1},{1,0},{2,3},{3,2},{4,5},{5,4},{6,7},{7,6},{8,9},{9,8},{10,11... | collective-permute-start | bytes 589832 | tf_op jit(solution)/shard_map/ppermute | solution.py:353
  128.5 1.0 copy-start.8
  129.4 1.0 copy-start.10
  130.4 0.9 copy-start.15
  131.3 0.9 copy-start.17
  132.3 0.9 copy-start.19
  133.2 0.9 copy-start.21
  139.4 7.4 %collective-permute-start.33 = (bf16[64,1536]{1,0:T(8,128)(2,1)S(1)}, bf16[64,1536]{1,0:T(8,128)(2,1)S(1)}, u32[]{:S(2)}, u32[]{:S(2)}) collective-permute-start(bf16[64,1536]{1,0:T(8,128)(2,1)S(1)} %collective-permute-done.31.x0), channel_id=1, source_target_pairs={{0,1},{1,0},{2,3},{3,2},{4,5},{5,4},{6,7},{7,6},{8,9},{9,8},{10,11... | collective-permute-start | bytes 589832 | tf_op jit(solution)/shard_map/ppermute | solution.py:353
  139.9 7.1 %collective-permute-start.34 = (bf16[64,1536]{1,0:T(8,128)(2,1)S(1)}, bf16[64,1536]{1,0:T(8,128)(2,1)S(1)}, u32[]{:S(2)}, u32[]{:S(2)}) collective-permute-start(bf16[64,1536]{1,0:T(8,128)(2,1)S(1)} %collective-permute-done.32.x1), channel_id=1, source_target_pairs={{0,1},{1,0},{2,3},{3,2},{4,5},{5,4},{6,7},{7,6},{8,9},{9,8},{10,11... | collective-permute-start | bytes 589832 | tf_op jit(solution)/shard_map/ppermute | solution.py:353
  140.0 1.8 copy-start
  141.8 3.6 %copy-start.1 = (bf16[1536,896]{1,0:T(8,128)(2,1)S(1)}, bf16[1536,896]{1,0:T(8,128)(2,1)}, u32[]{:S(2)}) copy-start(bf16[1536,896]{1,0:T(8,128)(2,1)} %get-tuple-element.43.weight_ref) | copy-start | bytes 8257540
  144.3 6.3 %collective-permute-start.22 = (bf16[128,1536]{1,0:T(8,128)(2,1)S(1)}, bf16[128,1536]{1,0:T(8,128)(2,1)S(1)}, u32[]{:S(2)}, u32[]{:S(2)}) collective-permute-start(bf16[128,1536]{1,0:T(8,128)(2,1)S(1)} %get-tuple-element.46), channel_id=1, source_target_pairs={{0,1},{1,0},{2,3},{3,2},{4,5},{5,4},{6,7},{7,6},{8,9},{9,8},{10,11... | collective-permute-start | bytes 1179656 | tf_op jit(solution)/shard_map/ppermute | solution.py:353
  144.8 4.1 %collective-permute-start.40 = (bf16[64,1536]{1,0:T(8,128)(2,1)S(1)}, bf16[64,1536]{1,0:T(8,128)(2,1)S(1)}, u32[]{:S(2)}, u32[]{:S(2)}) collective-permute-start(bf16[64,1536]{1,0:T(8,128)(2,1)S(1)} %collective-permute-done.38.x0), channel_id=1, source_target_pairs={{0,1},{1,0},{2,3},{3,2},{4,5},{5,4},{6,7},{7,6},{8,9},{9,8},{10,11... | collective-permute-start | bytes 589832 | tf_op jit(solution)/shard_map/ppermute | solution.py:353
  144.9 4.0 %collective-permute-start.41 = (bf16[64,1536]{1,0:T(8,128)(2,1)S(1)}, bf16[64,1536]{1,0:T(8,128)(2,1)S(1)}, u32[]{:S(2)}, u32[]{:S(2)}) collective-permute-start(bf16[64,1536]{1,0:T(8,128)(2,1)S(1)} %collective-permute-done.39.x1), channel_id=1, source_target_pairs={{0,1},{1,0},{2,3},{3,2},{4,5},{5,4},{6,7},{7,6},{8,9},{9,8},{10,11... | collective-permute-start | bytes 589832 | tf_op jit(solution)/shard_map/ppermute | solution.py:353
  146.8 4.5 %collective-permute-start.28 = (bf16[128,1536]{1,0:T(8,128)(2,1)S(1)}, bf16[128,1536]{1,0:T(8,128)(2,1)S(1)}, u32[]{:S(2)}, u32[]{:S(2)}) collective-permute-start(bf16[128,1536]{1,0:T(8,128)(2,1)S(1)} %get-tuple-element.48), channel_id=1, source_target_pairs={{0,1},{1,0},{2,3},{3,2},{4,5},{5,4},{6,7},{7,6},{8,9},{9,8},{10,11... | collective-permute-start | bytes 1179656 | tf_op jit(solution)/shard_map/ppermute | solution.py:353
  148.5 4.5 %collective-permute-start.35 = (bf16[128,1536]{1,0:T(8,128)(2,1)S(1)}, bf16[128,1536]{1,0:T(8,128)(2,1)S(1)}, u32[]{:S(2)}, u32[]{:S(2)}) collective-permute-start(bf16[128,1536]{1,0:T(8,128)(2,1)S(1)} %get-tuple-element.50), channel_id=1, source_target_pairs={{0,1},{1,0},{2,3},{3,2},{4,5},{5,4},{6,7},{7,6},{8,9},{9,8},{10,11... | collective-permute-start | bytes 1179656 | tf_op jit(solution)/shard_map/ppermute | solution.py:353
  150.4 3.3 %collective-permute-start.42 = (bf16[128,1536]{1,0:T(8,128)(2,1)S(1)}, bf16[128,1536]{1,0:T(8,128)(2,1)S(1)}, u32[]{:S(2)}, u32[]{:S(2)}) collective-permute-start(bf16[128,1536]{1,0:T(8,128)(2,1)S(1)} %get-tuple-element.52), channel_id=1, source_target_pairs={{0,1},{1,0},{2,3},{3,2},{4,5},{5,4},{6,7},{7,6},{8,9},{9,8},{10,11... | collective-permute-start | bytes 1179656 | tf_op jit(solution)/shard_map/ppermute | solution.py:353
  150.7 20.1 %collective-permute-start.23 = (bf16[64,1536]{1,0:T(8,128)(2,1)S(1)}, bf16[64,1536]{1,0:T(8,128)(2,1)S(1)}, u32[]{:S(2)}, u32[]{:S(2)}) collective-permute-start(bf16[64,1536]{1,0:T(8,128)(2,1)S(1)} %slice.33), channel_id=1, source_target_pairs={{0,2},{1,3},{2,0},{3,1},{4,6},{5,7},{6,4},{7,5},{8,10},{9,11},{10,... | collective-permute-start | bytes 589832 | tf_op jit(solution)/shard_map/ppermute | solution.py:353
  151.4 11.3 %collective-permute-start.29 = (bf16[64,1536]{1,0:T(8,128)(2,1)S(1)}, bf16[64,1536]{1,0:T(8,128)(2,1)S(1)}, u32[]{:S(2)}, u32[]{:S(2)}) collective-permute-start(bf16[64,1536]{1,0:T(8,128)(2,1)S(1)} %slice.35), channel_id=1, source_target_pairs={{0,2},{1,3},{2,0},{3,1},{4,6},{5,7},{6,4},{7,5},{8,10},{9,11},{10,... | collective-permute-start | bytes 589832 | tf_op jit(solution)/shard_map/ppermute | solution.py:353
  153.1 13.8 %collective-permute-start.36 = (bf16[64,1536]{1,0:T(8,128)(2,1)S(1)}, bf16[64,1536]{1,0:T(8,128)(2,1)S(1)}, u32[]{:S(2)}, u32[]{:S(2)}) collective-permute-start(bf16[64,1536]{1,0:T(8,128)(2,1)S(1)} %slice.37), channel_id=1, source_target_pairs={{0,2},{1,3},{2,0},{3,1},{4,6},{5,7},{6,4},{7,5},{8,10},{9,11},{10,... | collective-permute-start | bytes 589832 | tf_op jit(solution)/shard_map/ppermute | solution.py:353
  153.7 29.5 %copy-start.13 = (bf16[64,1536]{1,0:T(8,128)(2,1)S(1)}, bf16[64,1536]{1,0:T(8,128)(2,1)}, u32[]{:S(2)}) copy-start(bf16[64,1536]{1,0:T(8,128)(2,1)} %copy-done.12) | copy-start | bytes 589828
  153.8 16.8 %collective-permute-start.43 = (bf16[64,1536]{1,0:T(8,128)(2,1)S(1)}, bf16[64,1536]{1,0:T(8,128)(2,1)S(1)}, u32[]{:S(2)}, u32[]{:S(2)}) collective-permute-start(bf16[64,1536]{1,0:T(8,128)(2,1)S(1)} %slice.39), channel_id=1, source_target_pairs={{0,2},{1,3},{2,0},{3,1},{4,6},{5,7},{6,4},{7,5},{8,10},{9,11},{10,... | collective-permute-start | bytes 589832 | tf_op jit(solution)/shard_map/ppermute | solution.py:353
  162.7 8.1 %collective-permute-start.30 = (bf16[64,1536]{1,0:T(8,128)(2,1)S(1)}, bf16[64,1536]{1,0:T(8,128)(2,1)S(1)}, u32[]{:S(2)}, u32[]{:S(2)}) collective-permute-start(bf16[64,1536]{1,0:T(8,128)(2,1)S(1)} %add_convert_fusion.7), channel_id=1, source_target_pairs={{0,24},{4,28},{8,0},{12,4},{16,8},{20,12},{24,16},{28,20},{1,25},{... | collective-permute-start | bytes 589832 | tf_op jit(solution)/shard_map/ppermute | solution.py:356
  167.0 9.1 %collective-permute-start.37 = (bf16[64,1536]{1,0:T(8,128)(2,1)S(1)}, bf16[64,1536]{1,0:T(8,128)(2,1)S(1)}, u32[]{:S(2)}, u32[]{:S(2)}) collective-permute-start(bf16[64,1536]{1,0:T(8,128)(2,1)S(1)} %add_convert_fusion.6), channel_id=1, source_target_pairs={{0,8},{4,12},{8,16},{12,20},{16,24},{20,28},{24,0},{28,4},{1,9},{5... | collective-permute-start | bytes 589832 | tf_op jit(solution)/shard_map/ppermute | solution.py:356
  170.7 12.5 %collective-permute-start.44 = (bf16[64,1536]{1,0:T(8,128)(2,1)S(1)}, bf16[64,1536]{1,0:T(8,128)(2,1)S(1)}, u32[]{:S(2)}, u32[]{:S(2)}) collective-permute-start(bf16[64,1536]{1,0:T(8,128)(2,1)S(1)} %add_convert_fusion.5), channel_id=1, source_target_pairs={{0,16},{4,20},{8,24},{12,28},{16,0},{20,4},{24,8},{28,12},{1,17},{... | collective-permute-start | bytes 589832 | tf_op jit(solution)/shard_map/ppermute | solution.py:356
  (8 other events, 5.6 us)

commit v2 on v1

v2 whole, which is shorter than its diff:
```python
import functools

import jax
import jax.numpy as jnp
from jax import lax
from jax.experimental import pallas as pl
from jax.experimental.pallas import tpu as pltpu
from jax.sharding import PartitionSpec as P

H = 24
HD = 64
KVH = 8
LANES = 128
SUM_HIGH = 32
SUM_LOW = 64
OUTER = 4

VMEM = pl.BlockSpec(memory_space=pltpu.VMEM)
SMEM = pl.BlockSpec(memory_space=pltpu.SMEM)
HBM = pl.BlockSpec(memory_space=pl.ANY)
NT = (((1,), (1,)), ((), ()))
BF16 = jnp.bfloat16
F32 = jnp.float32


def params(mib):
    return pltpu.CompilerParams(vmem_limit_bytes=mib * 1024 * 1024)


def iota(shape, dim):
    return lax.broadcasted_iota(jnp.int32, shape, dim)


def dot(a, b):
    return jnp.dot(a, b, preferred_element_type=F32)


def one_hot(condition):
    return jnp.where(condition, 1.0, 0.0).astype(BF16)


def pack_kernel(main, tail, cuts, z_ref, gate_ref, up_ref, down_ref, *refs):
    outs, slots, (weights, sems, in_sems) = refs[: len(cuts)], refs[len(cuts) : -3], refs[-3:]
    tail_at = OUTER * main
    total = weights.shape[1]
    step = total // 2 if total % 32 == 0 else total
    loads = []
    for index, ref in enumerate((gate_ref, up_ref, down_ref)):
        for start in range(0, total, step):
            pick = pl.ds(start, step)
            loads.append(pltpu.make_async_copy(ref.at[pick], weights.at[index, pick], in_sems.at[len(loads)]))
            loads[-1].start()
    for load in loads:
        load.wait()
    gate_ref, up_ref, down_ref = (weights.at[index] for index in range(3))
    second = 2 * main + LANES
    copies = []
    for index, (shift, start, rows) in enumerate(cuts):
        out = slots[index]
        target = z_ref[0] ^ shift
        pick = slice(start, start + rows)
        column = pl.multiple_of(target * main, LANES)
        out[:, :main] = gate_ref[pick, pl.ds(column, main)]
        out[:, main : 2 * main] = up_ref[pick, pl.ds(column, main)]
        out[:, second : second + main] = down_ref[pick, pl.ds(column, main)]
        shape = (OUTER * tail, LANES)
        k, lane = iota(shape, 0) - target * tail, iota(shape, 1)
        first = one_hot((lane < tail) & (k == lane))
        next_to = one_hot((lane >= tail) & (lane < 2 * tail) & (k == lane - tail))
        ends = dot(gate_ref[pick, tail_at:], first) + dot(up_ref[pick, tail_at:], next_to)
        out[:, 2 * main : second] = ends.astype(BF16)
        out[:, second + main :] = dot(down_ref[pick, tail_at:], first).astype(BF16)
        copies.append(pltpu.make_async_copy(out, outs[index], sems.at[index]))
        copies[-1].start()
    for copy in copies:
        copy.wait()


def place_kernel(spots, at_ref, *refs):
    blocks, out = refs[:-1], refs[-1]
    for block, (start, step, mine) in zip(blocks, spots):
        side = at_ref[0] if mine else 1 - at_ref[0]
        out[pl.ds(pl.multiple_of(start + step * side, 16), block.shape[0]), :] = block[...]


def place(blocks, spots, at):
    rows = sum(block.shape[0] for block in blocks)
    return pl.pallas_call(
        functools.partial(place_kernel, spots),
        in_specs=[SMEM] + [VMEM] * len(blocks),
        out_specs=VMEM,
        out_shape=jax.ShapeDtypeStruct((rows, blocks[0].shape[1]), BF16),
        compiler_params=params(16),
        name="place",
    )(at, *blocks)


def attention_kernel(at_ref, q_hbm, k_hbm, v_hbm, keep_ref, send_ref, q_ref, k_ref, v_ref, bias, result, stats, lines, sems):
    rows, width = q_ref.shape
    requests, slab, _ = k_ref.shape
    block = 2 * (H // KVH) * HD
    steps = width // block
    span = rows - (requests - 1)
    heads = block // HD
    group = H // KVH
    first_key, half_row = at_ref[0], at_ref[1]

    def load(source, target, index):
        return pltpu.make_async_copy(source, target, sems.at[index])

    loads = [load(q_hbm, q_ref, 0)]
    loads += [load(k_hbm.at[r], k_ref.at[r], 1 + r) for r in range(requests)]
    loads += [load(v_hbm.at[r], v_ref.at[r], 1 + requests + r) for r in range(requests)]
    order = [0, 1, 1 + requests] + [i for i in range(2, len(loads)) if i != 1 + requests]
    for index in order:
        loads[index].start()

    place = first_key + iota((slab, rows), 0)
    limit = at_ref[2] - span + iota((slab, rows), 1)
    bias[...] = jnp.where(place <= limit, 0.0, -1e30)
    stats[...] = jnp.zeros_like(stats)
    lines[...] = jnp.zeros_like(lines)

    lane = iota((1, LANES), 1)
    low_lanes = lane < HD

    def in_half(a):
        return low_lanes if a == 0 else ~low_lanes

    def placed(value, h):
        return pltpu.roll(value, HD, 1) if h % 2 != h // group else value

    def record(old, column, top, total):
        high = total.astype(BF16).astype(F32)
        old = jnp.where(lane == column, top, old)
        old = jnp.where(lane == column + SUM_HIGH, high, old)
        return jnp.where(lane == column + SUM_LOW, total - high, old)

    for index in order[:3]:
        loads[index].wait()

    def one(step):
        near = pl.ds(step * LANES, LANES)

        def aligned(h):
            column = step * block + h // 2 * LANES
            tile = placed(q_ref[:, pl.ds(column, LANES)].astype(F32) * HD**-0.5, h)
            return jnp.where(in_half(h // group), tile, 0.0)

        keys, value = k_ref[0, :, near], v_ref[0, :, near]
        stat = stats[...]
        queries = [aligned(h) for h in range(heads)]
        sub = iota((8, 1), 0)
        for r in range(1, requests):
            line = jnp.zeros((8, LANES), F32)
            for h in range(heads):
                last = queries[h][rows - 8 :][8 - requests + r : 9 - requests + r]
                line = jnp.where(sub == h, jnp.broadcast_to(last, (8, LANES)), line)
            lines[r - 1, pl.ds(step * 8, 8), near] = line
        outs = []
        for a in range(2):
            query = jnp.concatenate(queries[a * group : (a + 1) * group], 0).astype(BF16)
            scores = lax.dot_general(keys, query, NT, preferred_element_type=F32)
            scores = scores + jnp.concatenate([bias[...]] * group, 1)
            top = jnp.maximum(jnp.max(scores, axis=0, keepdims=True), -1e29).astype(BF16).astype(F32)
            weights = jnp.exp((scores - top).astype(BF16))
            values = jnp.where(in_half(a), value, jnp.ones((), BF16)).astype(F32).T.astype(BF16)
            out = dot(values, weights).T
            top = jnp.broadcast_to(top, (8, top.shape[1])).T[:, :1]
            total = jnp.where(in_half(a), pltpu.roll(out, HD, 1), out)
            for r in range(group):
                h = a * group + r
                pick = slice(r * rows, (r + 1) * rows)
                stat = record(stat, step * heads + h, top[pick], total[pick])
                outs.append(placed(out[pick], h))
                if h % 2 == 1:
                    column = step * block + h // 2 * LANES
                    result[:, pl.ds(column, LANES)] = jnp.where(low_lanes, outs[h - 1], outs[h])
        stats[...] = stat

    for step in range(steps):
        one(step)
    count = 8 * steps
    sub, column = iota((count, 1), 0), iota((1, LANES), 1)
    spot = sub // 8 * heads + sub % 8
    live = sub % 8 < heads
    for r in range(1, requests):
        loads[1 + r].wait()
        loads[1 + requests + r].wait()
        row = rows - requests + r
        scores = lax.dot_general(lines[r - 1].astype(BF16), k_ref[r], NT, preferred_element_type=F32)
        usable = first_key + iota((1, slab), 1) < at_ref[2 + r]
        scores = jnp.where(usable, scores, -1e30)
        top = jnp.maximum(jnp.max(scores, axis=1, keepdims=True), -1e29).astype(BF16).astype(F32)
        weights = jnp.exp(scores - top)
        total = jnp.sum(weights, axis=1, keepdims=True)
        out = dot(weights.astype(BF16), v_ref[r])
        high = total.astype(BF16).astype(F32)
        stat = jnp.where(live & (column == spot), top, 0.0)
        stat = stat + jnp.where(live & (column == spot + SUM_HIGH), high, 0.0)
        stat = stat + jnp.where(live & (column == spot + SUM_LOW), total - high, 0.0)
        stats[row : row + 1, :] = jnp.sum(stat, axis=0, keepdims=True)
        for step in range(steps):
            tile = out[8 * step : 8 * step + 8, step * LANES : (step + 1) * LANES]
            turned = pltpu.roll(tile, HD, 1)
            for h in range(0, heads, 2):
                low = (turned if h // group else tile)[h : h + 1]
                high = (tile if (h + 1) // group else turned)[h + 1 : h + 2]
                at = step * block + h // 2 * LANES
                result[row : row + 1, at : at + LANES] = jnp.where(low_lanes, low, high)

    quarter = rows // 4
    for ref, which in ((keep_ref, half_row), (send_ref, 1 - half_row)):
        for part in range(2):
            pick = pl.ds(pl.multiple_of((2 * part + which) * quarter, 16), quarter)
            ref[part * quarter : (part + 1) * quarter, :width] = result[pick, :].astype(BF16)
            ref[part * quarter : (part + 1) * quarter, width:] = stats[pick, :].astype(BF16)


def attention(queries, keys, values, at):
    rows, width = queries.shape
    requests, slab, depth = keys.shape
    half = jax.ShapeDtypeStruct((rows // 2, width + LANES), BF16)
    return pl.pallas_call(
        attention_kernel,
        in_specs=[SMEM, HBM, HBM, HBM],
        out_specs=[VMEM, VMEM],
        out_shape=[half, half],
        scratch_shapes=[
            pltpu.VMEM(queries.shape, BF16),
            pltpu.VMEM(keys.shape, BF16),
            pltpu.VMEM(values.shape, BF16),
            pltpu.VMEM((slab, rows), F32),
            pltpu.VMEM((rows, width), F32),
            pltpu.VMEM((rows, LANES), F32),
            pltpu.VMEM((requests - 1, 8 * width // (2 * (H // KVH) * HD), depth), F32),
            pltpu.SemaphoreType.DMA((1 + 2 * requests,)),
        ],
        compiler_params=params(56),
        name="attention",
    )(at, queries, keys, values)


def expanded(scale, width):
    high = scale.astype(BF16).astype(F32)
    both = (high + pltpu.roll(scale - high, SUM_HIGH, 1)).astype(BF16)
    shape = (LANES, width)
    k, column = iota(shape, 0), iota(shape, 1)
    spread = one_hot(((k & (SUM_HIGH - 1)) == column // HD) & (k < 2 * SUM_HIGH))
    return dot(both, spread)


def merged(parts, width):
    tiles = [part[:, width:].astype(F32) for part in parts]
    valid = iota((1, LANES), 1) < width // HD
    top = functools.reduce(jnp.maximum, tiles)
    scales = [jnp.where(valid, jnp.exp(tile - top), 0.0) for tile in tiles]
    sums = [pltpu.roll(tile, LANES - SUM_HIGH, 1) + pltpu.roll(tile, LANES - SUM_LOW, 1) for tile in tiles]
    total = functools.reduce(jnp.add, [a * b for a, b in zip(sums, scales)])
    return top, total, scales, valid


def weighted(parts, scales, width):
    terms = [part[:, :width].astype(F32) * expanded(scale, width) for part, scale in zip(parts, scales)]
    return functools.reduce(jnp.add, terms).astype(BF16)


def join_kernel(at_ref, own_ref, other_ref, keep_ref, send_ref):
    rows, width = keep_ref.shape[0], own_ref.shape[1] - LANES
    for ref, which in ((send_ref, 1 - at_ref[0]), (keep_ref, at_ref[0])):
        pick = pl.ds(pl.multiple_of(which * rows, 16), rows)
        parts = [own_ref[pick, :], other_ref[pick, :]]
        top, total, scales, valid = merged(parts, width)
        ref[:, :width] = weighted(parts, scales, width)
        high = total.astype(BF16).astype(F32)
        stat = jnp.where(valid, top, 0.0)
        stat = stat + pltpu.roll(jnp.where(valid, high, 0.0), SUM_HIGH, 1)
        stat = stat + pltpu.roll(jnp.where(valid, total - high, 0.0), SUM_LOW, 1)
        ref[:, width:] = stat.astype(BF16)


def project_kernel(at_ref, own_ref, other_ref, w0, w1, w2, w3, residual_ref, gain_ref, normed_ref, out_ref, attended):
    width = own_ref.shape[1] - LANES
    parts = [own_ref[...], other_ref[...]]
    _, total, scales, valid = merged(parts, width)
    inverse = 1.0 / jnp.where(valid, total, 1.0)
    attended[...] = weighted(parts, [scale * inverse for scale in scales], width)
    mixed = None
    depth = w0.shape[0]
    for flip, weight in enumerate((w0, w1, w2, w3)):
        column = pl.multiple_of((at_ref[0] ^ flip) * depth, LANES)
        term = dot(attended[:, pl.ds(column, depth)], weight[...])
        mixed = term if mixed is None else mixed + term
    residual = (residual_ref[...].astype(F32) + mixed).astype(BF16)
    out_ref[...] = residual
    wide = residual.astype(F32)
    scale = lax.rsqrt(jnp.mean(wide * wide, axis=-1, keepdims=True) + 1e-05)
    normed_ref[...] = (wide * scale * gain_ref[...]).astype(BF16)


def feed_kernel(main, tail, count, order, z_ref, *refs):
    tokens, weights = refs[:count], refs[count : count + 4]
    keep_ref, send_ref, x = refs[count + 4 :]
    width = x.shape[1]
    block = width // OUTER
    rows = tokens[0].shape[0]
    columns = [pl.multiple_of((z_ref[0] ^ b) * block, LANES) for b in order]
    for index, ref in enumerate(tokens):
        for b in range(OUTER):
            x[index * rows : (index + 1) * rows, b * block : (b + 1) * block] = ref[:, pl.ds(columns[b], block)]

    def silu(v):
        return v / (1.0 + jnp.exp(-v))

    lane = iota((1, LANES), 1)
    second = 2 * main + LANES
    depth = weights[0].shape[0]
    hidden = []
    for first, last in (weights[:2], weights[2:]):
        sums = dot(x[:, :depth], first[:, :second]) + dot(x[:, depth:], last[:, :second])
        end = sums[:, 2 * main :]
        ends = silu(end) * pltpu.roll(end, LANES - tail, 1)
        hidden.append(
            jnp.concatenate(
                [
                    (silu(sums[:, :main]) * sums[:, main : 2 * main]).astype(BF16),
                    jnp.where(lane < tail, ends, 0.0).astype(BF16),
                ],
                1,
            )
        )
    half = count * rows // 2
    for b in range(OUTER):
        place = b * block
        which = place // depth
        pick = slice(place - which * depth, place - which * depth + block)
        out = lax.dot_general(hidden[0], weights[which][pick, second:], NT, preferred_element_type=F32)
        out = out + lax.dot_general(hidden[1], weights[2 + which][pick, second:], NT, preferred_element_type=F32)
        out = out.astype(BF16)
        keep_ref[:, pl.ds(columns[b], block)] = out[:half]
        send_ref[:, pl.ds(columns[b], block)] = out[half:]


def feed(main, tail, order, z, tokens, weights):
    rows, width = tokens[0].shape
    count = len(tokens)
    half = jax.ShapeDtypeStruct((count * rows // 2, width), BF16)
    return pl.pallas_call(
        functools.partial(feed_kernel, main, tail, count, order),
        in_specs=[SMEM] + [VMEM] * (count + 4),
        out_specs=[VMEM] * 2,
        out_shape=[half, half],
        scratch_shapes=[pltpu.VMEM((count * rows, width), BF16)],
        compiler_params=params(24),
        name="feed",
    )(z, *tokens, *weights)


def after(value, *others):
    return lax.optimization_barrier((value, *others))[0]


def per_device(
    residual_in,
    queries,
    key_cache,
    value_cache,
    cache_lengths,
    out_weight,
    norm_gain,
    gate_weight,
    up_weight,
    down_weight,
):
    dp_size, kv_size = lax.axis_size("dp"), lax.axis_size("kv")
    inner = dp_size // OUTER
    dp_index, kv_index = lax.axis_index("dp"), lax.axis_index("kv")
    z, y = (dp_index // inner).reshape(1), dp_index % inner
    core, chip = kv_index % 2, kv_index // 2
    units = gate_weight.shape[1]
    main = units // OUTER // LANES * LANES
    tail = units // OUTER - main
    width = residual_in.shape[1]

    def kv_flip(a, bit):
        return lax.ppermute(a, "kv", [(i, i ^ bit) for i in range(kv_size)])

    def z_flip(a, by):
        return lax.ppermute(a, "dp", [(i, i ^ (by * inner)) for i in range(dp_size)])

    def y_flip(a, bit):
        return lax.ppermute(a, "dp", [(i, i ^ bit) for i in range(dp_size)])

    w2 = kv_flip(out_weight, 2)
    w1 = kv_flip(out_weight, 1)

    rows = gate_weight.shape[0]
    cuts = [(flip, 0, rows) for flip in range(OUTER)]
    sizes = [(size, 3 * main + 2 * LANES) for _, _, size in cuts]
    packed = pl.pallas_call(
        functools.partial(pack_kernel, main, tail, cuts),
        in_specs=[SMEM] + [HBM] * 3,
        out_specs=[HBM] * len(cuts),
        out_shape=[jax.ShapeDtypeStruct(size, BF16) for size in sizes],
        scratch_shapes=[pltpu.VMEM(size, BF16) for size in sizes]
        + [
            pltpu.VMEM((3,) + gate_weight.shape, BF16),
            pltpu.SemaphoreType.DMA((len(cuts),)),
            pltpu.SemaphoreType.DMA((6,)),
        ],
        compiler_params=params(60),
        name="pack",
    )(after(z, w1), gate_weight, up_weight, down_weight.T)

    def shared(block):
        bit = 1
        while 2 * bit < inner:
            other = y_flip(block, bit)
            upper = (y & bit) > 0
            block = jnp.concatenate([jnp.where(upper, other, block), jnp.where(upper, block, other)], 0)
            bit *= 2
        return [block, y_flip(block, bit)]

    y_place = (y >= inner // 2).astype(jnp.int32).reshape(1)

    arrived = {index: z_flip(packed[index], index) for index in (1, 2)}
    blocks = {0: shared(packed[0])}
    at = jnp.concatenate([jnp.stack([kv_index * key_cache.shape[1], core]), cache_lengths])
    keep, send = attention(queries, key_cache, value_cache, after(at, *packed))
    arrived[3] = z_flip(after(packed[3], keep), 3)
    blocks[1] = shared(after(arrived[1], keep))
    other = kv_flip(after(send, blocks[0][1], arrived[1]), 1)
    half = jax.ShapeDtypeStruct((keep.shape[0] // 2, keep.shape[1]), BF16)
    keep, send = pl.pallas_call(
        join_kernel,
        in_specs=[SMEM, VMEM, VMEM],
        out_specs=[VMEM, VMEM],
        out_shape=[half, half],
        compiler_params=params(16),
        name="join",
    )(after(chip.reshape(1), arrived[2]), keep, other)
    other = kv_flip(send, 2)
    blocks[2] = shared(after(arrived[2], keep))
    w3 = kv_flip(after(w2, keep), 1)
    tokens = jax.ShapeDtypeStruct(residual_in.shape, BF16)
    normed, residual = pl.pallas_call(
        project_kernel,
        in_specs=[SMEM] + [VMEM] * 8,
        out_specs=[VMEM, VMEM],
        out_shape=[tokens, tokens],
        scratch_shapes=[pltpu.VMEM(residual_in.shape, BF16)],
        compiler_params=params(16),
        name="project",
    )(after(kv_index.reshape(1), blocks[1][1]), keep, other, out_weight, w1, w2, w3, residual_in, norm_gain.reshape(1, width))
    blocks[3] = shared(after(arrived[3], normed))

    order = (0, 1, 2, 3)
    deep = width // OUTER

    def laid(indices, base, *others):
        spots, parts = [], []
        for index in indices:
            for mine in (True, False):
                spots.append((index * deep - base, deep // 2, mine))
                parts.append(blocks[index][0 if mine else 1])
        return place(parts, spots, after(y_place, *others))

    near = [laid((0, 1), 0, normed)]
    count = residual_in.shape[0]
    here = {s: z_flip(normed, s) if s else normed for s in order}
    there = {s: kv_flip(here[s], 2) for s in order}
    near.append(laid((2, 3), 2 * deep, there[0], here[1], here[2]))
    weights = near + [kv_flip(part, 1) for part in near]

    def added(a, b):
        return (a.astype(F32) + b.astype(F32)).astype(BF16)

    mlp = None
    for shifts in ((0,), (1,), (2,), (3,)):
        tokens = [here[s] for s in shifts] + [there[s] for s in shifts]
        keep, send = feed(main, tail, order, z, tokens, weights)
        other = kv_flip(send, 2)
        for index, s in enumerate(shifts):
            pick = slice(index * count, (index + 1) * count)
            term = added(keep[pick], other[pick])
            if s:
                term = z_flip(term, s)
            mlp = term.astype(F32) if mlp is None else mlp + term.astype(F32)
    return (residual.astype(F32) + mlp).astype(BF16)


def solution(mesh):
    placed = (
        P(("dp", "kv"), None),
        P("dp", None),
        P("dp", "kv", None),
        P("dp", "kv", None),
        P("dp"),
        P("kv", None),
        P(),
        P("dp", "kv"),
        P("dp", "kv"),
        P("kv", "dp"),
    )
    return jax.shard_map(
        per_device, mesh=mesh, in_specs=placed, out_specs=P(("dp", "kv"), None), check_vma=False
    )
```

time: 185 us -> 130 us (0.70)
  waiting for transfers between devices: 74.8 us -> 43.7 us
  local copies, waits for them, and re-layouts: 21.7 us -> 5.53 us
  starting transfers between devices: 51.5 us -> 44.7 us
    unnamed x55 -> x18, local copies, waits for them, and re-layouts: 20.9 us -> 5.53 us
    ppermute x25 -> x15, waiting for transfers between devices: 16.8 us -> 3.05 us  [kv_flip(): return lax.ppermute(a, 'kv', [(i, i ^ bit) for i in range(kv_size)])]
    ppermute x12 -> x9, waiting for transfers between devices: 44 us -> 31.4 us  [z_flip(): return lax.ppermute(a, 'dp', [(i, i ^ by * inner) for i in range(dp_size)])]
    ppermute x8 -> x4, waiting for transfers between devices: 13.9 us -> 9.23 us  [y_flip(): return lax.ppermute(a, 'dp', [(i, i ^ bit) for i in range(dp_size)])]
    ppermute x25 -> x15, starting transfers between devices: 16.4 us -> 13.9 us  [kv_flip(): return lax.ppermute(a, 'kv', [(i, i ^ bit) for i in range(kv_size)])]
    ppermute x8 -> x4, starting transfers between devices: 7.88 us -> 5.59 us  [y_flip(): return lax.ppermute(a, 'dp', [(i, i ^ bit) for i in range(dp_size)])]
    ppermute x12 -> x9, starting transfers between devices: 27.1 us -> 25.2 us  [z_flip(): return lax.ppermute(a, 'dp', [(i, i ^ by * inner) for i in range(dp_size)])]
    pallas_call x7 -> x8, Pallas kernels: 30.1 us -> 29.1 us  [the longest x1 13.9 us: attention(): pl.pallas_call(attention_kernel, in_specs=[SMEM, HBM, HBM, HBM], out_spec...]
  transfers between devices with their start and end apart: 45 -> 28, of which waited for: 12 -> 10; matrix products, arithmetic and copies ran while one was open for 2% -> 1% of each run, Pallas kernels for 19% -> 25%
where the time goes in v2:
time: 130 us; the launch traced here: 129 us
  starting transfers between devices  44.7 us (34%)
  waiting for transfers between devices  43.7 us (34%)
  Pallas kernels  32.9 us (25%)
  local copies, waits for them, and re-layouts  5.53 us (4%)
  other arithmetic  2.22 us (2%)
    ppermute x9, waiting for transfers between devices, z_flip(): return lax.ppermute(a, 'dp', [(i, i ^ by * inner) for i in range(dp_size)])  31.4 us
    ppermute x9, starting transfers between devices, z_flip(): return lax.ppermute(a, 'dp', [(i, i ^ by * inner) for i in range(dp_size)])  25.2 us
    ppermute x15, starting transfers between devices, kv_flip(): return lax.ppermute(a, 'kv', [(i, i ^ bit) for i in range(kv_size)])  13.9 us
    pallas_call x1, Pallas kernels, attention(): pl.pallas_call(attention_kernel, in_specs=[SMEM, HBM, HBM, HBM], out_spec...  13.9 us
    ppermute x4, waiting for transfers between devices, y_flip(): return lax.ppermute(a, 'dp', [(i, i ^ bit) for i in range(dp_size)])  9.23 us
    pallas_call x4, Pallas kernels, feed(): pl.pallas_call(functools.partial(feed_kernel, main, tail, count, order),...  9.03 us
    ppermute x4, starting transfers between devices, y_flip(): return lax.ppermute(a, 'dp', [(i, i ^ bit) for i in range(dp_size)])  5.59 us
    unnamed x18, local copies, waits for them, and re-layouts  5.53 us
  transfers between devices with their start and end apart: 28, of which 10 were waited for; matrix products, arithmetic and copies ran while one was open for 1% of the time, Pallas kernels for 25%

profile of v2, /device:TPU:0, one launch (start us, length us, event | category | flops | bytes accessed | tf_op | source)
XLA Modules:
  0.0 129.2 jit_solution(12305181382353954630)
XLA Ops:
  0.0 0.5 collective-permute-start
  0.5 2.5 %collective-permute-start.7 = (bf16[384,1536]{1,0:T(8,128)(2,1)}, bf16[384,1536]{1,0:T(8,128)(2,1)S(1)}, u32[]{:S(2)}, u32[]{:S(2)}) collective-permute-start(bf16[384,1536]{1,0:T(8,128)(2,1)} %w0.1), channel_id=1, source_target_pairs={{0,2},{1,3},{2,0},{3,1},{4,6},{5,7},{6,4},{7,5},{8,10},{9,11},{10,... | collective-permute-start | bytes 3538952 | tf_op jit(solution)/shard_map/ppermute | solution.py:386
  2.9 0.2 collective-permute-done.w1
  3.1 3.3 %pack.1 = (bf16[192,1408]{1,0:T(8,128)(2,1)}, bf16[192,1408]{1,0:T(8,128)(2,1)}, bf16[192,1408]{1,0:T(8,128)(2,1)}, bf16[192,1408]{1,0:T(8,128)(2,1)}) custom-call(s32[1]{0:T(128)} %bitcast.1.z_ref, bf16[192,1728]{1,0:T(8,128)(2,1)} %gate_ref.1, bf16[192,1728]{1,0:T(8,128)(2,1)} %up_ref.1, bf16[192,1728]{1,0:T(8,128)(2,1)} %bitcast.7), custom_call_target="tpu_custom_call" | custom-call | tf_op jit(solution)/shard_map/pack/pallas_call | solution.py:400
  6.5 2.9 %collective-permute-start.4 = (bf16[192,1408]{1,0:T(8,128)(2,1)}, bf16[192,1408]{1,0:T(8,128)(2,1)}, u32[]{:S(2)}, u32[]{:S(2)}) collective-permute-start(bf16[192,1408]{1,0:T(8,128)(2,1)} %get-tuple-element.37.refs_0_), channel_id=1, source_target_pairs={{0,4},{4,0},{8,12},{12,8},{16,20},{20,16},{24,28},{28,24},{1,5},{5... | collective-permute-start | bytes 1622024 | tf_op jit(solution)/shard_map/ppermute | solution.py:392
  9.4 1.6 %collective-permute-start.1 = (bf16[192,1408]{1,0:T(8,128)(2,1)}, bf16[192,1408]{1,0:T(8,128)(2,1)}, u32[]{:S(2)}, u32[]{:S(2)}) collective-permute-start(bf16[192,1408]{1,0:T(8,128)(2,1)} %get-tuple-element.36), channel_id=1, source_target_pairs={{0,8},{4,12},{8,0},{12,4},{16,24},{20,28},{24,16},{28,20},{1,9},{5... | collective-permute-start | bytes 1622024 | tf_op jit(solution)/shard_map/ppermute | solution.py:389
  11.0 2.6 %collective-permute-start.3 = (bf16[192,1408]{1,0:T(8,128)(2,1)}, bf16[192,1408]{1,0:T(8,128)(2,1)}, u32[]{:S(2)}, u32[]{:S(2)}) collective-permute-start(bf16[192,1408]{1,0:T(8,128)(2,1)} %get-tuple-element.38), channel_id=1, source_target_pairs={{0,16},{4,20},{8,24},{12,28},{16,0},{20,4},{24,8},{28,12},{1,17},{... | collective-permute-start | bytes 1622024 | tf_op jit(solution)/shard_map/ppermute | solution.py:389
  13.6 1.2 pad_add_fusion.at_ref
  14.8 13.9 %attention.1 = (bf16[128,1664]{1,0:T(8,128)(2,1)}, bf16[128,1664]{1,0:T(8,128)(2,1)}) custom-call(s32[5]{0:T(128)} %pad_add_fusion.at_ref, bf16[256,1536]{1,0:T(8,128)(2,1)} %q_hbm.1, bf16[3,1024,512]{2,1,0:T(8,128)(2,1)} %k_hbm.1, bf16[3,1024,512]{2,1,0:T(8,128)(2,1)} %v_hbm.1), custom_call_target="tpu_custom_call" | custom-call | tf_op jit(solution)/shard_map/attention/pallas_call | solution.py:224
  28.8 6.5 %collective-permute-done.1.refs_2_ = bf16[192,1408]{1,0:T(8,128)(2,1)} collective-permute-done((bf16[192,1408]{1,0:T(8,128)(2,1)}, bf16[192,1408]{1,0:T(8,128)(2,1)}, u32[]{:S(2)}, u32[]{:S(2)}) %collective-permute-start.1) | collective-permute-done | bytes 540704 | tf_op jit(solution)/shard_map/ppermute | solution.py:389
  35.2 0.0 collective-permute-start.5
  35.3 2.4 %collective-permute-done.3.refs_0_ = bf16[192,1408]{1,0:T(8,128)(2,1)} collective-permute-done((bf16[192,1408]{1,0:T(8,128)(2,1)}, bf16[192,1408]{1,0:T(8,128)(2,1)}, u32[]{:S(2)}, u32[]{:S(2)}) %collective-permute-start.3) | collective-permute-done | bytes 540704 | tf_op jit(solution)/shard_map/ppermute | solution.py:389
  37.6 1.0 copy-done.4
  38.6 1.5 %join.1 = (bf16[64,1664]{1,0:T(8,128)(2,1)S(1)}, bf16[64,1664]{1,0:T(8,128)(2,1)S(1)}) custom-call(s32[1]{0:T(128)} %bitcast.5.at_ref, bf16[128,1664]{1,0:T(8,128)(2,1)S(1)} %copy-done.4, bf16[128,1664]{1,0:T(8,128)(2,1)} %collective-permute-done.5.other_ref), custom_call_target="tpu_custom_call" | custom-call | tf_op jit(solution)/shard_map/join/pallas_call | solution.py:434
  40.1 0.1 collective-permute-start.8
  40.2 0.6 collective-permute-start.2
  40.7 2.5 %collective-permute-start.13 = (bf16[192,1408]{1,0:T(8,128)(2,1)}, bf16[192,1408]{1,0:T(8,128)(2,1)}, u32[]{:S(2)}, u32[]{:S(2)}) collective-permute-start(bf16[192,1408]{1,0:T(8,128)(2,1)} %get-tuple-element.55), channel_id=1, source_target_pairs={{0,24},{4,28},{8,16},{12,20},{16,8},{20,12},{24,0},{28,4},{1,25},{... | collective-permute-start | bytes 1622024 | tf_op jit(solution)/shard_map/ppermute | solution.py:389
  43.2 1.5 %collective-permute-start.6 = (bf16[64,1664]{1,0:T(8,128)(2,1)S(1)}, bf16[64,1664]{1,0:T(8,128)(2,1)S(1)}, u32[]{:S(2)}, u32[]{:S(2)}) collective-permute-start(bf16[64,1664]{1,0:T(8,128)(2,1)S(1)} %get-tuple-element.48), channel_id=1, source_target_pairs={{0,2},{1,3},{2,0},{3,1},{4,6},{5,7},{6,4},{7,5},{8,10},{9,11},{10,... | collective-permute-start | bytes 638984 | tf_op jit(solution)/shard_map/ppermute | solution.py:386
  44.7 1.6 %collective-permute-start.12 = (bf16[192,1408]{1,0:T(8,128)(2,1)}, bf16[192,1408]{1,0:T(8,128)(2,1)}, u32[]{:S(2)}, u32[]{:S(2)}) collective-permute-start(bf16[192,1408]{1,0:T(8,128)(2,1)} %collective-permute-done.3.refs_0_), channel_id=1, source_target_pairs={{0,4},{4,0},{8,12},{12,8},{16,20},{20,16},{24,28},{28,24},{1,5},{5... | collective-permute-start | bytes 1622024 | tf_op jit(solution)/shard_map/ppermute | solution.py:392
  46.3 9.2 %collective-permute-done.2.refs_3_ = bf16[192,1408]{1,0:T(8,128)(2,1)S(1)} collective-permute-done((bf16[192,1408]{1,0:T(8,128)(2,1)}, bf16[192,1408]{1,0:T(8,128)(2,1)S(1)}, u32[]{:S(2)}, u32[]{:S(2)}) %collective-permute-start.2) | collective-permute-done | bytes 540704 | tf_op jit(solution)/shard_map/ppermute | solution.py:392
  55.5 0.8 copy-done.2
  56.3 0.0 collective-permute-done.6.other_ref
  56.3 0.0 collective-permute-done.8.w3
  56.4 0.0 copy-start.5
  56.4 0.9 copy-done.5
  57.3 2.3 %project.1 = (bf16[64,1536]{1,0:T(8,128)(2,1)}, bf16[64,1536]{1,0:T(8,128)(2,1)S(1)}) custom-call(s32[1]{0:T(128)} %bitcast.at_ref, bf16[64,1664]{1,0:T(8,128)(2,1)S(1)} %get-tuple-element.47.own_ref, bf16[64,1664]{1,0:T(8,128)(2,1)S(1)} %collective-permute-done.6.other_ref, bf16[384,1536]{1,0:T(8,128)(2,1)S(1)} %copy-done, ...), custom_call_target="tpu_custom_call" | custom-call | tf_op jit(solution)/shard_map/project/pallas_call | solution.py:446
  59.6 0.7 copy-done.6
  60.3 0.5 collective-permute-start.14
  60.8 8.2 %collective-permute-start.10 = (bf16[64,1536]{1,0:T(8,128)(2,1)}, bf16[64,1536]{1,0:T(8,128)(2,1)S(1)}, u32[]{:S(2)}, u32[]{:S(2)}) collective-permute-start(bf16[64,1536]{1,0:T(8,128)(2,1)} %get-tuple-element.51.refs_0_), channel_id=1, source_target_pairs={{0,8},{4,12},{8,0},{12,4},{16,24},{20,28},{24,16},{28,20},{1,9},{5... | collective-permute-start | bytes 589832 | tf_op jit(solution)/shard_map/ppermute | solution.py:389
  69.0 1.5 %collective-permute-start.9 = (bf16[64,1536]{1,0:T(8,128)(2,1)}, bf16[64,1536]{1,0:T(8,128)(2,1)S(1)}, u32[]{:S(2)}, u32[]{:S(2)}) collective-permute-start(bf16[64,1536]{1,0:T(8,128)(2,1)} %get-tuple-element.51.refs_0_), channel_id=1, source_target_pairs={{0,2},{1,3},{2,0},{3,1},{4,6},{5,7},{6,4},{7,5},{8,10},{9,11},{10,... | collective-permute-start | bytes 589832 | tf_op jit(solution)/shard_map/ppermute | solution.py:386
  70.5 1.0 copy-done.1
  71.5 1.0 copy-done.3
  72.6 1.4 %place.2.refs_2_ = bf16[768,1408]{1,0:T(8,128)(2,1)S(1)} custom-call(s32[1]{0:T(128)} %bitcast.6.at_ref, bf16[192,1408]{1,0:T(8,128)(2,1)S(1)} %copy-done.1, bf16[192,1408]{1,0:T(8,128)(2,1)} %collective-permute-done.4.refs_1_, bf16[192,1408]{1,0:T(8,128)(2,1)} %collective-permute-done.1.refs_2_, bf16[192,1408]{1,0:T(8,128)(2,1)S(1)} %copy-done.3), custom_call_target="tpu_custom_call" | custom-call | tf_op jit(solution)/shard_map/place/pallas_call | solution.py:88
  73.9 2.1 %collective-permute-done.10.refs_0_ = bf16[64,1536]{1,0:T(8,128)(2,1)S(1)} collective-permute-done((bf16[64,1536]{1,0:T(8,128)(2,1)}, bf16[64,1536]{1,0:T(8,128)(2,1)S(1)}, u32[]{:S(2)}, u32[]{:S(2)}) %collective-permute-start.10) | collective-permute-done | bytes 196640 | tf_op jit(solution)/shard_map/ppermute | solution.py:389
  76.1 3.8 %collective-permute-done.11.refs_0_ = bf16[64,1536]{1,0:T(8,128)(2,1)S(1)} collective-permute-done((bf16[64,1536]{1,0:T(8,128)(2,1)}, bf16[64,1536]{1,0:T(8,128)(2,1)S(1)}, u32[]{:S(2)}, u32[]{:S(2)}) %collective-permute-start.11) | collective-permute-done | bytes 196640 | tf_op jit(solution)/shard_map/ppermute | solution.py:389
  79.9 0.0 collective-permute-done.9.refs_1_
  79.9 0.0 collective-permute-done.12.refs_1_
  79.9 0.0 collective-permute-done.14.refs_3_
  79.9 1.5 %place.3.refs_3_ = bf16[768,1408]{1,0:T(8,128)(2,1)S(1)} custom-call(s32[1]{0:T(128)} %bitcast.6.at_ref, bf16[192,1408]{1,0:T(8,128)(2,1)} %collective-permute-done.3.refs_0_, bf16[192,1408]{1,0:T(8,128)(2,1)} %collective-permute-done.12.refs_1_, bf16[192,1408]{1,0:T(8,128)(2,1)} %collective-permute-done.13.refs_2_, ...), custom_call_target="tpu_custom_call" | custom-call | tf_op jit(solution)/shard_map/place/pallas_call | solution.py:88
  81.4 0.1 collective-permute-start.16
  81.5 1.5 %collective-permute-start.24 = (bf16[64,1536]{1,0:T(8,128)(2,1)}, bf16[64,1536]{1,0:T(8,128)(2,1)S(1)}, u32[]{:S(2)}, u32[]{:S(2)}) collective-permute-start(bf16[64,1536]{1,0:T(8,128)(2,1)} %get-tuple-element.51.refs_0_), channel_id=1, source_target_pairs={{0,24},{4,28},{8,16},{12,20},{16,8},{20,12},{24,0},{28,4},{1,25},{... | collective-permute-start | bytes 589832 | tf_op jit(solution)/shard_map/ppermute | solution.py:389
  83.0 1.5 %collective-permute-start.18 = (bf16[64,1536]{1,0:T(8,128)(2,1)S(1)}, bf16[64,1536]{1,0:T(8,128)(2,1)S(1)}, u32[]{:S(2)}, u32[]{:S(2)}) collective-permute-start(bf16[64,1536]{1,0:T(8,128)(2,1)S(1)} %collective-permute-done.10.refs_0_), channel_id=1, source_target_pairs={{0,2},{1,3},{2,0},{3,1},{4,6},{5,7},{6,4},{7,5},{8,10},{9,11},{10,... | collective-permute-start | bytes 589832 | tf_op jit(solution)/shard_map/ppermute | solution.py:386
  84.5 0.5 collective-permute-start.21
  85.0 6.0 %collective-permute-done.24.refs_0_ = bf16[64,1536]{1,0:T(8,128)(2,1)S(1)} collective-permute-done((bf16[64,1536]{1,0:T(8,128)(2,1)}, bf16[64,1536]{1,0:T(8,128)(2,1)S(1)}, u32[]{:S(2)}, u32[]{:S(2)}) %collective-permute-start.24) | collective-permute-done | bytes 196640 | tf_op jit(solution)/shard_map/ppermute | solution.py:389
  90.9 1.5 %collective-permute-start.25 = (bf16[64,1536]{1,0:T(8,128)(2,1)S(1)}, bf16[64,1536]{1,0:T(8,128)(2,1)S(1)}, u32[]{:S(2)}, u32[]{:S(2)}) collective-permute-start(bf16[64,1536]{1,0:T(8,128)(2,1)S(1)} %collective-permute-done.24.refs_0_), channel_id=1, source_target_pairs={{0,2},{1,3},{2,0},{3,1},{4,6},{5,7},{6,4},{7,5},{8,10},{9,11},{10,... | collective-permute-start | bytes 589832 | tf_op jit(solution)/shard_map/ppermute | solution.py:386
  92.4 2.0 %feed.5 = (bf16[64,1536]{1,0:T(8,128)(2,1)S(1)}, bf16[64,1536]{1,0:T(8,128)(2,1)S(1)}) custom-call(s32[1]{0:T(128)} %bitcast.1.z_ref, bf16[64,1536]{1,0:T(8,128)(2,1)S(1)} %collective-permute-done.10.refs_0_, bf16[64,1536]{1,0:T(8,128)(2,1)S(1)} %collective-permute-done.18.refs_1_, bf16[768,1408]{1,0:T(8,128)(2,1)S(1)} %place.2.refs_2_, ...), custom_call_target="tpu_custom_call" | custom-call | tf_op jit(solution)/shard_map/feed/pallas_call | solution.py:348
  94.5 0.6 collective-permute-start.19
  95.1 2.9 %feed.4 = (bf16[64,1536]{1,0:T(8,128)(2,1)S(1)}, bf16[64,1536]{1,0:T(8,128)(2,1)S(1)}) custom-call(s32[1]{0:T(128)} %bitcast.1.z_ref, bf16[64,1536]{1,0:T(8,128)(2,1)} %get-tuple-element.51.refs_0_, bf16[64,1536]{1,0:T(8,128)(2,1)S(1)} %collective-permute-done.9.refs_1_, bf16[768,1408]{1,0:T(8,128)(2,1)S(1)} %place.2.refs_2_, ...), custom_call_target="tpu_custom_call" | custom-call | tf_op jit(solution)/shard_map/feed/pallas_call | solution.py:348
  98.0 1.5 %collective-permute-start.17 = (bf16[64,1536]{1,0:T(8,128)(2,1)S(1)}, bf16[64,1536]{1,0:T(8,128)(2,1)S(1)}, u32[]{:S(2)}, u32[]{:S(2)}) collective-permute-start(bf16[64,1536]{1,0:T(8,128)(2,1)S(1)} %get-tuple-element.58), channel_id=1, source_target_pairs={{0,2},{1,3},{2,0},{3,1},{4,6},{5,7},{6,4},{7,5},{8,10},{9,11},{10,... | collective-permute-start | bytes 589832 | tf_op jit(solution)/shard_map/ppermute | solution.py:386
  99.6 2.0 %feed.6 = (bf16[64,1536]{1,0:T(8,128)(2,1)S(1)}, bf16[64,1536]{1,0:T(8,128)(2,1)S(1)}) custom-call(s32[1]{0:T(128)} %bitcast.1.z_ref, bf16[64,1536]{1,0:T(8,128)(2,1)S(1)} %collective-permute-done.11.refs_0_, bf16[64,1536]{1,0:T(8,128)(2,1)S(1)} %collective-permute-done.21.refs_1_, bf16[768,1408]{1,0:T(8,128)(2,1)S(1)} %place.2.refs_2_, ...), custom_call_target="tpu_custom_call" | custom-call | tf_op jit(solution)/shard_map/feed/pallas_call | solution.py:348
  101.6 0.6 collective-permute-start.22
  102.2 2.0 %feed.7 = (bf16[64,1536]{1,0:T(8,128)(2,1)S(1)}, bf16[64,1536]{1,0:T(8,128)(2,1)S(1)}) custom-call(s32[1]{0:T(128)} %bitcast.1.z_ref, bf16[64,1536]{1,0:T(8,128)(2,1)S(1)} %collective-permute-done.24.refs_0_, bf16[64,1536]{1,0:T(8,128)(2,1)S(1)} %collective-permute-done.25.refs_1_, bf16[768,1408]{1,0:T(8,128)(2,1)S(1)} %place.2.refs_2_, ...), custom_call_target="tpu_custom_call" | custom-call | tf_op jit(solution)/shard_map/feed/pallas_call | solution.py:348
  104.3 1.5 %collective-permute-start.26 = (bf16[64,1536]{1,0:T(8,128)(2,1)S(1)}, bf16[64,1536]{1,0:T(8,128)(2,1)S(1)}, u32[]{:S(2)}, u32[]{:S(2)}) collective-permute-start(bf16[64,1536]{1,0:T(8,128)(2,1)S(1)} %get-tuple-element.64), channel_id=1, source_target_pairs={{0,2},{1,3},{2,0},{3,1},{4,6},{5,7},{6,4},{7,5},{8,10},{9,11},{10,... | collective-permute-start | bytes 589832 | tf_op jit(solution)/shard_map/ppermute | solution.py:386
  105.8 0.0 collective-permute-done.19
  105.9 3.7 %collective-permute-start.20 = (bf16[64,1536]{1,0:T(8,128)(2,1)S(1)}, bf16[64,1536]{1,0:T(8,128)(2,1)S(1)}, u32[]{:S(2)}, u32[]{:S(2)}) collective-permute-start(bf16[64,1536]{1,0:T(8,128)(2,1)S(1)} %add_convert_fusion.3), channel_id=1, source_target_pairs={{0,8},{4,12},{8,0},{12,4},{16,24},{20,28},{24,16},{28,20},{1,9},{5... | collective-permute-start | bytes 589832 | tf_op jit(solution)/shard_map/ppermute | solution.py:389
  109.6 2.2 %collective-permute-done.22 = bf16[64,1536]{1,0:T(8,128)(2,1)S(1)} collective-permute-done((bf16[64,1536]{1,0:T(8,128)(2,1)S(1)}, bf16[64,1536]{1,0:T(8,128)(2,1)S(1)}, u32[]{:S(2)}, u32[]{:S(2)}) %collective-permute-start.22) | collective-permute-done | bytes 196640 | tf_op jit(solution)/shard_map/ppermute | solution.py:386
  111.8 2.8 %collective-permute-start.23 = (bf16[64,1536]{1,0:T(8,128)(2,1)S(1)}, bf16[64,1536]{1,0:T(8,128)(2,1)S(1)}, u32[]{:S(2)}, u32[]{:S(2)}) collective-permute-start(bf16[64,1536]{1,0:T(8,128)(2,1)S(1)} %add_convert_fusion.2), channel_id=1, source_target_pairs={{0,16},{4,20},{8,24},{12,28},{16,0},{20,4},{24,8},{28,12},{1,17},{... | collective-permute-start | bytes 589832 | tf_op jit(solution)/shard_map/ppermute | solution.py:389
  114.6 0.6 collective-permute-done.26
  115.2 0.1 add_convert_fusion.1
  115.3 2.5 %collective-permute-start.27 = (bf16[64,1536]{1,0:T(8,128)(2,1)S(1)}, bf16[64,1536]{1,0:T(8,128)(2,1)S(1)}, u32[]{:S(2)}, u32[]{:S(2)}) collective-permute-start(bf16[64,1536]{1,0:T(8,128)(2,1)S(1)} %add_convert_fusion.1), channel_id=1, source_target_pairs={{0,24},{4,28},{8,16},{12,20},{16,8},{20,12},{24,0},{28,4},{1,25},{... | collective-permute-start | bytes 589832 | tf_op jit(solution)/shard_map/ppermute | solution.py:389
  117.8 0.0 collective-permute-done.17
  117.8 0.0 collective-permute-done.20
  117.8 10.6 %collective-permute-done.23 = bf16[64,1536]{1,0:T(8,128)(2,1)S(1)} collective-permute-done((bf16[64,1536]{1,0:T(8,128)(2,1)S(1)}, bf16[64,1536]{1,0:T(8,128)(2,1)S(1)}, u32[]{:S(2)}, u32[]{:S(2)}) %collective-permute-start.23) | collective-permute-done | bytes 196640 | tf_op jit(solution)/shard_map/ppermute | solution.py:389
  128.4 0.8 add_convert_fusion
  (26 shorter events, 0.2 us)
Async XLA Ops:
  0.0 3.1 %collective-permute-start = (bf16[384,1536]{1,0:T(8,128)(2,1)}, bf16[384,1536]{1,0:T(8,128)(2,1)S(1)}, u32[]{:S(2)}, u32[]{:S(2)}) collective-permute-start(bf16[384,1536]{1,0:T(8,128)(2,1)} %w0.1), channel_id=1, source_target_pairs={{0,1},{1,0},{2,3},{3,2},{4,5},{5,4},{6,7},{7,6},{8,9},{9,8},{10,11... | collective-permute-start | bytes 3538952 | tf_op jit(solution)/shard_map/ppermute | solution.py:386
  0.5 39.6 %collective-permute-start.7 = (bf16[384,1536]{1,0:T(8,128)(2,1)}, bf16[384,1536]{1,0:T(8,128)(2,1)S(1)}, u32[]{:S(2)}, u32[]{:S(2)}) collective-permute-start(bf16[384,1536]{1,0:T(8,128)(2,1)} %w0.1), channel_id=1, source_target_pairs={{0,2},{1,3},{2,0},{3,1},{4,6},{5,7},{6,4},{7,5},{8,10},{9,11},{10,... | collective-permute-start | bytes 3538952 | tf_op jit(solution)/shard_map/ppermute | solution.py:386
  6.5 22.3 %collective-permute-start.4 = (bf16[192,1408]{1,0:T(8,128)(2,1)}, bf16[192,1408]{1,0:T(8,128)(2,1)}, u32[]{:S(2)}, u32[]{:S(2)}) collective-permute-start(bf16[192,1408]{1,0:T(8,128)(2,1)} %get-tuple-element.37.refs_0_), channel_id=1, source_target_pairs={{0,4},{4,0},{8,12},{12,8},{16,20},{20,16},{24,28},{28,24},{1,5},{5... | collective-permute-start | bytes 1622024 | tf_op jit(solution)/shard_map/ppermute | solution.py:392
  9.4 25.8 %collective-permute-start.1 = (bf16[192,1408]{1,0:T(8,128)(2,1)}, bf16[192,1408]{1,0:T(8,128)(2,1)}, u32[]{:S(2)}, u32[]{:S(2)}) collective-permute-start(bf16[192,1408]{1,0:T(8,128)(2,1)} %get-tuple-element.36), channel_id=1, source_target_pairs={{0,8},{4,12},{8,0},{12,4},{16,24},{20,28},{24,16},{28,20},{1,9},{5... | collective-permute-start | bytes 1622024 | tf_op jit(solution)/shard_map/ppermute | solution.py:389
  11.0 26.6 %collective-permute-start.3 = (bf16[192,1408]{1,0:T(8,128)(2,1)}, bf16[192,1408]{1,0:T(8,128)(2,1)}, u32[]{:S(2)}, u32[]{:S(2)}) collective-permute-start(bf16[192,1408]{1,0:T(8,128)(2,1)} %get-tuple-element.38), channel_id=1, source_target_pairs={{0,16},{4,20},{8,24},{12,28},{16,0},{20,4},{24,8},{28,12},{1,17},{... | collective-permute-start | bytes 1622024 | tf_op jit(solution)/shard_map/ppermute | solution.py:389
  14.8 29.9 %copy-start.8 = (f32[1536]{0:T(1024)S(1)}, f32[1536]{0:T(1024)}, u32[]{:S(2)}) copy-start(f32[1536]{0:T(1024)} %param.16) | copy-start | bytes 18436
  14.8 41.5 %copy-start = (bf16[384,1536]{1,0:T(8,128)(2,1)S(1)}, bf16[384,1536]{1,0:T(8,128)(2,1)}, u32[]{:S(2)}) copy-start(bf16[384,1536]{1,0:T(8,128)(2,1)} %w0.1) | copy-start | bytes 3538948
  35.2 2.4 %collective-permute-start.5 = (bf16[128,1664]{1,0:T(8,128)(2,1)}, bf16[128,1664]{1,0:T(8,128)(2,1)}, u32[]{:S(2)}, u32[]{:S(2)}) collective-permute-start(bf16[128,1664]{1,0:T(8,128)(2,1)} %get-tuple-element.46), channel_id=1, source_target_pairs={{0,1},{1,0},{2,3},{3,2},{4,5},{5,4},{6,7},{7,6},{8,9},{9,8},{10,11... | collective-permute-start | bytes 1277960 | tf_op jit(solution)/shard_map/ppermute | solution.py:386
  37.6 1.0 copy-start.4
  40.1 16.2 %collective-permute-start.8 = (bf16[384,1536]{1,0:T(8,128)(2,1)S(1)}, bf16[384,1536]{1,0:T(8,128)(2,1)S(1)}, u32[]{:S(2)}, u32[]{:S(2)}) collective-permute-start(bf16[384,1536]{1,0:T(8,128)(2,1)S(1)} %collective-permute-done.7.w2), channel_id=1, source_target_pairs={{0,1},{1,0},{2,3},{3,2},{4,5},{5,4},{6,7},{7,6},{8,9},{9,8},{10,11... | collective-permute-start | bytes 3538952 | tf_op jit(solution)/shard_map/ppermute | solution.py:386
  40.2 15.4 %collective-permute-start.2 = (bf16[192,1408]{1,0:T(8,128)(2,1)}, bf16[192,1408]{1,0:T(8,128)(2,1)S(1)}, u32[]{:S(2)}, u32[]{:S(2)}) collective-permute-start(bf16[192,1408]{1,0:T(8,128)(2,1)} %collective-permute-done.1.refs_2_), channel_id=1, source_target_pairs={{0,4},{4,0},{8,12},{12,8},{16,20},{20,16},{24,28},{28,24},{1,5},{5... | collective-permute-start | bytes 1622024 | tf_op jit(solution)/shard_map/ppermute | solution.py:392
  40.7 19.5 %collective-permute-start.13 = (bf16[192,1408]{1,0:T(8,128)(2,1)}, bf16[192,1408]{1,0:T(8,128)(2,1)}, u32[]{:S(2)}, u32[]{:S(2)}) collective-permute-start(bf16[192,1408]{1,0:T(8,128)(2,1)} %get-tuple-element.55), channel_id=1, source_target_pairs={{0,24},{4,28},{8,16},{12,20},{16,8},{20,12},{24,0},{28,4},{1,25},{... | collective-permute-start | bytes 1622024 | tf_op jit(solution)/shard_map/ppermute | solution.py:389
  43.2 13.1 %collective-permute-start.6 = (bf16[64,1664]{1,0:T(8,128)(2,1)S(1)}, bf16[64,1664]{1,0:T(8,128)(2,1)S(1)}, u32[]{:S(2)}, u32[]{:S(2)}) collective-permute-start(bf16[64,1664]{1,0:T(8,128)(2,1)S(1)} %get-tuple-element.48), channel_id=1, source_target_pairs={{0,2},{1,3},{2,0},{3,1},{4,6},{5,7},{6,4},{7,5},{8,10},{9,11},{10,... | collective-permute-start | bytes 638984 | tf_op jit(solution)/shard_map/ppermute | solution.py:386
  44.7 35.2 %collective-permute-start.12 = (bf16[192,1408]{1,0:T(8,128)(2,1)}, bf16[192,1408]{1,0:T(8,128)(2,1)}, u32[]{:S(2)}, u32[]{:S(2)}) collective-permute-start(bf16[192,1408]{1,0:T(8,128)(2,1)} %collective-permute-done.3.refs_0_), channel_id=1, source_target_pairs={{0,4},{4,0},{8,12},{12,8},{16,20},{20,16},{24,28},{28,24},{1,5},{5... | collective-permute-start | bytes 1622024 | tf_op jit(solution)/shard_map/ppermute | solution.py:392
  55.5 0.8 copy-start.2
  56.4 0.9 copy-start.5
  59.6 0.7 copy-start.6
  60.3 19.6 %collective-permute-start.14 = (bf16[192,1408]{1,0:T(8,128)(2,1)}, bf16[192,1408]{1,0:T(8,128)(2,1)S(1)}, u32[]{:S(2)}, u32[]{:S(2)}) collective-permute-start(bf16[192,1408]{1,0:T(8,128)(2,1)} %collective-permute-done.13.refs_2_), channel_id=1, source_target_pairs={{0,4},{4,0},{8,12},{12,8},{16,20},{20,16},{24,28},{28,24},{1,5},{5... | collective-permute-start | bytes 1622024 | tf_op jit(solution)/shard_map/ppermute | solution.py:392
  60.8 15.3 %collective-permute-start.10 = (bf16[64,1536]{1,0:T(8,128)(2,1)}, bf16[64,1536]{1,0:T(8,128)(2,1)S(1)}, u32[]{:S(2)}, u32[]{:S(2)}) collective-permute-start(bf16[64,1536]{1,0:T(8,128)(2,1)} %get-tuple-element.51.refs_0_), channel_id=1, source_target_pairs={{0,8},{4,12},{8,0},{12,4},{16,24},{20,28},{24,16},{28,20},{1,9},{5... | collective-permute-start | bytes 589832 | tf_op jit(solution)/shard_map/ppermute | solution.py:389
  69.0 10.9 %collective-permute-start.11 = (bf16[64,1536]{1,0:T(8,128)(2,1)}, bf16[64,1536]{1,0:T(8,128)(2,1)S(1)}, u32[]{:S(2)}, u32[]{:S(2)}) collective-permute-start(bf16[64,1536]{1,0:T(8,128)(2,1)} %get-tuple-element.51.refs_0_), channel_id=1, source_target_pairs={{0,16},{4,20},{8,24},{12,28},{16,0},{20,4},{24,8},{28,12},{1,17},{... | collective-permute-start | bytes 589832 | tf_op jit(solution)/shard_map/ppermute | solution.py:389
  69.0 10.9 %collective-permute-start.9 = (bf16[64,1536]{1,0:T(8,128)(2,1)}, bf16[64,1536]{1,0:T(8,128)(2,1)S(1)}, u32[]{:S(2)}, u32[]{:S(2)}) collective-permute-start(bf16[64,1536]{1,0:T(8,128)(2,1)} %get-tuple-element.51.refs_0_), channel_id=1, source_target_pairs={{0,2},{1,3},{2,0},{3,1},{4,6},{5,7},{6,4},{7,5},{8,10},{9,11},{10,... | collective-permute-start | bytes 589832 | tf_op jit(solution)/shard_map/ppermute | solution.py:386
  70.5 1.0 copy-start.1
  71.5 1.0 copy-start.3
  76.1 16.4 %collective-permute-start.15 = (bf16[768,1408]{1,0:T(8,128)(2,1)S(1)}, bf16[768,1408]{1,0:T(8,128)(2,1)S(1)}, u32[]{:S(2)}, u32[]{:S(2)}) collective-permute-start(bf16[768,1408]{1,0:T(8,128)(2,1)S(1)} %place.2.refs_2_), channel_id=1, source_target_pairs={{0,1},{1,0},{2,3},{3,2},{4,5},{5,4},{6,7},{7,6},{8,9},{9,8},{10,11... | collective-permute-start | bytes 6488072 | tf_op jit(solution)/shard_map/ppermute | solution.py:386
  81.4 11.0 %collective-permute-start.16 = (bf16[768,1408]{1,0:T(8,128)(2,1)S(1)}, bf16[768,1408]{1,0:T(8,128)(2,1)S(1)}, u32[]{:S(2)}, u32[]{:S(2)}) collective-permute-start(bf16[768,1408]{1,0:T(8,128)(2,1)S(1)} %place.3.refs_3_), channel_id=1, source_target_pairs={{0,1},{1,0},{2,3},{3,2},{4,5},{5,4},{6,7},{7,6},{8,9},{9,8},{10,11... | collective-permute-start | bytes 6488072 | tf_op jit(solution)/shard_map/ppermute | solution.py:386
  81.5 9.4 %collective-permute-start.24 = (bf16[64,1536]{1,0:T(8,128)(2,1)}, bf16[64,1536]{1,0:T(8,128)(2,1)S(1)}, u32[]{:S(2)}, u32[]{:S(2)}) collective-permute-start(bf16[64,1536]{1,0:T(8,128)(2,1)} %get-tuple-element.51.refs_0_), channel_id=1, source_target_pairs={{0,24},{4,28},{8,16},{12,20},{16,8},{20,12},{24,0},{28,4},{1,25},{... | collective-permute-start | bytes 589832 | tf_op jit(solution)/shard_map/ppermute | solution.py:389
  83.0 9.5 %collective-permute-start.18 = (bf16[64,1536]{1,0:T(8,128)(2,1)S(1)}, bf16[64,1536]{1,0:T(8,128)(2,1)S(1)}, u32[]{:S(2)}, u32[]{:S(2)}) collective-permute-start(bf16[64,1536]{1,0:T(8,128)(2,1)S(1)} %collective-permute-done.10.refs_0_), channel_id=1, source_target_pairs={{0,2},{1,3},{2,0},{3,1},{4,6},{5,7},{6,4},{7,5},{8,10},{9,11},{10,... | collective-permute-start | bytes 589832 | tf_op jit(solution)/shard_map/ppermute | solution.py:386
  84.5 15.1 %collective-permute-start.21 = (bf16[64,1536]{1,0:T(8,128)(2,1)S(1)}, bf16[64,1536]{1,0:T(8,128)(2,1)S(1)}, u32[]{:S(2)}, u32[]{:S(2)}) collective-permute-start(bf16[64,1536]{1,0:T(8,128)(2,1)S(1)} %collective-permute-done.11.refs_0_), channel_id=1, source_target_pairs={{0,2},{1,3},{2,0},{3,1},{4,6},{5,7},{6,4},{7,5},{8,10},{9,11},{10,... | collective-permute-start | bytes 589832 | tf_op jit(solution)/shard_map/ppermute | solution.py:386
  90.9 11.3 %collective-permute-start.25 = (bf16[64,1536]{1,0:T(8,128)(2,1)S(1)}, bf16[64,1536]{1,0:T(8,128)(2,1)S(1)}, u32[]{:S(2)}, u32[]{:S(2)}) collective-permute-start(bf16[64,1536]{1,0:T(8,128)(2,1)S(1)} %collective-permute-done.24.refs_0_), channel_id=1, source_target_pairs={{0,2},{1,3},{2,0},{3,1},{4,6},{5,7},{6,4},{7,5},{8,10},{9,11},{10,... | collective-permute-start | bytes 589832 | tf_op jit(solution)/shard_map/ppermute | solution.py:386
  94.5 11.4 %collective-permute-start.19 = (bf16[64,1536]{1,0:T(8,128)(2,1)S(1)}, bf16[64,1536]{1,0:T(8,128)(2,1)S(1)}, u32[]{:S(2)}, u32[]{:S(2)}) collective-permute-start(bf16[64,1536]{1,0:T(8,128)(2,1)S(1)} %get-tuple-element.60), channel_id=1, source_target_pairs={{0,2},{1,3},{2,0},{3,1},{4,6},{5,7},{6,4},{7,5},{8,10},{9,11},{10,... | collective-permute-start | bytes 589832 | tf_op jit(solution)/shard_map/ppermute | solution.py:386
  98.0 19.7 %collective-permute-start.17 = (bf16[64,1536]{1,0:T(8,128)(2,1)S(1)}, bf16[64,1536]{1,0:T(8,128)(2,1)S(1)}, u32[]{:S(2)}, u32[]{:S(2)}) collective-permute-start(bf16[64,1536]{1,0:T(8,128)(2,1)S(1)} %get-tuple-element.58), channel_id=1, source_target_pairs={{0,2},{1,3},{2,0},{3,1},{4,6},{5,7},{6,4},{7,5},{8,10},{9,11},{10,... | collective-permute-start | bytes 589832 | tf_op jit(solution)/shard_map/ppermute | solution.py:386
  101.6 26.8 %copy-start.7 = (bf16[64,1536]{1,0:T(8,128)(2,1)S(1)}, bf16[64,1536]{1,0:T(8,128)(2,1)}, u32[]{:S(2)}) copy-start(bf16[64,1536]{1,0:T(8,128)(2,1)} %copy-done.6) | copy-start | bytes 589828
  101.6 10.1 %collective-permute-start.22 = (bf16[64,1536]{1,0:T(8,128)(2,1)S(1)}, bf16[64,1536]{1,0:T(8,128)(2,1)S(1)}, u32[]{:S(2)}, u32[]{:S(2)}) collective-permute-start(bf16[64,1536]{1,0:T(8,128)(2,1)S(1)} %get-tuple-element.62), channel_id=1, source_target_pairs={{0,2},{1,3},{2,0},{3,1},{4,6},{5,7},{6,4},{7,5},{8,10},{9,11},{10,... | collective-permute-start | bytes 589832 | tf_op jit(solution)/shard_map/ppermute | solution.py:386
  104.3 10.9 %collective-permute-start.26 = (bf16[64,1536]{1,0:T(8,128)(2,1)S(1)}, bf16[64,1536]{1,0:T(8,128)(2,1)S(1)}, u32[]{:S(2)}, u32[]{:S(2)}) collective-permute-start(bf16[64,1536]{1,0:T(8,128)(2,1)S(1)} %get-tuple-element.64), channel_id=1, source_target_pairs={{0,2},{1,3},{2,0},{3,1},{4,6},{5,7},{6,4},{7,5},{8,10},{9,11},{10,... | collective-permute-start | bytes 589832 | tf_op jit(solution)/shard_map/ppermute | solution.py:386
  105.9 11.9 %collective-permute-start.20 = (bf16[64,1536]{1,0:T(8,128)(2,1)S(1)}, bf16[64,1536]{1,0:T(8,128)(2,1)S(1)}, u32[]{:S(2)}, u32[]{:S(2)}) collective-permute-start(bf16[64,1536]{1,0:T(8,128)(2,1)S(1)} %add_convert_fusion.3), channel_id=1, source_target_pairs={{0,8},{4,12},{8,0},{12,4},{16,24},{20,28},{24,16},{28,20},{1,9},{5... | collective-permute-start | bytes 589832 | tf_op jit(solution)/shard_map/ppermute | solution.py:389
  111.8 16.6 %collective-permute-start.23 = (bf16[64,1536]{1,0:T(8,128)(2,1)S(1)}, bf16[64,1536]{1,0:T(8,128)(2,1)S(1)}, u32[]{:S(2)}, u32[]{:S(2)}) collective-permute-start(bf16[64,1536]{1,0:T(8,128)(2,1)S(1)} %add_convert_fusion.2), channel_id=1, source_target_pairs={{0,16},{4,20},{8,24},{12,28},{16,0},{20,4},{24,8},{28,12},{1,17},{... | collective-permute-start | bytes 589832 | tf_op jit(solution)/shard_map/ppermute | solution.py:389
  115.3 13.1 %collective-permute-start.27 = (bf16[64,1536]{1,0:T(8,128)(2,1)S(1)}, bf16[64,1536]{1,0:T(8,128)(2,1)S(1)}, u32[]{:S(2)}, u32[]{:S(2)}) collective-permute-start(bf16[64,1536]{1,0:T(8,128)(2,1)S(1)} %add_convert_fusion.1), channel_id=1, source_target_pairs={{0,24},{4,28},{8,16},{12,20},{16,8},{20,12},{24,0},{28,4},{1,25},{... | collective-permute-start | bytes 589832 | tf_op jit(solution)/shard_map/ppermute | solution.py:389

commit v3 on v2

--- a/solution.py
+++ b/solution.py
@@ -95,7 +95,7 @@
     )(at, *blocks)
 
 
-def attention_kernel(at_ref, q_hbm, k_hbm, v_hbm, keep_ref, send_ref, q_ref, k_ref, v_ref, bias, result, stats, lines, sems):
+def attention_kernel(at_ref, lengths_ref, q_hbm, k_hbm, v_hbm, keep_ref, send_ref, q_ref, k_ref, v_ref, bias, result, stats, lines, sems):
     rows, width = q_ref.shape
     requests, slab, _ = k_ref.shape
     block = 2 * (H // KVH) * HD
@@ -103,7 +103,7 @@
     span = rows - (requests - 1)
     heads = block // HD
     group = H // KVH
-    first_key, half_row = at_ref[0], at_ref[1]
+    first_key, half_row = at_ref[0] * slab, lax.rem(at_ref[0], 2)
 
     def load(source, target, index):
         return pltpu.make_async_copy(source, target, sems.at[index])
@@ -116,7 +116,7 @@
         loads[index].start()
 
     place = first_key + iota((slab, rows), 0)
-    limit = at_ref[2] - span + iota((slab, rows), 1)
+    limit = lengths_ref[0] - span + iota((slab, rows), 1)
     bias[...] = jnp.where(place <= limit, 0.0, -1e30)
     stats[...] = jnp.zeros_like(stats)
     lines[...] = jnp.zeros_like(lines)
@@ -189,7 +189,7 @@
         loads[1 + requests + r].wait()
         row = rows - requests + r
         scores = lax.dot_general(lines[r - 1].astype(BF16), k_ref[r], NT, preferred_element_type=F32)
-        usable = first_key + iota((1, slab), 1) < at_ref[2 + r]
+        usable = first_key + iota((1, slab), 1) < lengths_ref[r]
         scores = jnp.where(usable, scores, -1e30)
         top = jnp.maximum(jnp.max(scores, axis=1, keepdims=True), -1e29).astype(BF16).astype(F32)
         weights = jnp.exp(scores - top)
@@ -217,13 +217,13 @@
             ref[part * quarter : (part + 1) * quarter, width:] = stats[pick, :].astype(BF16)
 
 
-def attention(queries, keys, values, at):
+def attention(queries, keys, values, at, lengths):
     rows, width = queries.shape
     requests, slab, depth = keys.shape
     half = jax.ShapeDtypeStruct((rows // 2, width + LANES), BF16)
     return pl.pallas_call(
         attention_kernel,
-        in_specs=[SMEM, HBM, HBM, HBM],
+        in_specs=[SMEM, SMEM, HBM, HBM, HBM],
         out_specs=[VMEM, VMEM],
         out_shape=[half, half],
         scratch_shapes=[
@@ -238,7 +238,7 @@
         ],
         compiler_params=params(56),
         name="attention",
-    )(at, queries, keys, values)
+    )(at, lengths, queries, keys, values)
 
 
 def expanded(scale, width):
@@ -266,31 +266,42 @@
 
 
 def join_kernel(at_ref, own_ref, other_ref, keep_ref, send_ref):
-    rows, width = keep_ref.shape[0], own_ref.shape[1] - LANES
+    width, part_width = own_ref.shape[1] - LANES, keep_ref.shape[1] - LANES
+    own, other = own_ref[...], other_ref[...]
+    top, total, scales, _ = merged([own, other], width)
+    valid = iota((1, LANES), 1) < part_width // HD
     for ref, which in ((send_ref, 1 - at_ref[0]), (keep_ref, at_ref[0])):
-        pick = pl.ds(pl.multiple_of(which * rows, 16), rows)
-        parts = [own_ref[pick, :], other_ref[pick, :]]
-        top, total, scales, valid = merged(parts, width)
-        ref[:, :width] = weighted(parts, scales, width)
-        high = total.astype(BF16).astype(F32)
-        stat = jnp.where(valid, top, 0.0)
-        stat = stat + pltpu.roll(jnp.where(valid, high, 0.0), SUM_HIGH, 1)
-        stat = stat + pltpu.roll(jnp.where(valid, total - high, 0.0), SUM_LOW, 1)
-        ref[:, width:] = stat.astype(BF16)
-
-
-def project_kernel(at_ref, own_ref, other_ref, w0, w1, w2, w3, residual_ref, gain_ref, normed_ref, out_ref, attended):
+
+        def here(tile):
+            moved = pltpu.roll(tile, LANES - part_width // HD, 1)
+            return jnp.where(valid, jnp.where(which == 1, moved, tile), 0.0)
+
+        pick = pl.ds(pl.multiple_of(which * part_width, LANES), part_width)
+        ref[:, :part_width] = weighted([own_ref[:, pick], other_ref[:, pick]], [here(scale) for scale in scales], part_width)
+        sums = here(total)
+        high = sums.astype(BF16).astype(F32)
+        stat = here(top) + pltpu.roll(high, SUM_HIGH, 1) + pltpu.roll(sums - high, SUM_LOW, 1)
+        ref[:, part_width:] = stat.astype(BF16)
+
+
+def project_kernel(at_ref, own_ref, other_ref, w0, w1, keep_ref, send_ref, attended, mixed):
     width = own_ref.shape[1] - LANES
     parts = [own_ref[...], other_ref[...]]
     _, total, scales, valid = merged(parts, width)
     inverse = 1.0 / jnp.where(valid, total, 1.0)
     attended[...] = weighted(parts, [scale * inverse for scale in scales], width)
-    mixed = None
     depth = w0.shape[0]
-    for flip, weight in enumerate((w0, w1, w2, w3)):
-        column = pl.multiple_of((at_ref[0] ^ flip) * depth, LANES)
-        term = dot(attended[:, pl.ds(column, depth)], weight[...])
-        mixed = term if mixed is None else mixed + term
+    core, chip = lax.rem(at_ref[0], 2), at_ref[0] // 2
+    first = dot(attended[:, pl.ds(pl.multiple_of(core * depth, LANES), depth)], w0[...])
+    second = dot(attended[:, pl.ds(pl.multiple_of((1 - core) * depth, LANES), depth)], w1[...])
+    mixed[...] = first + second
+    rows = keep_ref.shape[0]
+    keep_ref[...] = mixed[pl.ds(pl.multiple_of(chip * rows, 16), rows), :]
+    send_ref[...] = mixed[pl.ds(pl.multiple_of((1 - chip) * rows, 16), rows), :].astype(BF16)
+
+
+def norm_kernel(keep_ref, other_ref, residual_ref, gain_ref, normed_ref, out_ref):
+    mixed = keep_ref[...] + other_ref[...].astype(F32)
     residual = (residual_ref[...].astype(F32) + mixed).astype(BF16)
     out_ref[...] = residual
     wide = residual.astype(F32)
@@ -376,7 +387,7 @@
     inner = dp_size // OUTER
     dp_index, kv_index = lax.axis_index("dp"), lax.axis_index("kv")
     z, y = (dp_index // inner).reshape(1), dp_index % inner
-    core, chip = kv_index % 2, kv_index // 2
+    chip = kv_index // 2
     units = gate_weight.shape[1]
     main = units // OUTER // LANES * LANES
     tail = units // OUTER - main
@@ -390,9 +401,6 @@
 
     def y_flip(a, bit):
         return lax.ppermute(a, "dp", [(i, i ^ bit) for i in range(dp_size)])
-
-    w2 = kv_flip(out_weight, 2)
-    w1 = kv_flip(out_weight, 1)
 
     rows = gate_weight.shape[0]
     cuts = [(flip, 0, rows) for flip in range(OUTER)]
@@ -410,7 +418,7 @@
         ],
         compiler_params=params(60),
         name="pack",
-    )(after(z, w1), gate_weight, up_weight, down_weight.T)
+    )(z, gate_weight, up_weight, down_weight.T)
 
     def shared(block):
         bit = 1
@@ -423,14 +431,14 @@
 
     y_place = (y >= inner // 2).astype(jnp.int32).reshape(1)
 
-    arrived = {index: z_flip(packed[index], index) for index in (1, 2)}
+    arrived = {index: z_flip(packed[index], index) for index in (2, 1)}
     blocks = {0: shared(packed[0])}
-    at = jnp.concatenate([jnp.stack([kv_index * key_cache.shape[1], core]), cache_lengths])
-    keep, send = attention(queries, key_cache, value_cache, after(at, *packed))
+    w1 = kv_flip(after(out_weight, packed[0]), 1)
+    own = kv_index.reshape(1)
+    keep, send = attention(queries, key_cache, value_cache, after(own, *packed), cache_lengths)
     arrived[3] = z_flip(after(packed[3], keep), 3)
-    blocks[1] = shared(after(arrived[1], keep))
-    other = kv_flip(after(send, blocks[0][1], arrived[1]), 1)
-    half = jax.ShapeDtypeStruct((keep.shape[0] // 2, keep.shape[1]), BF16)
+    other = kv_flip(after(send, blocks[0][1], w1), 1)
+    half = jax.ShapeDtypeStruct((keep.shape[0], width // 2 + LANES), BF16)
     keep, send = pl.pallas_call(
         join_kernel,
         in_specs=[SMEM, VMEM, VMEM],
@@ -438,21 +446,32 @@
         out_shape=[half, half],
         compiler_params=params(16),
         name="join",
-    )(after(chip.reshape(1), arrived[2]), keep, other)
+    )(after(chip.reshape(1), arrived[1], arrived[2]), keep, other)
     other = kv_flip(send, 2)
+    blocks[1] = shared(after(arrived[1], keep))
     blocks[2] = shared(after(arrived[2], keep))
-    w3 = kv_flip(after(w2, keep), 1)
     tokens = jax.ShapeDtypeStruct(residual_in.shape, BF16)
+    partial, send = pl.pallas_call(
+        project_kernel,
+        in_specs=[SMEM] + [VMEM] * 4,
+        out_specs=[VMEM, VMEM],
+        out_shape=[jax.ShapeDtypeStruct(residual_in.shape, F32), tokens],
+        scratch_shapes=[
+            pltpu.VMEM((keep.shape[0], width // 2), BF16),
+            pltpu.VMEM((keep.shape[0], width), F32),
+        ],
+        compiler_params=params(16),
+        name="project",
+    )(own, keep, other, out_weight, w1)
+    other = kv_flip(send, 2)
     normed, residual = pl.pallas_call(
-        project_kernel,
-        in_specs=[SMEM] + [VMEM] * 8,
+        norm_kernel,
+        in_specs=[VMEM] * 4,
         out_specs=[VMEM, VMEM],
         out_shape=[tokens, tokens],
-        scratch_shapes=[pltpu.VMEM(residual_in.shape, BF16)],
         compiler_params=params(16),
-        name="project",
-    )(after(kv_index.reshape(1), blocks[1][1]), keep, other, out_weight, w1, w2, w3, residual_in, norm_gain.reshape(1, width))
-    blocks[3] = shared(after(arrived[3], normed))
+        name="norm",
+    )(after(partial, blocks[1][1]), other, residual_in, norm_gain.reshape(1, width))
 
     order = (0, 1, 2, 3)
     deep = width // OUTER
@@ -467,26 +486,28 @@
 
     near = [laid((0, 1), 0, normed)]
     count = residual_in.shape[0]
-    here = {s: z_flip(normed, s) if s else normed for s in order}
+    here = {0: normed, 1: z_flip(normed, 1), 3: z_flip(normed, 3)}
+    here[2] = z_flip(after(normed, here[3]), 2)
     there = {s: kv_flip(here[s], 2) for s in order}
-    near.append(laid((2, 3), 2 * deep, there[0], here[1], here[2]))
+    blocks[3] = shared(after(arrived[3], blocks[2][1], here[1]))
+    near.append(laid((2, 3), 2 * deep, there[1], here[3]))
     weights = near + [kv_flip(part, 1) for part in near]
 
     def added(a, b):
         return (a.astype(F32) + b.astype(F32)).astype(BF16)
 
-    mlp = None
-    for shifts in ((0,), (1,), (2,), (3,)):
-        tokens = [here[s] for s in shifts] + [there[s] for s in shifts]
-        keep, send = feed(main, tail, order, z, tokens, weights)
+    mlp = residual.astype(F32)
+    kept, arrivals, terms = [], [], []
+    for s in (3, 1, 2, 0):
+        turn = after(z, *kept[-1:], *arrivals[:-1], *terms[:-2])
+        keep, send = feed(main, tail, order, turn, [here[s], there[s]], weights)
         other = kv_flip(send, 2)
-        for index, s in enumerate(shifts):
-            pick = slice(index * count, (index + 1) * count)
-            term = added(keep[pick], other[pick])
-            if s:
-                term = z_flip(term, s)
-            mlp = term.astype(F32) if mlp is None else mlp + term.astype(F32)
-    return (residual.astype(F32) + mlp).astype(BF16)
+        kept.append(keep)
+        arrivals.append(other)
+        term = added(keep, other)
+        terms.append(z_flip(term, s) if s else term)
+        mlp = mlp + terms[-1].astype(F32)
+    return mlp.astype(BF16)
 
 
 def solution(mesh):

time: 130 us -> 124 us (0.954)
  waiting for transfers between devices: 43.7 us -> 37.5 us
  Pallas kernels: 32.9 us -> 29.7 us
  local copies, waits for them, and re-layouts: 5.53 us -> 8.26 us
  starting transfers between devices: 44.7 us -> 47.1 us
    ppermute x9, waiting for transfers between devices: 31.4 us -> 19.7 us  [z_flip(): return lax.ppermute(a, 'dp', [(i, i ^ by * inner) for i in range(dp_size)])]
    ppermute x9, starting transfers between devices: 25.2 us -> 28.7 us  [z_flip(): return lax.ppermute(a, 'dp', [(i, i ^ by * inner) for i in range(dp_size)])]
    ppermute x15 -> x14, waiting for transfers between devices: 3.05 us -> 6.18 us  [kv_flip(): return lax.ppermute(a, 'kv', [(i, i ^ bit) for i in range(kv_size)])]
    unnamed x18 -> x26, local copies, waits for them, and re-layouts: 5.53 us -> 8.25 us
    ppermute x4, waiting for transfers between devices: 9.23 us -> 11.6 us  [y_flip(): return lax.ppermute(a, 'dp', [(i, i ^ bit) for i in range(dp_size)])]
    pallas_call x2 -> x3, Pallas kernels: 16.2 us -> 15.3 us  [the longest x1 13.9 us: attention(): pl.pallas_call(attention_kernel, in_specs=[SMEM, SMEM, HBM, HBM, HBM], ou...]
    ppermute x15 -> x14, starting transfers between devices: 13.9 us -> 13.1 us  [kv_flip(): return lax.ppermute(a, 'kv', [(i, i ^ bit) for i in range(kv_size)])]
  transfers between devices with their start and end apart: 28 -> 27, of which waited for: 10 -> 13; matrix products, arithmetic and copies ran while one was open for 1% -> 0% of each run, Pallas kernels for 25% -> 21%
where the time goes in v3:
time: 124 us
  starting transfers between devices  47.1 us (38%)
  waiting for transfers between devices  37.5 us (30%)
  Pallas kernels  29.7 us (24%)
  local copies, waits for them, and re-layouts  8.26 us (7%)
    ppermute x9, starting transfers between devices, z_flip(): return lax.ppermute(a, 'dp', [(i, i ^ by * inner) for i in range(dp_size)])  28.7 us
    ppermute x9, waiting for transfers between devices, z_flip(): return lax.ppermute(a, 'dp', [(i, i ^ by * inner) for i in range(dp_size)])  19.7 us
    pallas_call x1, Pallas kernels, attention(): pl.pallas_call(attention_kernel, in_specs=[SMEM, SMEM, HBM, HBM, HBM], ou...  13.9 us
    ppermute x14, starting transfers between devices, kv_flip(): return lax.ppermute(a, 'kv', [(i, i ^ bit) for i in range(kv_size)])  13.1 us
    ppermute x4, waiting for transfers between devices, y_flip(): return lax.ppermute(a, 'dp', [(i, i ^ bit) for i in range(dp_size)])  11.6 us
    unnamed x26, local copies, waits for them, and re-layouts  8.25 us
    pallas_call x4, Pallas kernels, feed(): pl.pallas_call(functools.partial(feed_kernel, main, tail, count, order),...  8.14 us
    ppermute x14, waiting for transfers between devices, kv_flip(): return lax.ppermute(a, 'kv', [(i, i ^ bit) for i in range(kv_size)])  6.18 us
  transfers between devices with their start and end apart: 27, of which 13 were waited for; matrix products, arithmetic and copies ran while one was open for 0% of the time, Pallas kernels for 21%

profile of v3, /device:TPU:0, one launch (start us, length us, event | category | flops | bytes accessed | tf_op | source)
XLA Modules:
  0.0 123.7 jit_solution(7342356253403314806)
XLA Ops:
  0.0 3.3 %pack.1 = (bf16[192,1408]{1,0:T(8,128)(2,1)}, bf16[192,1408]{1,0:T(8,128)(2,1)}, bf16[192,1408]{1,0:T(8,128)(2,1)}, bf16[192,1408]{1,0:T(8,128)(2,1)}) custom-call(s32[1]{0:T(128)} %bitcast.2.z_ref, bf16[192,1728]{1,0:T(8,128)(2,1)} %gate_ref.1, bf16[192,1728]{1,0:T(8,128)(2,1)} %up_ref.1, bf16[192,1728]{1,0:T(8,128)(2,1)} %bitcast.5), custom_call_target="tpu_custom_call" | custom-call | tf_op jit(solution)/shard_map/pack/pallas_call | solution.py:408
  3.3 0.5 collective-permute-start.3
  3.8 2.6 %collective-permute-start.2 = (bf16[192,1408]{1,0:T(8,128)(2,1)}, bf16[192,1408]{1,0:T(8,128)(2,1)S(1)}, u32[]{:S(2)}, u32[]{:S(2)}) collective-permute-start(bf16[192,1408]{1,0:T(8,128)(2,1)} %get-tuple-element.43.refs_0_), channel_id=1, source_target_pairs={{0,4},{4,0},{8,12},{12,8},{16,20},{20,16},{24,28},{28,24},{1,5},{5... | collective-permute-start | bytes 1622024 | tf_op jit(solution)/shard_map/ppermute | solution.py:403
  6.4 1.6 %collective-permute-start = (bf16[192,1408]{1,0:T(8,128)(2,1)}, bf16[192,1408]{1,0:T(8,128)(2,1)}, u32[]{:S(2)}, u32[]{:S(2)}) collective-permute-start(bf16[192,1408]{1,0:T(8,128)(2,1)} %get-tuple-element.40), channel_id=1, source_target_pairs={{0,8},{4,12},{8,0},{12,4},{16,24},{20,28},{24,16},{28,20},{1,9},{5... | collective-permute-start | bytes 1622024 | tf_op jit(solution)/shard_map/ppermute | solution.py:400
  8.0 2.6 %collective-permute-start.1 = (bf16[192,1408]{1,0:T(8,128)(2,1)}, bf16[192,1408]{1,0:T(8,128)(2,1)S(1)}, u32[]{:S(2)}, u32[]{:S(2)}) collective-permute-start(bf16[192,1408]{1,0:T(8,128)(2,1)} %get-tuple-element.41), channel_id=1, source_target_pairs={{0,16},{4,20},{8,24},{12,28},{16,0},{20,4},{24,8},{28,12},{1,17},{... | collective-permute-start | bytes 1622024 | tf_op jit(solution)/shard_map/ppermute | solution.py:400
  10.6 13.9 %attention.1 = (bf16[128,1664]{1,0:T(8,128)(2,1)}, bf16[128,1664]{1,0:T(8,128)(2,1)}) custom-call(s32[1]{0:T(128)} %bitcast.at_ref, s32[3]{0:T(128)} %lengths_ref.1, bf16[256,1536]{1,0:T(8,128)(2,1)} %q_hbm.1, bf16[3,1024,512]{2,1,0:T(8,128)(2,1)} %k_hbm.1, bf16[3,1024,512]{2,1,0:T(8,128)(2,1)} %v_hbm.1), custom_call_target="tpu_custom_call" | custom-call | tf_op jit(solution)/shard_map/attention/pallas_call | solution.py:224
  24.5 0.0 copy-start.12
  24.5 0.8 copy-done.2
  25.3 0.0 collective-permute-done.3.w1
  25.3 0.0 collective-permute-start.4
  25.3 7.2 %collective-permute-done.refs_2_ = bf16[192,1408]{1,0:T(8,128)(2,1)} collective-permute-done((bf16[192,1408]{1,0:T(8,128)(2,1)}, bf16[192,1408]{1,0:T(8,128)(2,1)}, u32[]{:S(2)}, u32[]{:S(2)}) %collective-permute-start) | collective-permute-done | bytes 540704 | tf_op jit(solution)/shard_map/ppermute | solution.py:400
  32.6 2.3 %collective-permute-done.1.refs_0_ = bf16[192,1408]{1,0:T(8,128)(2,1)S(1)} collective-permute-done((bf16[192,1408]{1,0:T(8,128)(2,1)}, bf16[192,1408]{1,0:T(8,128)(2,1)S(1)}, u32[]{:S(2)}, u32[]{:S(2)}) %collective-permute-start.1) | collective-permute-done | bytes 540704 | tf_op jit(solution)/shard_map/ppermute | solution.py:400
  34.8 0.0 collective-permute-done.4.other_ref
  34.8 0.8 copy-done.9
  35.6 1.0 copy-done.8
  36.6 1.0 copy-done.10
  37.6 0.6 join.1
  38.2 0.6 collective-permute-start.6
  38.8 1.5 %collective-permute-start.5 = (bf16[128,896]{1,0:T(8,128)(2,1)S(1)}, bf16[128,896]{1,0:T(8,128)(2,1)S(1)}, u32[]{:S(2)}, u32[]{:S(2)}) collective-permute-start(bf16[128,896]{1,0:T(8,128)(2,1)S(1)} %get-tuple-element.51), channel_id=1, source_target_pairs={{0,2},{1,3},{2,0},{3,1},{4,6},{5,7},{6,4},{7,5},{8,10},{9,11},{10,... | collective-permute-start | bytes 688136 | tf_op jit(solution)/shard_map/ppermute | solution.py:397
  40.3 2.5 %collective-permute-start.13 = (bf16[192,1408]{1,0:T(8,128)(2,1)}, bf16[192,1408]{1,0:T(8,128)(2,1)}, u32[]{:S(2)}, u32[]{:S(2)}) collective-permute-start(bf16[192,1408]{1,0:T(8,128)(2,1)} %get-tuple-element.61), channel_id=1, source_target_pairs={{0,24},{4,28},{8,16},{12,20},{16,8},{20,12},{24,0},{28,4},{1,25},{... | collective-permute-start | bytes 1622024 | tf_op jit(solution)/shard_map/ppermute | solution.py:400
  42.7 1.5 %collective-permute-start.12 = (bf16[192,1408]{1,0:T(8,128)(2,1)S(1)}, bf16[192,1408]{1,0:T(8,128)(2,1)S(1)}, u32[]{:S(2)}, u32[]{:S(2)}) collective-permute-start(bf16[192,1408]{1,0:T(8,128)(2,1)S(1)} %collective-permute-done.1.refs_0_), channel_id=1, source_target_pairs={{0,4},{4,0},{8,12},{12,8},{16,20},{20,16},{24,28},{28,24},{1,5},{5... | collective-permute-start | bytes 1622024 | tf_op jit(solution)/shard_map/ppermute | solution.py:403
  44.3 0.5 collective-permute-done.5.other_ref
  44.8 1.2 project.1
  46.0 1.5 %collective-permute-start.7 = (bf16[64,1536]{1,0:T(8,128)(2,1)S(1)}, bf16[64,1536]{1,0:T(8,128)(2,1)S(1)}, u32[]{:S(2)}, u32[]{:S(2)}) collective-permute-start(bf16[64,1536]{1,0:T(8,128)(2,1)S(1)} %get-tuple-element.55), channel_id=1, source_target_pairs={{0,2},{1,3},{2,0},{3,1},{4,6},{5,7},{6,4},{7,5},{8,10},{9,11},{10,... | collective-permute-start | bytes 589832 | tf_op jit(solution)/shard_map/ppermute | solution.py:397
  47.5 6.2 %collective-permute-done.6.refs_3_ = bf16[192,1408]{1,0:T(8,128)(2,1)S(1)} collective-permute-done((bf16[192,1408]{1,0:T(8,128)(2,1)}, bf16[192,1408]{1,0:T(8,128)(2,1)S(1)}, u32[]{:S(2)}, u32[]{:S(2)}) %collective-permute-start.6) | collective-permute-done | bytes 540704 | tf_op jit(solution)/shard_map/ppermute | solution.py:403
  53.7 0.8 copy-done.6
  54.5 0.9 copy-done.11
  55.4 0.2 norm.1
  55.6 0.5 collective-permute-start.10
  56.1 5.3 %collective-permute-done.12.refs_1_ = bf16[192,1408]{1,0:T(8,128)(2,1)S(1)} collective-permute-done((bf16[192,1408]{1,0:T(8,128)(2,1)S(1)}, bf16[192,1408]{1,0:T(8,128)(2,1)S(1)}, u32[]{:S(2)}, u32[]{:S(2)}) %collective-permute-start.12) | collective-permute-done | bytes 540704 | tf_op jit(solution)/shard_map/ppermute | solution.py:403
  61.5 0.8 copy-done.4
  62.3 0.5 collective-permute-start.14
  62.8 4.3 %collective-permute-start.8 = (bf16[64,1536]{1,0:T(8,128)(2,1)S(1)}, bf16[64,1536]{1,0:T(8,128)(2,1)S(1)}, u32[]{:S(2)}, u32[]{:S(2)}) collective-permute-start(bf16[64,1536]{1,0:T(8,128)(2,1)S(1)} %get-tuple-element.69.refs_0_), channel_id=1, source_target_pairs={{0,24},{4,28},{8,16},{12,20},{16,8},{20,12},{24,0},{28,4},{1,25},{... | collective-permute-start | bytes 589832 | tf_op jit(solution)/shard_map/ppermute | solution.py:400
  67.1 1.5 %collective-permute-start.11 = (bf16[64,1536]{1,0:T(8,128)(2,1)S(1)}, bf16[64,1536]{1,0:T(8,128)(2,1)S(1)}, u32[]{:S(2)}, u32[]{:S(2)}) collective-permute-start(bf16[64,1536]{1,0:T(8,128)(2,1)S(1)} %collective-permute-done.10.refs_0_), channel_id=1, source_target_pairs={{0,2},{1,3},{2,0},{3,1},{4,6},{5,7},{6,4},{7,5},{8,10},{9,11},{10,... | collective-permute-start | bytes 589832 | tf_op jit(solution)/shard_map/ppermute | solution.py:397
  68.6 1.0 copy-done.3
  69.7 1.0 copy-done.7
  70.7 1.3 %place.2.refs_2_ = bf16[768,1408]{1,0:T(8,128)(2,1)S(1)} custom-call(s32[1]{0:T(128)} %bitcast.4.at_ref, bf16[192,1408]{1,0:T(8,128)(2,1)S(1)} %copy-done.1, bf16[192,1408]{1,0:T(8,128)(2,1)S(1)} %copy-done.3, bf16[192,1408]{1,0:T(8,128)(2,1)} %collective-permute-done.refs_2_, bf16[192,1408]{1,0:T(8,128)(2,1)S(1)} %copy-done.7), custom_call_target="tpu_custom_call" | custom-call | tf_op jit(solution)/shard_map/place/pallas_call | solution.py:88
  72.0 0.1 collective-permute-start.15
  72.1 0.7 collective-permute-done.11.refs_1_
  72.8 0.1 collective-permute-done.14.refs_3_
  72.9 1.2 place.3.refs_3_
  74.1 0.1 collective-permute-start.16
  74.2 1.6 %collective-permute-start.9 = (bf16[64,1536]{1,0:T(8,128)(2,1)S(1)}, bf16[64,1536]{1,0:T(8,128)(2,1)S(1)}, u32[]{:S(2)}, u32[]{:S(2)}) collective-permute-start(bf16[64,1536]{1,0:T(8,128)(2,1)S(1)} %collective-permute-done.8.refs_0_), channel_id=1, source_target_pairs={{0,2},{1,3},{2,0},{3,1},{4,6},{5,7},{6,4},{7,5},{8,10},{9,11},{10,... | collective-permute-start | bytes 589832 | tf_op jit(solution)/shard_map/ppermute | solution.py:397
  75.8 5.2 %collective-permute-start.21 = (bf16[64,1536]{1,0:T(8,128)(2,1)S(1)}, bf16[64,1536]{1,0:T(8,128)(2,1)S(1)}, u32[]{:S(2)}, u32[]{:S(2)}) collective-permute-start(bf16[64,1536]{1,0:T(8,128)(2,1)S(1)} %get-tuple-element.69.refs_0_), channel_id=1, source_target_pairs={{0,16},{4,20},{8,24},{12,28},{16,0},{20,4},{24,8},{28,12},{1,17},{... | collective-permute-start | bytes 589832 | tf_op jit(solution)/shard_map/ppermute | solution.py:400
  80.9 0.6 collective-permute-done.9.refs_1_
  81.5 2.0 %feed.4 = (bf16[64,1536]{1,0:T(8,128)(2,1)S(1)}, bf16[64,1536]{1,0:T(8,128)(2,1)S(1)}) custom-call(s32[1]{0:T(128)} %bitcast.2.z_ref, bf16[64,1536]{1,0:T(8,128)(2,1)S(1)} %collective-permute-done.8.refs_0_, bf16[64,1536]{1,0:T(8,128)(2,1)S(1)} %collective-permute-done.9.refs_1_, bf16[768,1408]{1,0:T(8,128)(2,1)S(1)} %place.2.refs_2_, ...), custom_call_target="tpu_custom_call" | custom-call | tf_op jit(solution)/shard_map/feed/pallas_call | solution.py:359
  83.6 1.6 %collective-permute-start.17 = (bf16[64,1536]{1,0:T(8,128)(2,1)S(1)}, bf16[64,1536]{1,0:T(8,128)(2,1)S(1)}, u32[]{:S(2)}, u32[]{:S(2)}) collective-permute-start(bf16[64,1536]{1,0:T(8,128)(2,1)S(1)} %get-tuple-element.64), channel_id=1, source_target_pairs={{0,2},{1,3},{2,0},{3,1},{4,6},{5,7},{6,4},{7,5},{8,10},{9,11},{10,... | collective-permute-start | bytes 589832 | tf_op jit(solution)/shard_map/ppermute | solution.py:397
  85.1 0.5 collective-permute-start.25
  85.7 4.7 %collective-permute-done.21.refs_0_ = bf16[64,1536]{1,0:T(8,128)(2,1)S(1)} collective-permute-done((bf16[64,1536]{1,0:T(8,128)(2,1)S(1)}, bf16[64,1536]{1,0:T(8,128)(2,1)S(1)}, u32[]{:S(2)}, u32[]{:S(2)}) %collective-permute-start.21) | collective-permute-done | bytes 196640 | tf_op jit(solution)/shard_map/ppermute | solution.py:400
  90.4 1.5 %collective-permute-start.22 = (bf16[64,1536]{1,0:T(8,128)(2,1)S(1)}, bf16[64,1536]{1,0:T(8,128)(2,1)S(1)}, u32[]{:S(2)}, u32[]{:S(2)}) collective-permute-start(bf16[64,1536]{1,0:T(8,128)(2,1)S(1)} %collective-permute-done.21.refs_0_), channel_id=1, source_target_pairs={{0,2},{1,3},{2,0},{3,1},{4,6},{5,7},{6,4},{7,5},{8,10},{9,11},{10,... | collective-permute-start | bytes 589832 | tf_op jit(solution)/shard_map/ppermute | solution.py:397
  91.9 2.0 %feed.5 = (bf16[64,1536]{1,0:T(8,128)(2,1)S(1)}, bf16[64,1536]{1,0:T(8,128)(2,1)S(1)}) custom-call(s32[1]{0:T(128)} %bitcast.2.z_ref, bf16[64,1536]{1,0:T(8,128)(2,1)S(1)} %collective-permute-done.10.refs_0_, bf16[64,1536]{1,0:T(8,128)(2,1)S(1)} %collective-permute-done.11.refs_1_, bf16[768,1408]{1,0:T(8,128)(2,1)S(1)} %place.2.refs_2_, ...), custom_call_target="tpu_custom_call" | custom-call | tf_op jit(solution)/shard_map/feed/pallas_call | solution.py:359
  93.9 0.6 collective-permute-start.19
  94.5 3.6 %collective-permute-start.18 = (bf16[64,1536]{1,0:T(8,128)(2,1)S(1)}, bf16[64,1536]{1,0:T(8,128)(2,1)S(1)}, u32[]{:S(2)}, u32[]{:S(2)}) collective-permute-start(bf16[64,1536]{1,0:T(8,128)(2,1)S(1)} %add_convert_fusion.4), channel_id=1, source_target_pairs={{0,24},{4,28},{8,16},{12,20},{16,8},{20,12},{24,0},{28,4},{1,25},{... | collective-permute-start | bytes 589832 | tf_op jit(solution)/shard_map/ppermute | solution.py:400
  98.2 1.7 %collective-permute-done.22.refs_1_ = bf16[64,1536]{1,0:T(8,128)(2,1)S(1)} collective-permute-done((bf16[64,1536]{1,0:T(8,128)(2,1)S(1)}, bf16[64,1536]{1,0:T(8,128)(2,1)S(1)}, u32[]{:S(2)}, u32[]{:S(2)}) %collective-permute-start.22) | collective-permute-done | bytes 196640 | tf_op jit(solution)/shard_map/ppermute | solution.py:397
  99.9 2.0 %feed.6 = (bf16[64,1536]{1,0:T(8,128)(2,1)S(1)}, bf16[64,1536]{1,0:T(8,128)(2,1)S(1)}) custom-call(s32[1]{0:T(128)} %bitcast.2.z_ref, bf16[64,1536]{1,0:T(8,128)(2,1)S(1)} %collective-permute-done.21.refs_0_, bf16[64,1536]{1,0:T(8,128)(2,1)S(1)} %collective-permute-done.22.refs_1_, bf16[768,1408]{1,0:T(8,128)(2,1)S(1)} %place.2.refs_2_, ...), custom_call_target="tpu_custom_call" | custom-call | tf_op jit(solution)/shard_map/feed/pallas_call | solution.py:359
  101.9 1.6 %collective-permute-start.23 = (bf16[64,1536]{1,0:T(8,128)(2,1)S(1)}, bf16[64,1536]{1,0:T(8,128)(2,1)S(1)}, u32[]{:S(2)}, u32[]{:S(2)}) collective-permute-start(bf16[64,1536]{1,0:T(8,128)(2,1)S(1)} %get-tuple-element.71), channel_id=1, source_target_pairs={{0,2},{1,3},{2,0},{3,1},{4,6},{5,7},{6,4},{7,5},{8,10},{9,11},{10,... | collective-permute-start | bytes 589832 | tf_op jit(solution)/shard_map/ppermute | solution.py:397
  103.5 7.2 %collective-permute-start.20 = (bf16[64,1536]{1,0:T(8,128)(2,1)S(1)}, bf16[64,1536]{1,0:T(8,128)(2,1)S(1)}, u32[]{:S(2)}, u32[]{:S(2)}) collective-permute-start(bf16[64,1536]{1,0:T(8,128)(2,1)S(1)} %add_convert_fusion.3), channel_id=1, source_target_pairs={{0,8},{4,12},{8,0},{12,4},{16,24},{20,28},{24,16},{28,20},{1,9},{5... | collective-permute-start | bytes 589832 | tf_op jit(solution)/shard_map/ppermute | solution.py:400
  110.7 2.0 %feed.7 = (bf16[64,1536]{1,0:T(8,128)(2,1)S(1)}, bf16[64,1536]{1,0:T(8,128)(2,1)S(1)}) custom-call(s32[1]{0:T(128)} %bitcast.2.z_ref, bf16[64,1536]{1,0:T(8,128)(2,1)S(1)} %get-tuple-element.69.refs_0_, bf16[64,1536]{1,0:T(8,128)(2,1)S(1)} %collective-permute-done.25.refs_1_, bf16[768,1408]{1,0:T(8,128)(2,1)S(1)} %place.2.refs_2_, ...), custom_call_target="tpu_custom_call" | custom-call | tf_op jit(solution)/shard_map/feed/pallas_call | solution.py:359
  112.7 0.7 collective-permute-start.26
  113.5 1.3 %collective-permute-start.24 = (bf16[64,1536]{1,0:T(8,128)(2,1)S(1)}, bf16[64,1536]{1,0:T(8,128)(2,1)S(1)}, u32[]{:S(2)}, u32[]{:S(2)}) collective-permute-start(bf16[64,1536]{1,0:T(8,128)(2,1)S(1)} %add_convert_fusion.2), channel_id=1, source_target_pairs={{0,16},{4,20},{8,24},{12,28},{16,0},{20,4},{24,8},{28,12},{1,17},{... | collective-permute-start | bytes 589832 | tf_op jit(solution)/shard_map/ppermute | solution.py:400
  114.8 1.1 collective-permute-done.20
  115.9 2.6 %collective-permute-done.26 = bf16[64,1536]{1,0:T(8,128)(2,1)S(1)} collective-permute-done((bf16[64,1536]{1,0:T(8,128)(2,1)S(1)}, bf16[64,1536]{1,0:T(8,128)(2,1)S(1)}, u32[]{:S(2)}, u32[]{:S(2)}) %collective-permute-start.26) | collective-permute-done | bytes 196640 | tf_op jit(solution)/shard_map/ppermute | solution.py:397
  118.5 4.4 %collective-permute-done.24 = bf16[64,1536]{1,0:T(8,128)(2,1)S(1)} collective-permute-done((bf16[64,1536]{1,0:T(8,128)(2,1)S(1)}, bf16[64,1536]{1,0:T(8,128)(2,1)S(1)}, u32[]{:S(2)}, u32[]{:S(2)}) %collective-permute-start.24) | collective-permute-done | bytes 196640 | tf_op jit(solution)/shard_map/ppermute | solution.py:400
  122.9 0.8 add_convert_fusion
  (32 shorter events, 0.2 us)
Async XLA Ops:
  3.3 22.0 %collective-permute-start.3 = (bf16[384,1536]{1,0:T(8,128)(2,1)}, bf16[384,1536]{1,0:T(8,128)(2,1)S(1)}, u32[]{:S(2)}, u32[]{:S(2)}) collective-permute-start(bf16[384,1536]{1,0:T(8,128)(2,1)} %w0.1), channel_id=1, source_target_pairs={{0,1},{1,0},{2,3},{3,2},{4,5},{5,4},{6,7},{7,6},{8,9},{9,8},{10,11... | collective-permute-start | bytes 3538952 | tf_op jit(solution)/shard_map/ppermute | solution.py:397
  3.8 20.7 %collective-permute-start.2 = (bf16[192,1408]{1,0:T(8,128)(2,1)}, bf16[192,1408]{1,0:T(8,128)(2,1)S(1)}, u32[]{:S(2)}, u32[]{:S(2)}) collective-permute-start(bf16[192,1408]{1,0:T(8,128)(2,1)} %get-tuple-element.43.refs_0_), channel_id=1, source_target_pairs={{0,4},{4,0},{8,12},{12,8},{16,20},{20,16},{24,28},{28,24},{1,5},{5... | collective-permute-start | bytes 1622024 | tf_op jit(solution)/shard_map/ppermute | solution.py:403
  6.4 26.1 %collective-permute-start = (bf16[192,1408]{1,0:T(8,128)(2,1)}, bf16[192,1408]{1,0:T(8,128)(2,1)}, u32[]{:S(2)}, u32[]{:S(2)}) collective-permute-start(bf16[192,1408]{1,0:T(8,128)(2,1)} %get-tuple-element.40), channel_id=1, source_target_pairs={{0,8},{4,12},{8,0},{12,4},{16,24},{20,28},{24,16},{28,20},{1,9},{5... | collective-permute-start | bytes 1622024 | tf_op jit(solution)/shard_map/ppermute | solution.py:400
  8.0 26.8 %collective-permute-start.1 = (bf16[192,1408]{1,0:T(8,128)(2,1)}, bf16[192,1408]{1,0:T(8,128)(2,1)S(1)}, u32[]{:S(2)}, u32[]{:S(2)}) collective-permute-start(bf16[192,1408]{1,0:T(8,128)(2,1)} %get-tuple-element.41), channel_id=1, source_target_pairs={{0,16},{4,20},{8,24},{12,28},{16,0},{20,4},{24,8},{28,12},{1,17},{... | collective-permute-start | bytes 1622024 | tf_op jit(solution)/shard_map/ppermute | solution.py:400
  10.6 34.2 %copy-start = (bf16[384,1536]{1,0:T(8,128)(2,1)S(1)}, bf16[384,1536]{1,0:T(8,128)(2,1)}, u32[]{:S(2)}) copy-start(bf16[384,1536]{1,0:T(8,128)(2,1)} %w0.1) | copy-start | bytes 3538948
  24.5 23.0 %copy-start.12 = (f32[1536]{0:T(1024)S(1)}, f32[1536]{0:T(1024)}, u32[]{:S(2)}) copy-start(f32[1536]{0:T(1024)} %param.16) | copy-start | bytes 18436
  24.5 0.8 copy-start.2
  25.3 9.5 %collective-permute-start.4 = (bf16[128,1664]{1,0:T(8,128)(2,1)}, bf16[128,1664]{1,0:T(8,128)(2,1)S(1)}, u32[]{:S(2)}, u32[]{:S(2)}) collective-permute-start(bf16[128,1664]{1,0:T(8,128)(2,1)} %get-tuple-element.49), channel_id=1, source_target_pairs={{0,1},{1,0},{2,3},{3,2},{4,5},{5,4},{6,7},{7,6},{8,9},{9,8},{10,11... | collective-permute-start | bytes 1277960 | tf_op jit(solution)/shard_map/ppermute | solution.py:397
  34.8 0.8 copy-start.9
  35.6 1.0 copy-start.8
  36.6 1.0 copy-start.10
  37.6 31.0 %copy-start.1 = (bf16[192,1408]{1,0:T(8,128)(2,1)S(1)}, bf16[192,1408]{1,0:T(8,128)(2,1)}, u32[]{:S(2)}) copy-start(bf16[192,1408]{1,0:T(8,128)(2,1)} %get-tuple-element.43.refs_0_) | copy-start | bytes 1622020
  38.2 15.5 %collective-permute-start.6 = (bf16[192,1408]{1,0:T(8,128)(2,1)}, bf16[192,1408]{1,0:T(8,128)(2,1)S(1)}, u32[]{:S(2)}, u32[]{:S(2)}) collective-permute-start(bf16[192,1408]{1,0:T(8,128)(2,1)} %collective-permute-done.refs_2_), channel_id=1, source_target_pairs={{0,4},{4,0},{8,12},{12,8},{16,20},{20,16},{24,28},{28,24},{1,5},{5... | collective-permute-start | bytes 1622024 | tf_op jit(solution)/shard_map/ppermute | solution.py:403
  38.8 6.0 %collective-permute-start.5 = (bf16[128,896]{1,0:T(8,128)(2,1)S(1)}, bf16[128,896]{1,0:T(8,128)(2,1)S(1)}, u32[]{:S(2)}, u32[]{:S(2)}) collective-permute-start(bf16[128,896]{1,0:T(8,128)(2,1)S(1)} %get-tuple-element.51), channel_id=1, source_target_pairs={{0,2},{1,3},{2,0},{3,1},{4,6},{5,7},{6,4},{7,5},{8,10},{9,11},{10,... | collective-permute-start | bytes 688136 | tf_op jit(solution)/shard_map/ppermute | solution.py:397
  40.3 15.9 %collective-permute-start.13 = (bf16[192,1408]{1,0:T(8,128)(2,1)}, bf16[192,1408]{1,0:T(8,128)(2,1)}, u32[]{:S(2)}, u32[]{:S(2)}) collective-permute-start(bf16[192,1408]{1,0:T(8,128)(2,1)} %get-tuple-element.61), channel_id=1, source_target_pairs={{0,24},{4,28},{8,16},{12,20},{16,8},{20,12},{24,0},{28,4},{1,25},{... | collective-permute-start | bytes 1622024 | tf_op jit(solution)/shard_map/ppermute | solution.py:400
  42.7 18.7 %collective-permute-start.12 = (bf16[192,1408]{1,0:T(8,128)(2,1)S(1)}, bf16[192,1408]{1,0:T(8,128)(2,1)S(1)}, u32[]{:S(2)}, u32[]{:S(2)}) collective-permute-start(bf16[192,1408]{1,0:T(8,128)(2,1)S(1)} %collective-permute-done.1.refs_0_), channel_id=1, source_target_pairs={{0,4},{4,0},{8,12},{12,8},{16,20},{20,16},{24,28},{28,24},{1,5},{5... | collective-permute-start | bytes 1622024 | tf_op jit(solution)/shard_map/ppermute | solution.py:403
  46.0 8.5 %collective-permute-start.7 = (bf16[64,1536]{1,0:T(8,128)(2,1)S(1)}, bf16[64,1536]{1,0:T(8,128)(2,1)S(1)}, u32[]{:S(2)}, u32[]{:S(2)}) collective-permute-start(bf16[64,1536]{1,0:T(8,128)(2,1)S(1)} %get-tuple-element.55), channel_id=1, source_target_pairs={{0,2},{1,3},{2,0},{3,1},{4,6},{5,7},{6,4},{7,5},{8,10},{9,11},{10,... | collective-permute-start | bytes 589832 | tf_op jit(solution)/shard_map/ppermute | solution.py:397
  53.7 0.8 copy-start.6
  54.5 0.9 copy-start.11
  55.6 6.7 %collective-permute-start.10 = (bf16[64,1536]{1,0:T(8,128)(2,1)S(1)}, bf16[64,1536]{1,0:T(8,128)(2,1)S(1)}, u32[]{:S(2)}, u32[]{:S(2)}) collective-permute-start(bf16[64,1536]{1,0:T(8,128)(2,1)S(1)} %get-tuple-element.69.refs_0_), channel_id=1, source_target_pairs={{0,8},{4,12},{8,0},{12,4},{16,24},{20,28},{24,16},{28,20},{1,9},{5... | collective-permute-start | bytes 589832 | tf_op jit(solution)/shard_map/ppermute | solution.py:400
  61.5 0.8 copy-start.4
  62.3 10.6 %collective-permute-start.14 = (bf16[192,1408]{1,0:T(8,128)(2,1)}, bf16[192,1408]{1,0:T(8,128)(2,1)S(1)}, u32[]{:S(2)}, u32[]{:S(2)}) collective-permute-start(bf16[192,1408]{1,0:T(8,128)(2,1)} %collective-permute-done.13.refs_2_), channel_id=1, source_target_pairs={{0,4},{4,0},{8,12},{12,8},{16,20},{20,16},{24,28},{28,24},{1,5},{5... | collective-permute-start | bytes 1622024 | tf_op jit(solution)/shard_map/ppermute | solution.py:403
  62.8 9.3 %collective-permute-start.8 = (bf16[64,1536]{1,0:T(8,128)(2,1)S(1)}, bf16[64,1536]{1,0:T(8,128)(2,1)S(1)}, u32[]{:S(2)}, u32[]{:S(2)}) collective-permute-start(bf16[64,1536]{1,0:T(8,128)(2,1)S(1)} %get-tuple-element.69.refs_0_), channel_id=1, source_target_pairs={{0,24},{4,28},{8,16},{12,20},{16,8},{20,12},{24,0},{28,4},{1,25},{... | collective-permute-start | bytes 589832 | tf_op jit(solution)/shard_map/ppermute | solution.py:400
  67.1 5.7 %collective-permute-start.11 = (bf16[64,1536]{1,0:T(8,128)(2,1)S(1)}, bf16[64,1536]{1,0:T(8,128)(2,1)S(1)}, u32[]{:S(2)}, u32[]{:S(2)}) collective-permute-start(bf16[64,1536]{1,0:T(8,128)(2,1)S(1)} %collective-permute-done.10.refs_0_), channel_id=1, source_target_pairs={{0,2},{1,3},{2,0},{3,1},{4,6},{5,7},{6,4},{7,5},{8,10},{9,11},{10,... | collective-permute-start | bytes 589832 | tf_op jit(solution)/shard_map/ppermute | solution.py:397
  68.6 1.0 copy-start.3
  69.7 1.0 copy-start.7
  70.7 2.2 %copy-start.5 = (bf16[192,1408]{1,0:T(8,128)(2,1)S(1)}, bf16[192,1408]{1,0:T(8,128)(2,1)}, u32[]{:S(2)}) copy-start(bf16[192,1408]{1,0:T(8,128)(2,1)} %copy-done.4) | copy-start | bytes 1622020
  72.0 9.5 %collective-permute-start.15 = (bf16[768,1408]{1,0:T(8,128)(2,1)S(1)}, bf16[768,1408]{1,0:T(8,128)(2,1)S(1)}, u32[]{:S(2)}, u32[]{:S(2)}) collective-permute-start(bf16[768,1408]{1,0:T(8,128)(2,1)S(1)} %place.2.refs_2_), channel_id=1, source_target_pairs={{0,1},{1,0},{2,3},{3,2},{4,5},{5,4},{6,7},{7,6},{8,9},{9,8},{10,11... | collective-permute-start | bytes 6488072 | tf_op jit(solution)/shard_map/ppermute | solution.py:397
  74.1 7.4 %collective-permute-start.16 = (bf16[768,1408]{1,0:T(8,128)(2,1)S(1)}, bf16[768,1408]{1,0:T(8,128)(2,1)S(1)}, u32[]{:S(2)}, u32[]{:S(2)}) collective-permute-start(bf16[768,1408]{1,0:T(8,128)(2,1)S(1)} %place.3.refs_3_), channel_id=1, source_target_pairs={{0,1},{1,0},{2,3},{3,2},{4,5},{5,4},{6,7},{7,6},{8,9},{9,8},{10,11... | collective-permute-start | bytes 6488072 | tf_op jit(solution)/shard_map/ppermute | solution.py:397
  74.2 7.3 %collective-permute-start.9 = (bf16[64,1536]{1,0:T(8,128)(2,1)S(1)}, bf16[64,1536]{1,0:T(8,128)(2,1)S(1)}, u32[]{:S(2)}, u32[]{:S(2)}) collective-permute-start(bf16[64,1536]{1,0:T(8,128)(2,1)S(1)} %collective-permute-done.8.refs_0_), channel_id=1, source_target_pairs={{0,2},{1,3},{2,0},{3,1},{4,6},{5,7},{6,4},{7,5},{8,10},{9,11},{10,... | collective-permute-start | bytes 589832 | tf_op jit(solution)/shard_map/ppermute | solution.py:397
  75.8 14.6 %collective-permute-start.21 = (bf16[64,1536]{1,0:T(8,128)(2,1)S(1)}, bf16[64,1536]{1,0:T(8,128)(2,1)S(1)}, u32[]{:S(2)}, u32[]{:S(2)}) collective-permute-start(bf16[64,1536]{1,0:T(8,128)(2,1)S(1)} %get-tuple-element.69.refs_0_), channel_id=1, source_target_pairs={{0,16},{4,20},{8,24},{12,28},{16,0},{20,4},{24,8},{28,12},{1,17},{... | collective-permute-start | bytes 589832 | tf_op jit(solution)/shard_map/ppermute | solution.py:400
  83.6 10.9 %collective-permute-start.17 = (bf16[64,1536]{1,0:T(8,128)(2,1)S(1)}, bf16[64,1536]{1,0:T(8,128)(2,1)S(1)}, u32[]{:S(2)}, u32[]{:S(2)}) collective-permute-start(bf16[64,1536]{1,0:T(8,128)(2,1)S(1)} %get-tuple-element.64), channel_id=1, source_target_pairs={{0,2},{1,3},{2,0},{3,1},{4,6},{5,7},{6,4},{7,5},{8,10},{9,11},{10,... | collective-permute-start | bytes 589832 | tf_op jit(solution)/shard_map/ppermute | solution.py:397
  85.1 25.6 %collective-permute-start.25 = (bf16[64,1536]{1,0:T(8,128)(2,1)S(1)}, bf16[64,1536]{1,0:T(8,128)(2,1)S(1)}, u32[]{:S(2)}, u32[]{:S(2)}) collective-permute-start(bf16[64,1536]{1,0:T(8,128)(2,1)S(1)} %get-tuple-element.69.refs_0_), channel_id=1, source_target_pairs={{0,2},{1,3},{2,0},{3,1},{4,6},{5,7},{6,4},{7,5},{8,10},{9,11},{10,... | collective-permute-start | bytes 589832 | tf_op jit(solution)/shard_map/ppermute | solution.py:397
  90.4 9.5 %collective-permute-start.22 = (bf16[64,1536]{1,0:T(8,128)(2,1)S(1)}, bf16[64,1536]{1,0:T(8,128)(2,1)S(1)}, u32[]{:S(2)}, u32[]{:S(2)}) collective-permute-start(bf16[64,1536]{1,0:T(8,128)(2,1)S(1)} %collective-permute-done.21.refs_0_), channel_id=1, source_target_pairs={{0,2},{1,3},{2,0},{3,1},{4,6},{5,7},{6,4},{7,5},{8,10},{9,11},{10,... | collective-permute-start | bytes 589832 | tf_op jit(solution)/shard_map/ppermute | solution.py:397
  93.9 9.6 %collective-permute-start.19 = (bf16[64,1536]{1,0:T(8,128)(2,1)S(1)}, bf16[64,1536]{1,0:T(8,128)(2,1)S(1)}, u32[]{:S(2)}, u32[]{:S(2)}) collective-permute-start(bf16[64,1536]{1,0:T(8,128)(2,1)S(1)} %get-tuple-element.67), channel_id=1, source_target_pairs={{0,2},{1,3},{2,0},{3,1},{4,6},{5,7},{6,4},{7,5},{8,10},{9,11},{10,... | collective-permute-start | bytes 589832 | tf_op jit(solution)/shard_map/ppermute | solution.py:397
  94.5 16.1 %collective-permute-start.18 = (bf16[64,1536]{1,0:T(8,128)(2,1)S(1)}, bf16[64,1536]{1,0:T(8,128)(2,1)S(1)}, u32[]{:S(2)}, u32[]{:S(2)}) collective-permute-start(bf16[64,1536]{1,0:T(8,128)(2,1)S(1)} %add_convert_fusion.4), channel_id=1, source_target_pairs={{0,24},{4,28},{8,16},{12,20},{16,8},{20,12},{24,0},{28,4},{1,25},{... | collective-permute-start | bytes 589832 | tf_op jit(solution)/shard_map/ppermute | solution.py:400
  101.9 11.5 %collective-permute-start.23 = (bf16[64,1536]{1,0:T(8,128)(2,1)S(1)}, bf16[64,1536]{1,0:T(8,128)(2,1)S(1)}, u32[]{:S(2)}, u32[]{:S(2)}) collective-permute-start(bf16[64,1536]{1,0:T(8,128)(2,1)S(1)} %get-tuple-element.71), channel_id=1, source_target_pairs={{0,2},{1,3},{2,0},{3,1},{4,6},{5,7},{6,4},{7,5},{8,10},{9,11},{10,... | collective-permute-start | bytes 589832 | tf_op jit(solution)/shard_map/ppermute | solution.py:397
  103.5 12.3 %collective-permute-start.20 = (bf16[64,1536]{1,0:T(8,128)(2,1)S(1)}, bf16[64,1536]{1,0:T(8,128)(2,1)S(1)}, u32[]{:S(2)}, u32[]{:S(2)}) collective-permute-start(bf16[64,1536]{1,0:T(8,128)(2,1)S(1)} %add_convert_fusion.3), channel_id=1, source_target_pairs={{0,8},{4,12},{8,0},{12,4},{16,24},{20,28},{24,16},{28,20},{1,9},{5... | collective-permute-start | bytes 589832 | tf_op jit(solution)/shard_map/ppermute | solution.py:400
  112.7 5.7 %collective-permute-start.26 = (bf16[64,1536]{1,0:T(8,128)(2,1)S(1)}, bf16[64,1536]{1,0:T(8,128)(2,1)S(1)}, u32[]{:S(2)}, u32[]{:S(2)}) collective-permute-start(bf16[64,1536]{1,0:T(8,128)(2,1)S(1)} %get-tuple-element.74), channel_id=1, source_target_pairs={{0,2},{1,3},{2,0},{3,1},{4,6},{5,7},{6,4},{7,5},{8,10},{9,11},{10,... | collective-permute-start | bytes 589832 | tf_op jit(solution)/shard_map/ppermute | solution.py:397
  113.5 9.4 %collective-permute-start.24 = (bf16[64,1536]{1,0:T(8,128)(2,1)S(1)}, bf16[64,1536]{1,0:T(8,128)(2,1)S(1)}, u32[]{:S(2)}, u32[]{:S(2)}) collective-permute-start(bf16[64,1536]{1,0:T(8,128)(2,1)S(1)} %add_convert_fusion.2), channel_id=1, source_target_pairs={{0,16},{4,20},{8,24},{12,28},{16,0},{20,4},{24,8},{28,12},{1,17},{... | collective-permute-start | bytes 589832 | tf_op jit(solution)/shard_map/ppermute | solution.py:400

commit v4 on v3

--- a/solution.py
+++ b/solution.py
@@ -436,17 +436,17 @@
     w1 = kv_flip(after(out_weight, packed[0]), 1)
     own = kv_index.reshape(1)
     keep, send = attention(queries, key_cache, value_cache, after(own, *packed), cache_lengths)
-    arrived[3] = z_flip(after(packed[3], keep), 3)
-    other = kv_flip(after(send, blocks[0][1], w1), 1)
+    arrived[3] = z_flip(after(packed[3], arrived[2]), 3)
+    other = kv_flip(send, 1)
     half = jax.ShapeDtypeStruct((keep.shape[0], width // 2 + LANES), BF16)
     keep, send = pl.pallas_call(
         join_kernel,
         in_specs=[SMEM, VMEM, VMEM],
         out_specs=[VMEM, VMEM],
         out_shape=[half, half],
-        compiler_params=params(16),
+        compiler_params=params(60),
         name="join",
-    )(after(chip.reshape(1), arrived[1], arrived[2]), keep, other)
+    )(after(chip.reshape(1), arrived[2], arrived[1], blocks[0][1], w1), keep, other)
     other = kv_flip(send, 2)
     blocks[1] = shared(after(arrived[1], keep))
     blocks[2] = shared(after(arrived[2], keep))
@@ -469,9 +469,9 @@
         in_specs=[VMEM] * 4,
         out_specs=[VMEM, VMEM],
         out_shape=[tokens, tokens],
-        compiler_params=params(16),
+        compiler_params=params(60),
         name="norm",
-    )(after(partial, blocks[1][1]), other, residual_in, norm_gain.reshape(1, width))
+    )(after(partial, arrived[3]), other, residual_in, norm_gain.reshape(1, width))
 
     order = (0, 1, 2, 3)
     deep = width // OUTER
@@ -487,10 +487,10 @@
     near = [laid((0, 1), 0, normed)]
     count = residual_in.shape[0]
     here = {0: normed, 1: z_flip(normed, 1), 3: z_flip(normed, 3)}
-    here[2] = z_flip(after(normed, here[3]), 2)
+    here[2] = z_flip(after(normed, here[1]), 2)
     there = {s: kv_flip(here[s], 2) for s in order}
-    blocks[3] = shared(after(arrived[3], blocks[2][1], here[1]))
-    near.append(laid((2, 3), 2 * deep, there[1], here[3]))
+    blocks[3] = shared(after(arrived[3], blocks[2][1]))
+    near.append(laid((2, 3), 2 * deep, there[0], there[1], here[3]))
     weights = near + [kv_flip(part, 1) for part in near]
 
     def added(a, b):

time: 124 us -> 119 us (0.960)
  starting transfers between devices: 47.1 us -> 42.2 us
  Pallas kernels: 29.7 us -> 33.5 us
  local copies, waits for them, and re-layouts: 8.26 us -> 5.66 us
    ppermute x4, waiting for transfers between devices: 11.6 us -> 1.1 us  [y_flip(): return lax.ppermute(a, 'dp', [(i, i ^ bit) for i in range(dp_size)])]
    ppermute x14, waiting for transfers between devices: 6.18 us -> 16.4 us  [kv_flip(): return lax.ppermute(a, 'kv', [(i, i ^ bit) for i in range(kv_size)])]
    ppermute x9, starting transfers between devices: 28.7 us -> 22.4 us  [z_flip(): return lax.ppermute(a, 'dp', [(i, i ^ by * inner) for i in range(dp_size)])]
    unnamed x26 -> x24, local copies, waits for them, and re-layouts: 8.25 us -> 5.06 us
    pallas_call x1, Pallas kernels: 0.57 us -> 2.55 us  [per_device(): pl.pallas_call(join_kernel, in_specs=[SMEM, VMEM, VMEM], out_specs=[VMEM,...]
    pallas_call x1, Pallas kernels: 0.2 us -> 2.03 us  [per_device(): pl.pallas_call(norm_kernel, in_specs=[VMEM] * 4, out_specs=[VMEM, VMEM],...]
  transfers between devices with their start and end apart: 27 -> 27, of which waited for: 13 -> 14; matrix products, arithmetic and copies ran while one was open for 0% -> 1% of each run, Pallas kernels for 21% -> 25%
where the time goes in v4:
time: 119 us
  starting transfers between devices  42.2 us (35%)
  waiting for transfers between devices  36.4 us (31%)
  Pallas kernels  33.5 us (28%)
  local copies, waits for them, and re-layouts  5.66 us (5%)
    ppermute x9, starting transfers between devices, z_flip(): return lax.ppermute(a, 'dp', [(i, i ^ by * inner) for i in range(dp_size)])  22.4 us
    ppermute x9, waiting for transfers between devices, z_flip(): return lax.ppermute(a, 'dp', [(i, i ^ by * inner) for i in range(dp_size)])  18.9 us
    ppermute x14, waiting for transfers between devices, kv_flip(): return lax.ppermute(a, 'kv', [(i, i ^ bit) for i in range(kv_size)])  16.4 us
    ppermute x14, starting transfers between devices, kv_flip(): return lax.ppermute(a, 'kv', [(i, i ^ bit) for i in range(kv_size)])  14.2 us
    pallas_call x1, Pallas kernels, attention(): pl.pallas_call(attention_kernel, in_specs=[SMEM, SMEM, HBM, HBM, HBM], ou...  13.9 us
    pallas_call x4, Pallas kernels, feed(): pl.pallas_call(functools.partial(feed_kernel, main, tail, count, order),...  8.1 us
    ppermute x4, starting transfers between devices, y_flip(): return lax.ppermute(a, 'dp', [(i, i ^ bit) for i in range(dp_size)])  5.61 us
    unnamed x24, local copies, waits for them, and re-layouts  5.06 us
  transfers between devices with their start and end apart: 27, of which 14 were waited for; matrix products, arithmetic and copies ran while one was open for 1% of the time, Pallas kernels for 25%

profile of v4, /device:TPU:0, one launch (start us, length us, event | category | flops | bytes accessed | tf_op | source)
XLA Modules:
  0.0 118.9 jit_solution(13896093465350623049)
XLA Ops:
  0.0 3.3 %pack.1 = (bf16[192,1408]{1,0:T(8,128)(2,1)}, bf16[192,1408]{1,0:T(8,128)(2,1)}, bf16[192,1408]{1,0:T(8,128)(2,1)}, bf16[192,1408]{1,0:T(8,128)(2,1)}) custom-call(s32[1]{0:T(128)} %bitcast.2.z_ref, bf16[192,1728]{1,0:T(8,128)(2,1)} %gate_ref.1, bf16[192,1728]{1,0:T(8,128)(2,1)} %up_ref.1, bf16[192,1728]{1,0:T(8,128)(2,1)} %bitcast.5), custom_call_target="tpu_custom_call" | custom-call | tf_op jit(solution)/shard_map/pack/pallas_call | solution.py:408
  3.3 0.5 collective-permute-start.3
  3.9 3.7 %collective-permute-start = (bf16[192,1408]{1,0:T(8,128)(2,1)}, bf16[192,1408]{1,0:T(8,128)(2,1)S(1)}, u32[]{:S(2)}, u32[]{:S(2)}) collective-permute-start(bf16[192,1408]{1,0:T(8,128)(2,1)} %get-tuple-element.39), channel_id=1, source_target_pairs={{0,16},{4,20},{8,24},{12,28},{16,0},{20,4},{24,8},{28,12},{1,17},{... | collective-permute-start | bytes 1622024 | tf_op jit(solution)/shard_map/ppermute | solution.py:400
  7.5 1.5 %collective-permute-start.2 = (bf16[192,1408]{1,0:T(8,128)(2,1)}, bf16[192,1408]{1,0:T(8,128)(2,1)S(1)}, u32[]{:S(2)}, u32[]{:S(2)}) collective-permute-start(bf16[192,1408]{1,0:T(8,128)(2,1)} %get-tuple-element.41.refs_0_), channel_id=1, source_target_pairs={{0,4},{4,0},{8,12},{12,8},{16,20},{20,16},{24,28},{28,24},{1,5},{5... | collective-permute-start | bytes 1622024 | tf_op jit(solution)/shard_map/ppermute | solution.py:403
  9.0 1.6 %collective-permute-start.1 = (bf16[192,1408]{1,0:T(8,128)(2,1)}, bf16[192,1408]{1,0:T(8,128)(2,1)}, u32[]{:S(2)}, u32[]{:S(2)}) collective-permute-start(bf16[192,1408]{1,0:T(8,128)(2,1)} %get-tuple-element.40), channel_id=1, source_target_pairs={{0,8},{4,12},{8,0},{12,4},{16,24},{20,28},{24,16},{28,20},{1,9},{5... | collective-permute-start | bytes 1622024 | tf_op jit(solution)/shard_map/ppermute | solution.py:400
  10.6 13.9 %attention.1 = (bf16[128,1664]{1,0:T(8,128)(2,1)}, bf16[128,1664]{1,0:T(8,128)(2,1)}) custom-call(s32[1]{0:T(128)} %bitcast.at_ref, s32[3]{0:T(128)} %lengths_ref.1, bf16[256,1536]{1,0:T(8,128)(2,1)} %q_hbm.1, bf16[3,1024,512]{2,1,0:T(8,128)(2,1)} %k_hbm.1, bf16[3,1024,512]{2,1,0:T(8,128)(2,1)} %v_hbm.1), custom_call_target="tpu_custom_call" | custom-call | tf_op jit(solution)/shard_map/attention/pallas_call | solution.py:224
  24.5 0.0 copy-start.11
  24.6 0.1 collective-permute-start.4
  24.6 7.6 %collective-permute-done.refs_0_ = bf16[192,1408]{1,0:T(8,128)(2,1)S(1)} collective-permute-done((bf16[192,1408]{1,0:T(8,128)(2,1)}, bf16[192,1408]{1,0:T(8,128)(2,1)S(1)}, u32[]{:S(2)}, u32[]{:S(2)}) %collective-permute-start) | collective-permute-done | bytes 540704 | tf_op jit(solution)/shard_map/ppermute | solution.py:400
  32.3 3.6 %collective-permute-start.6 = (bf16[192,1408]{1,0:T(8,128)(2,1)}, bf16[192,1408]{1,0:T(8,128)(2,1)}, u32[]{:S(2)}, u32[]{:S(2)}) collective-permute-start(bf16[192,1408]{1,0:T(8,128)(2,1)} %get-tuple-element.51), channel_id=1, source_target_pairs={{0,24},{4,28},{8,16},{12,20},{16,8},{20,12},{24,0},{28,4},{1,25},{... | collective-permute-start | bytes 1622024 | tf_op jit(solution)/shard_map/ppermute | solution.py:400
  35.8 0.0 collective-permute-done.2.refs_1_
  35.8 0.8 copy-done.2
  36.6 0.0 collective-permute-done.1.refs_2_
  36.6 0.0 collective-permute-done.3.w1
  36.7 2.5 %join.1 = (bf16[128,896]{1,0:T(8,128)(2,1)}, bf16[128,896]{1,0:T(8,128)(2,1)}) custom-call(s32[1]{0:T(128)} %bitcast.1.at_ref, bf16[128,1664]{1,0:T(8,128)(2,1)} %get-tuple-element.46.own_ref, bf16[128,1664]{1,0:T(8,128)(2,1)} %collective-permute-done.4.other_ref), custom_call_target="tpu_custom_call" | custom-call | tf_op jit(solution)/shard_map/join/pallas_call | solution.py:442
  39.2 1.4 %collective-permute-start.14 = (bf16[192,1408]{1,0:T(8,128)(2,1)S(1)}, bf16[192,1408]{1,0:T(8,128)(2,1)S(1)}, u32[]{:S(2)}, u32[]{:S(2)}) collective-permute-start(bf16[192,1408]{1,0:T(8,128)(2,1)S(1)} %collective-permute-done.refs_0_), channel_id=1, source_target_pairs={{0,4},{4,0},{8,12},{12,8},{16,20},{20,16},{24,28},{28,24},{1,5},{5... | collective-permute-start | bytes 1622024 | tf_op jit(solution)/shard_map/ppermute | solution.py:403
  40.6 1.5 %collective-permute-start.5 = (bf16[128,896]{1,0:T(8,128)(2,1)}, bf16[128,896]{1,0:T(8,128)(2,1)S(1)}, u32[]{:S(2)}, u32[]{:S(2)}) collective-permute-start(bf16[128,896]{1,0:T(8,128)(2,1)} %get-tuple-element.49), channel_id=1, source_target_pairs={{0,2},{1,3},{2,0},{3,1},{4,6},{5,7},{6,4},{7,5},{8,10},{9,11},{10,... | collective-permute-start | bytes 688136 | tf_op jit(solution)/shard_map/ppermute | solution.py:397
  42.1 5.7 %collective-permute-done.5.other_ref = bf16[128,896]{1,0:T(8,128)(2,1)S(1)} collective-permute-done((bf16[128,896]{1,0:T(8,128)(2,1)}, bf16[128,896]{1,0:T(8,128)(2,1)S(1)}, u32[]{:S(2)}, u32[]{:S(2)}) %collective-permute-start.5) | collective-permute-done | bytes 229408 | tf_op jit(solution)/shard_map/ppermute | solution.py:397
  47.9 0.9 copy-done.7
  48.8 1.1 project.1
  49.9 0.8 copy-done.6
  50.7 1.5 %collective-permute-start.7 = (bf16[64,1536]{1,0:T(8,128)(2,1)S(1)}, bf16[64,1536]{1,0:T(8,128)(2,1)S(1)}, u32[]{:S(2)}, u32[]{:S(2)}) collective-permute-start(bf16[64,1536]{1,0:T(8,128)(2,1)S(1)} %get-tuple-element.53), channel_id=1, source_target_pairs={{0,2},{1,3},{2,0},{3,1},{4,6},{5,7},{6,4},{7,5},{8,10},{9,11},{10,... | collective-permute-start | bytes 589832 | tf_op jit(solution)/shard_map/ppermute | solution.py:397
  52.2 0.6 collective-permute-start.10
  52.8 0.4 collective-permute-done.14.refs_1_
  53.1 0.8 copy-done.4
  53.9 2.1 %collective-permute-start.15 = (bf16[192,1408]{1,0:T(8,128)(2,1)}, bf16[192,1408]{1,0:T(8,128)(2,1)S(1)}, u32[]{:S(2)}, u32[]{:S(2)}) collective-permute-start(bf16[192,1408]{1,0:T(8,128)(2,1)} %collective-permute-done.6.refs_2_), channel_id=1, source_target_pairs={{0,4},{4,0},{8,12},{12,8},{16,20},{20,16},{24,28},{28,24},{1,5},{5... | collective-permute-start | bytes 1622024 | tf_op jit(solution)/shard_map/ppermute | solution.py:403
  56.0 0.6 reshape.21.gain_ref
  56.6 0.7 copy-done.9
  57.3 2.0 %norm.1 = (bf16[64,1536]{1,0:T(8,128)(2,1)}, bf16[64,1536]{1,0:T(8,128)(2,1)}) custom-call(f32[64,1536]{1,0:T(8,128)} %copy-done.6, bf16[64,1536]{1,0:T(8,128)(2,1)} %copy-done.9, bf16[64,1536]{1,0:T(8,128)(2,1)} %residual_ref.1, f32[1,1536]{1,0:T(1,128)} %reshape.21.gain_ref), custom_call_target="tpu_custom_call" | custom-call | tf_op jit(solution)/shard_map/norm/pallas_call | solution.py:467
  59.3 5.5 %collective-permute-start.12 = (bf16[64,1536]{1,0:T(8,128)(2,1)}, bf16[64,1536]{1,0:T(8,128)(2,1)S(1)}, u32[]{:S(2)}, u32[]{:S(2)}) collective-permute-start(bf16[64,1536]{1,0:T(8,128)(2,1)} %get-tuple-element.67.refs_0_), channel_id=1, source_target_pairs={{0,8},{4,12},{8,0},{12,4},{16,24},{20,28},{24,16},{28,20},{1,9},{5... | collective-permute-start | bytes 589832 | tf_op jit(solution)/shard_map/ppermute | solution.py:400
  64.8 1.5 %collective-permute-start.11 = (bf16[64,1536]{1,0:T(8,128)(2,1)}, bf16[64,1536]{1,0:T(8,128)(2,1)S(1)}, u32[]{:S(2)}, u32[]{:S(2)}) collective-permute-start(bf16[64,1536]{1,0:T(8,128)(2,1)} %get-tuple-element.67.refs_0_), channel_id=1, source_target_pairs={{0,2},{1,3},{2,0},{3,1},{4,6},{5,7},{6,4},{7,5},{8,10},{9,11},{10,... | collective-permute-start | bytes 589832 | tf_op jit(solution)/shard_map/ppermute | solution.py:397
  66.3 1.2 collective-permute-start.8
  67.5 2.7 %collective-permute-done.12.refs_0_ = bf16[64,1536]{1,0:T(8,128)(2,1)S(1)} collective-permute-done((bf16[64,1536]{1,0:T(8,128)(2,1)}, bf16[64,1536]{1,0:T(8,128)(2,1)S(1)}, u32[]{:S(2)}, u32[]{:S(2)}) %collective-permute-start.12) | collective-permute-done | bytes 196640 | tf_op jit(solution)/shard_map/ppermute | solution.py:400
  70.2 1.8 %collective-permute-start.13 = (bf16[64,1536]{1,0:T(8,128)(2,1)S(1)}, bf16[64,1536]{1,0:T(8,128)(2,1)S(1)}, u32[]{:S(2)}, u32[]{:S(2)}) collective-permute-start(bf16[64,1536]{1,0:T(8,128)(2,1)S(1)} %collective-permute-done.12.refs_0_), channel_id=1, source_target_pairs={{0,2},{1,3},{2,0},{3,1},{4,6},{5,7},{6,4},{7,5},{8,10},{9,11},{10,... | collective-permute-start | bytes 589832 | tf_op jit(solution)/shard_map/ppermute | solution.py:397
  72.0 1.0 copy-done.3
  73.0 1.3 %place.2.refs_2_ = bf16[768,1408]{1,0:T(8,128)(2,1)S(1)} custom-call(s32[1]{0:T(128)} %bitcast.4.at_ref, bf16[192,1408]{1,0:T(8,128)(2,1)S(1)} %copy-done.1, bf16[192,1408]{1,0:T(8,128)(2,1)S(1)} %copy-done.3, bf16[192,1408]{1,0:T(8,128)(2,1)} %collective-permute-done.1.refs_2_, bf16[192,1408]{1,0:T(8,128)(2,1)S(1)} %collective-permute-done.10.refs_3_), custom_call_target="tpu_custom_call" | custom-call | tf_op jit(solution)/shard_map/place/pallas_call | solution.py:88
  74.3 0.1 collective-permute-start.16
  74.4 0.2 collective-permute-done.8.refs_0_
  74.6 1.3 %collective-permute-done.13.refs_1_ = bf16[64,1536]{1,0:T(8,128)(2,1)S(1)} collective-permute-done((bf16[64,1536]{1,0:T(8,128)(2,1)S(1)}, bf16[64,1536]{1,0:T(8,128)(2,1)S(1)}, u32[]{:S(2)}, u32[]{:S(2)}) %collective-permute-start.13) | collective-permute-done | bytes 196640 | tf_op jit(solution)/shard_map/ppermute | solution.py:397
  75.9 0.7 collective-permute-done.15.refs_3_
  76.6 1.2 %place.3.refs_3_ = bf16[768,1408]{1,0:T(8,128)(2,1)S(1)} custom-call(s32[1]{0:T(128)} %bitcast.4.at_ref, bf16[192,1408]{1,0:T(8,128)(2,1)S(1)} %collective-permute-done.refs_0_, bf16[192,1408]{1,0:T(8,128)(2,1)S(1)} %copy-done.5, bf16[192,1408]{1,0:T(8,128)(2,1)} %collective-permute-done.6.refs_2_, bf16[192,1408]{1,0:T(8,128)(2,1)S(1)} %collective-permute-done.15.refs_3_), custom_call_target="tpu_custom_call" | custom-call | tf_op jit(solution)/shard_map/place/pallas_call | solution.py:88
  77.8 0.1 collective-permute-start.17
  77.9 1.3 %collective-permute-start.9 = (bf16[64,1536]{1,0:T(8,128)(2,1)S(1)}, bf16[64,1536]{1,0:T(8,128)(2,1)S(1)}, u32[]{:S(2)}, u32[]{:S(2)}) collective-permute-start(bf16[64,1536]{1,0:T(8,128)(2,1)S(1)} %collective-permute-done.8.refs_0_), channel_id=1, source_target_pairs={{0,2},{1,3},{2,0},{3,1},{4,6},{5,7},{6,4},{7,5},{8,10},{9,11},{10,... | collective-permute-start | bytes 589832 | tf_op jit(solution)/shard_map/ppermute | solution.py:397
  79.1 2.0 %collective-permute-start.22 = (bf16[64,1536]{1,0:T(8,128)(2,1)S(1)}, bf16[64,1536]{1,0:T(8,128)(2,1)S(1)}, u32[]{:S(2)}, u32[]{:S(2)}) collective-permute-start(bf16[64,1536]{1,0:T(8,128)(2,1)S(1)} %copy-done.8), channel_id=1, source_target_pairs={{0,16},{4,20},{8,24},{12,28},{16,0},{20,4},{24,8},{28,12},{1,17},{... | collective-permute-start | bytes 589832 | tf_op jit(solution)/shard_map/ppermute | solution.py:400
  81.1 4.1 %collective-permute-done.9.refs_1_ = bf16[64,1536]{1,0:T(8,128)(2,1)S(1)} collective-permute-done((bf16[64,1536]{1,0:T(8,128)(2,1)S(1)}, bf16[64,1536]{1,0:T(8,128)(2,1)S(1)}, u32[]{:S(2)}, u32[]{:S(2)}) %collective-permute-start.9) | collective-permute-done | bytes 196640 | tf_op jit(solution)/shard_map/ppermute | solution.py:397
  85.2 2.0 %feed.4 = (bf16[64,1536]{1,0:T(8,128)(2,1)S(1)}, bf16[64,1536]{1,0:T(8,128)(2,1)S(1)}) custom-call(s32[1]{0:T(128)} %bitcast.2.z_ref, bf16[64,1536]{1,0:T(8,128)(2,1)S(1)} %collective-permute-done.8.refs_0_, bf16[64,1536]{1,0:T(8,128)(2,1)S(1)} %collective-permute-done.9.refs_1_, bf16[768,1408]{1,0:T(8,128)(2,1)S(1)} %place.2.refs_2_, ...), custom_call_target="tpu_custom_call" | custom-call | tf_op jit(solution)/shard_map/feed/pallas_call | solution.py:359
  87.2 1.3 %collective-permute-start.18 = (bf16[64,1536]{1,0:T(8,128)(2,1)S(1)}, bf16[64,1536]{1,0:T(8,128)(2,1)S(1)}, u32[]{:S(2)}, u32[]{:S(2)}) collective-permute-start(bf16[64,1536]{1,0:T(8,128)(2,1)S(1)} %get-tuple-element.62), channel_id=1, source_target_pairs={{0,2},{1,3},{2,0},{3,1},{4,6},{5,7},{6,4},{7,5},{8,10},{9,11},{10,... | collective-permute-start | bytes 589832 | tf_op jit(solution)/shard_map/ppermute | solution.py:397
  88.5 2.7 %collective-permute-done.22.refs_0_ = bf16[64,1536]{1,0:T(8,128)(2,1)S(1)} collective-permute-done((bf16[64,1536]{1,0:T(8,128)(2,1)S(1)}, bf16[64,1536]{1,0:T(8,128)(2,1)S(1)}, u32[]{:S(2)}, u32[]{:S(2)}) %collective-permute-start.22) | collective-permute-done | bytes 196640 | tf_op jit(solution)/shard_map/ppermute | solution.py:400
  91.2 0.8 collective-permute-start.23
  92.1 2.0 %feed.5 = (bf16[64,1536]{1,0:T(8,128)(2,1)S(1)}, bf16[64,1536]{1,0:T(8,128)(2,1)S(1)}) custom-call(s32[1]{0:T(128)} %bitcast.2.z_ref, bf16[64,1536]{1,0:T(8,128)(2,1)S(1)} %collective-permute-done.12.refs_0_, bf16[64,1536]{1,0:T(8,128)(2,1)S(1)} %collective-permute-done.13.refs_1_, bf16[768,1408]{1,0:T(8,128)(2,1)S(1)} %place.2.refs_2_, ...), custom_call_target="tpu_custom_call" | custom-call | tf_op jit(solution)/shard_map/feed/pallas_call | solution.py:359
  94.1 1.3 %collective-permute-start.20 = (bf16[64,1536]{1,0:T(8,128)(2,1)S(1)}, bf16[64,1536]{1,0:T(8,128)(2,1)S(1)}, u32[]{:S(2)}, u32[]{:S(2)}) collective-permute-start(bf16[64,1536]{1,0:T(8,128)(2,1)S(1)} %get-tuple-element.65), channel_id=1, source_target_pairs={{0,2},{1,3},{2,0},{3,1},{4,6},{5,7},{6,4},{7,5},{8,10},{9,11},{10,... | collective-permute-start | bytes 589832 | tf_op jit(solution)/shard_map/ppermute | solution.py:397
  95.4 2.0 %collective-permute-start.19 = (bf16[64,1536]{1,0:T(8,128)(2,1)S(1)}, bf16[64,1536]{1,0:T(8,128)(2,1)S(1)}, u32[]{:S(2)}, u32[]{:S(2)}) collective-permute-start(bf16[64,1536]{1,0:T(8,128)(2,1)S(1)} %add_convert_fusion.4), channel_id=1, source_target_pairs={{0,24},{4,28},{8,16},{12,20},{16,8},{20,12},{24,0},{28,4},{1,25},{... | collective-permute-start | bytes 589832 | tf_op jit(solution)/shard_map/ppermute | solution.py:400
  97.4 1.6 %collective-permute-done.23.refs_1_ = bf16[64,1536]{1,0:T(8,128)(2,1)S(1)} collective-permute-done((bf16[64,1536]{1,0:T(8,128)(2,1)S(1)}, bf16[64,1536]{1,0:T(8,128)(2,1)S(1)}, u32[]{:S(2)}, u32[]{:S(2)}) %collective-permute-start.23) | collective-permute-done | bytes 196640 | tf_op jit(solution)/shard_map/ppermute | solution.py:397
  99.1 2.0 %feed.6 = (bf16[64,1536]{1,0:T(8,128)(2,1)S(1)}, bf16[64,1536]{1,0:T(8,128)(2,1)S(1)}) custom-call(s32[1]{0:T(128)} %bitcast.2.z_ref, bf16[64,1536]{1,0:T(8,128)(2,1)S(1)} %collective-permute-done.22.refs_0_, bf16[64,1536]{1,0:T(8,128)(2,1)S(1)} %collective-permute-done.23.refs_1_, bf16[768,1408]{1,0:T(8,128)(2,1)S(1)} %place.2.refs_2_, ...), custom_call_target="tpu_custom_call" | custom-call | tf_op jit(solution)/shard_map/feed/pallas_call | solution.py:359
  101.1 1.1 collective-permute-start.24
  102.2 0.4 collective-permute-done.20
  102.7 2.3 %collective-permute-start.21 = (bf16[64,1536]{1,0:T(8,128)(2,1)S(1)}, bf16[64,1536]{1,0:T(8,128)(2,1)S(1)}, u32[]{:S(2)}, u32[]{:S(2)}) collective-permute-start(bf16[64,1536]{1,0:T(8,128)(2,1)S(1)} %add_convert_fusion.3), channel_id=1, source_target_pairs={{0,8},{4,12},{8,0},{12,4},{16,24},{20,28},{24,16},{28,20},{1,9},{5... | collective-permute-start | bytes 589832 | tf_op jit(solution)/shard_map/ppermute | solution.py:400
  105.0 2.0 %feed.7 = (bf16[64,1536]{1,0:T(8,128)(2,1)S(1)}, bf16[64,1536]{1,0:T(8,128)(2,1)S(1)}) custom-call(s32[1]{0:T(128)} %bitcast.2.z_ref, bf16[64,1536]{1,0:T(8,128)(2,1)S(1)} %copy-done.8, bf16[64,1536]{1,0:T(8,128)(2,1)S(1)} %collective-permute-done.11.refs_1_, bf16[768,1408]{1,0:T(8,128)(2,1)S(1)} %place.2.refs_2_, bf16[768,1408]{1,0:T(8,128)(2,1)S(1)} %place.3.refs_3_, ...), custom_call_target="tpu_custom_call" | custom-call | tf_op jit(solution)/shard_map/feed/pallas_call | solution.py:359
  107.0 1.5 %collective-permute-start.26 = (bf16[64,1536]{1,0:T(8,128)(2,1)S(1)}, bf16[64,1536]{1,0:T(8,128)(2,1)S(1)}, u32[]{:S(2)}, u32[]{:S(2)}) collective-permute-start(bf16[64,1536]{1,0:T(8,128)(2,1)S(1)} %get-tuple-element.72), channel_id=1, source_target_pairs={{0,2},{1,3},{2,0},{3,1},{4,6},{5,7},{6,4},{7,5},{8,10},{9,11},{10,... | collective-permute-start | bytes 589832 | tf_op jit(solution)/shard_map/ppermute | solution.py:397
  108.6 0.6 collective-permute-start.25
  109.2 0.3 collective-permute-done.21
  109.6 3.2 %collective-permute-done.26 = bf16[64,1536]{1,0:T(8,128)(2,1)S(1)} collective-permute-done((bf16[64,1536]{1,0:T(8,128)(2,1)S(1)}, bf16[64,1536]{1,0:T(8,128)(2,1)S(1)}, u32[]{:S(2)}, u32[]{:S(2)}) %collective-permute-start.26) | collective-permute-done | bytes 196640 | tf_op jit(solution)/shard_map/ppermute | solution.py:397
  112.8 5.3 %collective-permute-done.25 = bf16[64,1536]{1,0:T(8,128)(2,1)S(1)} collective-permute-done((bf16[64,1536]{1,0:T(8,128)(2,1)S(1)}, bf16[64,1536]{1,0:T(8,128)(2,1)S(1)}, u32[]{:S(2)}, u32[]{:S(2)}) %collective-permute-start.25) | collective-permute-done | bytes 196640 | tf_op jit(solution)/shard_map/ppermute | solution.py:400
  118.1 0.8 add_convert_fusion
  (30 shorter events, 0.2 us)
Async XLA Ops:
  3.3 33.3 %collective-permute-start.3 = (bf16[384,1536]{1,0:T(8,128)(2,1)}, bf16[384,1536]{1,0:T(8,128)(2,1)S(1)}, u32[]{:S(2)}, u32[]{:S(2)}) collective-permute-start(bf16[384,1536]{1,0:T(8,128)(2,1)} %w0.1), channel_id=1, source_target_pairs={{0,1},{1,0},{2,3},{3,2},{4,5},{5,4},{6,7},{7,6},{8,9},{9,8},{10,11... | collective-permute-start | bytes 3538952 | tf_op jit(solution)/shard_map/ppermute | solution.py:397
  3.9 28.4 %collective-permute-start = (bf16[192,1408]{1,0:T(8,128)(2,1)}, bf16[192,1408]{1,0:T(8,128)(2,1)S(1)}, u32[]{:S(2)}, u32[]{:S(2)}) collective-permute-start(bf16[192,1408]{1,0:T(8,128)(2,1)} %get-tuple-element.39), channel_id=1, source_target_pairs={{0,16},{4,20},{8,24},{12,28},{16,0},{20,4},{24,8},{28,12},{1,17},{... | collective-permute-start | bytes 1622024 | tf_op jit(solution)/shard_map/ppermute | solution.py:400
  7.5 28.3 %collective-permute-start.2 = (bf16[192,1408]{1,0:T(8,128)(2,1)}, bf16[192,1408]{1,0:T(8,128)(2,1)S(1)}, u32[]{:S(2)}, u32[]{:S(2)}) collective-permute-start(bf16[192,1408]{1,0:T(8,128)(2,1)} %get-tuple-element.41.refs_0_), channel_id=1, source_target_pairs={{0,4},{4,0},{8,12},{12,8},{16,20},{20,16},{24,28},{28,24},{1,5},{5... | collective-permute-start | bytes 1622024 | tf_op jit(solution)/shard_map/ppermute | solution.py:403
  9.0 27.6 %collective-permute-start.1 = (bf16[192,1408]{1,0:T(8,128)(2,1)}, bf16[192,1408]{1,0:T(8,128)(2,1)}, u32[]{:S(2)}, u32[]{:S(2)}) collective-permute-start(bf16[192,1408]{1,0:T(8,128)(2,1)} %get-tuple-element.40), channel_id=1, source_target_pairs={{0,8},{4,12},{8,0},{12,4},{16,24},{20,28},{24,16},{28,20},{1,9},{5... | collective-permute-start | bytes 1622024 | tf_op jit(solution)/shard_map/ppermute | solution.py:400
  10.6 37.2 %copy-start = (bf16[384,1536]{1,0:T(8,128)(2,1)S(1)}, bf16[384,1536]{1,0:T(8,128)(2,1)}, u32[]{:S(2)}) copy-start(bf16[384,1536]{1,0:T(8,128)(2,1)} %w0.1) | copy-start | bytes 3538948
  24.5 31.5 %copy-start.11 = (f32[1536]{0:T(1024)S(1)}, f32[1536]{0:T(1024)}, u32[]{:S(2)}) copy-start(f32[1536]{0:T(1024)} %param.16) | copy-start | bytes 18436
  24.6 12.1 %collective-permute-start.4 = (bf16[128,1664]{1,0:T(8,128)(2,1)}, bf16[128,1664]{1,0:T(8,128)(2,1)}, u32[]{:S(2)}, u32[]{:S(2)}) collective-permute-start(bf16[128,1664]{1,0:T(8,128)(2,1)} %get-tuple-element.47), channel_id=1, source_target_pairs={{0,1},{1,0},{2,3},{3,2},{4,5},{5,4},{6,7},{7,6},{8,9},{9,8},{10,11... | collective-permute-start | bytes 1277960 | tf_op jit(solution)/shard_map/ppermute | solution.py:397
  32.3 20.5 %collective-permute-start.6 = (bf16[192,1408]{1,0:T(8,128)(2,1)}, bf16[192,1408]{1,0:T(8,128)(2,1)}, u32[]{:S(2)}, u32[]{:S(2)}) collective-permute-start(bf16[192,1408]{1,0:T(8,128)(2,1)} %get-tuple-element.51), channel_id=1, source_target_pairs={{0,24},{4,28},{8,16},{12,20},{16,8},{20,12},{24,0},{28,4},{1,25},{... | collective-permute-start | bytes 1622024 | tf_op jit(solution)/shard_map/ppermute | solution.py:400
  35.8 0.8 copy-start.2
  36.7 35.3 %copy-start.1 = (bf16[192,1408]{1,0:T(8,128)(2,1)S(1)}, bf16[192,1408]{1,0:T(8,128)(2,1)}, u32[]{:S(2)}) copy-start(bf16[192,1408]{1,0:T(8,128)(2,1)} %get-tuple-element.41.refs_0_) | copy-start | bytes 1622020
  39.2 13.9 %collective-permute-start.14 = (bf16[192,1408]{1,0:T(8,128)(2,1)S(1)}, bf16[192,1408]{1,0:T(8,128)(2,1)S(1)}, u32[]{:S(2)}, u32[]{:S(2)}) collective-permute-start(bf16[192,1408]{1,0:T(8,128)(2,1)S(1)} %collective-permute-done.refs_0_), channel_id=1, source_target_pairs={{0,4},{4,0},{8,12},{12,8},{16,20},{20,16},{24,28},{28,24},{1,5},{5... | collective-permute-start | bytes 1622024 | tf_op jit(solution)/shard_map/ppermute | solution.py:403
  40.6 7.2 %collective-permute-start.5 = (bf16[128,896]{1,0:T(8,128)(2,1)}, bf16[128,896]{1,0:T(8,128)(2,1)S(1)}, u32[]{:S(2)}, u32[]{:S(2)}) collective-permute-start(bf16[128,896]{1,0:T(8,128)(2,1)} %get-tuple-element.49), channel_id=1, source_target_pairs={{0,2},{1,3},{2,0},{3,1},{4,6},{5,7},{6,4},{7,5},{8,10},{9,11},{10,... | collective-permute-start | bytes 688136 | tf_op jit(solution)/shard_map/ppermute | solution.py:397
  47.9 0.9 copy-start.7
  49.9 0.8 copy-start.6
  50.7 5.9 %collective-permute-start.7 = (bf16[64,1536]{1,0:T(8,128)(2,1)S(1)}, bf16[64,1536]{1,0:T(8,128)(2,1)S(1)}, u32[]{:S(2)}, u32[]{:S(2)}) collective-permute-start(bf16[64,1536]{1,0:T(8,128)(2,1)S(1)} %get-tuple-element.53), channel_id=1, source_target_pairs={{0,2},{1,3},{2,0},{3,1},{4,6},{5,7},{6,4},{7,5},{8,10},{9,11},{10,... | collective-permute-start | bytes 589832 | tf_op jit(solution)/shard_map/ppermute | solution.py:397
  52.2 19.8 %collective-permute-start.10 = (bf16[192,1408]{1,0:T(8,128)(2,1)}, bf16[192,1408]{1,0:T(8,128)(2,1)S(1)}, u32[]{:S(2)}, u32[]{:S(2)}) collective-permute-start(bf16[192,1408]{1,0:T(8,128)(2,1)} %collective-permute-done.1.refs_2_), channel_id=1, source_target_pairs={{0,4},{4,0},{8,12},{12,8},{16,20},{20,16},{24,28},{28,24},{1,5},{5... | collective-permute-start | bytes 1622024 | tf_op jit(solution)/shard_map/ppermute | solution.py:403
  53.1 0.8 copy-start.4
  53.9 22.7 %collective-permute-start.15 = (bf16[192,1408]{1,0:T(8,128)(2,1)}, bf16[192,1408]{1,0:T(8,128)(2,1)S(1)}, u32[]{:S(2)}, u32[]{:S(2)}) collective-permute-start(bf16[192,1408]{1,0:T(8,128)(2,1)} %collective-permute-done.6.refs_2_), channel_id=1, source_target_pairs={{0,4},{4,0},{8,12},{12,8},{16,20},{20,16},{24,28},{28,24},{1,5},{5... | collective-permute-start | bytes 1622024 | tf_op jit(solution)/shard_map/ppermute | solution.py:403
  56.6 0.7 copy-start.9
  59.3 10.8 %collective-permute-start.12 = (bf16[64,1536]{1,0:T(8,128)(2,1)}, bf16[64,1536]{1,0:T(8,128)(2,1)S(1)}, u32[]{:S(2)}, u32[]{:S(2)}) collective-permute-start(bf16[64,1536]{1,0:T(8,128)(2,1)} %get-tuple-element.67.refs_0_), channel_id=1, source_target_pairs={{0,8},{4,12},{8,0},{12,4},{16,24},{20,28},{24,16},{28,20},{1,9},{5... | collective-permute-start | bytes 589832 | tf_op jit(solution)/shard_map/ppermute | solution.py:400
  64.8 9.6 %collective-permute-start.11 = (bf16[64,1536]{1,0:T(8,128)(2,1)}, bf16[64,1536]{1,0:T(8,128)(2,1)S(1)}, u32[]{:S(2)}, u32[]{:S(2)}) collective-permute-start(bf16[64,1536]{1,0:T(8,128)(2,1)} %get-tuple-element.67.refs_0_), channel_id=1, source_target_pairs={{0,2},{1,3},{2,0},{3,1},{4,6},{5,7},{6,4},{7,5},{8,10},{9,11},{10,... | collective-permute-start | bytes 589832 | tf_op jit(solution)/shard_map/ppermute | solution.py:397
  66.3 8.3 %collective-permute-start.8 = (bf16[64,1536]{1,0:T(8,128)(2,1)}, bf16[64,1536]{1,0:T(8,128)(2,1)S(1)}, u32[]{:S(2)}, u32[]{:S(2)}) collective-permute-start(bf16[64,1536]{1,0:T(8,128)(2,1)} %get-tuple-element.67.refs_0_), channel_id=1, source_target_pairs={{0,24},{4,28},{8,16},{12,20},{16,8},{20,12},{24,0},{28,4},{1,25},{... | collective-permute-start | bytes 589832 | tf_op jit(solution)/shard_map/ppermute | solution.py:400
  70.2 5.7 %collective-permute-start.13 = (bf16[64,1536]{1,0:T(8,128)(2,1)S(1)}, bf16[64,1536]{1,0:T(8,128)(2,1)S(1)}, u32[]{:S(2)}, u32[]{:S(2)}) collective-permute-start(bf16[64,1536]{1,0:T(8,128)(2,1)S(1)} %collective-permute-done.12.refs_0_), channel_id=1, source_target_pairs={{0,2},{1,3},{2,0},{3,1},{4,6},{5,7},{6,4},{7,5},{8,10},{9,11},{10,... | collective-permute-start | bytes 589832 | tf_op jit(solution)/shard_map/ppermute | solution.py:397
  72.0 1.0 copy-start.3
  73.0 3.6 %copy-start.5 = (bf16[192,1408]{1,0:T(8,128)(2,1)S(1)}, bf16[192,1408]{1,0:T(8,128)(2,1)}, u32[]{:S(2)}) copy-start(bf16[192,1408]{1,0:T(8,128)(2,1)} %copy-done.4) | copy-start | bytes 1622020
  74.3 4.8 %copy-start.8 = (bf16[64,1536]{1,0:T(8,128)(2,1)S(1)}, bf16[64,1536]{1,0:T(8,128)(2,1)}, u32[]{:S(2)}) copy-start(bf16[64,1536]{1,0:T(8,128)(2,1)} %get-tuple-element.67.refs_0_) | copy-start | bytes 589828
  74.3 10.9 %collective-permute-start.16 = (bf16[768,1408]{1,0:T(8,128)(2,1)S(1)}, bf16[768,1408]{1,0:T(8,128)(2,1)S(1)}, u32[]{:S(2)}, u32[]{:S(2)}) collective-permute-start(bf16[768,1408]{1,0:T(8,128)(2,1)S(1)} %place.2.refs_2_), channel_id=1, source_target_pairs={{0,1},{1,0},{2,3},{3,2},{4,5},{5,4},{6,7},{7,6},{8,9},{9,8},{10,11... | collective-permute-start | bytes 6488072 | tf_op jit(solution)/shard_map/ppermute | solution.py:397
  77.8 7.4 %collective-permute-start.17 = (bf16[768,1408]{1,0:T(8,128)(2,1)S(1)}, bf16[768,1408]{1,0:T(8,128)(2,1)S(1)}, u32[]{:S(2)}, u32[]{:S(2)}) collective-permute-start(bf16[768,1408]{1,0:T(8,128)(2,1)S(1)} %place.3.refs_3_), channel_id=1, source_target_pairs={{0,1},{1,0},{2,3},{3,2},{4,5},{5,4},{6,7},{7,6},{8,9},{9,8},{10,11... | collective-permute-start | bytes 6488072 | tf_op jit(solution)/shard_map/ppermute | solution.py:397
  77.9 7.3 %collective-permute-start.9 = (bf16[64,1536]{1,0:T(8,128)(2,1)S(1)}, bf16[64,1536]{1,0:T(8,128)(2,1)S(1)}, u32[]{:S(2)}, u32[]{:S(2)}) collective-permute-start(bf16[64,1536]{1,0:T(8,128)(2,1)S(1)} %collective-permute-done.8.refs_0_), channel_id=1, source_target_pairs={{0,2},{1,3},{2,0},{3,1},{4,6},{5,7},{6,4},{7,5},{8,10},{9,11},{10,... | collective-permute-start | bytes 589832 | tf_op jit(solution)/shard_map/ppermute | solution.py:397
  79.1 12.1 %collective-permute-start.22 = (bf16[64,1536]{1,0:T(8,128)(2,1)S(1)}, bf16[64,1536]{1,0:T(8,128)(2,1)S(1)}, u32[]{:S(2)}, u32[]{:S(2)}) collective-permute-start(bf16[64,1536]{1,0:T(8,128)(2,1)S(1)} %copy-done.8), channel_id=1, source_target_pairs={{0,16},{4,20},{8,24},{12,28},{16,0},{20,4},{24,8},{28,12},{1,17},{... | collective-permute-start | bytes 589832 | tf_op jit(solution)/shard_map/ppermute | solution.py:400
  87.2 8.1 %collective-permute-start.18 = (bf16[64,1536]{1,0:T(8,128)(2,1)S(1)}, bf16[64,1536]{1,0:T(8,128)(2,1)S(1)}, u32[]{:S(2)}, u32[]{:S(2)}) collective-permute-start(bf16[64,1536]{1,0:T(8,128)(2,1)S(1)} %get-tuple-element.62), channel_id=1, source_target_pairs={{0,2},{1,3},{2,0},{3,1},{4,6},{5,7},{6,4},{7,5},{8,10},{9,11},{10,... | collective-permute-start | bytes 589832 | tf_op jit(solution)/shard_map/ppermute | solution.py:397
  91.2 7.8 %collective-permute-start.23 = (bf16[64,1536]{1,0:T(8,128)(2,1)S(1)}, bf16[64,1536]{1,0:T(8,128)(2,1)S(1)}, u32[]{:S(2)}, u32[]{:S(2)}) collective-permute-start(bf16[64,1536]{1,0:T(8,128)(2,1)S(1)} %collective-permute-done.22.refs_0_), channel_id=1, source_target_pairs={{0,2},{1,3},{2,0},{3,1},{4,6},{5,7},{6,4},{7,5},{8,10},{9,11},{10,... | collective-permute-start | bytes 589832 | tf_op jit(solution)/shard_map/ppermute | solution.py:397
  94.1 8.6 %collective-permute-start.20 = (bf16[64,1536]{1,0:T(8,128)(2,1)S(1)}, bf16[64,1536]{1,0:T(8,128)(2,1)S(1)}, u32[]{:S(2)}, u32[]{:S(2)}) collective-permute-start(bf16[64,1536]{1,0:T(8,128)(2,1)S(1)} %get-tuple-element.65), channel_id=1, source_target_pairs={{0,2},{1,3},{2,0},{3,1},{4,6},{5,7},{6,4},{7,5},{8,10},{9,11},{10,... | collective-permute-start | bytes 589832 | tf_op jit(solution)/shard_map/ppermute | solution.py:397
  95.4 9.6 %collective-permute-start.19 = (bf16[64,1536]{1,0:T(8,128)(2,1)S(1)}, bf16[64,1536]{1,0:T(8,128)(2,1)S(1)}, u32[]{:S(2)}, u32[]{:S(2)}) collective-permute-start(bf16[64,1536]{1,0:T(8,128)(2,1)S(1)} %add_convert_fusion.4), channel_id=1, source_target_pairs={{0,24},{4,28},{8,16},{12,20},{16,8},{20,12},{24,0},{28,4},{1,25},{... | collective-permute-start | bytes 589832 | tf_op jit(solution)/shard_map/ppermute | solution.py:400
  101.1 7.4 %collective-permute-start.24 = (bf16[64,1536]{1,0:T(8,128)(2,1)S(1)}, bf16[64,1536]{1,0:T(8,128)(2,1)S(1)}, u32[]{:S(2)}, u32[]{:S(2)}) collective-permute-start(bf16[64,1536]{1,0:T(8,128)(2,1)S(1)} %get-tuple-element.69), channel_id=1, source_target_pairs={{0,2},{1,3},{2,0},{3,1},{4,6},{5,7},{6,4},{7,5},{8,10},{9,11},{10,... | collective-permute-start | bytes 589832 | tf_op jit(solution)/shard_map/ppermute | solution.py:397
  102.7 6.9 %collective-permute-start.21 = (bf16[64,1536]{1,0:T(8,128)(2,1)S(1)}, bf16[64,1536]{1,0:T(8,128)(2,1)S(1)}, u32[]{:S(2)}, u32[]{:S(2)}) collective-permute-start(bf16[64,1536]{1,0:T(8,128)(2,1)S(1)} %add_convert_fusion.3), channel_id=1, source_target_pairs={{0,8},{4,12},{8,0},{12,4},{16,24},{20,28},{24,16},{28,20},{1,9},{5... | collective-permute-start | bytes 589832 | tf_op jit(solution)/shard_map/ppermute | solution.py:400
  105.0 13.1 %copy-start.10 = (bf16[64,1536]{1,0:T(8,128)(2,1)S(1)}, bf16[64,1536]{1,0:T(8,128)(2,1)}, u32[]{:S(2)}) copy-start(bf16[64,1536]{1,0:T(8,128)(2,1)} %get-tuple-element.54) | copy-start | bytes 589828
  107.0 5.7 %collective-permute-start.26 = (bf16[64,1536]{1,0:T(8,128)(2,1)S(1)}, bf16[64,1536]{1,0:T(8,128)(2,1)S(1)}, u32[]{:S(2)}, u32[]{:S(2)}) collective-permute-start(bf16[64,1536]{1,0:T(8,128)(2,1)S(1)} %get-tuple-element.72), channel_id=1, source_target_pairs={{0,2},{1,3},{2,0},{3,1},{4,6},{5,7},{6,4},{7,5},{8,10},{9,11},{10,... | collective-permute-start | bytes 589832 | tf_op jit(solution)/shard_map/ppermute | solution.py:397
  108.6 9.5 %collective-permute-start.25 = (bf16[64,1536]{1,0:T(8,128)(2,1)S(1)}, bf16[64,1536]{1,0:T(8,128)(2,1)S(1)}, u32[]{:S(2)}, u32[]{:S(2)}) collective-permute-start(bf16[64,1536]{1,0:T(8,128)(2,1)S(1)} %add_convert_fusion.2), channel_id=1, source_target_pairs={{0,16},{4,20},{8,24},{12,28},{16,0},{20,4},{24,8},{28,12},{1,17},{... | collective-permute-start | bytes 589832 | tf_op jit(solution)/shard_map/ppermute | solution.py:400

commit v5 on v4

--- a/solution.py
+++ b/solution.py
@@ -471,7 +471,7 @@
         out_shape=[tokens, tokens],
         compiler_params=params(60),
         name="norm",
-    )(after(partial, arrived[3]), other, residual_in, norm_gain.reshape(1, width))
+    )(partial, other, residual_in, norm_gain.reshape(1, width))
 
     order = (0, 1, 2, 3)
     deep = width // OUTER
@@ -486,10 +486,11 @@
 
     near = [laid((0, 1), 0, normed)]
     count = residual_in.shape[0]
-    here = {0: normed, 1: z_flip(normed, 1), 3: z_flip(normed, 3)}
-    here[2] = z_flip(after(normed, here[1]), 2)
+    ready = after(normed, arrived[3])
+    here = {0: normed, 1: z_flip(ready, 1), 3: z_flip(ready, 3)}
+    here[2] = z_flip(after(ready, here[1]), 2)
     there = {s: kv_flip(here[s], 2) for s in order}
-    blocks[3] = shared(after(arrived[3], blocks[2][1]))
+    blocks[3] = shared(after(arrived[3], blocks[2][1], normed))
     near.append(laid((2, 3), 2 * deep, there[0], there[1], here[3]))
     weights = near + [kv_flip(part, 1) for part in near]
 

time: 119 us -> 118 us (level)
  starting transfers between devices: 42.2 us -> 26.7 us
  waiting for transfers between devices: 36.4 us -> 50.5 us
    ppermute x14, waiting for transfers between devices: 16.4 us -> 28.7 us  [kv_flip(): return lax.ppermute(a, 'kv', [(i, i ^ bit) for i in range(kv_size)])]
    ppermute x9, starting transfers between devices: 22.4 us -> 11.2 us  [z_flip(): return lax.ppermute(a, 'dp', [(i, i ^ by * inner) for i in range(dp_size)])]
    ppermute x4, waiting for transfers between devices: 1.1 us -> 4.03 us  [y_flip(): return lax.ppermute(a, 'dp', [(i, i ^ bit) for i in range(dp_size)])]
    ppermute x14, starting transfers between devices: 14.2 us -> 11.4 us  [kv_flip(): return lax.ppermute(a, 'kv', [(i, i ^ bit) for i in range(kv_size)])]
    ppermute x4, starting transfers between devices: 5.61 us -> 4.04 us  [y_flip(): return lax.ppermute(a, 'dp', [(i, i ^ bit) for i in range(dp_size)])]
  transfers between devices with their start and end apart: 27 -> 27, of which waited for: 14 -> 15; matrix products, arithmetic and copies ran while one was open for 1% -> 1% of each run, Pallas kernels for 25% -> 26%
where the time goes in v5:
time: 118 us
  waiting for transfers between devices  50.5 us (43%)
  Pallas kernels  33.5 us (28%)
  starting transfers between devices  26.7 us (23%)
  local copies, waits for them, and re-layouts  5.67 us (5%)
    ppermute x14, waiting for transfers between devices, kv_flip(): return lax.ppermute(a, 'kv', [(i, i ^ bit) for i in range(kv_size)])  28.7 us
    ppermute x9, waiting for transfers between devices, z_flip(): return lax.ppermute(a, 'dp', [(i, i ^ by * inner) for i in range(dp_size)])  17.7 us
    pallas_call x1, Pallas kernels, attention(): pl.pallas_call(attention_kernel, in_specs=[SMEM, SMEM, HBM, HBM, HBM], ou...  13.9 us
    ppermute x14, starting transfers between devices, kv_flip(): return lax.ppermute(a, 'kv', [(i, i ^ bit) for i in range(kv_size)])  11.4 us
    ppermute x9, starting transfers between devices, z_flip(): return lax.ppermute(a, 'dp', [(i, i ^ by * inner) for i in range(dp_size)])  11.2 us
    pallas_call x4, Pallas kernels, feed(): pl.pallas_call(functools.partial(feed_kernel, main, tail, count, order),...  8.11 us
    unnamed x24, local copies, waits for them, and re-layouts  5.07 us
    ppermute x4, starting transfers between devices, y_flip(): return lax.ppermute(a, 'dp', [(i, i ^ bit) for i in range(dp_size)])  4.04 us
  transfers between devices with their start and end apart: 27, of which 15 were waited for; matrix products, arithmetic and copies ran while one was open for 1% of the time, Pallas kernels for 26%

profile of v5, /device:TPU:0, one launch (start us, length us, event | category | flops | bytes accessed | tf_op | source)
XLA Modules:
  0.0 117.6 jit_solution(15552912141834535069)
XLA Ops:
  0.0 3.3 %pack.1 = (bf16[192,1408]{1,0:T(8,128)(2,1)}, bf16[192,1408]{1,0:T(8,128)(2,1)}, bf16[192,1408]{1,0:T(8,128)(2,1)}, bf16[192,1408]{1,0:T(8,128)(2,1)}) custom-call(s32[1]{0:T(128)} %bitcast.2.z_ref, bf16[192,1728]{1,0:T(8,128)(2,1)} %gate_ref.1, bf16[192,1728]{1,0:T(8,128)(2,1)} %up_ref.1, bf16[192,1728]{1,0:T(8,128)(2,1)} %bitcast.5), custom_call_target="tpu_custom_call" | custom-call | tf_op jit(solution)/shard_map/pack/pallas_call | solution.py:408
  3.3 0.5 collective-permute-start.3
  3.9 3.7 %collective-permute-start = (bf16[192,1408]{1,0:T(8,128)(2,1)}, bf16[192,1408]{1,0:T(8,128)(2,1)S(1)}, u32[]{:S(2)}, u32[]{:S(2)}) collective-permute-start(bf16[192,1408]{1,0:T(8,128)(2,1)} %get-tuple-element.39), channel_id=1, source_target_pairs={{0,16},{4,20},{8,24},{12,28},{16,0},{20,4},{24,8},{28,12},{1,17},{... | collective-permute-start | bytes 1622024 | tf_op jit(solution)/shard_map/ppermute | solution.py:400
  7.5 1.5 %collective-permute-start.2 = (bf16[192,1408]{1,0:T(8,128)(2,1)}, bf16[192,1408]{1,0:T(8,128)(2,1)S(1)}, u32[]{:S(2)}, u32[]{:S(2)}) collective-permute-start(bf16[192,1408]{1,0:T(8,128)(2,1)} %get-tuple-element.41.refs_0_), channel_id=1, source_target_pairs={{0,4},{4,0},{8,12},{12,8},{16,20},{20,16},{24,28},{28,24},{1,5},{5... | collective-permute-start | bytes 1622024 | tf_op jit(solution)/shard_map/ppermute | solution.py:403
  9.0 1.6 %collective-permute-start.1 = (bf16[192,1408]{1,0:T(8,128)(2,1)}, bf16[192,1408]{1,0:T(8,128)(2,1)}, u32[]{:S(2)}, u32[]{:S(2)}) collective-permute-start(bf16[192,1408]{1,0:T(8,128)(2,1)} %get-tuple-element.40), channel_id=1, source_target_pairs={{0,8},{4,12},{8,0},{12,4},{16,24},{20,28},{24,16},{28,20},{1,9},{5... | collective-permute-start | bytes 1622024 | tf_op jit(solution)/shard_map/ppermute | solution.py:400
  10.6 13.9 %attention.1 = (bf16[128,1664]{1,0:T(8,128)(2,1)}, bf16[128,1664]{1,0:T(8,128)(2,1)}) custom-call(s32[1]{0:T(128)} %bitcast.at_ref, s32[3]{0:T(128)} %lengths_ref.1, bf16[256,1536]{1,0:T(8,128)(2,1)} %q_hbm.1, bf16[3,1024,512]{2,1,0:T(8,128)(2,1)} %k_hbm.1, bf16[3,1024,512]{2,1,0:T(8,128)(2,1)} %v_hbm.1), custom_call_target="tpu_custom_call" | custom-call | tf_op jit(solution)/shard_map/attention/pallas_call | solution.py:224
  24.5 0.0 copy-start.11
  24.6 0.1 collective-permute-start.4
  24.6 7.6 %collective-permute-done.refs_0_ = bf16[192,1408]{1,0:T(8,128)(2,1)S(1)} collective-permute-done((bf16[192,1408]{1,0:T(8,128)(2,1)}, bf16[192,1408]{1,0:T(8,128)(2,1)S(1)}, u32[]{:S(2)}, u32[]{:S(2)}) %collective-permute-start) | collective-permute-done | bytes 540704 | tf_op jit(solution)/shard_map/ppermute | solution.py:400
  32.3 3.6 %collective-permute-start.7 = (bf16[192,1408]{1,0:T(8,128)(2,1)}, bf16[192,1408]{1,0:T(8,128)(2,1)}, u32[]{:S(2)}, u32[]{:S(2)}) collective-permute-start(bf16[192,1408]{1,0:T(8,128)(2,1)} %get-tuple-element.54), channel_id=1, source_target_pairs={{0,24},{4,28},{8,16},{12,20},{16,8},{20,12},{24,0},{28,4},{1,25},{... | collective-permute-start | bytes 1622024 | tf_op jit(solution)/shard_map/ppermute | solution.py:400
  35.8 0.0 collective-permute-done.2.refs_1_
  35.8 0.8 copy-done.2
  36.6 0.0 collective-permute-done.1.refs_2_
  36.6 0.0 collective-permute-done.3.w1
  36.7 2.5 %join.1 = (bf16[128,896]{1,0:T(8,128)(2,1)}, bf16[128,896]{1,0:T(8,128)(2,1)}) custom-call(s32[1]{0:T(128)} %bitcast.1.at_ref, bf16[128,1664]{1,0:T(8,128)(2,1)} %get-tuple-element.46.own_ref, bf16[128,1664]{1,0:T(8,128)(2,1)} %collective-permute-done.4.other_ref), custom_call_target="tpu_custom_call" | custom-call | tf_op jit(solution)/shard_map/join/pallas_call | solution.py:442
  39.2 1.4 %collective-permute-start.14 = (bf16[192,1408]{1,0:T(8,128)(2,1)S(1)}, bf16[192,1408]{1,0:T(8,128)(2,1)S(1)}, u32[]{:S(2)}, u32[]{:S(2)}) collective-permute-start(bf16[192,1408]{1,0:T(8,128)(2,1)S(1)} %collective-permute-done.refs_0_), channel_id=1, source_target_pairs={{0,4},{4,0},{8,12},{12,8},{16,20},{20,16},{24,28},{28,24},{1,5},{5... | collective-permute-start | bytes 1622024 | tf_op jit(solution)/shard_map/ppermute | solution.py:403
  40.6 1.5 %collective-permute-start.5 = (bf16[128,896]{1,0:T(8,128)(2,1)}, bf16[128,896]{1,0:T(8,128)(2,1)S(1)}, u32[]{:S(2)}, u32[]{:S(2)}) collective-permute-start(bf16[128,896]{1,0:T(8,128)(2,1)} %get-tuple-element.49), channel_id=1, source_target_pairs={{0,2},{1,3},{2,0},{3,1},{4,6},{5,7},{6,4},{7,5},{8,10},{9,11},{10,... | collective-permute-start | bytes 688136 | tf_op jit(solution)/shard_map/ppermute | solution.py:397
  42.1 5.7 %collective-permute-done.5.other_ref = bf16[128,896]{1,0:T(8,128)(2,1)S(1)} collective-permute-done((bf16[128,896]{1,0:T(8,128)(2,1)}, bf16[128,896]{1,0:T(8,128)(2,1)S(1)}, u32[]{:S(2)}, u32[]{:S(2)}) %collective-permute-start.5) | collective-permute-done | bytes 229408 | tf_op jit(solution)/shard_map/ppermute | solution.py:397
  47.9 0.9 copy-done.7
  48.8 1.1 project.1
  49.9 0.8 copy-done.6
  50.7 1.5 %collective-permute-start.6 = (bf16[64,1536]{1,0:T(8,128)(2,1)S(1)}, bf16[64,1536]{1,0:T(8,128)(2,1)S(1)}, u32[]{:S(2)}, u32[]{:S(2)}) collective-permute-start(bf16[64,1536]{1,0:T(8,128)(2,1)S(1)} %get-tuple-element.51), channel_id=1, source_target_pairs={{0,2},{1,3},{2,0},{3,1},{4,6},{5,7},{6,4},{7,5},{8,10},{9,11},{10,... | collective-permute-start | bytes 589832 | tf_op jit(solution)/shard_map/ppermute | solution.py:397
  52.2 0.6 reshape.21.gain_ref
  52.8 0.6 collective-permute-start.10
  53.4 3.0 %collective-permute-done.6.other_ref = bf16[64,1536]{1,0:T(8,128)(2,1)S(1)} collective-permute-done((bf16[64,1536]{1,0:T(8,128)(2,1)S(1)}, bf16[64,1536]{1,0:T(8,128)(2,1)S(1)}, u32[]{:S(2)}, u32[]{:S(2)}) %collective-permute-start.6) | collective-permute-done | bytes 196640 | tf_op jit(solution)/shard_map/ppermute | solution.py:397
  56.4 0.7 copy-done.9
  57.1 2.0 %norm.1 = (bf16[64,1536]{1,0:T(8,128)(2,1)}, bf16[64,1536]{1,0:T(8,128)(2,1)}) custom-call(f32[64,1536]{1,0:T(8,128)} %copy-done.6, bf16[64,1536]{1,0:T(8,128)(2,1)} %copy-done.9, bf16[64,1536]{1,0:T(8,128)(2,1)} %residual_ref.1, f32[1,1536]{1,0:T(1,128)} %reshape.21.gain_ref), custom_call_target="tpu_custom_call" | custom-call | tf_op jit(solution)/shard_map/norm/pallas_call | solution.py:467
  59.1 0.8 copy-done.4
  59.9 0.5 collective-permute-start.15
  60.5 1.1 collective-permute-start.12
  61.5 1.2 %collective-permute-start.8 = (bf16[64,1536]{1,0:T(8,128)(2,1)}, bf16[64,1536]{1,0:T(8,128)(2,1)S(1)}, u32[]{:S(2)}, u32[]{:S(2)}) collective-permute-start(bf16[64,1536]{1,0:T(8,128)(2,1)} %get-tuple-element.67.refs_0_), channel_id=1, source_target_pairs={{0,24},{4,28},{8,16},{12,20},{16,8},{20,12},{24,0},{28,4},{1,25},{... | collective-permute-start | bytes 589832 | tf_op jit(solution)/shard_map/ppermute | solution.py:400
  62.7 1.5 %collective-permute-start.11 = (bf16[64,1536]{1,0:T(8,128)(2,1)}, bf16[64,1536]{1,0:T(8,128)(2,1)S(1)}, u32[]{:S(2)}, u32[]{:S(2)}) collective-permute-start(bf16[64,1536]{1,0:T(8,128)(2,1)} %get-tuple-element.67.refs_0_), channel_id=1, source_target_pairs={{0,2},{1,3},{2,0},{3,1},{4,6},{5,7},{6,4},{7,5},{8,10},{9,11},{10,... | collective-permute-start | bytes 589832 | tf_op jit(solution)/shard_map/ppermute | solution.py:397
  64.2 3.3 %collective-permute-done.12.refs_0_ = bf16[64,1536]{1,0:T(8,128)(2,1)S(1)} collective-permute-done((bf16[64,1536]{1,0:T(8,128)(2,1)}, bf16[64,1536]{1,0:T(8,128)(2,1)S(1)}, u32[]{:S(2)}, u32[]{:S(2)}) %collective-permute-start.12) | collective-permute-done | bytes 196640 | tf_op jit(solution)/shard_map/ppermute | solution.py:400
  67.5 1.5 %collective-permute-start.13 = (bf16[64,1536]{1,0:T(8,128)(2,1)S(1)}, bf16[64,1536]{1,0:T(8,128)(2,1)S(1)}, u32[]{:S(2)}, u32[]{:S(2)}) collective-permute-start(bf16[64,1536]{1,0:T(8,128)(2,1)S(1)} %collective-permute-done.12.refs_0_), channel_id=1, source_target_pairs={{0,2},{1,3},{2,0},{3,1},{4,6},{5,7},{6,4},{7,5},{8,10},{9,11},{10,... | collective-permute-start | bytes 589832 | tf_op jit(solution)/shard_map/ppermute | solution.py:397
  69.0 1.0 copy-done.3
  70.0 1.3 %place.2.refs_2_ = bf16[768,1408]{1,0:T(8,128)(2,1)S(1)} custom-call(s32[1]{0:T(128)} %bitcast.4.at_ref, bf16[192,1408]{1,0:T(8,128)(2,1)S(1)} %copy-done.1, bf16[192,1408]{1,0:T(8,128)(2,1)S(1)} %copy-done.3, bf16[192,1408]{1,0:T(8,128)(2,1)} %collective-permute-done.1.refs_2_, bf16[192,1408]{1,0:T(8,128)(2,1)S(1)} %collective-permute-done.10.refs_3_), custom_call_target="tpu_custom_call" | custom-call | tf_op jit(solution)/shard_map/place/pallas_call | solution.py:88
  71.3 0.1 collective-permute-start.16
  71.4 1.7 %collective-permute-done.13.refs_1_ = bf16[64,1536]{1,0:T(8,128)(2,1)S(1)} collective-permute-done((bf16[64,1536]{1,0:T(8,128)(2,1)S(1)}, bf16[64,1536]{1,0:T(8,128)(2,1)S(1)}, u32[]{:S(2)}, u32[]{:S(2)}) %collective-permute-start.13) | collective-permute-done | bytes 196640 | tf_op jit(solution)/shard_map/ppermute | solution.py:397
  73.2 4.0 %collective-permute-done.15.refs_3_ = bf16[192,1408]{1,0:T(8,128)(2,1)S(1)} collective-permute-done((bf16[192,1408]{1,0:T(8,128)(2,1)}, bf16[192,1408]{1,0:T(8,128)(2,1)S(1)}, u32[]{:S(2)}, u32[]{:S(2)}) %collective-permute-start.15) | collective-permute-done | bytes 540704 | tf_op jit(solution)/shard_map/ppermute | solution.py:403
  77.2 1.2 %place.3.refs_3_ = bf16[768,1408]{1,0:T(8,128)(2,1)S(1)} custom-call(s32[1]{0:T(128)} %bitcast.4.at_ref, bf16[192,1408]{1,0:T(8,128)(2,1)S(1)} %collective-permute-done.refs_0_, bf16[192,1408]{1,0:T(8,128)(2,1)S(1)} %copy-done.5, bf16[192,1408]{1,0:T(8,128)(2,1)} %collective-permute-done.7.refs_2_, bf16[192,1408]{1,0:T(8,128)(2,1)S(1)} %collective-permute-done.15.refs_3_), custom_call_target="tpu_custom_call" | custom-call | tf_op jit(solution)/shard_map/place/pallas_call | solution.py:88
  78.4 0.1 collective-permute-start.17
  78.5 0.7 collective-permute-start.9
  79.1 6.6 %collective-permute-done.9.refs_1_ = bf16[64,1536]{1,0:T(8,128)(2,1)S(1)} collective-permute-done((bf16[64,1536]{1,0:T(8,128)(2,1)S(1)}, bf16[64,1536]{1,0:T(8,128)(2,1)S(1)}, u32[]{:S(2)}, u32[]{:S(2)}) %collective-permute-start.9) | collective-permute-done | bytes 196640 | tf_op jit(solution)/shard_map/ppermute | solution.py:397
  85.8 2.0 %feed.4 = (bf16[64,1536]{1,0:T(8,128)(2,1)S(1)}, bf16[64,1536]{1,0:T(8,128)(2,1)S(1)}) custom-call(s32[1]{0:T(128)} %bitcast.2.z_ref, bf16[64,1536]{1,0:T(8,128)(2,1)S(1)} %collective-permute-done.8.refs_0_, bf16[64,1536]{1,0:T(8,128)(2,1)S(1)} %collective-permute-done.9.refs_1_, bf16[768,1408]{1,0:T(8,128)(2,1)S(1)} %place.2.refs_2_, ...), custom_call_target="tpu_custom_call" | custom-call | tf_op jit(solution)/shard_map/feed/pallas_call | solution.py:359
  87.8 0.7 collective-permute-start.18
  88.5 1.1 collective-permute-done.22.refs_0_
  89.6 0.5 collective-permute-start.23
  90.2 2.0 %feed.5 = (bf16[64,1536]{1,0:T(8,128)(2,1)S(1)}, bf16[64,1536]{1,0:T(8,128)(2,1)S(1)}) custom-call(s32[1]{0:T(128)} %bitcast.2.z_ref, bf16[64,1536]{1,0:T(8,128)(2,1)S(1)} %collective-permute-done.12.refs_0_, bf16[64,1536]{1,0:T(8,128)(2,1)S(1)} %collective-permute-done.13.refs_1_, bf16[768,1408]{1,0:T(8,128)(2,1)S(1)} %place.2.refs_2_, ...), custom_call_target="tpu_custom_call" | custom-call | tf_op jit(solution)/shard_map/feed/pallas_call | solution.py:359
  92.2 1.6 %collective-permute-start.20 = (bf16[64,1536]{1,0:T(8,128)(2,1)S(1)}, bf16[64,1536]{1,0:T(8,128)(2,1)S(1)}, u32[]{:S(2)}, u32[]{:S(2)}) collective-permute-start(bf16[64,1536]{1,0:T(8,128)(2,1)S(1)} %get-tuple-element.65), channel_id=1, source_target_pairs={{0,2},{1,3},{2,0},{3,1},{4,6},{5,7},{6,4},{7,5},{8,10},{9,11},{10,... | collective-permute-start | bytes 589832 | tf_op jit(solution)/shard_map/ppermute | solution.py:397
  93.7 2.0 %collective-permute-done.18 = bf16[64,1536]{1,0:T(8,128)(2,1)S(1)} collective-permute-done((bf16[64,1536]{1,0:T(8,128)(2,1)S(1)}, bf16[64,1536]{1,0:T(8,128)(2,1)S(1)}, u32[]{:S(2)}, u32[]{:S(2)}) %collective-permute-start.18) | collective-permute-done | bytes 196640 | tf_op jit(solution)/shard_map/ppermute | solution.py:397
  95.8 0.1 collective-permute-start.19
  95.8 4.1 %collective-permute-done.23.refs_1_ = bf16[64,1536]{1,0:T(8,128)(2,1)S(1)} collective-permute-done((bf16[64,1536]{1,0:T(8,128)(2,1)S(1)}, bf16[64,1536]{1,0:T(8,128)(2,1)S(1)}, u32[]{:S(2)}, u32[]{:S(2)}) %collective-permute-start.23) | collective-permute-done | bytes 196640 | tf_op jit(solution)/shard_map/ppermute | solution.py:397
  99.9 2.0 %feed.6 = (bf16[64,1536]{1,0:T(8,128)(2,1)S(1)}, bf16[64,1536]{1,0:T(8,128)(2,1)S(1)}) custom-call(s32[1]{0:T(128)} %bitcast.2.z_ref, bf16[64,1536]{1,0:T(8,128)(2,1)S(1)} %collective-permute-done.22.refs_0_, bf16[64,1536]{1,0:T(8,128)(2,1)S(1)} %collective-permute-done.23.refs_1_, bf16[768,1408]{1,0:T(8,128)(2,1)S(1)} %place.2.refs_2_, ...), custom_call_target="tpu_custom_call" | custom-call | tf_op jit(solution)/shard_map/feed/pallas_call | solution.py:359
  102.0 0.7 collective-permute-start.24
  102.6 0.9 collective-permute-done.20
  103.5 0.1 collective-permute-start.21
  103.6 2.0 %feed.7 = (bf16[64,1536]{1,0:T(8,128)(2,1)S(1)}, bf16[64,1536]{1,0:T(8,128)(2,1)S(1)}) custom-call(s32[1]{0:T(128)} %bitcast.2.z_ref, bf16[64,1536]{1,0:T(8,128)(2,1)S(1)} %copy-done.8, bf16[64,1536]{1,0:T(8,128)(2,1)S(1)} %collective-permute-done.11.refs_1_, bf16[768,1408]{1,0:T(8,128)(2,1)S(1)} %place.2.refs_2_, bf16[768,1408]{1,0:T(8,128)(2,1)S(1)} %place.3.refs_3_, ...), custom_call_target="tpu_custom_call" | custom-call | tf_op jit(solution)/shard_map/feed/pallas_call | solution.py:359
  105.7 0.7 collective-permute-start.26
  106.3 2.7 %collective-permute-done.24 = bf16[64,1536]{1,0:T(8,128)(2,1)S(1)} collective-permute-done((bf16[64,1536]{1,0:T(8,128)(2,1)S(1)}, bf16[64,1536]{1,0:T(8,128)(2,1)S(1)}, u32[]{:S(2)}, u32[]{:S(2)}) %collective-permute-start.24) | collective-permute-done | bytes 196640 | tf_op jit(solution)/shard_map/ppermute | solution.py:397
  109.1 0.1 collective-permute-start.25
  109.1 0.8 collective-permute-done.21
  110.0 2.0 %collective-permute-done.26 = bf16[64,1536]{1,0:T(8,128)(2,1)S(1)} collective-permute-done((bf16[64,1536]{1,0:T(8,128)(2,1)S(1)}, bf16[64,1536]{1,0:T(8,128)(2,1)S(1)}, u32[]{:S(2)}, u32[]{:S(2)}) %collective-permute-start.26) | collective-permute-done | bytes 196640 | tf_op jit(solution)/shard_map/ppermute | solution.py:397
  111.9 4.8 %collective-permute-done.25 = bf16[64,1536]{1,0:T(8,128)(2,1)S(1)} collective-permute-done((bf16[64,1536]{1,0:T(8,128)(2,1)S(1)}, bf16[64,1536]{1,0:T(8,128)(2,1)S(1)}, u32[]{:S(2)}, u32[]{:S(2)}) %collective-permute-start.25) | collective-permute-done | bytes 196640 | tf_op jit(solution)/shard_map/ppermute | solution.py:400
  116.8 0.8 add_convert_fusion
  (30 shorter events, 0.2 us)
Async XLA Ops:
  3.3 33.3 %collective-permute-start.3 = (bf16[384,1536]{1,0:T(8,128)(2,1)}, bf16[384,1536]{1,0:T(8,128)(2,1)S(1)}, u32[]{:S(2)}, u32[]{:S(2)}) collective-permute-start(bf16[384,1536]{1,0:T(8,128)(2,1)} %w0.1), channel_id=1, source_target_pairs={{0,1},{1,0},{2,3},{3,2},{4,5},{5,4},{6,7},{7,6},{8,9},{9,8},{10,11... | collective-permute-start | bytes 3538952 | tf_op jit(solution)/shard_map/ppermute | solution.py:397
  3.9 28.4 %collective-permute-start = (bf16[192,1408]{1,0:T(8,128)(2,1)}, bf16[192,1408]{1,0:T(8,128)(2,1)S(1)}, u32[]{:S(2)}, u32[]{:S(2)}) collective-permute-start(bf16[192,1408]{1,0:T(8,128)(2,1)} %get-tuple-element.39), channel_id=1, source_target_pairs={{0,16},{4,20},{8,24},{12,28},{16,0},{20,4},{24,8},{28,12},{1,17},{... | collective-permute-start | bytes 1622024 | tf_op jit(solution)/shard_map/ppermute | solution.py:400
  7.5 28.3 %collective-permute-start.2 = (bf16[192,1408]{1,0:T(8,128)(2,1)}, bf16[192,1408]{1,0:T(8,128)(2,1)S(1)}, u32[]{:S(2)}, u32[]{:S(2)}) collective-permute-start(bf16[192,1408]{1,0:T(8,128)(2,1)} %get-tuple-element.41.refs_0_), channel_id=1, source_target_pairs={{0,4},{4,0},{8,12},{12,8},{16,20},{20,16},{24,28},{28,24},{1,5},{5... | collective-permute-start | bytes 1622024 | tf_op jit(solution)/shard_map/ppermute | solution.py:403
  9.0 27.6 %collective-permute-start.1 = (bf16[192,1408]{1,0:T(8,128)(2,1)}, bf16[192,1408]{1,0:T(8,128)(2,1)}, u32[]{:S(2)}, u32[]{:S(2)}) collective-permute-start(bf16[192,1408]{1,0:T(8,128)(2,1)} %get-tuple-element.40), channel_id=1, source_target_pairs={{0,8},{4,12},{8,0},{12,4},{16,24},{20,28},{24,16},{28,20},{1,9},{5... | collective-permute-start | bytes 1622024 | tf_op jit(solution)/shard_map/ppermute | solution.py:400
  10.6 37.2 %copy-start = (bf16[384,1536]{1,0:T(8,128)(2,1)S(1)}, bf16[384,1536]{1,0:T(8,128)(2,1)}, u32[]{:S(2)}) copy-start(bf16[384,1536]{1,0:T(8,128)(2,1)} %w0.1) | copy-start | bytes 3538948
  24.5 27.7 %copy-start.11 = (f32[1536]{0:T(1024)S(1)}, f32[1536]{0:T(1024)}, u32[]{:S(2)}) copy-start(f32[1536]{0:T(1024)} %param.16) | copy-start | bytes 18436
  24.6 12.1 %collective-permute-start.4 = (bf16[128,1664]{1,0:T(8,128)(2,1)}, bf16[128,1664]{1,0:T(8,128)(2,1)}, u32[]{:S(2)}, u32[]{:S(2)}) collective-permute-start(bf16[128,1664]{1,0:T(8,128)(2,1)} %get-tuple-element.47), channel_id=1, source_target_pairs={{0,1},{1,0},{2,3},{3,2},{4,5},{5,4},{6,7},{7,6},{8,9},{9,8},{10,11... | collective-permute-start | bytes 1277960 | tf_op jit(solution)/shard_map/ppermute | solution.py:397
  32.3 26.8 %collective-permute-start.7 = (bf16[192,1408]{1,0:T(8,128)(2,1)}, bf16[192,1408]{1,0:T(8,128)(2,1)}, u32[]{:S(2)}, u32[]{:S(2)}) collective-permute-start(bf16[192,1408]{1,0:T(8,128)(2,1)} %get-tuple-element.54), channel_id=1, source_target_pairs={{0,24},{4,28},{8,16},{12,20},{16,8},{20,12},{24,0},{28,4},{1,25},{... | collective-permute-start | bytes 1622024 | tf_op jit(solution)/shard_map/ppermute | solution.py:400
  35.8 0.8 copy-start.2
  36.7 32.3 %copy-start.1 = (bf16[192,1408]{1,0:T(8,128)(2,1)S(1)}, bf16[192,1408]{1,0:T(8,128)(2,1)}, u32[]{:S(2)}) copy-start(bf16[192,1408]{1,0:T(8,128)(2,1)} %get-tuple-element.41.refs_0_) | copy-start | bytes 1622020
  39.2 19.9 %collective-permute-start.14 = (bf16[192,1408]{1,0:T(8,128)(2,1)S(1)}, bf16[192,1408]{1,0:T(8,128)(2,1)S(1)}, u32[]{:S(2)}, u32[]{:S(2)}) collective-permute-start(bf16[192,1408]{1,0:T(8,128)(2,1)S(1)} %collective-permute-done.refs_0_), channel_id=1, source_target_pairs={{0,4},{4,0},{8,12},{12,8},{16,20},{20,16},{24,28},{28,24},{1,5},{5... | collective-permute-start | bytes 1622024 | tf_op jit(solution)/shard_map/ppermute | solution.py:403
  40.6 7.2 %collective-permute-start.5 = (bf16[128,896]{1,0:T(8,128)(2,1)}, bf16[128,896]{1,0:T(8,128)(2,1)S(1)}, u32[]{:S(2)}, u32[]{:S(2)}) collective-permute-start(bf16[128,896]{1,0:T(8,128)(2,1)} %get-tuple-element.49), channel_id=1, source_target_pairs={{0,2},{1,3},{2,0},{3,1},{4,6},{5,7},{6,4},{7,5},{8,10},{9,11},{10,... | collective-permute-start | bytes 688136 | tf_op jit(solution)/shard_map/ppermute | solution.py:397
  47.9 0.9 copy-start.7
  49.9 0.8 copy-start.6
  50.7 5.7 %collective-permute-start.6 = (bf16[64,1536]{1,0:T(8,128)(2,1)S(1)}, bf16[64,1536]{1,0:T(8,128)(2,1)S(1)}, u32[]{:S(2)}, u32[]{:S(2)}) collective-permute-start(bf16[64,1536]{1,0:T(8,128)(2,1)S(1)} %get-tuple-element.51), channel_id=1, source_target_pairs={{0,2},{1,3},{2,0},{3,1},{4,6},{5,7},{6,4},{7,5},{8,10},{9,11},{10,... | collective-permute-start | bytes 589832 | tf_op jit(solution)/shard_map/ppermute | solution.py:397
  52.8 16.2 %collective-permute-start.10 = (bf16[192,1408]{1,0:T(8,128)(2,1)}, bf16[192,1408]{1,0:T(8,128)(2,1)S(1)}, u32[]{:S(2)}, u32[]{:S(2)}) collective-permute-start(bf16[192,1408]{1,0:T(8,128)(2,1)} %collective-permute-done.1.refs_2_), channel_id=1, source_target_pairs={{0,4},{4,0},{8,12},{12,8},{16,20},{20,16},{24,28},{28,24},{1,5},{5... | collective-permute-start | bytes 1622024 | tf_op jit(solution)/shard_map/ppermute | solution.py:403
  56.4 0.7 copy-start.9
  59.1 0.8 copy-start.4
  59.9 17.3 %collective-permute-start.15 = (bf16[192,1408]{1,0:T(8,128)(2,1)}, bf16[192,1408]{1,0:T(8,128)(2,1)S(1)}, u32[]{:S(2)}, u32[]{:S(2)}) collective-permute-start(bf16[192,1408]{1,0:T(8,128)(2,1)} %collective-permute-done.7.refs_2_), channel_id=1, source_target_pairs={{0,4},{4,0},{8,12},{12,8},{16,20},{20,16},{24,28},{28,24},{1,5},{5... | collective-permute-start | bytes 1622024 | tf_op jit(solution)/shard_map/ppermute | solution.py:403
  60.5 7.0 %collective-permute-start.12 = (bf16[64,1536]{1,0:T(8,128)(2,1)}, bf16[64,1536]{1,0:T(8,128)(2,1)S(1)}, u32[]{:S(2)}, u32[]{:S(2)}) collective-permute-start(bf16[64,1536]{1,0:T(8,128)(2,1)} %get-tuple-element.67.refs_0_), channel_id=1, source_target_pairs={{0,8},{4,12},{8,0},{12,4},{16,24},{20,28},{24,16},{28,20},{1,9},{5... | collective-permute-start | bytes 589832 | tf_op jit(solution)/shard_map/ppermute | solution.py:400
  61.5 9.9 %collective-permute-start.8 = (bf16[64,1536]{1,0:T(8,128)(2,1)}, bf16[64,1536]{1,0:T(8,128)(2,1)S(1)}, u32[]{:S(2)}, u32[]{:S(2)}) collective-permute-start(bf16[64,1536]{1,0:T(8,128)(2,1)} %get-tuple-element.67.refs_0_), channel_id=1, source_target_pairs={{0,24},{4,28},{8,16},{12,20},{16,8},{20,12},{24,0},{28,4},{1,25},{... | collective-permute-start | bytes 589832 | tf_op jit(solution)/shard_map/ppermute | solution.py:400
  62.7 8.7 %collective-permute-start.11 = (bf16[64,1536]{1,0:T(8,128)(2,1)}, bf16[64,1536]{1,0:T(8,128)(2,1)S(1)}, u32[]{:S(2)}, u32[]{:S(2)}) collective-permute-start(bf16[64,1536]{1,0:T(8,128)(2,1)} %get-tuple-element.67.refs_0_), channel_id=1, source_target_pairs={{0,2},{1,3},{2,0},{3,1},{4,6},{5,7},{6,4},{7,5},{8,10},{9,11},{10,... | collective-permute-start | bytes 589832 | tf_op jit(solution)/shard_map/ppermute | solution.py:397
  67.5 5.7 %collective-permute-start.13 = (bf16[64,1536]{1,0:T(8,128)(2,1)S(1)}, bf16[64,1536]{1,0:T(8,128)(2,1)S(1)}, u32[]{:S(2)}, u32[]{:S(2)}) collective-permute-start(bf16[64,1536]{1,0:T(8,128)(2,1)S(1)} %collective-permute-done.12.refs_0_), channel_id=1, source_target_pairs={{0,2},{1,3},{2,0},{3,1},{4,6},{5,7},{6,4},{7,5},{8,10},{9,11},{10,... | collective-permute-start | bytes 589832 | tf_op jit(solution)/shard_map/ppermute | solution.py:397
  69.0 1.0 copy-start.3
  70.0 7.1 %copy-start.5 = (bf16[192,1408]{1,0:T(8,128)(2,1)S(1)}, bf16[192,1408]{1,0:T(8,128)(2,1)}, u32[]{:S(2)}) copy-start(bf16[192,1408]{1,0:T(8,128)(2,1)} %copy-done.4) | copy-start | bytes 1622020
  71.3 7.8 %copy-start.8 = (bf16[64,1536]{1,0:T(8,128)(2,1)S(1)}, bf16[64,1536]{1,0:T(8,128)(2,1)}, u32[]{:S(2)}) copy-start(bf16[64,1536]{1,0:T(8,128)(2,1)} %get-tuple-element.67.refs_0_) | copy-start | bytes 589828
  71.3 14.5 %collective-permute-start.16 = (bf16[768,1408]{1,0:T(8,128)(2,1)S(1)}, bf16[768,1408]{1,0:T(8,128)(2,1)S(1)}, u32[]{:S(2)}, u32[]{:S(2)}) collective-permute-start(bf16[768,1408]{1,0:T(8,128)(2,1)S(1)} %place.2.refs_2_), channel_id=1, source_target_pairs={{0,1},{1,0},{2,3},{3,2},{4,5},{5,4},{6,7},{7,6},{8,9},{9,8},{10,11... | collective-permute-start | bytes 6488072 | tf_op jit(solution)/shard_map/ppermute | solution.py:397
  78.4 7.4 %collective-permute-start.17 = (bf16[768,1408]{1,0:T(8,128)(2,1)S(1)}, bf16[768,1408]{1,0:T(8,128)(2,1)S(1)}, u32[]{:S(2)}, u32[]{:S(2)}) collective-permute-start(bf16[768,1408]{1,0:T(8,128)(2,1)S(1)} %place.3.refs_3_), channel_id=1, source_target_pairs={{0,1},{1,0},{2,3},{3,2},{4,5},{5,4},{6,7},{7,6},{8,9},{9,8},{10,11... | collective-permute-start | bytes 6488072 | tf_op jit(solution)/shard_map/ppermute | solution.py:397
  78.5 7.3 %collective-permute-start.9 = (bf16[64,1536]{1,0:T(8,128)(2,1)S(1)}, bf16[64,1536]{1,0:T(8,128)(2,1)S(1)}, u32[]{:S(2)}, u32[]{:S(2)}) collective-permute-start(bf16[64,1536]{1,0:T(8,128)(2,1)S(1)} %collective-permute-done.8.refs_0_), channel_id=1, source_target_pairs={{0,2},{1,3},{2,0},{3,1},{4,6},{5,7},{6,4},{7,5},{8,10},{9,11},{10,... | collective-permute-start | bytes 589832 | tf_op jit(solution)/shard_map/ppermute | solution.py:397
  79.1 10.5 %collective-permute-start.22 = (bf16[64,1536]{1,0:T(8,128)(2,1)S(1)}, bf16[64,1536]{1,0:T(8,128)(2,1)S(1)}, u32[]{:S(2)}, u32[]{:S(2)}) collective-permute-start(bf16[64,1536]{1,0:T(8,128)(2,1)S(1)} %copy-done.8), channel_id=1, source_target_pairs={{0,16},{4,20},{8,24},{12,28},{16,0},{20,4},{24,8},{28,12},{1,17},{... | collective-permute-start | bytes 589832 | tf_op jit(solution)/shard_map/ppermute | solution.py:400
  87.8 7.9 %collective-permute-start.18 = (bf16[64,1536]{1,0:T(8,128)(2,1)S(1)}, bf16[64,1536]{1,0:T(8,128)(2,1)S(1)}, u32[]{:S(2)}, u32[]{:S(2)}) collective-permute-start(bf16[64,1536]{1,0:T(8,128)(2,1)S(1)} %get-tuple-element.62), channel_id=1, source_target_pairs={{0,2},{1,3},{2,0},{3,1},{4,6},{5,7},{6,4},{7,5},{8,10},{9,11},{10,... | collective-permute-start | bytes 589832 | tf_op jit(solution)/shard_map/ppermute | solution.py:397
  89.6 10.3 %collective-permute-start.23 = (bf16[64,1536]{1,0:T(8,128)(2,1)S(1)}, bf16[64,1536]{1,0:T(8,128)(2,1)S(1)}, u32[]{:S(2)}, u32[]{:S(2)}) collective-permute-start(bf16[64,1536]{1,0:T(8,128)(2,1)S(1)} %collective-permute-done.22.refs_0_), channel_id=1, source_target_pairs={{0,2},{1,3},{2,0},{3,1},{4,6},{5,7},{6,4},{7,5},{8,10},{9,11},{10,... | collective-permute-start | bytes 589832 | tf_op jit(solution)/shard_map/ppermute | solution.py:397
  92.2 11.3 %collective-permute-start.20 = (bf16[64,1536]{1,0:T(8,128)(2,1)S(1)}, bf16[64,1536]{1,0:T(8,128)(2,1)S(1)}, u32[]{:S(2)}, u32[]{:S(2)}) collective-permute-start(bf16[64,1536]{1,0:T(8,128)(2,1)S(1)} %get-tuple-element.65), channel_id=1, source_target_pairs={{0,2},{1,3},{2,0},{3,1},{4,6},{5,7},{6,4},{7,5},{8,10},{9,11},{10,... | collective-permute-start | bytes 589832 | tf_op jit(solution)/shard_map/ppermute | solution.py:397
  95.8 7.9 %collective-permute-start.19 = (bf16[64,1536]{1,0:T(8,128)(2,1)S(1)}, bf16[64,1536]{1,0:T(8,128)(2,1)S(1)}, u32[]{:S(2)}, u32[]{:S(2)}) collective-permute-start(bf16[64,1536]{1,0:T(8,128)(2,1)S(1)} %add_convert_fusion.4), channel_id=1, source_target_pairs={{0,24},{4,28},{8,16},{12,20},{16,8},{20,12},{24,0},{28,4},{1,25},{... | collective-permute-start | bytes 589832 | tf_op jit(solution)/shard_map/ppermute | solution.py:400
  102.0 7.0 %collective-permute-start.24 = (bf16[64,1536]{1,0:T(8,128)(2,1)S(1)}, bf16[64,1536]{1,0:T(8,128)(2,1)S(1)}, u32[]{:S(2)}, u32[]{:S(2)}) collective-permute-start(bf16[64,1536]{1,0:T(8,128)(2,1)S(1)} %get-tuple-element.69), channel_id=1, source_target_pairs={{0,2},{1,3},{2,0},{3,1},{4,6},{5,7},{6,4},{7,5},{8,10},{9,11},{10,... | collective-permute-start | bytes 589832 | tf_op jit(solution)/shard_map/ppermute | solution.py:397
  103.5 6.4 %collective-permute-start.21 = (bf16[64,1536]{1,0:T(8,128)(2,1)S(1)}, bf16[64,1536]{1,0:T(8,128)(2,1)S(1)}, u32[]{:S(2)}, u32[]{:S(2)}) collective-permute-start(bf16[64,1536]{1,0:T(8,128)(2,1)S(1)} %add_convert_fusion.3), channel_id=1, source_target_pairs={{0,8},{4,12},{8,0},{12,4},{16,24},{20,28},{24,16},{28,20},{1,9},{5... | collective-permute-start | bytes 589832 | tf_op jit(solution)/shard_map/ppermute | solution.py:400
  103.6 13.1 %copy-start.10 = (bf16[64,1536]{1,0:T(8,128)(2,1)S(1)}, bf16[64,1536]{1,0:T(8,128)(2,1)}, u32[]{:S(2)}) copy-start(bf16[64,1536]{1,0:T(8,128)(2,1)} %get-tuple-element.52) | copy-start | bytes 589828
  105.7 6.2 %collective-permute-start.26 = (bf16[64,1536]{1,0:T(8,128)(2,1)S(1)}, bf16[64,1536]{1,0:T(8,128)(2,1)S(1)}, u32[]{:S(2)}, u32[]{:S(2)}) collective-permute-start(bf16[64,1536]{1,0:T(8,128)(2,1)S(1)} %get-tuple-element.72), channel_id=1, source_target_pairs={{0,2},{1,3},{2,0},{3,1},{4,6},{5,7},{6,4},{7,5},{8,10},{9,11},{10,... | collective-permute-start | bytes 589832 | tf_op jit(solution)/shard_map/ppermute | solution.py:397
  109.1 7.7 %collective-permute-start.25 = (bf16[64,1536]{1,0:T(8,128)(2,1)S(1)}, bf16[64,1536]{1,0:T(8,128)(2,1)S(1)}, u32[]{:S(2)}, u32[]{:S(2)}) collective-permute-start(bf16[64,1536]{1,0:T(8,128)(2,1)S(1)} %add_convert_fusion.2), channel_id=1, source_target_pairs={{0,16},{4,20},{8,24},{12,28},{16,0},{20,4},{24,8},{28,12},{1,17},{... | collective-permute-start | bytes 589832 | tf_op jit(solution)/shard_map/ppermute | solution.py:400

commit v6 on v5

--- a/solution.py
+++ b/solution.py
@@ -42,36 +42,39 @@
 def pack_kernel(main, tail, cuts, z_ref, gate_ref, up_ref, down_ref, *refs):
     outs, slots, (weights, sems, in_sems) = refs[: len(cuts)], refs[len(cuts) : -3], refs[-3:]
     tail_at = OUTER * main
+    second = 2 * main + LANES
     total = weights.shape[1]
     step = total // 2 if total % 32 == 0 else total
-    loads = []
-    for index, ref in enumerate((gate_ref, up_ref, down_ref)):
-        for start in range(0, total, step):
+    loads, copies = [], []
+    for start in range(0, total, step):
+        for index, ref in enumerate((gate_ref, up_ref, down_ref)):
             pick = pl.ds(start, step)
             loads.append(pltpu.make_async_copy(ref.at[pick], weights.at[index, pick], in_sems.at[len(loads)]))
             loads[-1].start()
-    for load in loads:
-        load.wait()
-    gate_ref, up_ref, down_ref = (weights.at[index] for index in range(3))
-    second = 2 * main + LANES
-    copies = []
-    for index, (shift, start, rows) in enumerate(cuts):
-        out = slots[index]
-        target = z_ref[0] ^ shift
-        pick = slice(start, start + rows)
-        column = pl.multiple_of(target * main, LANES)
-        out[:, :main] = gate_ref[pick, pl.ds(column, main)]
-        out[:, main : 2 * main] = up_ref[pick, pl.ds(column, main)]
-        out[:, second : second + main] = down_ref[pick, pl.ds(column, main)]
-        shape = (OUTER * tail, LANES)
-        k, lane = iota(shape, 0) - target * tail, iota(shape, 1)
-        first = one_hot((lane < tail) & (k == lane))
-        next_to = one_hot((lane >= tail) & (lane < 2 * tail) & (k == lane - tail))
-        ends = dot(gate_ref[pick, tail_at:], first) + dot(up_ref[pick, tail_at:], next_to)
-        out[:, 2 * main : second] = ends.astype(BF16)
-        out[:, second + main :] = dot(down_ref[pick, tail_at:], first).astype(BF16)
-        copies.append(pltpu.make_async_copy(out, outs[index], sems.at[index]))
-        copies[-1].start()
+    shape = (OUTER * tail, LANES)
+    lane = iota(shape, 1)
+    targets = [z_ref[0] ^ shift for shift in cuts]
+    firsts = [one_hot((lane < tail) & (iota(shape, 0) == lane + target * tail)) for target in targets]
+    seconds = [
+        one_hot((lane >= tail) & (lane < 2 * tail) & (iota(shape, 0) == lane - tail + target * tail))
+        for target in targets
+    ]
+    for start in range(0, total, step):
+        for load in loads[start // step * 3 : start // step * 3 + 3]:
+            load.wait()
+        pick = slice(start, start + step)
+        gate, up, down = (weights.at[index] for index in range(3))
+        for index, out in enumerate(slots):
+            column = pl.multiple_of(targets[index] * main, LANES)
+            out[pick, :main] = gate[pick, pl.ds(column, main)]
+            out[pick, main : 2 * main] = up[pick, pl.ds(column, main)]
+            out[pick, second : second + main] = down[pick, pl.ds(column, main)]
+            ends = dot(gate[pick, tail_at:], firsts[index]) + dot(up[pick, tail_at:], seconds[index])
+            out[pick, 2 * main : second] = ends.astype(BF16)
+            out[pick, second + main :] = dot(down[pick, tail_at:], firsts[index]).astype(BF16)
+            rows = pl.ds(start, step)
+            copies.append(pltpu.make_async_copy(out.at[rows], outs[index].at[rows], sems.at[len(copies)]))
+            copies[-1].start()
     for copy in copies:
         copy.wait()
 
@@ -403,8 +406,8 @@
         return lax.ppermute(a, "dp", [(i, i ^ bit) for i in range(dp_size)])
 
     rows = gate_weight.shape[0]
-    cuts = [(flip, 0, rows) for flip in range(OUTER)]
-    sizes = [(size, 3 * main + 2 * LANES) for _, _, size in cuts]
+    cuts = list(range(OUTER))
+    sizes = [(rows, 3 * main + 2 * LANES)] * OUTER
     packed = pl.pallas_call(
         functools.partial(pack_kernel, main, tail, cuts),
         in_specs=[SMEM] + [HBM] * 3,
@@ -413,7 +416,7 @@
         scratch_shapes=[pltpu.VMEM(size, BF16) for size in sizes]
         + [
             pltpu.VMEM((3,) + gate_weight.shape, BF16),
-            pltpu.SemaphoreType.DMA((len(cuts),)),
+            pltpu.SemaphoreType.DMA((2 * OUTER,)),
             pltpu.SemaphoreType.DMA((6,)),
         ],
         compiler_params=params(60),
@@ -488,7 +491,7 @@
     count = residual_in.shape[0]
     ready = after(normed, arrived[3])
     here = {0: normed, 1: z_flip(ready, 1), 3: z_flip(ready, 3)}
-    here[2] = z_flip(after(ready, here[1]), 2)
+    here[2] = z_flip(ready, 2)
     there = {s: kv_flip(here[s], 2) for s in order}
     blocks[3] = shared(after(arrived[3], blocks[2][1], normed))
     near.append(laid((2, 3), 2 * deep, there[0], there[1], here[3]))

time: 118 us -> 118 us (level)
  no operation moved by 1% of the time
where the time goes in v6:
time: 118 us; the launch traced here: 117 us
  waiting for transfers between devices  50.7 us (43%)
  Pallas kernels  33.2 us (28%)
  starting transfers between devices  26.5 us (22%)
  local copies, waits for them, and re-layouts  5.67 us (5%)
    ppermute x14, waiting for transfers between devices, kv_flip(): return lax.ppermute(a, 'kv', [(i, i ^ bit) for i in range(kv_size)])  28.9 us
    ppermute x9, waiting for transfers between devices, z_flip(): return lax.ppermute(a, 'dp', [(i, i ^ by * inner) for i in range(dp_size)])  17.8 us
    pallas_call x1, Pallas kernels, attention(): pl.pallas_call(attention_kernel, in_specs=[SMEM, SMEM, HBM, HBM, HBM], ou...  13.9 us
    ppermute x14, starting transfers between devices, kv_flip(): return lax.ppermute(a, 'kv', [(i, i ^ bit) for i in range(kv_size)])  11.3 us
    ppermute x9, starting transfers between devices, z_flip(): return lax.ppermute(a, 'dp', [(i, i ^ by * inner) for i in range(dp_size)])  11.2 us
    pallas_call x4, Pallas kernels, feed(): pl.pallas_call(functools.partial(feed_kernel, main, tail, count, order),...  8.11 us
    unnamed x24, local copies, waits for them, and re-layouts  5.07 us
    ppermute x4, starting transfers between devices, y_flip(): return lax.ppermute(a, 'dp', [(i, i ^ bit) for i in range(dp_size)])  4.02 us
  transfers between devices with their start and end apart: 27, of which 15 were waited for; matrix products, arithmetic and copies ran while one was open for 1% of the time, Pallas kernels for 26%

profile of v6, /device:TPU:0, one launch (start us, length us, event | category | flops | bytes accessed | tf_op | source)
XLA Modules:
  0.0 117.2 jit_solution(13392778423677865329)
XLA Ops:
  0.0 2.9 %pack.1 = (bf16[192,1408]{1,0:T(8,128)(2,1)}, bf16[192,1408]{1,0:T(8,128)(2,1)}, bf16[192,1408]{1,0:T(8,128)(2,1)}, bf16[192,1408]{1,0:T(8,128)(2,1)}) custom-call(s32[1]{0:T(128)} %bitcast.2.z_ref, bf16[192,1728]{1,0:T(8,128)(2,1)} %gate_ref.1, bf16[192,1728]{1,0:T(8,128)(2,1)} %up_ref.1, bf16[192,1728]{1,0:T(8,128)(2,1)} %bitcast.5), custom_call_target="tpu_custom_call" | custom-call | tf_op jit(solution)/shard_map/pack/pallas_call | solution.py:411
  2.9 0.5 collective-permute-start.3
  3.5 3.7 %collective-permute-start = (bf16[192,1408]{1,0:T(8,128)(2,1)}, bf16[192,1408]{1,0:T(8,128)(2,1)S(1)}, u32[]{:S(2)}, u32[]{:S(2)}) collective-permute-start(bf16[192,1408]{1,0:T(8,128)(2,1)} %get-tuple-element.38), channel_id=1, source_target_pairs={{0,16},{4,20},{8,24},{12,28},{16,0},{20,4},{24,8},{28,12},{1,17},{... | collective-permute-start | bytes 1622024 | tf_op jit(solution)/shard_map/ppermute | solution.py:403
  7.1 1.5 %collective-permute-start.2 = (bf16[192,1408]{1,0:T(8,128)(2,1)}, bf16[192,1408]{1,0:T(8,128)(2,1)S(1)}, u32[]{:S(2)}, u32[]{:S(2)}) collective-permute-start(bf16[192,1408]{1,0:T(8,128)(2,1)} %get-tuple-element.40.refs_0_), channel_id=1, source_target_pairs={{0,4},{4,0},{8,12},{12,8},{16,20},{20,16},{24,28},{28,24},{1,5},{5... | collective-permute-start | bytes 1622024 | tf_op jit(solution)/shard_map/ppermute | solution.py:406
  8.6 1.6 %collective-permute-start.1 = (bf16[192,1408]{1,0:T(8,128)(2,1)}, bf16[192,1408]{1,0:T(8,128)(2,1)}, u32[]{:S(2)}, u32[]{:S(2)}) collective-permute-start(bf16[192,1408]{1,0:T(8,128)(2,1)} %get-tuple-element.39), channel_id=1, source_target_pairs={{0,8},{4,12},{8,0},{12,4},{16,24},{20,28},{24,16},{28,20},{1,9},{5... | collective-permute-start | bytes 1622024 | tf_op jit(solution)/shard_map/ppermute | solution.py:403
  10.2 13.9 %attention.1 = (bf16[128,1664]{1,0:T(8,128)(2,1)}, bf16[128,1664]{1,0:T(8,128)(2,1)}) custom-call(s32[1]{0:T(128)} %bitcast.at_ref, s32[3]{0:T(128)} %lengths_ref.1, bf16[256,1536]{1,0:T(8,128)(2,1)} %q_hbm.1, bf16[3,1024,512]{2,1,0:T(8,128)(2,1)} %k_hbm.1, bf16[3,1024,512]{2,1,0:T(8,128)(2,1)} %v_hbm.1), custom_call_target="tpu_custom_call" | custom-call | tf_op jit(solution)/shard_map/attention/pallas_call | solution.py:227
  24.1 0.0 copy-start.11
  24.2 0.1 collective-permute-start.4
  24.2 7.6 %collective-permute-done.refs_0_ = bf16[192,1408]{1,0:T(8,128)(2,1)S(1)} collective-permute-done((bf16[192,1408]{1,0:T(8,128)(2,1)}, bf16[192,1408]{1,0:T(8,128)(2,1)S(1)}, u32[]{:S(2)}, u32[]{:S(2)}) %collective-permute-start) | collective-permute-done | bytes 540704 | tf_op jit(solution)/shard_map/ppermute | solution.py:403
  31.9 3.6 %collective-permute-start.7 = (bf16[192,1408]{1,0:T(8,128)(2,1)}, bf16[192,1408]{1,0:T(8,128)(2,1)}, u32[]{:S(2)}, u32[]{:S(2)}) collective-permute-start(bf16[192,1408]{1,0:T(8,128)(2,1)} %get-tuple-element.53), channel_id=1, source_target_pairs={{0,24},{4,28},{8,16},{12,20},{16,8},{20,12},{24,0},{28,4},{1,25},{... | collective-permute-start | bytes 1622024 | tf_op jit(solution)/shard_map/ppermute | solution.py:403
  35.4 0.0 collective-permute-done.2.refs_1_
  35.5 0.8 copy-done.2
  36.2 0.0 collective-permute-done.1.refs_2_
  36.3 0.0 collective-permute-done.3.w1
  36.3 2.5 %join.1 = (bf16[128,896]{1,0:T(8,128)(2,1)}, bf16[128,896]{1,0:T(8,128)(2,1)}) custom-call(s32[1]{0:T(128)} %bitcast.1.at_ref, bf16[128,1664]{1,0:T(8,128)(2,1)} %get-tuple-element.45.own_ref, bf16[128,1664]{1,0:T(8,128)(2,1)} %collective-permute-done.4.other_ref), custom_call_target="tpu_custom_call" | custom-call | tf_op jit(solution)/shard_map/join/pallas_call | solution.py:445
  38.8 1.4 %collective-permute-start.14 = (bf16[192,1408]{1,0:T(8,128)(2,1)S(1)}, bf16[192,1408]{1,0:T(8,128)(2,1)S(1)}, u32[]{:S(2)}, u32[]{:S(2)}) collective-permute-start(bf16[192,1408]{1,0:T(8,128)(2,1)S(1)} %collective-permute-done.refs_0_), channel_id=1, source_target_pairs={{0,4},{4,0},{8,12},{12,8},{16,20},{20,16},{24,28},{28,24},{1,5},{5... | collective-permute-start | bytes 1622024 | tf_op jit(solution)/shard_map/ppermute | solution.py:406
  40.2 1.5 %collective-permute-start.5 = (bf16[128,896]{1,0:T(8,128)(2,1)}, bf16[128,896]{1,0:T(8,128)(2,1)S(1)}, u32[]{:S(2)}, u32[]{:S(2)}) collective-permute-start(bf16[128,896]{1,0:T(8,128)(2,1)} %get-tuple-element.48), channel_id=1, source_target_pairs={{0,2},{1,3},{2,0},{3,1},{4,6},{5,7},{6,4},{7,5},{8,10},{9,11},{10,... | collective-permute-start | bytes 688136 | tf_op jit(solution)/shard_map/ppermute | solution.py:400
  41.7 5.7 %collective-permute-done.5.other_ref = bf16[128,896]{1,0:T(8,128)(2,1)S(1)} collective-permute-done((bf16[128,896]{1,0:T(8,128)(2,1)}, bf16[128,896]{1,0:T(8,128)(2,1)S(1)}, u32[]{:S(2)}, u32[]{:S(2)}) %collective-permute-start.5) | collective-permute-done | bytes 229408 | tf_op jit(solution)/shard_map/ppermute | solution.py:400
  47.5 0.9 copy-done.7
  48.4 1.2 project.1
  49.6 0.8 copy-done.6
  50.4 1.5 %collective-permute-start.6 = (bf16[64,1536]{1,0:T(8,128)(2,1)S(1)}, bf16[64,1536]{1,0:T(8,128)(2,1)S(1)}, u32[]{:S(2)}, u32[]{:S(2)}) collective-permute-start(bf16[64,1536]{1,0:T(8,128)(2,1)S(1)} %get-tuple-element.50), channel_id=1, source_target_pairs={{0,2},{1,3},{2,0},{3,1},{4,6},{5,7},{6,4},{7,5},{8,10},{9,11},{10,... | collective-permute-start | bytes 589832 | tf_op jit(solution)/shard_map/ppermute | solution.py:400
  51.8 0.6 reshape.21.gain_ref
  52.4 0.5 collective-permute-start.10
  53.0 3.0 %collective-permute-done.6.other_ref = bf16[64,1536]{1,0:T(8,128)(2,1)S(1)} collective-permute-done((bf16[64,1536]{1,0:T(8,128)(2,1)S(1)}, bf16[64,1536]{1,0:T(8,128)(2,1)S(1)}, u32[]{:S(2)}, u32[]{:S(2)}) %collective-permute-start.6) | collective-permute-done | bytes 196640 | tf_op jit(solution)/shard_map/ppermute | solution.py:400
  56.0 0.7 copy-done.9
  56.7 2.0 %norm.1 = (bf16[64,1536]{1,0:T(8,128)(2,1)}, bf16[64,1536]{1,0:T(8,128)(2,1)}) custom-call(f32[64,1536]{1,0:T(8,128)} %copy-done.6, bf16[64,1536]{1,0:T(8,128)(2,1)} %copy-done.9, bf16[64,1536]{1,0:T(8,128)(2,1)} %residual_ref.1, f32[1,1536]{1,0:T(1,128)} %reshape.21.gain_ref), custom_call_target="tpu_custom_call" | custom-call | tf_op jit(solution)/shard_map/norm/pallas_call | solution.py:470
  58.7 0.8 copy-done.4
  59.6 0.5 collective-permute-start.15
  60.1 1.0 collective-permute-start.12
  61.1 1.2 %collective-permute-start.8 = (bf16[64,1536]{1,0:T(8,128)(2,1)}, bf16[64,1536]{1,0:T(8,128)(2,1)S(1)}, u32[]{:S(2)}, u32[]{:S(2)}) collective-permute-start(bf16[64,1536]{1,0:T(8,128)(2,1)} %get-tuple-element.54.refs_0_), channel_id=1, source_target_pairs={{0,24},{4,28},{8,16},{12,20},{16,8},{20,12},{24,0},{28,4},{1,25},{... | collective-permute-start | bytes 589832 | tf_op jit(solution)/shard_map/ppermute | solution.py:403
  62.3 1.5 %collective-permute-start.11 = (bf16[64,1536]{1,0:T(8,128)(2,1)}, bf16[64,1536]{1,0:T(8,128)(2,1)S(1)}, u32[]{:S(2)}, u32[]{:S(2)}) collective-permute-start(bf16[64,1536]{1,0:T(8,128)(2,1)} %get-tuple-element.54.refs_0_), channel_id=1, source_target_pairs={{0,2},{1,3},{2,0},{3,1},{4,6},{5,7},{6,4},{7,5},{8,10},{9,11},{10,... | collective-permute-start | bytes 589832 | tf_op jit(solution)/shard_map/ppermute | solution.py:400
  63.8 3.4 %collective-permute-done.12.refs_0_ = bf16[64,1536]{1,0:T(8,128)(2,1)S(1)} collective-permute-done((bf16[64,1536]{1,0:T(8,128)(2,1)}, bf16[64,1536]{1,0:T(8,128)(2,1)S(1)}, u32[]{:S(2)}, u32[]{:S(2)}) %collective-permute-start.12) | collective-permute-done | bytes 196640 | tf_op jit(solution)/shard_map/ppermute | solution.py:403
  67.2 1.5 %collective-permute-start.13 = (bf16[64,1536]{1,0:T(8,128)(2,1)S(1)}, bf16[64,1536]{1,0:T(8,128)(2,1)S(1)}, u32[]{:S(2)}, u32[]{:S(2)}) collective-permute-start(bf16[64,1536]{1,0:T(8,128)(2,1)S(1)} %collective-permute-done.12.refs_0_), channel_id=1, source_target_pairs={{0,2},{1,3},{2,0},{3,1},{4,6},{5,7},{6,4},{7,5},{8,10},{9,11},{10,... | collective-permute-start | bytes 589832 | tf_op jit(solution)/shard_map/ppermute | solution.py:400
  68.7 1.0 copy-done.3
  69.7 1.3 %place.2.refs_2_ = bf16[768,1408]{1,0:T(8,128)(2,1)S(1)} custom-call(s32[1]{0:T(128)} %bitcast.4.at_ref, bf16[192,1408]{1,0:T(8,128)(2,1)S(1)} %copy-done.1, bf16[192,1408]{1,0:T(8,128)(2,1)S(1)} %copy-done.3, bf16[192,1408]{1,0:T(8,128)(2,1)} %collective-permute-done.1.refs_2_, bf16[192,1408]{1,0:T(8,128)(2,1)S(1)} %collective-permute-done.10.refs_3_), custom_call_target="tpu_custom_call" | custom-call | tf_op jit(solution)/shard_map/place/pallas_call | solution.py:91
  71.0 0.1 collective-permute-start.16
  71.1 1.8 %collective-permute-done.13.refs_1_ = bf16[64,1536]{1,0:T(8,128)(2,1)S(1)} collective-permute-done((bf16[64,1536]{1,0:T(8,128)(2,1)S(1)}, bf16[64,1536]{1,0:T(8,128)(2,1)S(1)}, u32[]{:S(2)}, u32[]{:S(2)}) %collective-permute-start.13) | collective-permute-done | bytes 196640 | tf_op jit(solution)/shard_map/ppermute | solution.py:400
  72.9 4.0 %collective-permute-done.15.refs_3_ = bf16[192,1408]{1,0:T(8,128)(2,1)S(1)} collective-permute-done((bf16[192,1408]{1,0:T(8,128)(2,1)}, bf16[192,1408]{1,0:T(8,128)(2,1)S(1)}, u32[]{:S(2)}, u32[]{:S(2)}) %collective-permute-start.15) | collective-permute-done | bytes 540704 | tf_op jit(solution)/shard_map/ppermute | solution.py:406
  76.8 1.2 %place.3.refs_3_ = bf16[768,1408]{1,0:T(8,128)(2,1)S(1)} custom-call(s32[1]{0:T(128)} %bitcast.4.at_ref, bf16[192,1408]{1,0:T(8,128)(2,1)S(1)} %collective-permute-done.refs_0_, bf16[192,1408]{1,0:T(8,128)(2,1)S(1)} %copy-done.5, bf16[192,1408]{1,0:T(8,128)(2,1)} %collective-permute-done.7.refs_2_, bf16[192,1408]{1,0:T(8,128)(2,1)S(1)} %collective-permute-done.15.refs_3_), custom_call_target="tpu_custom_call" | custom-call | tf_op jit(solution)/shard_map/place/pallas_call | solution.py:91
  78.0 0.1 collective-permute-start.17
  78.1 0.6 collective-permute-start.9
  78.7 6.7 %collective-permute-done.9.refs_1_ = bf16[64,1536]{1,0:T(8,128)(2,1)S(1)} collective-permute-done((bf16[64,1536]{1,0:T(8,128)(2,1)S(1)}, bf16[64,1536]{1,0:T(8,128)(2,1)S(1)}, u32[]{:S(2)}, u32[]{:S(2)}) %collective-permute-start.9) | collective-permute-done | bytes 196640 | tf_op jit(solution)/shard_map/ppermute | solution.py:400
  85.4 2.0 %feed.4 = (bf16[64,1536]{1,0:T(8,128)(2,1)S(1)}, bf16[64,1536]{1,0:T(8,128)(2,1)S(1)}) custom-call(s32[1]{0:T(128)} %bitcast.2.z_ref, bf16[64,1536]{1,0:T(8,128)(2,1)S(1)} %collective-permute-done.8.refs_0_, bf16[64,1536]{1,0:T(8,128)(2,1)S(1)} %collective-permute-done.9.refs_1_, bf16[768,1408]{1,0:T(8,128)(2,1)S(1)} %place.2.refs_2_, ...), custom_call_target="tpu_custom_call" | custom-call | tf_op jit(solution)/shard_map/feed/pallas_call | solution.py:362
  87.5 0.6 collective-permute-start.18
  88.1 1.1 collective-permute-done.22.refs_0_
  89.2 0.6 collective-permute-start.23
  89.8 2.0 %feed.5 = (bf16[64,1536]{1,0:T(8,128)(2,1)S(1)}, bf16[64,1536]{1,0:T(8,128)(2,1)S(1)}) custom-call(s32[1]{0:T(128)} %bitcast.2.z_ref, bf16[64,1536]{1,0:T(8,128)(2,1)S(1)} %collective-permute-done.12.refs_0_, bf16[64,1536]{1,0:T(8,128)(2,1)S(1)} %collective-permute-done.13.refs_1_, bf16[768,1408]{1,0:T(8,128)(2,1)S(1)} %place.2.refs_2_, ...), custom_call_target="tpu_custom_call" | custom-call | tf_op jit(solution)/shard_map/feed/pallas_call | solution.py:362
  91.8 1.5 %collective-permute-start.20 = (bf16[64,1536]{1,0:T(8,128)(2,1)S(1)}, bf16[64,1536]{1,0:T(8,128)(2,1)S(1)}, u32[]{:S(2)}, u32[]{:S(2)}) collective-permute-start(bf16[64,1536]{1,0:T(8,128)(2,1)S(1)} %get-tuple-element.64), channel_id=1, source_target_pairs={{0,2},{1,3},{2,0},{3,1},{4,6},{5,7},{6,4},{7,5},{8,10},{9,11},{10,... | collective-permute-start | bytes 589832 | tf_op jit(solution)/shard_map/ppermute | solution.py:400
  93.3 2.0 %collective-permute-done.18 = bf16[64,1536]{1,0:T(8,128)(2,1)S(1)} collective-permute-done((bf16[64,1536]{1,0:T(8,128)(2,1)S(1)}, bf16[64,1536]{1,0:T(8,128)(2,1)S(1)}, u32[]{:S(2)}, u32[]{:S(2)}) %collective-permute-start.18) | collective-permute-done | bytes 196640 | tf_op jit(solution)/shard_map/ppermute | solution.py:400
  95.4 0.1 collective-permute-start.19
  95.5 4.1 %collective-permute-done.23.refs_1_ = bf16[64,1536]{1,0:T(8,128)(2,1)S(1)} collective-permute-done((bf16[64,1536]{1,0:T(8,128)(2,1)S(1)}, bf16[64,1536]{1,0:T(8,128)(2,1)S(1)}, u32[]{:S(2)}, u32[]{:S(2)}) %collective-permute-start.23) | collective-permute-done | bytes 196640 | tf_op jit(solution)/shard_map/ppermute | solution.py:400
  99.6 2.0 %feed.6 = (bf16[64,1536]{1,0:T(8,128)(2,1)S(1)}, bf16[64,1536]{1,0:T(8,128)(2,1)S(1)}) custom-call(s32[1]{0:T(128)} %bitcast.2.z_ref, bf16[64,1536]{1,0:T(8,128)(2,1)S(1)} %collective-permute-done.22.refs_0_, bf16[64,1536]{1,0:T(8,128)(2,1)S(1)} %collective-permute-done.23.refs_1_, bf16[768,1408]{1,0:T(8,128)(2,1)S(1)} %place.2.refs_2_, ...), custom_call_target="tpu_custom_call" | custom-call | tf_op jit(solution)/shard_map/feed/pallas_call | solution.py:362
  101.6 0.6 collective-permute-start.24
  102.2 0.9 collective-permute-done.20
  103.2 0.1 collective-permute-start.21
  103.3 2.0 %feed.7 = (bf16[64,1536]{1,0:T(8,128)(2,1)S(1)}, bf16[64,1536]{1,0:T(8,128)(2,1)S(1)}) custom-call(s32[1]{0:T(128)} %bitcast.2.z_ref, bf16[64,1536]{1,0:T(8,128)(2,1)S(1)} %copy-done.8, bf16[64,1536]{1,0:T(8,128)(2,1)S(1)} %collective-permute-done.11.refs_1_, bf16[768,1408]{1,0:T(8,128)(2,1)S(1)} %place.2.refs_2_, bf16[768,1408]{1,0:T(8,128)(2,1)S(1)} %place.3.refs_3_, ...), custom_call_target="tpu_custom_call" | custom-call | tf_op jit(solution)/shard_map/feed/pallas_call | solution.py:362
  105.3 0.6 collective-permute-start.26
  105.9 2.7 %collective-permute-done.24 = bf16[64,1536]{1,0:T(8,128)(2,1)S(1)} collective-permute-done((bf16[64,1536]{1,0:T(8,128)(2,1)S(1)}, bf16[64,1536]{1,0:T(8,128)(2,1)S(1)}, u32[]{:S(2)}, u32[]{:S(2)}) %collective-permute-start.24) | collective-permute-done | bytes 196640 | tf_op jit(solution)/shard_map/ppermute | solution.py:400
  108.7 0.1 collective-permute-start.25
  108.8 0.8 collective-permute-done.21
  109.6 2.0 %collective-permute-done.26 = bf16[64,1536]{1,0:T(8,128)(2,1)S(1)} collective-permute-done((bf16[64,1536]{1,0:T(8,128)(2,1)S(1)}, bf16[64,1536]{1,0:T(8,128)(2,1)S(1)}, u32[]{:S(2)}, u32[]{:S(2)}) %collective-permute-start.26) | collective-permute-done | bytes 196640 | tf_op jit(solution)/shard_map/ppermute | solution.py:400
  111.5 4.9 %collective-permute-done.25 = bf16[64,1536]{1,0:T(8,128)(2,1)S(1)} collective-permute-done((bf16[64,1536]{1,0:T(8,128)(2,1)S(1)}, bf16[64,1536]{1,0:T(8,128)(2,1)S(1)}, u32[]{:S(2)}, u32[]{:S(2)}) %collective-permute-start.25) | collective-permute-done | bytes 196640 | tf_op jit(solution)/shard_map/ppermute | solution.py:403
  116.4 0.8 add_convert_fusion
  (30 shorter events, 0.2 us)
Async XLA Ops:
  2.9 33.3 %collective-permute-start.3 = (bf16[384,1536]{1,0:T(8,128)(2,1)}, bf16[384,1536]{1,0:T(8,128)(2,1)S(1)}, u32[]{:S(2)}, u32[]{:S(2)}) collective-permute-start(bf16[384,1536]{1,0:T(8,128)(2,1)} %w0.1), channel_id=1, source_target_pairs={{0,1},{1,0},{2,3},{3,2},{4,5},{5,4},{6,7},{7,6},{8,9},{9,8},{10,11... | collective-permute-start | bytes 3538952 | tf_op jit(solution)/shard_map/ppermute | solution.py:400
  3.5 28.4 %collective-permute-start = (bf16[192,1408]{1,0:T(8,128)(2,1)}, bf16[192,1408]{1,0:T(8,128)(2,1)S(1)}, u32[]{:S(2)}, u32[]{:S(2)}) collective-permute-start(bf16[192,1408]{1,0:T(8,128)(2,1)} %get-tuple-element.38), channel_id=1, source_target_pairs={{0,16},{4,20},{8,24},{12,28},{16,0},{20,4},{24,8},{28,12},{1,17},{... | collective-permute-start | bytes 1622024 | tf_op jit(solution)/shard_map/ppermute | solution.py:403
  7.1 28.3 %collective-permute-start.2 = (bf16[192,1408]{1,0:T(8,128)(2,1)}, bf16[192,1408]{1,0:T(8,128)(2,1)S(1)}, u32[]{:S(2)}, u32[]{:S(2)}) collective-permute-start(bf16[192,1408]{1,0:T(8,128)(2,1)} %get-tuple-element.40.refs_0_), channel_id=1, source_target_pairs={{0,4},{4,0},{8,12},{12,8},{16,20},{20,16},{24,28},{28,24},{1,5},{5... | collective-permute-start | bytes 1622024 | tf_op jit(solution)/shard_map/ppermute | solution.py:406
  8.6 27.6 %collective-permute-start.1 = (bf16[192,1408]{1,0:T(8,128)(2,1)}, bf16[192,1408]{1,0:T(8,128)(2,1)}, u32[]{:S(2)}, u32[]{:S(2)}) collective-permute-start(bf16[192,1408]{1,0:T(8,128)(2,1)} %get-tuple-element.39), channel_id=1, source_target_pairs={{0,8},{4,12},{8,0},{12,4},{16,24},{20,28},{24,16},{28,20},{1,9},{5... | collective-permute-start | bytes 1622024 | tf_op jit(solution)/shard_map/ppermute | solution.py:403
  10.2 37.2 %copy-start = (bf16[384,1536]{1,0:T(8,128)(2,1)S(1)}, bf16[384,1536]{1,0:T(8,128)(2,1)}, u32[]{:S(2)}) copy-start(bf16[384,1536]{1,0:T(8,128)(2,1)} %w0.1) | copy-start | bytes 3538948
  24.1 27.7 %copy-start.11 = (f32[1536]{0:T(1024)S(1)}, f32[1536]{0:T(1024)}, u32[]{:S(2)}) copy-start(f32[1536]{0:T(1024)} %param.16) | copy-start | bytes 18436
  24.2 12.1 %collective-permute-start.4 = (bf16[128,1664]{1,0:T(8,128)(2,1)}, bf16[128,1664]{1,0:T(8,128)(2,1)}, u32[]{:S(2)}, u32[]{:S(2)}) collective-permute-start(bf16[128,1664]{1,0:T(8,128)(2,1)} %get-tuple-element.46), channel_id=1, source_target_pairs={{0,1},{1,0},{2,3},{3,2},{4,5},{5,4},{6,7},{7,6},{8,9},{9,8},{10,11... | collective-permute-start | bytes 1277960 | tf_op jit(solution)/shard_map/ppermute | solution.py:400
  31.9 26.8 %collective-permute-start.7 = (bf16[192,1408]{1,0:T(8,128)(2,1)}, bf16[192,1408]{1,0:T(8,128)(2,1)}, u32[]{:S(2)}, u32[]{:S(2)}) collective-permute-start(bf16[192,1408]{1,0:T(8,128)(2,1)} %get-tuple-element.53), channel_id=1, source_target_pairs={{0,24},{4,28},{8,16},{12,20},{16,8},{20,12},{24,0},{28,4},{1,25},{... | collective-permute-start | bytes 1622024 | tf_op jit(solution)/shard_map/ppermute | solution.py:403
  35.4 0.8 copy-start.2
  36.3 32.4 %copy-start.1 = (bf16[192,1408]{1,0:T(8,128)(2,1)S(1)}, bf16[192,1408]{1,0:T(8,128)(2,1)}, u32[]{:S(2)}) copy-start(bf16[192,1408]{1,0:T(8,128)(2,1)} %get-tuple-element.40.refs_0_) | copy-start | bytes 1622020
  38.8 19.9 %collective-permute-start.14 = (bf16[192,1408]{1,0:T(8,128)(2,1)S(1)}, bf16[192,1408]{1,0:T(8,128)(2,1)S(1)}, u32[]{:S(2)}, u32[]{:S(2)}) collective-permute-start(bf16[192,1408]{1,0:T(8,128)(2,1)S(1)} %collective-permute-done.refs_0_), channel_id=1, source_target_pairs={{0,4},{4,0},{8,12},{12,8},{16,20},{20,16},{24,28},{28,24},{1,5},{5... | collective-permute-start | bytes 1622024 | tf_op jit(solution)/shard_map/ppermute | solution.py:406
  40.2 7.2 %collective-permute-start.5 = (bf16[128,896]{1,0:T(8,128)(2,1)}, bf16[128,896]{1,0:T(8,128)(2,1)S(1)}, u32[]{:S(2)}, u32[]{:S(2)}) collective-permute-start(bf16[128,896]{1,0:T(8,128)(2,1)} %get-tuple-element.48), channel_id=1, source_target_pairs={{0,2},{1,3},{2,0},{3,1},{4,6},{5,7},{6,4},{7,5},{8,10},{9,11},{10,... | collective-permute-start | bytes 688136 | tf_op jit(solution)/shard_map/ppermute | solution.py:400
  47.5 0.9 copy-start.7
  49.6 0.8 copy-start.6
  50.4 5.7 %collective-permute-start.6 = (bf16[64,1536]{1,0:T(8,128)(2,1)S(1)}, bf16[64,1536]{1,0:T(8,128)(2,1)S(1)}, u32[]{:S(2)}, u32[]{:S(2)}) collective-permute-start(bf16[64,1536]{1,0:T(8,128)(2,1)S(1)} %get-tuple-element.50), channel_id=1, source_target_pairs={{0,2},{1,3},{2,0},{3,1},{4,6},{5,7},{6,4},{7,5},{8,10},{9,11},{10,... | collective-permute-start | bytes 589832 | tf_op jit(solution)/shard_map/ppermute | solution.py:400
  52.4 16.2 %collective-permute-start.10 = (bf16[192,1408]{1,0:T(8,128)(2,1)}, bf16[192,1408]{1,0:T(8,128)(2,1)S(1)}, u32[]{:S(2)}, u32[]{:S(2)}) collective-permute-start(bf16[192,1408]{1,0:T(8,128)(2,1)} %collective-permute-done.1.refs_2_), channel_id=1, source_target_pairs={{0,4},{4,0},{8,12},{12,8},{16,20},{20,16},{24,28},{28,24},{1,5},{5... | collective-permute-start | bytes 1622024 | tf_op jit(solution)/shard_map/ppermute | solution.py:406
  56.0 0.7 copy-start.9
  58.7 0.8 copy-start.4
  59.6 17.3 %collective-permute-start.15 = (bf16[192,1408]{1,0:T(8,128)(2,1)}, bf16[192,1408]{1,0:T(8,128)(2,1)S(1)}, u32[]{:S(2)}, u32[]{:S(2)}) collective-permute-start(bf16[192,1408]{1,0:T(8,128)(2,1)} %collective-permute-done.7.refs_2_), channel_id=1, source_target_pairs={{0,4},{4,0},{8,12},{12,8},{16,20},{20,16},{24,28},{28,24},{1,5},{5... | collective-permute-start | bytes 1622024 | tf_op jit(solution)/shard_map/ppermute | solution.py:406
  60.1 7.1 %collective-permute-start.12 = (bf16[64,1536]{1,0:T(8,128)(2,1)}, bf16[64,1536]{1,0:T(8,128)(2,1)S(1)}, u32[]{:S(2)}, u32[]{:S(2)}) collective-permute-start(bf16[64,1536]{1,0:T(8,128)(2,1)} %get-tuple-element.54.refs_0_), channel_id=1, source_target_pairs={{0,8},{4,12},{8,0},{12,4},{16,24},{20,28},{24,16},{28,20},{1,9},{5... | collective-permute-start | bytes 589832 | tf_op jit(solution)/shard_map/ppermute | solution.py:403
  61.1 10.0 %collective-permute-start.8 = (bf16[64,1536]{1,0:T(8,128)(2,1)}, bf16[64,1536]{1,0:T(8,128)(2,1)S(1)}, u32[]{:S(2)}, u32[]{:S(2)}) collective-permute-start(bf16[64,1536]{1,0:T(8,128)(2,1)} %get-tuple-element.54.refs_0_), channel_id=1, source_target_pairs={{0,24},{4,28},{8,16},{12,20},{16,8},{20,12},{24,0},{28,4},{1,25},{... | collective-permute-start | bytes 589832 | tf_op jit(solution)/shard_map/ppermute | solution.py:403
  62.3 8.8 %collective-permute-start.11 = (bf16[64,1536]{1,0:T(8,128)(2,1)}, bf16[64,1536]{1,0:T(8,128)(2,1)S(1)}, u32[]{:S(2)}, u32[]{:S(2)}) collective-permute-start(bf16[64,1536]{1,0:T(8,128)(2,1)} %get-tuple-element.54.refs_0_), channel_id=1, source_target_pairs={{0,2},{1,3},{2,0},{3,1},{4,6},{5,7},{6,4},{7,5},{8,10},{9,11},{10,... | collective-permute-start | bytes 589832 | tf_op jit(solution)/shard_map/ppermute | solution.py:400
  67.2 5.7 %collective-permute-start.13 = (bf16[64,1536]{1,0:T(8,128)(2,1)S(1)}, bf16[64,1536]{1,0:T(8,128)(2,1)S(1)}, u32[]{:S(2)}, u32[]{:S(2)}) collective-permute-start(bf16[64,1536]{1,0:T(8,128)(2,1)S(1)} %collective-permute-done.12.refs_0_), channel_id=1, source_target_pairs={{0,2},{1,3},{2,0},{3,1},{4,6},{5,7},{6,4},{7,5},{8,10},{9,11},{10,... | collective-permute-start | bytes 589832 | tf_op jit(solution)/shard_map/ppermute | solution.py:400
  68.7 1.0 copy-start.3
  69.7 7.1 %copy-start.5 = (bf16[192,1408]{1,0:T(8,128)(2,1)S(1)}, bf16[192,1408]{1,0:T(8,128)(2,1)}, u32[]{:S(2)}) copy-start(bf16[192,1408]{1,0:T(8,128)(2,1)} %copy-done.4) | copy-start | bytes 1622020
  71.0 7.8 %copy-start.8 = (bf16[64,1536]{1,0:T(8,128)(2,1)S(1)}, bf16[64,1536]{1,0:T(8,128)(2,1)}, u32[]{:S(2)}) copy-start(bf16[64,1536]{1,0:T(8,128)(2,1)} %get-tuple-element.54.refs_0_) | copy-start | bytes 589828
  71.0 14.4 %collective-permute-start.16 = (bf16[768,1408]{1,0:T(8,128)(2,1)S(1)}, bf16[768,1408]{1,0:T(8,128)(2,1)S(1)}, u32[]{:S(2)}, u32[]{:S(2)}) collective-permute-start(bf16[768,1408]{1,0:T(8,128)(2,1)S(1)} %place.2.refs_2_), channel_id=1, source_target_pairs={{0,1},{1,0},{2,3},{3,2},{4,5},{5,4},{6,7},{7,6},{8,9},{9,8},{10,11... | collective-permute-start | bytes 6488072 | tf_op jit(solution)/shard_map/ppermute | solution.py:400
  78.0 7.4 %collective-permute-start.17 = (bf16[768,1408]{1,0:T(8,128)(2,1)S(1)}, bf16[768,1408]{1,0:T(8,128)(2,1)S(1)}, u32[]{:S(2)}, u32[]{:S(2)}) collective-permute-start(bf16[768,1408]{1,0:T(8,128)(2,1)S(1)} %place.3.refs_3_), channel_id=1, source_target_pairs={{0,1},{1,0},{2,3},{3,2},{4,5},{5,4},{6,7},{7,6},{8,9},{9,8},{10,11... | collective-permute-start | bytes 6488072 | tf_op jit(solution)/shard_map/ppermute | solution.py:400
  78.1 7.3 %collective-permute-start.9 = (bf16[64,1536]{1,0:T(8,128)(2,1)S(1)}, bf16[64,1536]{1,0:T(8,128)(2,1)S(1)}, u32[]{:S(2)}, u32[]{:S(2)}) collective-permute-start(bf16[64,1536]{1,0:T(8,128)(2,1)S(1)} %collective-permute-done.8.refs_0_), channel_id=1, source_target_pairs={{0,2},{1,3},{2,0},{3,1},{4,6},{5,7},{6,4},{7,5},{8,10},{9,11},{10,... | collective-permute-start | bytes 589832 | tf_op jit(solution)/shard_map/ppermute | solution.py:400
  78.7 10.5 %collective-permute-start.22 = (bf16[64,1536]{1,0:T(8,128)(2,1)S(1)}, bf16[64,1536]{1,0:T(8,128)(2,1)S(1)}, u32[]{:S(2)}, u32[]{:S(2)}) collective-permute-start(bf16[64,1536]{1,0:T(8,128)(2,1)S(1)} %copy-done.8), channel_id=1, source_target_pairs={{0,16},{4,20},{8,24},{12,28},{16,0},{20,4},{24,8},{28,12},{1,17},{... | collective-permute-start | bytes 589832 | tf_op jit(solution)/shard_map/ppermute | solution.py:403
  87.5 7.9 %collective-permute-start.18 = (bf16[64,1536]{1,0:T(8,128)(2,1)S(1)}, bf16[64,1536]{1,0:T(8,128)(2,1)S(1)}, u32[]{:S(2)}, u32[]{:S(2)}) collective-permute-start(bf16[64,1536]{1,0:T(8,128)(2,1)S(1)} %get-tuple-element.61), channel_id=1, source_target_pairs={{0,2},{1,3},{2,0},{3,1},{4,6},{5,7},{6,4},{7,5},{8,10},{9,11},{10,... | collective-permute-start | bytes 589832 | tf_op jit(solution)/shard_map/ppermute | solution.py:400
  89.2 10.4 %collective-permute-start.23 = (bf16[64,1536]{1,0:T(8,128)(2,1)S(1)}, bf16[64,1536]{1,0:T(8,128)(2,1)S(1)}, u32[]{:S(2)}, u32[]{:S(2)}) collective-permute-start(bf16[64,1536]{1,0:T(8,128)(2,1)S(1)} %collective-permute-done.22.refs_0_), channel_id=1, source_target_pairs={{0,2},{1,3},{2,0},{3,1},{4,6},{5,7},{6,4},{7,5},{8,10},{9,11},{10,... | collective-permute-start | bytes 589832 | tf_op jit(solution)/shard_map/ppermute | solution.py:400
  91.8 11.3 %collective-permute-start.20 = (bf16[64,1536]{1,0:T(8,128)(2,1)S(1)}, bf16[64,1536]{1,0:T(8,128)(2,1)S(1)}, u32[]{:S(2)}, u32[]{:S(2)}) collective-permute-start(bf16[64,1536]{1,0:T(8,128)(2,1)S(1)} %get-tuple-element.64), channel_id=1, source_target_pairs={{0,2},{1,3},{2,0},{3,1},{4,6},{5,7},{6,4},{7,5},{8,10},{9,11},{10,... | collective-permute-start | bytes 589832 | tf_op jit(solution)/shard_map/ppermute | solution.py:400
  95.4 7.9 %collective-permute-start.19 = (bf16[64,1536]{1,0:T(8,128)(2,1)S(1)}, bf16[64,1536]{1,0:T(8,128)(2,1)S(1)}, u32[]{:S(2)}, u32[]{:S(2)}) collective-permute-start(bf16[64,1536]{1,0:T(8,128)(2,1)S(1)} %add_convert_fusion.4), channel_id=1, source_target_pairs={{0,24},{4,28},{8,16},{12,20},{16,8},{20,12},{24,0},{28,4},{1,25},{... | collective-permute-start | bytes 589832 | tf_op jit(solution)/shard_map/ppermute | solution.py:403
  101.6 7.0 %collective-permute-start.24 = (bf16[64,1536]{1,0:T(8,128)(2,1)S(1)}, bf16[64,1536]{1,0:T(8,128)(2,1)S(1)}, u32[]{:S(2)}, u32[]{:S(2)}) collective-permute-start(bf16[64,1536]{1,0:T(8,128)(2,1)S(1)} %get-tuple-element.67), channel_id=1, source_target_pairs={{0,2},{1,3},{2,0},{3,1},{4,6},{5,7},{6,4},{7,5},{8,10},{9,11},{10,... | collective-permute-start | bytes 589832 | tf_op jit(solution)/shard_map/ppermute | solution.py:400
  103.2 6.4 %collective-permute-start.21 = (bf16[64,1536]{1,0:T(8,128)(2,1)S(1)}, bf16[64,1536]{1,0:T(8,128)(2,1)S(1)}, u32[]{:S(2)}, u32[]{:S(2)}) collective-permute-start(bf16[64,1536]{1,0:T(8,128)(2,1)S(1)} %add_convert_fusion.3), channel_id=1, source_target_pairs={{0,8},{4,12},{8,0},{12,4},{16,24},{20,28},{24,16},{28,20},{1,9},{5... | collective-permute-start | bytes 589832 | tf_op jit(solution)/shard_map/ppermute | solution.py:403
  103.3 13.1 %copy-start.10 = (bf16[64,1536]{1,0:T(8,128)(2,1)S(1)}, bf16[64,1536]{1,0:T(8,128)(2,1)}, u32[]{:S(2)}) copy-start(bf16[64,1536]{1,0:T(8,128)(2,1)} %get-tuple-element.51) | copy-start | bytes 589828
  105.3 6.2 %collective-permute-start.26 = (bf16[64,1536]{1,0:T(8,128)(2,1)S(1)}, bf16[64,1536]{1,0:T(8,128)(2,1)S(1)}, u32[]{:S(2)}, u32[]{:S(2)}) collective-permute-start(bf16[64,1536]{1,0:T(8,128)(2,1)S(1)} %get-tuple-element.70), channel_id=1, source_target_pairs={{0,2},{1,3},{2,0},{3,1},{4,6},{5,7},{6,4},{7,5},{8,10},{9,11},{10,... | collective-permute-start | bytes 589832 | tf_op jit(solution)/shard_map/ppermute | solution.py:400
  108.7 7.7 %collective-permute-start.25 = (bf16[64,1536]{1,0:T(8,128)(2,1)S(1)}, bf16[64,1536]{1,0:T(8,128)(2,1)S(1)}, u32[]{:S(2)}, u32[]{:S(2)}) collective-permute-start(bf16[64,1536]{1,0:T(8,128)(2,1)S(1)} %add_convert_fusion.2), channel_id=1, source_target_pairs={{0,16},{4,20},{8,24},{12,28},{16,0},{20,4},{24,8},{28,12},{1,17},{... | collective-permute-start | bytes 589832 | tf_op jit(solution)/shard_map/ppermute | solution.py:403

commit v7 on v6

--- a/solution.py
+++ b/solution.py
@@ -13,6 +13,7 @@
 LANES = 128
 SUM_HIGH = 32
 SUM_LOW = 64
+TOP_LOW = 96
 OUTER = 4
 
 VMEM = pl.BlockSpec(memory_space=pltpu.VMEM)
@@ -33,6 +34,15 @@
 
 def dot(a, b):
     return jnp.dot(a, b, preferred_element_type=F32)
+
+
+def rounded(value):
+    return value.astype(BF16).astype(F32)
+
+
+def two_part(value):
+    high = rounded(value)
+    return high + rounded(value - high)
 
 
 def one_hot(condition):
@@ -135,7 +145,9 @@
 
     def record(old, column, top, total):
         high = total.astype(BF16).astype(F32)
-        old = jnp.where(lane == column, top, old)
+        top_high = rounded(top)
+        old = jnp.where(lane == column, top_high, old)
+        old = jnp.where(lane == column + TOP_LOW, top - top_high, old)
         old = jnp.where(lane == column + SUM_HIGH, high, old)
         return jnp.where(lane == column + SUM_LOW, total - high, old)
 
@@ -165,7 +177,7 @@
             query = jnp.concatenate(queries[a * group : (a + 1) * group], 0).astype(BF16)
             scores = lax.dot_general(keys, query, NT, preferred_element_type=F32)
             scores = scores + jnp.concatenate([bias[...]] * group, 1)
-            top = jnp.maximum(jnp.max(scores, axis=0, keepdims=True), -1e29).astype(BF16).astype(F32)
+            top = two_part(jnp.maximum(jnp.max(scores, axis=0, keepdims=True), -1e29))
             weights = jnp.exp((scores - top).astype(BF16))
             values = jnp.where(in_half(a), value, jnp.ones((), BF16)).astype(F32).T.astype(BF16)
             out = dot(values, weights).T
@@ -194,12 +206,14 @@
         scores = lax.dot_general(lines[r - 1].astype(BF16), k_ref[r], NT, preferred_element_type=F32)
         usable = first_key + iota((1, slab), 1) < lengths_ref[r]
         scores = jnp.where(usable, scores, -1e30)
-        top = jnp.maximum(jnp.max(scores, axis=1, keepdims=True), -1e29).astype(BF16).astype(F32)
+        top = two_part(jnp.maximum(jnp.max(scores, axis=1, keepdims=True), -1e29))
         weights = jnp.exp(scores - top)
         total = jnp.sum(weights, axis=1, keepdims=True)
         out = dot(weights.astype(BF16), v_ref[r])
         high = total.astype(BF16).astype(F32)
-        stat = jnp.where(live & (column == spot), top, 0.0)
+        top_high = rounded(top)
+        stat = jnp.where(live & (column == spot), top_high, 0.0)
+        stat = stat + jnp.where(live & (column == spot + TOP_LOW), top - top_high, 0.0)
         stat = stat + jnp.where(live & (column == spot + SUM_HIGH), high, 0.0)
         stat = stat + jnp.where(live & (column == spot + SUM_LOW), total - high, 0.0)
         stats[row : row + 1, :] = jnp.sum(stat, axis=0, keepdims=True)
@@ -256,8 +270,9 @@
 def merged(parts, width):
     tiles = [part[:, width:].astype(F32) for part in parts]
     valid = iota((1, LANES), 1) < width // HD
-    top = functools.reduce(jnp.maximum, tiles)
-    scales = [jnp.where(valid, jnp.exp(tile - top), 0.0) for tile in tiles]
+    tops = [tile + pltpu.roll(tile, LANES - TOP_LOW, 1) for tile in tiles]
+    top = functools.reduce(jnp.maximum, tops)
+    scales = [jnp.where(valid, jnp.exp(one - top), 0.0) for one in tops]
     sums = [pltpu.roll(tile, LANES - SUM_HIGH, 1) + pltpu.roll(tile, LANES - SUM_LOW, 1) for tile in tiles]
     total = functools.reduce(jnp.add, [a * b for a, b in zip(sums, scales)])
     return top, total, scales, valid
@@ -283,7 +298,10 @@
         ref[:, :part_width] = weighted([own_ref[:, pick], other_ref[:, pick]], [here(scale) for scale in scales], part_width)
         sums = here(total)
         high = sums.astype(BF16).astype(F32)
-        stat = here(top) + pltpu.roll(high, SUM_HIGH, 1) + pltpu.roll(sums - high, SUM_LOW, 1)
+        own_top = here(top)
+        top_high = rounded(own_top)
+        stat = top_high + pltpu.roll(own_top - top_high, TOP_LOW, 1)
+        stat = stat + pltpu.roll(high, SUM_HIGH, 1) + pltpu.roll(sums - high, SUM_LOW, 1)
         ref[:, part_width:] = stat.astype(BF16)
 
 

time: 118 us -> 118 us (level)
  waiting for transfers between devices: 50.7 us -> 48.3 us
  Pallas kernels: 33.2 us -> 34.7 us
    ppermute x9, waiting for transfers between devices: 17.8 us -> 16.1 us  [z_flip(): return lax.ppermute(a, 'dp', [(i, i ^ by * inner) for i in range(dp_size)])]
    pallas_call x1, Pallas kernels: 13.9 us -> 15.5 us  [attention(): pl.pallas_call(attention_kernel, in_specs=[SMEM, SMEM, HBM, HBM, HBM], ou...]
  transfers between devices with their start and end apart: 27 -> 27, of which waited for: 15 -> 15; matrix products, arithmetic and copies ran while one was open for 1% -> 1% of each run, Pallas kernels for 26% -> 27%
where the time goes in v7:
time: 118 us; the launch traced here: 117 us
  waiting for transfers between devices  48.3 us (41%)
  Pallas kernels  34.7 us (29%)
  starting transfers between devices  27.3 us (23%)
  local copies, waits for them, and re-layouts  5.67 us (5%)
    ppermute x14, waiting for transfers between devices, kv_flip(): return lax.ppermute(a, 'kv', [(i, i ^ bit) for i in range(kv_size)])  28.1 us
    ppermute x9, waiting for transfers between devices, z_flip(): return lax.ppermute(a, 'dp', [(i, i ^ by * inner) for i in range(dp_size)])  16.1 us
    pallas_call x1, Pallas kernels, attention(): pl.pallas_call(attention_kernel, in_specs=[SMEM, SMEM, HBM, HBM, HBM], ou...  15.5 us
    ppermute x14, starting transfers between devices, kv_flip(): return lax.ppermute(a, 'kv', [(i, i ^ bit) for i in range(kv_size)])  12 us
    ppermute x9, starting transfers between devices, z_flip(): return lax.ppermute(a, 'dp', [(i, i ^ by * inner) for i in range(dp_size)])  11.3 us
    pallas_call x4, Pallas kernels, feed(): pl.pallas_call(functools.partial(feed_kernel, main, tail, count, order),...  8.11 us
    unnamed x24, local copies, waits for them, and re-layouts  5.07 us
    ppermute x4, starting transfers between devices, y_flip(): return lax.ppermute(a, 'dp', [(i, i ^ bit) for i in range(dp_size)])  4.06 us
  transfers between devices with their start and end apart: 27, of which 15 were waited for; matrix products, arithmetic and copies ran while one was open for 1% of the time, Pallas kernels for 27%

profile of v7, /device:TPU:0, one launch (start us, length us, event | category | flops | bytes accessed | tf_op | source)
XLA Modules:
  0.0 117.2 jit_solution(2957996873611213311)
XLA Ops:
  0.0 2.9 %pack.1 = (bf16[192,1408]{1,0:T(8,128)(2,1)}, bf16[192,1408]{1,0:T(8,128)(2,1)}, bf16[192,1408]{1,0:T(8,128)(2,1)}, bf16[192,1408]{1,0:T(8,128)(2,1)}) custom-call(s32[1]{0:T(128)} %bitcast.2.z_ref, bf16[192,1728]{1,0:T(8,128)(2,1)} %gate_ref.1, bf16[192,1728]{1,0:T(8,128)(2,1)} %up_ref.1, bf16[192,1728]{1,0:T(8,128)(2,1)} %bitcast.5), custom_call_target="tpu_custom_call" | custom-call | tf_op jit(solution)/shard_map/pack/pallas_call | solution.py:429
  2.9 0.5 collective-permute-start.3
  3.5 3.7 %collective-permute-start = (bf16[192,1408]{1,0:T(8,128)(2,1)}, bf16[192,1408]{1,0:T(8,128)(2,1)S(1)}, u32[]{:S(2)}, u32[]{:S(2)}) collective-permute-start(bf16[192,1408]{1,0:T(8,128)(2,1)} %get-tuple-element.38), channel_id=1, source_target_pairs={{0,16},{4,20},{8,24},{12,28},{16,0},{20,4},{24,8},{28,12},{1,17},{... | collective-permute-start | bytes 1622024 | tf_op jit(solution)/shard_map/ppermute | solution.py:421
  7.1 1.5 %collective-permute-start.2 = (bf16[192,1408]{1,0:T(8,128)(2,1)}, bf16[192,1408]{1,0:T(8,128)(2,1)S(1)}, u32[]{:S(2)}, u32[]{:S(2)}) collective-permute-start(bf16[192,1408]{1,0:T(8,128)(2,1)} %get-tuple-element.40.refs_0_), channel_id=1, source_target_pairs={{0,4},{4,0},{8,12},{12,8},{16,20},{20,16},{24,28},{28,24},{1,5},{5... | collective-permute-start | bytes 1622024 | tf_op jit(solution)/shard_map/ppermute | solution.py:424
  8.6 1.6 %collective-permute-start.1 = (bf16[192,1408]{1,0:T(8,128)(2,1)}, bf16[192,1408]{1,0:T(8,128)(2,1)}, u32[]{:S(2)}, u32[]{:S(2)}) collective-permute-start(bf16[192,1408]{1,0:T(8,128)(2,1)} %get-tuple-element.39), channel_id=1, source_target_pairs={{0,8},{4,12},{8,0},{12,4},{16,24},{20,28},{24,16},{28,20},{1,9},{5... | collective-permute-start | bytes 1622024 | tf_op jit(solution)/shard_map/ppermute | solution.py:421
  10.2 15.5 %attention.1 = (bf16[128,1664]{1,0:T(8,128)(2,1)}, bf16[128,1664]{1,0:T(8,128)(2,1)}) custom-call(s32[1]{0:T(128)} %bitcast.at_ref, s32[3]{0:T(128)} %lengths_ref.1, bf16[256,1536]{1,0:T(8,128)(2,1)} %q_hbm.1, bf16[3,1024,512]{2,1,0:T(8,128)(2,1)} %k_hbm.1, bf16[3,1024,512]{2,1,0:T(8,128)(2,1)} %v_hbm.1), custom_call_target="tpu_custom_call" | custom-call | tf_op jit(solution)/shard_map/attention/pallas_call | solution.py:241
  25.7 0.0 copy-start.11
  25.8 0.1 collective-permute-start.4
  25.8 6.0 %collective-permute-done.refs_0_ = bf16[192,1408]{1,0:T(8,128)(2,1)S(1)} collective-permute-done((bf16[192,1408]{1,0:T(8,128)(2,1)}, bf16[192,1408]{1,0:T(8,128)(2,1)S(1)}, u32[]{:S(2)}, u32[]{:S(2)}) %collective-permute-start) | collective-permute-done | bytes 540704 | tf_op jit(solution)/shard_map/ppermute | solution.py:421
  31.9 3.6 %collective-permute-start.7 = (bf16[192,1408]{1,0:T(8,128)(2,1)}, bf16[192,1408]{1,0:T(8,128)(2,1)}, u32[]{:S(2)}, u32[]{:S(2)}) collective-permute-start(bf16[192,1408]{1,0:T(8,128)(2,1)} %get-tuple-element.53), channel_id=1, source_target_pairs={{0,24},{4,28},{8,16},{12,20},{16,8},{20,12},{24,0},{28,4},{1,25},{... | collective-permute-start | bytes 1622024 | tf_op jit(solution)/shard_map/ppermute | solution.py:421
  35.5 0.8 copy-done.2
  36.2 0.0 collective-permute-done.1.refs_2_
  36.3 2.7 %join.1 = (bf16[128,896]{1,0:T(8,128)(2,1)}, bf16[128,896]{1,0:T(8,128)(2,1)}) custom-call(s32[1]{0:T(128)} %bitcast.1.at_ref, bf16[128,1664]{1,0:T(8,128)(2,1)} %get-tuple-element.45.own_ref, bf16[128,1664]{1,0:T(8,128)(2,1)} %collective-permute-done.4.other_ref), custom_call_target="tpu_custom_call" | custom-call | tf_op jit(solution)/shard_map/join/pallas_call | solution.py:463
  38.9 1.4 %collective-permute-start.14 = (bf16[192,1408]{1,0:T(8,128)(2,1)S(1)}, bf16[192,1408]{1,0:T(8,128)(2,1)S(1)}, u32[]{:S(2)}, u32[]{:S(2)}) collective-permute-start(bf16[192,1408]{1,0:T(8,128)(2,1)S(1)} %collective-permute-done.refs_0_), channel_id=1, source_target_pairs={{0,4},{4,0},{8,12},{12,8},{16,20},{20,16},{24,28},{28,24},{1,5},{5... | collective-permute-start | bytes 1622024 | tf_op jit(solution)/shard_map/ppermute | solution.py:424
  40.3 1.5 %collective-permute-start.5 = (bf16[128,896]{1,0:T(8,128)(2,1)}, bf16[128,896]{1,0:T(8,128)(2,1)S(1)}, u32[]{:S(2)}, u32[]{:S(2)}) collective-permute-start(bf16[128,896]{1,0:T(8,128)(2,1)} %get-tuple-element.48), channel_id=1, source_target_pairs={{0,2},{1,3},{2,0},{3,1},{4,6},{5,7},{6,4},{7,5},{8,10},{9,11},{10,... | collective-permute-start | bytes 688136 | tf_op jit(solution)/shard_map/ppermute | solution.py:418
  41.8 5.7 %collective-permute-done.5.other_ref = bf16[128,896]{1,0:T(8,128)(2,1)S(1)} collective-permute-done((bf16[128,896]{1,0:T(8,128)(2,1)}, bf16[128,896]{1,0:T(8,128)(2,1)S(1)}, u32[]{:S(2)}, u32[]{:S(2)}) %collective-permute-start.5) | collective-permute-done | bytes 229408 | tf_op jit(solution)/shard_map/ppermute | solution.py:418
  47.6 0.9 copy-done.7
  48.5 1.0 project.1
  49.5 0.8 copy-done.6
  50.3 1.5 %collective-permute-start.6 = (bf16[64,1536]{1,0:T(8,128)(2,1)S(1)}, bf16[64,1536]{1,0:T(8,128)(2,1)S(1)}, u32[]{:S(2)}, u32[]{:S(2)}) collective-permute-start(bf16[64,1536]{1,0:T(8,128)(2,1)S(1)} %get-tuple-element.50), channel_id=1, source_target_pairs={{0,2},{1,3},{2,0},{3,1},{4,6},{5,7},{6,4},{7,5},{8,10},{9,11},{10,... | collective-permute-start | bytes 589832 | tf_op jit(solution)/shard_map/ppermute | solution.py:418
  51.8 0.6 reshape.21.gain_ref
  52.4 0.6 collective-permute-start.10
  52.9 3.0 %collective-permute-done.6.other_ref = bf16[64,1536]{1,0:T(8,128)(2,1)S(1)} collective-permute-done((bf16[64,1536]{1,0:T(8,128)(2,1)S(1)}, bf16[64,1536]{1,0:T(8,128)(2,1)S(1)}, u32[]{:S(2)}, u32[]{:S(2)}) %collective-permute-start.6) | collective-permute-done | bytes 196640 | tf_op jit(solution)/shard_map/ppermute | solution.py:418
  55.9 0.7 copy-done.9
  56.6 2.0 %norm.1 = (bf16[64,1536]{1,0:T(8,128)(2,1)}, bf16[64,1536]{1,0:T(8,128)(2,1)}) custom-call(f32[64,1536]{1,0:T(8,128)} %copy-done.6, bf16[64,1536]{1,0:T(8,128)(2,1)} %copy-done.9, bf16[64,1536]{1,0:T(8,128)(2,1)} %residual_ref.1, f32[1,1536]{1,0:T(1,128)} %reshape.21.gain_ref), custom_call_target="tpu_custom_call" | custom-call | tf_op jit(solution)/shard_map/norm/pallas_call | solution.py:488
  58.6 0.0 collective-permute-done.7.refs_2_
  58.7 0.8 copy-done.4
  59.5 0.6 collective-permute-start.15
  60.0 1.1 collective-permute-start.12
  61.1 1.2 %collective-permute-start.8 = (bf16[64,1536]{1,0:T(8,128)(2,1)}, bf16[64,1536]{1,0:T(8,128)(2,1)S(1)}, u32[]{:S(2)}, u32[]{:S(2)}) collective-permute-start(bf16[64,1536]{1,0:T(8,128)(2,1)} %get-tuple-element.54.refs_0_), channel_id=1, source_target_pairs={{0,24},{4,28},{8,16},{12,20},{16,8},{20,12},{24,0},{28,4},{1,25},{... | collective-permute-start | bytes 589832 | tf_op jit(solution)/shard_map/ppermute | solution.py:421
  62.3 1.5 %collective-permute-start.11 = (bf16[64,1536]{1,0:T(8,128)(2,1)}, bf16[64,1536]{1,0:T(8,128)(2,1)S(1)}, u32[]{:S(2)}, u32[]{:S(2)}) collective-permute-start(bf16[64,1536]{1,0:T(8,128)(2,1)} %get-tuple-element.54.refs_0_), channel_id=1, source_target_pairs={{0,2},{1,3},{2,0},{3,1},{4,6},{5,7},{6,4},{7,5},{8,10},{9,11},{10,... | collective-permute-start | bytes 589832 | tf_op jit(solution)/shard_map/ppermute | solution.py:418
  63.8 3.3 %collective-permute-done.12.refs_0_ = bf16[64,1536]{1,0:T(8,128)(2,1)S(1)} collective-permute-done((bf16[64,1536]{1,0:T(8,128)(2,1)}, bf16[64,1536]{1,0:T(8,128)(2,1)S(1)}, u32[]{:S(2)}, u32[]{:S(2)}) %collective-permute-start.12) | collective-permute-done | bytes 196640 | tf_op jit(solution)/shard_map/ppermute | solution.py:421
  67.1 1.5 %collective-permute-start.13 = (bf16[64,1536]{1,0:T(8,128)(2,1)S(1)}, bf16[64,1536]{1,0:T(8,128)(2,1)S(1)}, u32[]{:S(2)}, u32[]{:S(2)}) collective-permute-start(bf16[64,1536]{1,0:T(8,128)(2,1)S(1)} %collective-permute-done.12.refs_0_), channel_id=1, source_target_pairs={{0,2},{1,3},{2,0},{3,1},{4,6},{5,7},{6,4},{7,5},{8,10},{9,11},{10,... | collective-permute-start | bytes 589832 | tf_op jit(solution)/shard_map/ppermute | solution.py:418
  68.6 1.0 copy-done.3
  69.6 1.3 %place.2.refs_2_ = bf16[768,1408]{1,0:T(8,128)(2,1)S(1)} custom-call(s32[1]{0:T(128)} %bitcast.4.at_ref, bf16[192,1408]{1,0:T(8,128)(2,1)S(1)} %copy-done.1, bf16[192,1408]{1,0:T(8,128)(2,1)S(1)} %copy-done.3, bf16[192,1408]{1,0:T(8,128)(2,1)} %collective-permute-done.1.refs_2_, bf16[192,1408]{1,0:T(8,128)(2,1)S(1)} %collective-permute-done.10.refs_3_), custom_call_target="tpu_custom_call" | custom-call | tf_op jit(solution)/shard_map/place/pallas_call | solution.py:101
  70.9 0.1 collective-permute-start.16
  71.0 0.0 collective-permute-done.8.refs_0_
  71.0 1.8 %collective-permute-done.13.refs_1_ = bf16[64,1536]{1,0:T(8,128)(2,1)S(1)} collective-permute-done((bf16[64,1536]{1,0:T(8,128)(2,1)S(1)}, bf16[64,1536]{1,0:T(8,128)(2,1)S(1)}, u32[]{:S(2)}, u32[]{:S(2)}) %collective-permute-start.13) | collective-permute-done | bytes 196640 | tf_op jit(solution)/shard_map/ppermute | solution.py:418
  72.7 4.0 %collective-permute-done.15.refs_3_ = bf16[192,1408]{1,0:T(8,128)(2,1)S(1)} collective-permute-done((bf16[192,1408]{1,0:T(8,128)(2,1)}, bf16[192,1408]{1,0:T(8,128)(2,1)S(1)}, u32[]{:S(2)}, u32[]{:S(2)}) %collective-permute-start.15) | collective-permute-done | bytes 540704 | tf_op jit(solution)/shard_map/ppermute | solution.py:424
  76.8 1.2 %place.3.refs_3_ = bf16[768,1408]{1,0:T(8,128)(2,1)S(1)} custom-call(s32[1]{0:T(128)} %bitcast.4.at_ref, bf16[192,1408]{1,0:T(8,128)(2,1)S(1)} %collective-permute-done.refs_0_, bf16[192,1408]{1,0:T(8,128)(2,1)S(1)} %copy-done.5, bf16[192,1408]{1,0:T(8,128)(2,1)} %collective-permute-done.7.refs_2_, bf16[192,1408]{1,0:T(8,128)(2,1)S(1)} %collective-permute-done.15.refs_3_), custom_call_target="tpu_custom_call" | custom-call | tf_op jit(solution)/shard_map/place/pallas_call | solution.py:101
  78.0 0.1 collective-permute-start.17
  78.0 0.8 collective-permute-start.9
  78.9 6.5 %collective-permute-done.9.refs_1_ = bf16[64,1536]{1,0:T(8,128)(2,1)S(1)} collective-permute-done((bf16[64,1536]{1,0:T(8,128)(2,1)S(1)}, bf16[64,1536]{1,0:T(8,128)(2,1)S(1)}, u32[]{:S(2)}, u32[]{:S(2)}) %collective-permute-start.9) | collective-permute-done | bytes 196640 | tf_op jit(solution)/shard_map/ppermute | solution.py:418
  85.4 2.0 %feed.4 = (bf16[64,1536]{1,0:T(8,128)(2,1)S(1)}, bf16[64,1536]{1,0:T(8,128)(2,1)S(1)}) custom-call(s32[1]{0:T(128)} %bitcast.2.z_ref, bf16[64,1536]{1,0:T(8,128)(2,1)S(1)} %collective-permute-done.8.refs_0_, bf16[64,1536]{1,0:T(8,128)(2,1)S(1)} %collective-permute-done.9.refs_1_, bf16[768,1408]{1,0:T(8,128)(2,1)S(1)} %place.2.refs_2_, ...), custom_call_target="tpu_custom_call" | custom-call | tf_op jit(solution)/shard_map/feed/pallas_call | solution.py:380
  87.4 0.8 collective-permute-start.18
  88.2 1.0 collective-permute-done.22.refs_0_
  89.2 0.5 collective-permute-start.23
  89.7 2.0 %feed.5 = (bf16[64,1536]{1,0:T(8,128)(2,1)S(1)}, bf16[64,1536]{1,0:T(8,128)(2,1)S(1)}) custom-call(s32[1]{0:T(128)} %bitcast.2.z_ref, bf16[64,1536]{1,0:T(8,128)(2,1)S(1)} %collective-permute-done.12.refs_0_, bf16[64,1536]{1,0:T(8,128)(2,1)S(1)} %collective-permute-done.13.refs_1_, bf16[768,1408]{1,0:T(8,128)(2,1)S(1)} %place.2.refs_2_, ...), custom_call_target="tpu_custom_call" | custom-call | tf_op jit(solution)/shard_map/feed/pallas_call | solution.py:380
  91.8 1.5 %collective-permute-start.20 = (bf16[64,1536]{1,0:T(8,128)(2,1)S(1)}, bf16[64,1536]{1,0:T(8,128)(2,1)S(1)}, u32[]{:S(2)}, u32[]{:S(2)}) collective-permute-start(bf16[64,1536]{1,0:T(8,128)(2,1)S(1)} %get-tuple-element.64), channel_id=1, source_target_pairs={{0,2},{1,3},{2,0},{3,1},{4,6},{5,7},{6,4},{7,5},{8,10},{9,11},{10,... | collective-permute-start | bytes 589832 | tf_op jit(solution)/shard_map/ppermute | solution.py:418
  93.3 2.0 %collective-permute-done.18 = bf16[64,1536]{1,0:T(8,128)(2,1)S(1)} collective-permute-done((bf16[64,1536]{1,0:T(8,128)(2,1)S(1)}, bf16[64,1536]{1,0:T(8,128)(2,1)S(1)}, u32[]{:S(2)}, u32[]{:S(2)}) %collective-permute-start.18) | collective-permute-done | bytes 196640 | tf_op jit(solution)/shard_map/ppermute | solution.py:418
  95.3 0.1 collective-permute-start.19
  95.5 4.0 %collective-permute-done.23.refs_1_ = bf16[64,1536]{1,0:T(8,128)(2,1)S(1)} collective-permute-done((bf16[64,1536]{1,0:T(8,128)(2,1)S(1)}, bf16[64,1536]{1,0:T(8,128)(2,1)S(1)}, u32[]{:S(2)}, u32[]{:S(2)}) %collective-permute-start.23) | collective-permute-done | bytes 196640 | tf_op jit(solution)/shard_map/ppermute | solution.py:418
  99.5 2.0 %feed.6 = (bf16[64,1536]{1,0:T(8,128)(2,1)S(1)}, bf16[64,1536]{1,0:T(8,128)(2,1)S(1)}) custom-call(s32[1]{0:T(128)} %bitcast.2.z_ref, bf16[64,1536]{1,0:T(8,128)(2,1)S(1)} %collective-permute-done.22.refs_0_, bf16[64,1536]{1,0:T(8,128)(2,1)S(1)} %collective-permute-done.23.refs_1_, bf16[768,1408]{1,0:T(8,128)(2,1)S(1)} %place.2.refs_2_, ...), custom_call_target="tpu_custom_call" | custom-call | tf_op jit(solution)/shard_map/feed/pallas_call | solution.py:380
  101.5 0.8 collective-permute-start.24
  102.3 0.7 collective-permute-done.20
  103.1 0.1 collective-permute-start.21
  103.2 2.0 %feed.7 = (bf16[64,1536]{1,0:T(8,128)(2,1)S(1)}, bf16[64,1536]{1,0:T(8,128)(2,1)S(1)}) custom-call(s32[1]{0:T(128)} %bitcast.2.z_ref, bf16[64,1536]{1,0:T(8,128)(2,1)S(1)} %copy-done.8, bf16[64,1536]{1,0:T(8,128)(2,1)S(1)} %collective-permute-done.11.refs_1_, bf16[768,1408]{1,0:T(8,128)(2,1)S(1)} %place.2.refs_2_, bf16[768,1408]{1,0:T(8,128)(2,1)S(1)} %place.3.refs_3_, ...), custom_call_target="tpu_custom_call" | custom-call | tf_op jit(solution)/shard_map/feed/pallas_call | solution.py:380
  105.2 0.8 collective-permute-start.26
  106.0 2.6 %collective-permute-done.24 = bf16[64,1536]{1,0:T(8,128)(2,1)S(1)} collective-permute-done((bf16[64,1536]{1,0:T(8,128)(2,1)S(1)}, bf16[64,1536]{1,0:T(8,128)(2,1)S(1)}, u32[]{:S(2)}, u32[]{:S(2)}) %collective-permute-start.24) | collective-permute-done | bytes 196640 | tf_op jit(solution)/shard_map/ppermute | solution.py:418
  108.6 0.1 collective-permute-start.25
  108.7 0.9 collective-permute-done.21
  109.6 1.8 %collective-permute-done.26 = bf16[64,1536]{1,0:T(8,128)(2,1)S(1)} collective-permute-done((bf16[64,1536]{1,0:T(8,128)(2,1)S(1)}, bf16[64,1536]{1,0:T(8,128)(2,1)S(1)}, u32[]{:S(2)}, u32[]{:S(2)}) %collective-permute-start.26) | collective-permute-done | bytes 196640 | tf_op jit(solution)/shard_map/ppermute | solution.py:418
  111.5 4.9 %collective-permute-done.25 = bf16[64,1536]{1,0:T(8,128)(2,1)S(1)} collective-permute-done((bf16[64,1536]{1,0:T(8,128)(2,1)S(1)}, bf16[64,1536]{1,0:T(8,128)(2,1)S(1)}, u32[]{:S(2)}, u32[]{:S(2)}) %collective-permute-start.25) | collective-permute-done | bytes 196640 | tf_op jit(solution)/shard_map/ppermute | solution.py:421
  116.3 0.8 add_convert_fusion
  (30 shorter events, 0.2 us)
Async XLA Ops:
  2.9 33.3 %collective-permute-start.3 = (bf16[384,1536]{1,0:T(8,128)(2,1)}, bf16[384,1536]{1,0:T(8,128)(2,1)S(1)}, u32[]{:S(2)}, u32[]{:S(2)}) collective-permute-start(bf16[384,1536]{1,0:T(8,128)(2,1)} %w0.1), channel_id=1, source_target_pairs={{0,1},{1,0},{2,3},{3,2},{4,5},{5,4},{6,7},{7,6},{8,9},{9,8},{10,11... | collective-permute-start | bytes 3538952 | tf_op jit(solution)/shard_map/ppermute | solution.py:418
  3.5 28.4 %collective-permute-start = (bf16[192,1408]{1,0:T(8,128)(2,1)}, bf16[192,1408]{1,0:T(8,128)(2,1)S(1)}, u32[]{:S(2)}, u32[]{:S(2)}) collective-permute-start(bf16[192,1408]{1,0:T(8,128)(2,1)} %get-tuple-element.38), channel_id=1, source_target_pairs={{0,16},{4,20},{8,24},{12,28},{16,0},{20,4},{24,8},{28,12},{1,17},{... | collective-permute-start | bytes 1622024 | tf_op jit(solution)/shard_map/ppermute | solution.py:421
  7.1 28.3 %collective-permute-start.2 = (bf16[192,1408]{1,0:T(8,128)(2,1)}, bf16[192,1408]{1,0:T(8,128)(2,1)S(1)}, u32[]{:S(2)}, u32[]{:S(2)}) collective-permute-start(bf16[192,1408]{1,0:T(8,128)(2,1)} %get-tuple-element.40.refs_0_), channel_id=1, source_target_pairs={{0,4},{4,0},{8,12},{12,8},{16,20},{20,16},{24,28},{28,24},{1,5},{5... | collective-permute-start | bytes 1622024 | tf_op jit(solution)/shard_map/ppermute | solution.py:424
  8.6 27.6 %collective-permute-start.1 = (bf16[192,1408]{1,0:T(8,128)(2,1)}, bf16[192,1408]{1,0:T(8,128)(2,1)}, u32[]{:S(2)}, u32[]{:S(2)}) collective-permute-start(bf16[192,1408]{1,0:T(8,128)(2,1)} %get-tuple-element.39), channel_id=1, source_target_pairs={{0,8},{4,12},{8,0},{12,4},{16,24},{20,28},{24,16},{28,20},{1,9},{5... | collective-permute-start | bytes 1622024 | tf_op jit(solution)/shard_map/ppermute | solution.py:421
  10.2 37.4 %copy-start = (bf16[384,1536]{1,0:T(8,128)(2,1)S(1)}, bf16[384,1536]{1,0:T(8,128)(2,1)}, u32[]{:S(2)}) copy-start(bf16[384,1536]{1,0:T(8,128)(2,1)} %w0.1) | copy-start | bytes 3538948
  25.7 26.0 %copy-start.11 = (f32[1536]{0:T(1024)S(1)}, f32[1536]{0:T(1024)}, u32[]{:S(2)}) copy-start(f32[1536]{0:T(1024)} %param.16) | copy-start | bytes 18436
  25.8 10.5 %collective-permute-start.4 = (bf16[128,1664]{1,0:T(8,128)(2,1)}, bf16[128,1664]{1,0:T(8,128)(2,1)}, u32[]{:S(2)}, u32[]{:S(2)}) collective-permute-start(bf16[128,1664]{1,0:T(8,128)(2,1)} %get-tuple-element.46), channel_id=1, source_target_pairs={{0,1},{1,0},{2,3},{3,2},{4,5},{5,4},{6,7},{7,6},{8,9},{9,8},{10,11... | collective-permute-start | bytes 1277960 | tf_op jit(solution)/shard_map/ppermute | solution.py:418
  31.9 26.8 %collective-permute-start.7 = (bf16[192,1408]{1,0:T(8,128)(2,1)}, bf16[192,1408]{1,0:T(8,128)(2,1)}, u32[]{:S(2)}, u32[]{:S(2)}) collective-permute-start(bf16[192,1408]{1,0:T(8,128)(2,1)} %get-tuple-element.53), channel_id=1, source_target_pairs={{0,24},{4,28},{8,16},{12,20},{16,8},{20,12},{24,0},{28,4},{1,25},{... | collective-permute-start | bytes 1622024 | tf_op jit(solution)/shard_map/ppermute | solution.py:421
  35.4 0.8 copy-start.2
  36.3 32.3 %copy-start.1 = (bf16[192,1408]{1,0:T(8,128)(2,1)S(1)}, bf16[192,1408]{1,0:T(8,128)(2,1)}, u32[]{:S(2)}) copy-start(bf16[192,1408]{1,0:T(8,128)(2,1)} %get-tuple-element.40.refs_0_) | copy-start | bytes 1622020
  38.9 19.7 %collective-permute-start.14 = (bf16[192,1408]{1,0:T(8,128)(2,1)S(1)}, bf16[192,1408]{1,0:T(8,128)(2,1)S(1)}, u32[]{:S(2)}, u32[]{:S(2)}) collective-permute-start(bf16[192,1408]{1,0:T(8,128)(2,1)S(1)} %collective-permute-done.refs_0_), channel_id=1, source_target_pairs={{0,4},{4,0},{8,12},{12,8},{16,20},{20,16},{24,28},{28,24},{1,5},{5... | collective-permute-start | bytes 1622024 | tf_op jit(solution)/shard_map/ppermute | solution.py:424
  40.3 7.2 %collective-permute-start.5 = (bf16[128,896]{1,0:T(8,128)(2,1)}, bf16[128,896]{1,0:T(8,128)(2,1)S(1)}, u32[]{:S(2)}, u32[]{:S(2)}) collective-permute-start(bf16[128,896]{1,0:T(8,128)(2,1)} %get-tuple-element.48), channel_id=1, source_target_pairs={{0,2},{1,3},{2,0},{3,1},{4,6},{5,7},{6,4},{7,5},{8,10},{9,11},{10,... | collective-permute-start | bytes 688136 | tf_op jit(solution)/shard_map/ppermute | solution.py:418
  47.6 0.9 copy-start.7
  49.5 0.8 copy-start.6
  50.3 5.7 %collective-permute-start.6 = (bf16[64,1536]{1,0:T(8,128)(2,1)S(1)}, bf16[64,1536]{1,0:T(8,128)(2,1)S(1)}, u32[]{:S(2)}, u32[]{:S(2)}) collective-permute-start(bf16[64,1536]{1,0:T(8,128)(2,1)S(1)} %get-tuple-element.50), channel_id=1, source_target_pairs={{0,2},{1,3},{2,0},{3,1},{4,6},{5,7},{6,4},{7,5},{8,10},{9,11},{10,... | collective-permute-start | bytes 589832 | tf_op jit(solution)/shard_map/ppermute | solution.py:418
  52.4 16.2 %collective-permute-start.10 = (bf16[192,1408]{1,0:T(8,128)(2,1)}, bf16[192,1408]{1,0:T(8,128)(2,1)S(1)}, u32[]{:S(2)}, u32[]{:S(2)}) collective-permute-start(bf16[192,1408]{1,0:T(8,128)(2,1)} %collective-permute-done.1.refs_2_), channel_id=1, source_target_pairs={{0,4},{4,0},{8,12},{12,8},{16,20},{20,16},{24,28},{28,24},{1,5},{5... | collective-permute-start | bytes 1622024 | tf_op jit(solution)/shard_map/ppermute | solution.py:424
  55.9 0.7 copy-start.9
  58.7 0.8 copy-start.4
  59.5 17.3 %collective-permute-start.15 = (bf16[192,1408]{1,0:T(8,128)(2,1)}, bf16[192,1408]{1,0:T(8,128)(2,1)S(1)}, u32[]{:S(2)}, u32[]{:S(2)}) collective-permute-start(bf16[192,1408]{1,0:T(8,128)(2,1)} %collective-permute-done.7.refs_2_), channel_id=1, source_target_pairs={{0,4},{4,0},{8,12},{12,8},{16,20},{20,16},{24,28},{28,24},{1,5},{5... | collective-permute-start | bytes 1622024 | tf_op jit(solution)/shard_map/ppermute | solution.py:424
  60.0 7.0 %collective-permute-start.12 = (bf16[64,1536]{1,0:T(8,128)(2,1)}, bf16[64,1536]{1,0:T(8,128)(2,1)S(1)}, u32[]{:S(2)}, u32[]{:S(2)}) collective-permute-start(bf16[64,1536]{1,0:T(8,128)(2,1)} %get-tuple-element.54.refs_0_), channel_id=1, source_target_pairs={{0,8},{4,12},{8,0},{12,4},{16,24},{20,28},{24,16},{28,20},{1,9},{5... | collective-permute-start | bytes 589832 | tf_op jit(solution)/shard_map/ppermute | solution.py:421
  61.1 9.8 %collective-permute-start.8 = (bf16[64,1536]{1,0:T(8,128)(2,1)}, bf16[64,1536]{1,0:T(8,128)(2,1)S(1)}, u32[]{:S(2)}, u32[]{:S(2)}) collective-permute-start(bf16[64,1536]{1,0:T(8,128)(2,1)} %get-tuple-element.54.refs_0_), channel_id=1, source_target_pairs={{0,24},{4,28},{8,16},{12,20},{16,8},{20,12},{24,0},{28,4},{1,25},{... | collective-permute-start | bytes 589832 | tf_op jit(solution)/shard_map/ppermute | solution.py:421
  62.3 8.7 %collective-permute-start.11 = (bf16[64,1536]{1,0:T(8,128)(2,1)}, bf16[64,1536]{1,0:T(8,128)(2,1)S(1)}, u32[]{:S(2)}, u32[]{:S(2)}) collective-permute-start(bf16[64,1536]{1,0:T(8,128)(2,1)} %get-tuple-element.54.refs_0_), channel_id=1, source_target_pairs={{0,2},{1,3},{2,0},{3,1},{4,6},{5,7},{6,4},{7,5},{8,10},{9,11},{10,... | collective-permute-start | bytes 589832 | tf_op jit(solution)/shard_map/ppermute | solution.py:418
  67.1 5.7 %collective-permute-start.13 = (bf16[64,1536]{1,0:T(8,128)(2,1)S(1)}, bf16[64,1536]{1,0:T(8,128)(2,1)S(1)}, u32[]{:S(2)}, u32[]{:S(2)}) collective-permute-start(bf16[64,1536]{1,0:T(8,128)(2,1)S(1)} %collective-permute-done.12.refs_0_), channel_id=1, source_target_pairs={{0,2},{1,3},{2,0},{3,1},{4,6},{5,7},{6,4},{7,5},{8,10},{9,11},{10,... | collective-permute-start | bytes 589832 | tf_op jit(solution)/shard_map/ppermute | solution.py:418
  68.6 1.0 copy-start.3
  69.6 7.2 %copy-start.5 = (bf16[192,1408]{1,0:T(8,128)(2,1)S(1)}, bf16[192,1408]{1,0:T(8,128)(2,1)}, u32[]{:S(2)}) copy-start(bf16[192,1408]{1,0:T(8,128)(2,1)} %copy-done.4) | copy-start | bytes 1622020
  70.9 8.0 %copy-start.8 = (bf16[64,1536]{1,0:T(8,128)(2,1)S(1)}, bf16[64,1536]{1,0:T(8,128)(2,1)}, u32[]{:S(2)}) copy-start(bf16[64,1536]{1,0:T(8,128)(2,1)} %get-tuple-element.54.refs_0_) | copy-start | bytes 589828
  70.9 14.5 %collective-permute-start.16 = (bf16[768,1408]{1,0:T(8,128)(2,1)S(1)}, bf16[768,1408]{1,0:T(8,128)(2,1)S(1)}, u32[]{:S(2)}, u32[]{:S(2)}) collective-permute-start(bf16[768,1408]{1,0:T(8,128)(2,1)S(1)} %place.2.refs_2_), channel_id=1, source_target_pairs={{0,1},{1,0},{2,3},{3,2},{4,5},{5,4},{6,7},{7,6},{8,9},{9,8},{10,11... | collective-permute-start | bytes 6488072 | tf_op jit(solution)/shard_map/ppermute | solution.py:418
  78.0 7.4 %collective-permute-start.17 = (bf16[768,1408]{1,0:T(8,128)(2,1)S(1)}, bf16[768,1408]{1,0:T(8,128)(2,1)S(1)}, u32[]{:S(2)}, u32[]{:S(2)}) collective-permute-start(bf16[768,1408]{1,0:T(8,128)(2,1)S(1)} %place.3.refs_3_), channel_id=1, source_target_pairs={{0,1},{1,0},{2,3},{3,2},{4,5},{5,4},{6,7},{7,6},{8,9},{9,8},{10,11... | collective-permute-start | bytes 6488072 | tf_op jit(solution)/shard_map/ppermute | solution.py:418
  78.0 7.3 %collective-permute-start.9 = (bf16[64,1536]{1,0:T(8,128)(2,1)S(1)}, bf16[64,1536]{1,0:T(8,128)(2,1)S(1)}, u32[]{:S(2)}, u32[]{:S(2)}) collective-permute-start(bf16[64,1536]{1,0:T(8,128)(2,1)S(1)} %collective-permute-done.8.refs_0_), channel_id=1, source_target_pairs={{0,2},{1,3},{2,0},{3,1},{4,6},{5,7},{6,4},{7,5},{8,10},{9,11},{10,... | collective-permute-start | bytes 589832 | tf_op jit(solution)/shard_map/ppermute | solution.py:418
  78.9 10.4 %collective-permute-start.22 = (bf16[64,1536]{1,0:T(8,128)(2,1)S(1)}, bf16[64,1536]{1,0:T(8,128)(2,1)S(1)}, u32[]{:S(2)}, u32[]{:S(2)}) collective-permute-start(bf16[64,1536]{1,0:T(8,128)(2,1)S(1)} %copy-done.8), channel_id=1, source_target_pairs={{0,16},{4,20},{8,24},{12,28},{16,0},{20,4},{24,8},{28,12},{1,17},{... | collective-permute-start | bytes 589832 | tf_op jit(solution)/shard_map/ppermute | solution.py:421
  87.4 7.9 %collective-permute-start.18 = (bf16[64,1536]{1,0:T(8,128)(2,1)S(1)}, bf16[64,1536]{1,0:T(8,128)(2,1)S(1)}, u32[]{:S(2)}, u32[]{:S(2)}) collective-permute-start(bf16[64,1536]{1,0:T(8,128)(2,1)S(1)} %get-tuple-element.61), channel_id=1, source_target_pairs={{0,2},{1,3},{2,0},{3,1},{4,6},{5,7},{6,4},{7,5},{8,10},{9,11},{10,... | collective-permute-start | bytes 589832 | tf_op jit(solution)/shard_map/ppermute | solution.py:418
  89.2 10.3 %collective-permute-start.23 = (bf16[64,1536]{1,0:T(8,128)(2,1)S(1)}, bf16[64,1536]{1,0:T(8,128)(2,1)S(1)}, u32[]{:S(2)}, u32[]{:S(2)}) collective-permute-start(bf16[64,1536]{1,0:T(8,128)(2,1)S(1)} %collective-permute-done.22.refs_0_), channel_id=1, source_target_pairs={{0,2},{1,3},{2,0},{3,1},{4,6},{5,7},{6,4},{7,5},{8,10},{9,11},{10,... | collective-permute-start | bytes 589832 | tf_op jit(solution)/shard_map/ppermute | solution.py:418
  91.8 11.3 %collective-permute-start.20 = (bf16[64,1536]{1,0:T(8,128)(2,1)S(1)}, bf16[64,1536]{1,0:T(8,128)(2,1)S(1)}, u32[]{:S(2)}, u32[]{:S(2)}) collective-permute-start(bf16[64,1536]{1,0:T(8,128)(2,1)S(1)} %get-tuple-element.64), channel_id=1, source_target_pairs={{0,2},{1,3},{2,0},{3,1},{4,6},{5,7},{6,4},{7,5},{8,10},{9,11},{10,... | collective-permute-start | bytes 589832 | tf_op jit(solution)/shard_map/ppermute | solution.py:418
  95.3 7.8 %collective-permute-start.19 = (bf16[64,1536]{1,0:T(8,128)(2,1)S(1)}, bf16[64,1536]{1,0:T(8,128)(2,1)S(1)}, u32[]{:S(2)}, u32[]{:S(2)}) collective-permute-start(bf16[64,1536]{1,0:T(8,128)(2,1)S(1)} %add_convert_fusion.4), channel_id=1, source_target_pairs={{0,24},{4,28},{8,16},{12,20},{16,8},{20,12},{24,0},{28,4},{1,25},{... | collective-permute-start | bytes 589832 | tf_op jit(solution)/shard_map/ppermute | solution.py:421
  101.5 7.1 %collective-permute-start.24 = (bf16[64,1536]{1,0:T(8,128)(2,1)S(1)}, bf16[64,1536]{1,0:T(8,128)(2,1)S(1)}, u32[]{:S(2)}, u32[]{:S(2)}) collective-permute-start(bf16[64,1536]{1,0:T(8,128)(2,1)S(1)} %get-tuple-element.67), channel_id=1, source_target_pairs={{0,2},{1,3},{2,0},{3,1},{4,6},{5,7},{6,4},{7,5},{8,10},{9,11},{10,... | collective-permute-start | bytes 589832 | tf_op jit(solution)/shard_map/ppermute | solution.py:418
  103.1 6.5 %collective-permute-start.21 = (bf16[64,1536]{1,0:T(8,128)(2,1)S(1)}, bf16[64,1536]{1,0:T(8,128)(2,1)S(1)}, u32[]{:S(2)}, u32[]{:S(2)}) collective-permute-start(bf16[64,1536]{1,0:T(8,128)(2,1)S(1)} %add_convert_fusion.3), channel_id=1, source_target_pairs={{0,8},{4,12},{8,0},{12,4},{16,24},{20,28},{24,16},{28,20},{1,9},{5... | collective-permute-start | bytes 589832 | tf_op jit(solution)/shard_map/ppermute | solution.py:421
  103.2 13.1 %copy-start.10 = (bf16[64,1536]{1,0:T(8,128)(2,1)S(1)}, bf16[64,1536]{1,0:T(8,128)(2,1)}, u32[]{:S(2)}) copy-start(bf16[64,1536]{1,0:T(8,128)(2,1)} %get-tuple-element.51) | copy-start | bytes 589828
  105.2 6.3 %collective-permute-start.26 = (bf16[64,1536]{1,0:T(8,128)(2,1)S(1)}, bf16[64,1536]{1,0:T(8,128)(2,1)S(1)}, u32[]{:S(2)}, u32[]{:S(2)}) collective-permute-start(bf16[64,1536]{1,0:T(8,128)(2,1)S(1)} %get-tuple-element.70), channel_id=1, source_target_pairs={{0,2},{1,3},{2,0},{3,1},{4,6},{5,7},{6,4},{7,5},{8,10},{9,11},{10,... | collective-permute-start | bytes 589832 | tf_op jit(solution)/shard_map/ppermute | solution.py:418
  108.6 7.7 %collective-permute-start.25 = (bf16[64,1536]{1,0:T(8,128)(2,1)S(1)}, bf16[64,1536]{1,0:T(8,128)(2,1)S(1)}, u32[]{:S(2)}, u32[]{:S(2)}) collective-permute-start(bf16[64,1536]{1,0:T(8,128)(2,1)S(1)} %add_convert_fusion.2), channel_id=1, source_target_pairs={{0,16},{4,20},{8,24},{12,28},{16,0},{20,4},{24,8},{28,12},{1,17},{... | collective-permute-start | bytes 589832 | tf_op jit(solution)/shard_map/ppermute | solution.py:421
